TPU v7x, 32 devices: a whole 2x2x4 slice. The times are simulated.
32 devices in a mesh: load: 4 (over y, x), gz: 8 (over z, core).
Axes of the slice: x: 2, y: 2, z: 4, core: 2. Of those that a mesh axis runs over, the one named last changes fastest.
Arguments:
- density: float32 [16, 32, 128], P('gz', 'load'), may hold values from 0.1 to 1
- labels: int32 [16, 32, 128], P('gz'), may hold values from 0 to 11
- forces: float32 [8, 3, 16, 32, 128], P('load', None, 'gz'), may hold values from -6 to 6
- case_weights: int32 [8], replicated, may hold values from 1 to 4
Outputs:
- new_density: float32 [16, 32, 128], P('gz', 'load')
- displacement: float32 [8, 3, 16, 32, 128], P('load', None, 'gz')
All inputs are finite; a program needn't handle non-finite values.
Results may differ from a plain program's by a relative error of at most 0.00016.
Values sent between devices are 32-bit elements; how exact they have to be, the bound alone decides.
No kernel may reach another device: no remote copies, remote signals or barrier semaphores. Data moves between devices by JAX's collectives and lax.ppermute only.
A program may use at most 64 MiB of HBM per device.

v0:
```python
import jax
import jax.numpy as jnp
import numpy as np
from jax import lax
from jax.sharding import PartitionSpec as P

SWEEPS = 3


EMIN = 0.001
LOWER_EIG = 0.1
UPPER_EIG = 2.5
MOVE_LIMIT = 0.2
FLOOR_DENSITY = 0.001
CORNER_OFFSETS = [(corner // 4, corner // 2 % 2, corner % 2) for corner in range(8)]


def with_halo(cells, sides, width):
    for axis, dim in sides:
        count = lax.axis_size(axis)
        ends = count - 1
        head = lax.slice_in_dim(cells, 0, width, axis=dim)
        tail = lax.slice_in_dim(cells, cells.shape[dim] - width, cells.shape[dim], axis=dim)
        cells = jnp.concatenate(
            [
                lax.ppermute(tail, axis, [(i, (i + 1) % count) for i in range(ends)]),
                cells,
                lax.ppermute(head, axis, [((i + 1) % count, i) for i in range(ends)]),
            ],
            axis=dim,
        )
    return cells


def passed_along(block, axis, distance):
    devices = range(lax.axis_size(axis))
    route = [(i - distance, i) for i in devices if i - distance in devices]
    return lax.ppermute(block, axis, route)


def element_matrix():
    poisson = 0.3
    lame_first = poisson / ((1 + poisson) * (1 - 2 * poisson))
    shear_modulus = 1.0 / (2 * (1 + poisson))
    elastic = np.zeros((6, 6))
    elastic[:3, :3] = lame_first
    for which in range(3):
        elastic[which, which] += 2 * shear_modulus
        elastic[which + 3, which + 3] = shear_modulus
    points = [0.5 - 0.5 / np.sqrt(3.0), 0.5 + 0.5 / np.sqrt(3.0)]
    result = np.zeros((24, 24))
    for point_z in points:
        for point_y in points:
            for point_x in points:
                strain = np.zeros((6, 24))
                for corner in range(8):
                    corner_z, corner_y, corner_x = CORNER_OFFSETS[corner]
                    along_x = point_x if corner_x else 1.0 - point_x
                    along_y = point_y if corner_y else 1.0 - point_y
                    along_z = point_z if corner_z else 1.0 - point_z
                    sign_x = 1.0 if corner_x else -1.0
                    sign_y = 1.0 if corner_y else -1.0
                    sign_z = 1.0 if corner_z else -1.0
                    grad_x = sign_x * along_y * along_z
                    grad_y = sign_y * along_x * along_z
                    grad_z = sign_z * along_x * along_y
                    column = 3 * corner
                    strain[0, column] = grad_x
                    strain[1, column + 1] = grad_y
                    strain[2, column + 2] = grad_z
                    strain[3, column] = grad_y
                    strain[3, column + 1] = grad_x
                    strain[4, column + 1] = grad_z
                    strain[4, column + 2] = grad_y
                    strain[5, column] = grad_z
                    strain[5, column + 2] = grad_x
                result += strain.T @ elastic @ strain / 8.0
    return result


def corner_views(padded, layers, rows, columns):
    views = []
    for shift_z, shift_y, shift_x in CORNER_OFFSETS:
        views.append(
            padded[
                :,
                :,
                shift_z : shift_z + layers,
                shift_y : shift_y + rows,
                shift_x : shift_x + columns,
            ]
        )
    return views


def element_forces(views, stiffness, scale):
    stacked = jnp.concatenate(views, axis=1)
    product = (
        jnp.einsum("ij,bjzyx->bizyx", stiffness, stacked, precision=lax.Precision.HIGHEST) * scale
    )
    return [product[:, 3 * target : 3 * target + 3] for target in range(8)]


def assemble(weighted, first, layers):
    total = None
    for target in range(8):
        shift_z, shift_y, shift_x = CORNER_OFFSETS[target]
        piece = weighted[target]
        rows = piece.shape[3]
        columns = piece.shape[4]
        padded = jnp.pad(piece, ((0, 0), (0, 0), (1, 1), (1, 0), (1, 0)))
        part_sum = padded[
            :,
            :,
            first - shift_z : first - shift_z + layers,
            1 - shift_y : 1 - shift_y + rows,
            1 - shift_x : 1 - shift_x + columns,
        ]
        total = part_sum if total is None else total + part_sum
    return total


def smooth(padded, layers, rows, columns):
    total = None
    for off_z in (-1, 0, 1):
        for off_y in (-1, 0, 1):
            for off_x in (-1, 0, 1):
                weight = 1.5 - float(np.sqrt(off_z * off_z + off_y * off_y + off_x * off_x))
                if weight > 0:
                    term = (
                        weight
                        * padded[
                            1 + off_z : 1 + off_z + layers,
                            1 + off_y : 1 + off_y + rows,
                            1 + off_x : 1 + off_x + columns,
                        ]
                    )
                    total = term if total is None else total + term
    return total


def pad_plane(field):
    return jnp.pad(field, ((0, 0), (0, 0), (0, 0), (0, 1), (0, 1)))


def apply_stiffness(field, stiffness, scale_ext):
    layers = field.shape[2]
    rows = field.shape[3]
    columns = field.shape[4]
    padded = pad_plane(with_halo(field, (("gz", 2),), 1))
    views = corner_views(padded, layers + 1, rows, columns)
    return assemble(element_forces(views, stiffness, scale_ext), 2, layers)


def on_device(density, labels, forces, case_weights):
    stiffness = jnp.asarray(element_matrix(), jnp.float32)
    cases = forces.shape[0]
    layers = forces.shape[2]
    rows = forces.shape[3]
    columns = forces.shape[4]
    own_rows = density.shape[1]
    dense_full = lax.all_gather(density, "load", axis=1, tiled=True)
    solid = jnp.where(labels == 2, jnp.float32(1.0), dense_full)
    moduli = EMIN + (1.0 - EMIN) * solid * solid * solid
    below = passed_along(moduli[-1:], "gz", 1)
    moduli_ext = jnp.concatenate([below, moduli], axis=0)
    scale_ext = moduli_ext[None, None]
    free = (labels != 1).astype(jnp.float32)[None, None]
    diag_terms = []
    for target in range(8):
        entries = jnp.stack([stiffness[3 * target + comp, 3 * target + comp] for comp in range(3)])
        diag_terms.append(entries[None, :, None, None, None] * scale_ext)
    diagonal = assemble(diag_terms, 2, layers)
    inverse_diag = free / diagonal
    theta = 0.5 * (UPPER_EIG + LOWER_EIG)
    delta = 0.5 * (UPPER_EIG - LOWER_EIG)
    sigma = theta / delta
    residual = forces * free
    step_dir = inverse_diag * residual / theta
    solution = step_dir
    factor = 1.0 / sigma
    for sweep in range(SWEEPS):
        residual = residual - free * jnp.concatenate(
            [
                apply_stiffness(step_dir[case : case + 1], stiffness, scale_ext)
                for case in range(cases)
            ],
            axis=0,
        )
        next_factor = 1.0 / (2.0 * sigma - factor)
        step_dir = (
            next_factor * factor * step_dir + 2.0 * next_factor / delta * inverse_diag * residual
        )
        solution = solution + step_dir
        factor = next_factor
    above = passed_along(solution[:, :, :1], "gz", -1)
    views = corner_views(
        pad_plane(jnp.concatenate([solution, above], axis=2)), layers, rows, columns
    )
    pushed = element_forces(views, stiffness, jnp.float32(1.0))
    energy = None
    for target in range(8):
        term = jnp.sum(views[target] * pushed[target], axis=1)
        energy = term if energy is None else energy + term
    weights_all = case_weights.astype(jnp.float32)
    weights_own = lax.dynamic_slice_in_dim(weights_all, lax.axis_index("load") * cases, cases, 0)
    weighted = jnp.sum(weights_own[:, None, None, None] * energy, axis=0) / jnp.sum(weights_all)
    term_local = 3.0 * (1.0 - EMIN) * solid * solid * weighted
    row_start = lax.axis_index("load") * own_rows
    cell_count = layers * lax.axis_size("gz") * rows * columns
    own_sens = lax.psum_scatter(term_local, "load", scatter_dimension=1, tiled=True)
    numer_rim, denom_rim = (
        with_halo(density * own_sens, (("load", 1), ("gz", 0)), 1),
        with_halo(density, (("load", 1), ("gz", 0)), 1),
    )
    numer_rim = jnp.pad(numer_rim, ((0, 0), (0, 0), (1, 1)))
    denom_rim = jnp.pad(denom_rim, ((0, 0), (0, 0), (1, 1)))
    filtered = smooth(numer_rim, layers, own_rows, columns) / smooth(
        denom_rim, layers, own_rows, columns
    )
    total = lax.psum(jnp.sum(filtered), ("load", "gz"))
    mean_value = total / cell_count
    own_labels = lax.dynamic_slice_in_dim(labels, row_start, own_rows, 1)
    candidate = density * jnp.sqrt(filtered / mean_value)
    lower = jnp.maximum(density - MOVE_LIMIT, FLOOR_DENSITY)
    upper = jnp.minimum(density + MOVE_LIMIT, 1.0)
    new_density = jnp.clip(candidate, lower, upper)
    new_density = jnp.where(own_labels == 2, jnp.float32(1.0), new_density)
    return (new_density, solution)


def solution(mesh):
    return jax.shard_map(
        on_device,
        mesh=mesh,
        in_specs=(
            P("gz", "load", None),
            P("gz", None, None),
            P("load", None, "gz", None, None),
            P(),
        ),
        out_specs=(P("gz", "load", None), P("load", None, "gz", None, None)),
        check_vma=False,
    )
```

profile of v0, /device:TPU:0, one launch (start us, length us, event | category | flops | bytes accessed | tf_op | source)
XLA Modules:
  0.0 242.8 jit_solution(4110546272236609909)
XLA Ops:
  7.2 9.8 %all_gather.3 = f32[2,32,128]{2,1,0:T(8,128)S(1)} all-gather(f32[2,8,128]{2,1,0:T(8,128)} %param.5), channel_id=1, replica_groups=mesh['load'=4,'gz'=8] {'load'}, dimensions={1}, use_global_device_ids=true | all-gather | bytes 40960 | tf_op jit(solution)/shard_map/all_gather | solution.py:162
  17.0 0.8 fusion.80
  17.8 1.3 collective-permute-start
  19.1 0.8 fusion.153
  19.9 3.2 %collective-permute-start.18 = (f32[2,1,128]{2,1,0:T(1,128)S(1)}, f32[2,1,128]{2,1,0:T(1,128)S(1)}, u32[]{:S(2)}, u32[]{:S(2)}) collective-permute-start(f32[2,1,128]{2,1,0:T(1,128)S(1)} %get-tuple-element.141), channel_id=1, source_target_pairs={{0,8},{8,16},{16,24},{1,9},{9,17},{17,25},{2,10},{10,18},{18,26},{... | collective-permute-start | bytes 3080 | tf_op jit(solution)/shard_map/ppermute | solution.py:26
  23.2 0.8 compare_convert_fusion
  23.9 1.3 convert_reduce_fusion
  26.5 1.5 broadcast_multiply_fusion.3
  28.0 1.1 fusion.35
  29.2 3.9 %collective-permute-start.1 = (f32[1,3,1,32,128]{4,1,3,2,0:T(4,128)S(1)}, f32[1,3,1,32,128]{4,1,3,2,0:T(4,128)S(1)}, u32[]{:S(2)}, u32[]{:S(2)}) collective-permute-start(f32[1,3,1,32,128]{4,1,3,2,0:T(4,128)S(1)} %get-tuple-element.112), channel_id=1, source_target_pairs={{0,1},{1,2},{2,3},{3,4},{4,5},{5,6},{6,7},{8,9},{9,10},{10,11},{11... | collective-permute-start | bytes 147464 | tf_op jit(solution)/shard_map/ppermute | solution.py:26
  33.2 1.3 collective-permute-start.2
  34.5 3.0 %collective-permute-start.3 = (f32[1,3,1,32,128]{4,1,3,2,0:T(4,128)S(1)}, f32[1,3,1,32,128]{4,1,3,2,0:T(4,128)S(1)}, u32[]{:S(2)}, u32[]{:S(2)}) collective-permute-start(f32[1,3,1,32,128]{4,1,3,2,0:T(4,128)S(1)} %get-tuple-element.111), channel_id=1, source_target_pairs={{0,1},{1,2},{2,3},{3,4},{4,5},{5,6},{6,7},{8,9},{9,10},{10,11},{11... | collective-permute-start | bytes 147464 | tf_op jit(solution)/shard_map/ppermute | solution.py:26
  37.5 1.3 collective-permute-start.4
  38.8 1.3 collective-permute-start.19
  40.2 1.5 collective-permute-done.4
  41.9 1.2 fusion.142
  43.1 1.0 pad_maximum_fusion.2
  44.3 3.8 %concatenate.138 = f32[1,24,3,32,128]{4,1,3,2,0:T(8,128)S(1)} concatenate(f32[1,3,3,32,128]{4,1,3,2,0:T(4,128)} %get-tuple-element.124, f32[1,3,3,32,128]{4,1,3,2,0:T(4,128)S(1)} %copy-done.16, f32[1,3,3,32,128]{4,1,3,2,0:T(4,128)S(1)} %copy-done.15, f32[1,3,3,32,128]{4,1,3,2,0:T(4,128)S(1)} %get-tuple-element.82, f32[1,3,3,32,128]{4,1,3,2,0:T(4,128)} %get-tuple-element.123, ...), dimensions={1} | concatenate | bytes 2359296 | tf_op jit(solution)/shard_map/concatenate | solution.py:97
  48.1 1.1 fusion.1
  49.3 1.1 fusion.136
  50.3 1.4 fusion.143
  51.7 9.3 %concatenate.142 = f32[1,24,3,32,128]{4,1,3,2,0:T(8,128)S(1)} concatenate(f32[1,3,3,32,128]{4,1,3,2,0:T(4,128)} %get-tuple-element.145, f32[1,3,3,32,128]{4,1,3,2,0:T(4,128)} %get-tuple-element.90, f32[1,3,3,32,128]{4,1,3,2,0:T(4,128)} %get-tuple-element.89, f32[1,3,3,32,128]{4,1,3,2,0:T(4,128)} %get-tuple-element.88, f32[1,3,3,32,128]{4,1,3,2,0:T(4,128)} %get-tuple-element.146, ...), dimensions={1} | concatenate | bytes 2359296 | tf_op jit(solution)/shard_map/concatenate | solution.py:97
  61.1 1.1 fusion.3
  65.4 4.8 %collective-permute-start.5 = (f32[1,3,1,32,128]{4,1,3,2,0:T(4,128)S(1)}, f32[1,3,1,32,128]{4,1,3,2,0:T(4,128)S(1)}, u32[]{:S(2)}, u32[]{:S(2)}) collective-permute-start(f32[1,3,1,32,128]{4,1,3,2,0:T(4,128)S(1)} %get-tuple-element.106), channel_id=1, source_target_pairs={{0,1},{1,2},{2,3},{3,4},{4,5},{5,6},{6,7},{8,9},{9,10},{10,11},{11... | collective-permute-start | bytes 147464 | tf_op jit(solution)/shard_map/ppermute | solution.py:26
  70.2 1.3 collective-permute-start.6
  71.6 3.0 %collective-permute-start.7 = (f32[1,3,1,32,128]{4,1,3,2,0:T(4,128)}, f32[1,3,1,32,128]{4,1,3,2,0:T(4,128)S(1)}, u32[]{:S(2)}, u32[]{:S(2)}) collective-permute-start(f32[1,3,1,32,128]{4,1,3,2,0:T(4,128)} %get-tuple-element.105), channel_id=1, source_target_pairs={{0,1},{1,2},{2,3},{3,4},{4,5},{5,6},{6,7},{8,9},{9,10},{10,11},{11... | collective-permute-start | bytes 147464 | tf_op jit(solution)/shard_map/ppermute | solution.py:26
  74.6 1.5 collective-permute-start.8
  77.4 2.9 %concatenate.147 = f32[1,24,3,32,128]{4,1,3,2,0:T(8,128)S(1)} concatenate(f32[1,3,3,32,128]{4,1,3,2,0:T(4,128)} %get-tuple-element.120, f32[1,3,3,32,128]{4,1,3,2,0:T(4,128)S(1)} %get-tuple-element.72, f32[1,3,3,32,128]{4,1,3,2,0:T(4,128)S(1)} %get-tuple-element.71, f32[1,3,3,32,128]{4,1,3,2,0:T(4,128)S(1)} %get-tuple-element.70, f32[1,3,3,32,128]{4,1,3,2,0:T(4,128)S(1)} %get-tuple-element.119, ...), dimensions={1} | concatenate | bytes 2359296 | tf_op jit(solution)/shard_map/concatenate | solution.py:97
  80.4 1.1 fusion.5
  81.5 1.1 fusion.134
  82.7 1.4 fusion.141
  84.2 0.8 pad_maximum_fusion.8
  85.0 9.3 %concatenate.151 = f32[1,24,3,32,128]{4,1,3,2,0:T(8,128)S(1)} concatenate(f32[1,3,3,32,128]{4,1,3,2,0:T(4,128)} %get-tuple-element.122, f32[1,3,3,32,128]{4,1,3,2,0:T(4,128)} %get-tuple-element.78, f32[1,3,3,32,128]{4,1,3,2,0:T(4,128)} %get-tuple-element.77, f32[1,3,3,32,128]{4,1,3,2,0:T(4,128)} %get-tuple-element.76, f32[1,3,3,32,128]{4,1,3,2,0:T(4,128)} %get-tuple-element.121, ...), dimensions={1} | concatenate | bytes 2359296 | tf_op jit(solution)/shard_map/concatenate | solution.py:97
  94.3 1.1 fusion.7
  98.4 1.3 collective-permute-start.10
  99.7 4.4 %collective-permute-start.9 = (f32[1,3,1,32,128]{4,1,3,2,0:T(4,128)S(1)}, f32[1,3,1,32,128]{4,1,3,2,0:T(4,128)S(1)}, u32[]{:S(2)}, u32[]{:S(2)}) collective-permute-start(f32[1,3,1,32,128]{4,1,3,2,0:T(4,128)S(1)} %get-tuple-element.99), channel_id=1, source_target_pairs={{0,1},{1,2},{2,3},{3,4},{4,5},{5,6},{6,7},{8,9},{9,10},{10,11},{11... | collective-permute-start | bytes 147464 | tf_op jit(solution)/shard_map/ppermute | solution.py:26
  104.2 3.6 %collective-permute-start.11 = (f32[1,3,1,32,128]{4,1,3,2,0:T(4,128)}, f32[1,3,1,32,128]{4,1,3,2,0:T(4,128)S(1)}, u32[]{:S(2)}, u32[]{:S(2)}) collective-permute-start(f32[1,3,1,32,128]{4,1,3,2,0:T(4,128)} %get-tuple-element.98), channel_id=1, source_target_pairs={{0,1},{1,2},{2,3},{3,4},{4,5},{5,6},{6,7},{8,9},{9,10},{10,11},{11... | collective-permute-start | bytes 147464 | tf_op jit(solution)/shard_map/ppermute | solution.py:26
  107.9 1.5 collective-permute-start.12
  110.7 2.9 %concatenate.156 = f32[1,24,3,32,128]{4,1,3,2,0:T(8,128)S(1)} concatenate(f32[1,3,3,32,128]{4,1,3,2,0:T(4,128)} %get-tuple-element.116, f32[1,3,3,32,128]{4,1,3,2,0:T(4,128)S(1)} %get-tuple-element.60, f32[1,3,3,32,128]{4,1,3,2,0:T(4,128)S(1)} %get-tuple-element.59, f32[1,3,3,32,128]{4,1,3,2,0:T(4,128)S(1)} %get-tuple-element.58, f32[1,3,3,32,128]{4,1,3,2,0:T(4,128)S(1)} %get-tuple-element.115, ...), dimensions={1} | concatenate | bytes 2359296 | tf_op jit(solution)/shard_map/concatenate | solution.py:97
  113.7 1.1 fusion.9
  114.8 1.1 fusion.132
  115.9 0.9 select_maximum_fusion
  116.9 1.4 fusion.139
  118.3 1.7 pad_maximum_fusion.12
  120.0 9.3 %concatenate.160 = f32[1,24,3,32,128]{4,1,3,2,0:T(8,128)S(1)} concatenate(f32[1,3,3,32,128]{4,1,3,2,0:T(4,128)} %get-tuple-element.118, f32[1,3,3,32,128]{4,1,3,2,0:T(4,128)} %get-tuple-element.66, f32[1,3,3,32,128]{4,1,3,2,0:T(4,128)} %get-tuple-element.65, f32[1,3,3,32,128]{4,1,3,2,0:T(4,128)} %get-tuple-element.64, f32[1,3,3,32,128]{4,1,3,2,0:T(4,128)} %get-tuple-element.117, ...), dimensions={1} | concatenate | bytes 2359296 | tf_op jit(solution)/shard_map/concatenate | solution.py:97
  129.3 1.1 fusion.11
  133.4 1.3 collective-permute-start.13
  135.4 1.9 collective-permute-done.13
  137.4 1.4 pad_slice_fusion
  138.8 0.8 fusion.19
  139.5 5.3 %concatenate.163 = f32[2,24,2,32,128]{4,1,3,2,0:T(8,128)S(1)} concatenate(f32[2,3,2,32,128]{4,1,3,2,0:T(4,128)S(1)} %fusion.33, f32[2,3,2,32,128]{4,1,3,2,0:T(4,128)} %get-tuple-element.96, f32[2,3,2,32,128]{4,1,3,2,0:T(4,128)S(1)} %get-tuple-element.92, f32[2,3,2,32,128]{4,1,3,2,0:T(4,128)S(1)} %get-tuple-element.93, f32[2,3,2,32,128]{4,1,3,2,0:T(4,128)} %fusion.19, ...), dimensions={1} | concatenate | bytes 3145728 | tf_op jit(solution)/shard_map/concatenate | solution.py:97
  144.9 1.5 convolution_bitcast_fusion
  146.4 1.6 fusion.26
  148.1 1.3 fusion.79
  149.4 5.4 %collective-permute-start.20 = (f32[1,10,128]{2,1,0:T(8,128)S(1)}, f32[1,10,128]{2,1,0:T(8,128)S(1)}, u32[]{:S(2)}, u32[]{:S(2)}) collective-permute-start(f32[1,10,128]{2,1,0:T(8,128)S(1)} %get-tuple-element.133), channel_id=1, source_target_pairs={{0,1},{1,2},{2,3},{3,4},{4,5},{5,6},{6,7},{8,9},{9,10},{10,11},{11... | collective-permute-start | bytes 15368 | tf_op jit(solution)/shard_map/ppermute | solution.py:26
  154.9 1.3 collective-permute-start.21
  156.2 19.8 %reduce-scatter.2.cloned.1.call-done = f32[2,8,128]{2,1,0:T(8,128)} async-done(((f32[2,32,128]{2,1,0:T(8,128)}), f32[2,8,128]{2,1,0:T(8,128)}) %reduce-scatter.2.cloned.1.call-update) | async-done | bytes 8208 | tf_op jit(solution)/shard_map/reduce_scatter | solution.py:211
  176.7 3.3 %collective-permute-start.14 = (f32[2,1,128]{2,1,0:T(1,128)S(1)}, f32[2,1,128]{2,1,0:T(1,128)S(1)}, u32[]{:S(2)}, u32[]{:S(2)}) collective-permute-start(f32[2,1,128]{2,1,0:T(1,128)S(1)} %get-tuple-element.139), channel_id=1, source_target_pairs={{0,8},{8,16},{16,24},{1,9},{9,17},{17,25},{2,10},{10,18},{18,26},{... | collective-permute-start | bytes 3080 | tf_op jit(solution)/shard_map/ppermute | solution.py:26
  180.0 1.3 collective-permute-start.15
  181.5 4.0 %collective-permute-done.15 = f32[2,1,128]{2,1,0:T(1,128)S(1)} collective-permute-done((f32[2,1,128]{2,1,0:T(1,128)S(1)}, f32[2,1,128]{2,1,0:T(1,128)S(1)}, u32[]{:S(2)}, u32[]{:S(2)}) %collective-permute-start.15) | collective-permute-done | bytes 1056 | tf_op jit(solution)/shard_map/ppermute | solution.py:28
  185.5 1.3 collective-permute-start.16
  186.8 1.3 collective-permute-start.17
  188.8 2.8 %collective-permute-done.17 = f32[1,10,128]{2,1,0:T(8,128)S(1)} collective-permute-done((f32[1,10,128]{2,1,0:T(8,128)S(1)}, f32[1,10,128]{2,1,0:T(8,128)S(1)}, u32[]{:S(2)}, u32[]{:S(2)}) %collective-permute-start.17) | collective-permute-done | bytes 5152 | tf_op jit(solution)/shard_map/ppermute | solution.py:28
  192.4 42.3 %psum.7 = f32[]{:T(128)} all-reduce(f32[]{:T(128)} %get-tuple-element.14), channel_id=1, replica_groups=mesh['load'=4,'gz'=8] {'load','gz'}, use_global_device_ids=true, to_apply=%region_12.13 | all-reduce | flops 1 | bytes 8 | tf_op jit(solution)/shard_map/psum | solution.py:221
  (129 shorter events, 17.5 us)
Async XLA Ops:
  7.2 168.8 %reduce-scatter.2.cloned.1.call-start = ((), (), s32[]{:S(2)}) async-start(), calls=%async_computation.1 | async-start | bytes 40960 | tf_op jit(solution)/shard_map/reduce_scatter | solution.py:211
  17.0 2.9 %copy-start.21 = (f32[2,32,128]{2,1,0:T(8,128)}, f32[2,32,128]{2,1,0:T(8,128)S(1)}, u32[]{:S(2)}) copy-start(f32[2,32,128]{2,1,0:T(8,128)S(1)} %all_gather.3) | copy-start | bytes 98308
  17.8 8.7 %collective-permute-start = (f32[1,32,128]{2,1,0:T(8,128)S(1)}, f32[1,32,128]{2,1,0:T(8,128)S(1)}, u32[]{:S(2)}, u32[]{:S(2)}) collective-permute-start(f32[1,32,128]{2,1,0:T(8,128)S(1)} %slice.1063), channel_id=1, source_target_pairs={{0,1},{1,2},{2,3},{3,4},{4,5},{5,6},{6,7},{8,9},{9,10},{10,11},{11... | collective-permute-start | bytes 49160 | tf_op jit(solution)/shard_map/ppermute | solution.py:38
  19.9 114.8 %collective-permute-start.18 = (f32[2,1,128]{2,1,0:T(1,128)S(1)}, f32[2,1,128]{2,1,0:T(1,128)S(1)}, u32[]{:S(2)}, u32[]{:S(2)}) collective-permute-start(f32[2,1,128]{2,1,0:T(1,128)S(1)} %get-tuple-element.141), channel_id=1, source_target_pairs={{0,8},{8,16},{16,24},{1,9},{9,17},{17,25},{2,10},{10,18},{18,26},{... | collective-permute-start | bytes 3080 | tf_op jit(solution)/shard_map/ppermute | solution.py:26
  29.2 9.6 %collective-permute-start.1 = (f32[1,3,1,32,128]{4,1,3,2,0:T(4,128)S(1)}, f32[1,3,1,32,128]{4,1,3,2,0:T(4,128)S(1)}, u32[]{:S(2)}, u32[]{:S(2)}) collective-permute-start(f32[1,3,1,32,128]{4,1,3,2,0:T(4,128)S(1)} %get-tuple-element.112), channel_id=1, source_target_pairs={{0,1},{1,2},{2,3},{3,4},{4,5},{5,6},{6,7},{8,9},{9,10},{10,11},{11... | collective-permute-start | bytes 147464 | tf_op jit(solution)/shard_map/ppermute | solution.py:26
  33.2 7.0 %collective-permute-start.2 = (f32[1,3,1,32,128]{4,1,3,2,0:T(4,128)S(1)}, f32[1,3,1,32,128]{4,1,3,2,0:T(4,128)S(1)}, u32[]{:S(2)}, u32[]{:S(2)}) collective-permute-start(f32[1,3,1,32,128]{4,1,3,2,0:T(4,128)S(1)} %get-tuple-element.109), channel_id=1, source_target_pairs={{1,0},{2,1},{3,2},{4,3},{5,4},{6,5},{7,6},{9,8},{10,9},{11,10},{12... | collective-permute-start | bytes 147464 | tf_op jit(solution)/shard_map/ppermute | solution.py:28
  34.5 5.7 %collective-permute-start.3 = (f32[1,3,1,32,128]{4,1,3,2,0:T(4,128)S(1)}, f32[1,3,1,32,128]{4,1,3,2,0:T(4,128)S(1)}, u32[]{:S(2)}, u32[]{:S(2)}) collective-permute-start(f32[1,3,1,32,128]{4,1,3,2,0:T(4,128)S(1)} %get-tuple-element.111), channel_id=1, source_target_pairs={{0,1},{1,2},{2,3},{3,4},{4,5},{5,6},{6,7},{8,9},{9,10},{10,11},{11... | collective-permute-start | bytes 147464 | tf_op jit(solution)/shard_map/ppermute | solution.py:26
  37.5 4.2 %collective-permute-start.4 = (f32[1,3,1,32,128]{4,1,3,2,0:T(4,128)S(1)}, f32[1,3,1,32,128]{4,1,3,2,0:T(4,128)S(1)}, u32[]{:S(2)}, u32[]{:S(2)}) collective-permute-start(f32[1,3,1,32,128]{4,1,3,2,0:T(4,128)S(1)} %get-tuple-element.110), channel_id=1, source_target_pairs={{1,0},{2,1},{3,2},{4,3},{5,4},{6,5},{7,6},{9,8},{10,9},{11,10},{12... | collective-permute-start | bytes 147464 | tf_op jit(solution)/shard_map/ppermute | solution.py:28
  38.8 95.9 %collective-permute-start.19 = (f32[2,1,128]{2,1,0:T(1,128)S(1)}, f32[2,1,128]{2,1,0:T(1,128)S(1)}, u32[]{:S(2)}, u32[]{:S(2)}) collective-permute-start(f32[2,1,128]{2,1,0:T(1,128)S(1)} %get-tuple-element.142), channel_id=1, source_target_pairs={{8,0},{16,8},{24,16},{9,1},{17,9},{25,17},{10,2},{18,10},{26,18},{... | collective-permute-start | bytes 3080 | tf_op jit(solution)/shard_map/ppermute | solution.py:28
  43.1 1.0 copy-start.15
  43.1 1.3 copy-start.16
  44.3 3.8 %copy-start.18 = (f32[24,24,1,1]{1,0,3,2:T(8,128)S(1)}, f32[24,24,1,1]{1,0,3,2:T(8,128)}, u32[]{:S(2)}) copy-start(f32[24,24,1,1]{1,0,3,2:T(8,128)} %constant.231) | copy-start | bytes 6916
  62.2 0.9 copy-start.13
  62.2 1.0 copy-start.14
  63.6 0.9 copy-start
  65.4 9.2 %collective-permute-start.5 = (f32[1,3,1,32,128]{4,1,3,2,0:T(4,128)S(1)}, f32[1,3,1,32,128]{4,1,3,2,0:T(4,128)S(1)}, u32[]{:S(2)}, u32[]{:S(2)}) collective-permute-start(f32[1,3,1,32,128]{4,1,3,2,0:T(4,128)S(1)} %get-tuple-element.106), channel_id=1, source_target_pairs={{0,1},{1,2},{2,3},{3,4},{4,5},{5,6},{6,7},{8,9},{9,10},{10,11},{11... | collective-permute-start | bytes 147464 | tf_op jit(solution)/shard_map/ppermute | solution.py:26
  70.2 5.9 %collective-permute-start.6 = (f32[1,3,1,32,128]{4,1,3,2,0:T(4,128)S(1)}, f32[1,3,1,32,128]{4,1,3,2,0:T(4,128)S(1)}, u32[]{:S(2)}, u32[]{:S(2)}) collective-permute-start(f32[1,3,1,32,128]{4,1,3,2,0:T(4,128)S(1)} %get-tuple-element.103), channel_id=1, source_target_pairs={{1,0},{2,1},{3,2},{4,3},{5,4},{6,5},{7,6},{9,8},{10,9},{11,10},{12... | collective-permute-start | bytes 147464 | tf_op jit(solution)/shard_map/ppermute | solution.py:28
  71.6 11.1 %collective-permute-start.7 = (f32[1,3,1,32,128]{4,1,3,2,0:T(4,128)}, f32[1,3,1,32,128]{4,1,3,2,0:T(4,128)S(1)}, u32[]{:S(2)}, u32[]{:S(2)}) collective-permute-start(f32[1,3,1,32,128]{4,1,3,2,0:T(4,128)} %get-tuple-element.105), channel_id=1, source_target_pairs={{0,1},{1,2},{2,3},{3,4},{4,5},{5,6},{6,7},{8,9},{9,10},{10,11},{11... | collective-permute-start | bytes 147464 | tf_op jit(solution)/shard_map/ppermute | solution.py:26
  74.6 8.0 %collective-permute-start.8 = (f32[1,3,1,32,128]{4,1,3,2,0:T(4,128)S(1)}, f32[1,3,1,32,128]{4,1,3,2,0:T(4,128)S(1)}, u32[]{:S(2)}, u32[]{:S(2)}) collective-permute-start(f32[1,3,1,32,128]{4,1,3,2,0:T(4,128)S(1)} %get-tuple-element.104), channel_id=1, source_target_pairs={{1,0},{2,1},{3,2},{4,3},{5,4},{6,5},{7,6},{9,8},{10,9},{11,10},{12... | collective-permute-start | bytes 147464 | tf_op jit(solution)/shard_map/ppermute | solution.py:28
  95.5 0.9 copy-start.8
  95.5 1.0 copy-start.9
  95.5 1.1 copy-start.10
  95.5 1.2 copy-start.11
  95.5 1.2 copy-start.12
  97.4 2.3 copy-start.1
  98.4 9.4 %collective-permute-start.10 = (f32[1,3,1,32,128]{4,1,3,2,0:T(4,128)S(1)}, f32[1,3,1,32,128]{4,1,3,2,0:T(4,128)S(1)}, u32[]{:S(2)}, u32[]{:S(2)}) collective-permute-start(f32[1,3,1,32,128]{4,1,3,2,0:T(4,128)S(1)} %get-tuple-element.97), channel_id=1, source_target_pairs={{1,0},{2,1},{3,2},{4,3},{5,4},{6,5},{7,6},{9,8},{10,9},{11,10},{12... | collective-permute-start | bytes 147464 | tf_op jit(solution)/shard_map/ppermute | solution.py:28
  99.7 9.7 %collective-permute-start.9 = (f32[1,3,1,32,128]{4,1,3,2,0:T(4,128)S(1)}, f32[1,3,1,32,128]{4,1,3,2,0:T(4,128)S(1)}, u32[]{:S(2)}, u32[]{:S(2)}) collective-permute-start(f32[1,3,1,32,128]{4,1,3,2,0:T(4,128)S(1)} %get-tuple-element.99), channel_id=1, source_target_pairs={{0,1},{1,2},{2,3},{3,4},{4,5},{5,6},{6,7},{8,9},{9,10},{10,11},{11... | collective-permute-start | bytes 147464 | tf_op jit(solution)/shard_map/ppermute | solution.py:26
  104.2 11.7 %collective-permute-start.11 = (f32[1,3,1,32,128]{4,1,3,2,0:T(4,128)}, f32[1,3,1,32,128]{4,1,3,2,0:T(4,128)S(1)}, u32[]{:S(2)}, u32[]{:S(2)}) collective-permute-start(f32[1,3,1,32,128]{4,1,3,2,0:T(4,128)} %get-tuple-element.98), channel_id=1, source_target_pairs={{0,1},{1,2},{2,3},{3,4},{4,5},{5,6},{6,7},{8,9},{9,10},{10,11},{11... | collective-permute-start | bytes 147464 | tf_op jit(solution)/shard_map/ppermute | solution.py:26
  107.9 8.1 %collective-permute-start.12 = (f32[1,3,1,32,128]{4,1,3,2,0:T(4,128)}, f32[1,3,1,32,128]{4,1,3,2,0:T(4,128)}, u32[]{:S(2)}, u32[]{:S(2)}) collective-permute-start(f32[1,3,1,32,128]{4,1,3,2,0:T(4,128)} %get-tuple-element.100), channel_id=1, source_target_pairs={{1,0},{2,1},{3,2},{4,3},{5,4},{6,5},{7,6},{9,8},{10,9},{11,10},{12... | collective-permute-start | bytes 147464 | tf_op jit(solution)/shard_map/ppermute | solution.py:28
  130.4 0.9 copy-start.3
  130.4 1.0 copy-start.4
  130.4 1.1 copy-start.5
  130.4 1.2 copy-start.6
  130.5 1.2 copy-start.7
  132.0 0.9 copy-start.2
  132.1 0.9 copy-start.23
  132.4 2.4 copy-start.19
  133.4 3.9 %collective-permute-start.13 = (f32[2,3,1,32,128]{4,1,3,2,0:T(4,128)S(1)}, f32[2,3,1,32,128]{4,1,3,2,0:T(4,128)S(1)}, u32[]{:S(2)}, u32[]{:S(2)}) collective-permute-start(f32[2,3,1,32,128]{4,1,3,2,0:T(4,128)S(1)} %slice.1168), channel_id=1, source_target_pairs={{1,0},{2,1},{3,2},{4,3},{5,4},{6,5},{7,6},{9,8},{10,9},{11,10},{12... | collective-permute-start | bytes 294920 | tf_op jit(solution)/shard_map/ppermute | solution.py:38
  134.7 4.0 %copy-start.25 = (f32[2,1,128]{2,1,0:T(1,128)}, f32[2,1,128]{2,1,0:T(1,128)S(1)}, u32[]{:S(2)}) copy-start(f32[2,1,128]{2,1,0:T(1,128)S(1)} %collective-permute-done.18) | copy-start | bytes 3076
  134.8 4.0 %copy-start.27 = (f32[2,1,128]{2,1,0:T(1,128)}, f32[2,1,128]{2,1,0:T(1,128)S(1)}, u32[]{:S(2)}) copy-start(f32[2,1,128]{2,1,0:T(1,128)S(1)} %collective-permute-done.19) | copy-start | bytes 3076
  139.5 5.3 %copy-start.29 = (f32[24,24,1,1,1]{1,0,4,3,2:T(8,128)S(1)}, f32[24,24,1,1,1]{1,0,4,3,2:T(8,128)}, u32[]{:S(2)}) copy-start(f32[24,24,1,1,1]{1,0,4,3,2:T(8,128)} %constant.232) | copy-start | bytes 6916
  146.3 1.7 copy-start.30
  146.3 1.8 copy-start.17
  146.3 1.8 copy-start.22
  146.3 3.1 %copy-start.24 = (f32[2,10,128]{2,1,0:T(8,128)S(1)}, f32[2,10,128]{2,1,0:T(8,128)}, u32[]{:S(2)}) copy-start(f32[2,10,128]{2,1,0:T(8,128)} %pad_maximum_fusion.17) | copy-start | bytes 30724
  146.4 29.6 %copy-start.20 = (f32[2,8,128]{2,1,0:T(8,128)S(1)}, f32[2,8,128]{2,1,0:T(8,128)}, u32[]{:S(2)}) copy-start(f32[2,8,128]{2,1,0:T(8,128)} %param.5) | copy-start | bytes 24580
  146.4 35.0 %copy-start.26 = (f32[2,1,128]{2,1,0:T(1,128)S(1)}, f32[2,1,128]{2,1,0:T(1,128)}, u32[]{:S(2)}) copy-start(f32[2,1,128]{2,1,0:T(1,128)} %copy-done.25) | copy-start | bytes 3076
  146.4 35.0 %copy-start.28 = (f32[2,1,128]{2,1,0:T(1,128)S(1)}, f32[2,1,128]{2,1,0:T(1,128)}, u32[]{:S(2)}) copy-start(f32[2,1,128]{2,1,0:T(1,128)} %copy-done.27) | copy-start | bytes 3076
  149.4 31.9 %collective-permute-start.20 = (f32[1,10,128]{2,1,0:T(8,128)S(1)}, f32[1,10,128]{2,1,0:T(8,128)S(1)}, u32[]{:S(2)}, u32[]{:S(2)}) collective-permute-start(f32[1,10,128]{2,1,0:T(8,128)S(1)} %get-tuple-element.133), channel_id=1, source_target_pairs={{0,1},{1,2},{2,3},{3,4},{4,5},{5,6},{6,7},{8,9},{9,10},{10,11},{11... | collective-permute-start | bytes 15368 | tf_op jit(solution)/shard_map/ppermute | solution.py:26
  154.9 26.4 %collective-permute-start.21 = (f32[1,10,128]{2,1,0:T(8,128)S(1)}, f32[1,10,128]{2,1,0:T(8,128)S(1)}, u32[]{:S(2)}, u32[]{:S(2)}) collective-permute-start(f32[1,10,128]{2,1,0:T(8,128)S(1)} %get-tuple-element.134), channel_id=1, source_target_pairs={{1,0},{2,1},{3,2},{4,3},{5,4},{6,5},{7,6},{9,8},{10,9},{11,10},{12... | collective-permute-start | bytes 15368 | tf_op jit(solution)/shard_map/ppermute | solution.py:28
  176.7 4.8 %collective-permute-start.14 = (f32[2,1,128]{2,1,0:T(1,128)S(1)}, f32[2,1,128]{2,1,0:T(1,128)S(1)}, u32[]{:S(2)}, u32[]{:S(2)}) collective-permute-start(f32[2,1,128]{2,1,0:T(1,128)S(1)} %get-tuple-element.139), channel_id=1, source_target_pairs={{0,8},{8,16},{16,24},{1,9},{9,17},{17,25},{2,10},{10,18},{18,26},{... | collective-permute-start | bytes 3080 | tf_op jit(solution)/shard_map/ppermute | solution.py:26
  180.0 5.5 %collective-permute-start.15 = (f32[2,1,128]{2,1,0:T(1,128)S(1)}, f32[2,1,128]{2,1,0:T(1,128)S(1)}, u32[]{:S(2)}, u32[]{:S(2)}) collective-permute-start(f32[2,1,128]{2,1,0:T(1,128)S(1)} %get-tuple-element.140), channel_id=1, source_target_pairs={{8,0},{16,8},{24,16},{9,1},{17,9},{25,17},{10,2},{18,10},{26,18},{... | collective-permute-start | bytes 3080 | tf_op jit(solution)/shard_map/ppermute | solution.py:28
  185.5 3.3 %collective-permute-start.16 = (f32[1,10,128]{2,1,0:T(8,128)S(1)}, f32[1,10,128]{2,1,0:T(8,128)S(1)}, u32[]{:S(2)}, u32[]{:S(2)}) collective-permute-start(f32[1,10,128]{2,1,0:T(8,128)S(1)} %get-tuple-element.131), channel_id=1, source_target_pairs={{0,1},{1,2},{2,3},{3,4},{4,5},{5,6},{6,7},{8,9},{9,10},{10,11},{11... | collective-permute-start | bytes 15368 | tf_op jit(solution)/shard_map/ppermute | solution.py:26
  186.8 4.8 %collective-permute-start.17 = (f32[1,10,128]{2,1,0:T(8,128)S(1)}, f32[1,10,128]{2,1,0:T(8,128)S(1)}, u32[]{:S(2)}, u32[]{:S(2)}) collective-permute-start(f32[1,10,128]{2,1,0:T(8,128)S(1)} %get-tuple-element.132), channel_id=1, source_target_pairs={{1,0},{2,1},{3,2},{4,3},{5,4},{6,5},{7,6},{9,8},{10,9},{11,10},{12... | collective-permute-start | bytes 15368 | tf_op jit(solution)/shard_map/ppermute | solution.py:28
Sparse Core Ops, SparseCore 0:
  149.5 26.4 reduce-scatter.1
where the time goes:
time: 246 us; the launch traced here: 243 us
  local copies, waits for them, and re-layouts  62.6 us (25%)
  starting transfers between devices  52.1 us (21%)
  blocking collectives  52.1 us (21%)
  waiting for transfers between devices  30.1 us (12%)
  other arithmetic  22.1 us (9%)
  between operations  15.6 us (6%)
  matrix products  8.21 us (3%)
    concatenate x7, local copies, waits for them, and re-layouts, element_forces(): stacked = jnp.concatenate(views, axis=1)  42.9 us
    psum x1, blocking collectives, on_device(): total = lax.psum(jnp.sum(filtered), ('load', 'gz'))  42.3 us
    ppermute x10, starting transfers between devices, with_halo(): lax.ppermute(tail, axis, [(i, (i + 1) % count) for i in range(ends)])  36.2 us
    reduce_scatter x1, waiting for transfers between devices, on_device(): lax.psum_scatter(term_local, 'load', scatter_dimension=1, tiled=True)  19.8 us
    ppermute x10, starting transfers between devices, with_halo(): lax.ppermute(head, axis, [((i + 1) % count, i) for i in range(ends)])  13.3 us
    all_gather x1, blocking collectives, on_device(): dense_full = lax.all_gather(density, 'load', axis=1, tiled=True)  9.83 us
    ppermute x10, waiting for transfers between devices, with_halo(): lax.ppermute(head, axis, [((i + 1) % count, i) for i in range(ends)])  8.33 us
    dot_general x7, matrix products, element_forces(): jnp.einsum('ij,bjzyx->bizyx', stiffness, stacked, precision=lax.Precision...  8.21 us
  transfers between devices with their start and end apart: 23, of which 5 were waited for; matrix products, arithmetic and copies ran while one was open for 31% of the time, Pallas kernels for 0%

commit v1 on v0

v1 whole, which is shorter than its diff:
```python
import functools

import jax
import jax.numpy as jnp
from jax import lax
from jax.experimental import pallas as pl
from jax.experimental.pallas import tpu as pltpu
from jax.sharding import PartitionSpec as P

SWEEPS = 3
EMIN = 0.001
LOWER_EIG = 0.1
UPPER_EIG = 2.5
MOVE_LIMIT = 0.2
FLOOR_DENSITY = 0.001
POISSON = 0.3
LAME = POISSON / ((1 + POISSON) * (1 - 2 * POISSON))
SHEAR = 1.0 / (2 * (1 + POISSON))
KE_DIAG = (LAME + 4 * SHEAR) / 9
EDGE = 1.5 - 2.0**0.5
PLANE = ("ss", "sd", "ds", "dd")


def next_x(a):
    lanes = a.shape[1]
    lane = lax.broadcasted_iota(jnp.int32, a.shape, 1)
    return jnp.where(lane == lanes - 1, 0.0, pltpu.roll(a, lanes - 1, 1))


def last_x(a):
    lane = lax.broadcasted_iota(jnp.int32, a.shape, 1)
    return jnp.where(lane == 0, 0.0, pltpu.roll(a, 1, 1))


def next_y(a):
    rows = a.shape[0]
    row = lax.broadcasted_iota(jnp.int32, a.shape, 0)
    return jnp.where(row == rows - 1, 0.0, pltpu.roll(a, rows - 1, 0))


def last_y(a):
    row = lax.broadcasted_iota(jnp.int32, a.shape, 0)
    return jnp.where(row == 0, 0.0, pltpu.roll(a, 1, 0))


def to_modes_xy(u):
    ux = next_x(u)
    s, d = ux + u, ux - u
    sy, dy = next_y(s), next_y(d)
    return {"ss": sy + s, "sd": sy - s, "ds": dy + d, "dd": dy - d}


def from_modes_xy(g):
    s = (g["ss"] - g["sd"]) + last_y(g["ss"] + g["sd"])
    d = (g["ds"] - g["dd"]) + last_y(g["ds"] + g["dd"])
    return (s - d) + last_x(s + d)


def modes_z(low, high):
    modes = []
    for comp in range(3):
        one = {}
        for pq in PLANE:
            if pq != "ss":
                one[pq + "s"] = high[comp][pq] + low[comp][pq]
            one[pq + "d"] = high[comp][pq] - low[comp][pq]
        modes.append(one)
    return modes


NORMAL = ((0, "dss"), (1, "sds"), (2, "ssd"))
BENDS = (((1, "dds"), (2, "dsd")), ((0, "dds"), (2, "sdd")), ((0, "dsd"), (1, "sdd")))
SHEARS = (((0, "sds"), (1, "dss")), ((0, "ssd"), (2, "dss")), ((1, "ssd"), (2, "sds")))
TWIST = ((0, "sdd"), (1, "dsd"), (2, "dds"))


def mode_forces(modes, e1):
    m = lambda key: modes[key[0]][key[1]]
    out = [{}, {}, {}]

    def put(key, value):
        out[key[0]][key[1]] = value

    e4 = e1 + e1
    e2 = e1 * (1.0 / 3.0)
    e3 = e1 * ((LAME + 4 * SHEAR) / (9 * SHEAR))
    trace = (LAME / (2 * SHEAR)) * (m(NORMAL[0]) + m(NORMAL[1]) + m(NORMAL[2]))
    for key in NORMAL:
        put(key, e4 * (trace + m(key)))
    for a, b in BENDS:
        t = (LAME / (3 * SHEAR)) * (m(a) + m(b))
        put(a, e1 * (t + m(a)))
        put(b, e1 * (t + m(b)))
    for a, b in SHEARS:
        f = e1 * (m(a) + m(b))
        put(a, f)
        put(b, f)
    t = m(TWIST[0]) + m(TWIST[1]) + m(TWIST[2])
    for key in TWIST:
        put(key, e2 * (t + m(key)))
    for comp in range(3):
        put((comp, "ddd"), e3 * modes[comp]["ddd"])
    return out


def mode_energy(modes):
    m = lambda key: modes[key[0]][key[1]]
    sq = lambda v: v * v
    n = [m(key) for key in NORMAL]
    total = (3 * LAME / SHEAR) * sq(n[0] + n[1] + n[2]) + 6.0 * (sq(n[0]) + sq(n[1]) + sq(n[2]))
    shear = None
    for a, b in SHEARS:
        t = sq(m(a) + m(b))
        shear = t if shear is None else shear + t
    total = total + 3.0 * shear
    sums, own = None, None
    for a, b in BENDS:
        t = sq(m(a) + m(b))
        o = sq(m(a)) + sq(m(b))
        sums = t if sums is None else sums + t
        own = o if own is None else own + o
    total = total + (LAME / SHEAR) * sums + 3.0 * own
    a, b, c = (m(key) for key in TWIST)
    total = total + (sq(a + b) + sq(a + c) + sq(b + c))
    bulk = sq(modes[0]["ddd"]) + sq(modes[1]["ddd"]) + sq(modes[2]["ddd"])
    return total + ((LAME + 4 * SHEAR) / (3 * SHEAR)) * bulk


def filter_planes(a):
    x = last_x(a) + next_x(a)
    cross = x + (last_y(a) + next_y(a))
    diagonal = last_y(x) + next_y(x)
    return 1.5 * a + 0.5 * cross + EDGE * diagonal, 0.5 * a + EDGE * cross


def filter_layers(layers):
    pairs = [filter_planes(a) for a in layers]
    return [
        pairs[at][0] + (pairs[at - 1][1] + pairs[at + 1][1]) for at in range(1, len(layers) - 1)
    ]


def smooth_kernel(hops, count_gz, *refs):
    blocks = 1 + 2 * hops
    weights_ref = refs[0]
    design_refs = refs[1 : 1 + blocks]
    force_refs = refs[1 + blocks : 1 + 2 * blocks]
    disp_hbm, sens_ref, rec_ref = refs[1 + 2 * blocks : 4 + 2 * blocks]
    (e1_ref, inv_ref, res_ref, step_ref, sol_ref, mode_ref, carry_ref, node_ref) = refs[4 + 2 * blocks : 12 + 2 * blocks]
    disp_ref, weight_ref, disp_sem = refs[12 + 2 * blocks :]

    cases, _, layers, rows, columns = disp_ref.shape
    nodes = layers + 2 * SWEEPS + 1
    gz = lax.axis_index("gz")
    load = lax.axis_index("load")

    def from_hop(refs, hop, pick):
        if hop == 0:
            return pick(refs[0])
        far = abs(hop)
        first, second = pick(refs[2 * far - 1]), pick(refs[2 * far])
        meets_above = (gz // far) % 2 == (0 if hop > 0 else 1)
        return jnp.where(meets_above, first, second)

    def inside(layer):
        owner = gz + layer // layers
        return jnp.logical_and(owner >= 0, owner < count_gz)

    def design(kind, layer):
        hop = layer // layers
        return from_hop(design_refs, hop, lambda ref: ref[kind, layer - hop * layers])

    below = None
    for at in range(nodes + 1):
        layer = at - SWEEPS - 1
        dense, marks = design(0, layer), design(1, layer)
        solid = jnp.where(marks == 2.0, 1.0, dense)
        live = jnp.where(inside(layer), 1.0, 0.0)
        moduli = (EMIN + (1.0 - EMIN) * solid * solid * solid) * live
        if 0 <= layer < layers:
            weight_ref[layer] = (3.0 * (1.0 - EMIN)) * solid * solid * dense
        if 1 <= at < nodes:
            e1_ref[at - 1] = moduli * (SHEAR / 16)
        spread = moduli + last_x(moduli)
        spread = spread + last_y(spread)
        if at > 0:
            diag = KE_DIAG * (below + spread)
            free = jnp.logical_and(marks != 1.0, inside(layer))
            inv_ref[at - 1] = jnp.where(free, 1.0 / jnp.where(free, diag, 1.0), 0.0)
        below = spread

    theta = 0.5 * (UPPER_EIG + LOWER_EIG)
    delta = 0.5 * (UPPER_EIG - LOWER_EIG)
    sigma = theta / delta

    def load_modes(slot, chunk):
        return [
            {pq: mode_ref[slot, comp * 4 + i, chunk] for i, pq in enumerate(PLANE)}
            for comp in range(3)
        ]

    def store_modes(slot, field_ref, node):
        for comp in range(3):
            planes = to_modes_xy(field_ref[comp, node])
            for i, pq in enumerate(PLANE):
                mode_ref[slot, comp * 4 + i] = planes[pq]

    def one_case(case, weighted):
        for at in range(nodes):
            node = at - SWEEPS
            hop = node // layers
            for comp in range(3):
                force = from_hop(force_refs, hop, lambda ref: ref[case, comp, node - hop * layers])
                step = inv_ref[at] * force * (1.0 / theta)
                res_ref[comp, at] = force
                step_ref[comp, at] = step
                if SWEEPS <= at <= SWEEPS + layers:
                    sol_ref[comp, at - SWEEPS] = step

        factor = 1.0 / sigma
        for sweep in range(1, SWEEPS + 1):
            factor_next = 1.0 / (2.0 * sigma - factor)
            keep, take = factor_next * factor, 2.0 * factor_next / delta
            first = sweep - 1
            store_modes(first % 2, step_ref, first)
            for element in range(first, nodes - sweep):
                store_modes((element + 1) % 2, step_ref, element + 1)
                whole = element > first
                for chunk_at in range(0, rows, 8):
                    chunk = pl.ds(chunk_at, 8)
                    low = load_modes(element % 2, chunk)
                    high = load_modes((element + 1) % 2, chunk)
                    f = mode_forces(modes_z(low, high), e1_ref[element, chunk])
                    for comp in range(3):
                        for i, pq in enumerate(PLANE):
                            diff = f[comp][pq + "d"]
                            if pq == "ss":
                                down, up = -diff, diff
                            else:
                                both = f[comp][pq + "s"]
                                down, up = both - diff, both + diff
                            if whole:
                                node_ref[comp * 4 + i, chunk] = carry_ref[comp * 4 + i, chunk] + down
                            carry_ref[comp * 4 + i, chunk] = up
                if whole:
                    for comp in range(3):
                        g = {pq: node_ref[comp * 4 + i] for i, pq in enumerate(PLANE)}
                        res = res_ref[comp, element] - from_modes_xy(g)
                        step = keep * step_ref[comp, element] + take * (inv_ref[element] * res)
                        if sweep < SWEEPS:
                            res_ref[comp, element] = res
                            step_ref[comp, element] = step
                        if SWEEPS <= element <= SWEEPS + layers:
                            sol = sol_ref[comp, element - SWEEPS] + step
                            sol_ref[comp, element - SWEEPS] = sol
                            if sweep == SWEEPS and element < SWEEPS + layers:
                                disp_ref[case, comp, element - SWEEPS] = sol
            factor = factor_next
        pltpu.make_async_copy(disp_ref.at[case], disp_hbm.at[case], disp_sem.at[case]).start()

        weight = weights_ref[load * cases + case].astype(jnp.float32)
        store_modes(0, sol_ref, 0)
        for layer in range(layers):
            store_modes((layer + 1) % 2, sol_ref, layer + 1)
            for chunk_at in range(0, rows, 8):
                chunk = pl.ds(chunk_at, 8)
                low = load_modes(layer % 2, chunk)
                high = load_modes((layer + 1) % 2, chunk)
                energy = weight * mode_energy(modes_z(low, high))
                node_ref[12 + layer, chunk] = jnp.where(case == 0, 0.0, node_ref[12 + layer, chunk]) + energy
        return weighted

    lax.fori_loop(0, cases, one_case, 0)
    weight_sum = weights_ref[0]
    for at in range(1, weights_ref.shape[0]):
        weight_sum = weight_sum + weights_ref[at]
    weight_sum = jnp.full((8, columns), weight_sum.astype(jnp.float32))
    scale = (SHEAR / 48) / weight_sum

    spans = filter_layers([design(0, layer) for layer in range(-2, layers + 2)])
    recs = [
        jnp.where(inside(layer), 1.0 / jnp.where(inside(layer), span, 1.0), 0.0)
        for layer, span in zip(range(-1, layers + 1), spans)
    ]
    shares = filter_layers(recs)
    total = jnp.zeros((8, columns), jnp.float32)
    for layer in range(layers):
        rec_ref[layer] = recs[layer + 1]
        for chunk_at in range(0, rows, 8):
            chunk = pl.ds(chunk_at, 8)
            sens = weight_ref[layer, chunk] * (node_ref[12 + layer, chunk] * scale)
            sens_ref[pl.ds(layer * rows + chunk_at, 8)] = sens
            total = total + sens * shares[layer][chunk_at : chunk_at + 8]
    sens_ref[pl.ds(layers * rows, 8)] = total
    for case in range(cases):
        pltpu.make_async_copy(disp_ref.at[case], disp_hbm.at[case], disp_sem.at[case]).wait()


def stage_kernel(labels_ref, density_ref, forces_ref, marks_ref, own_density_ref, own_forces_ref):
    marks_ref[...] = labels_ref[...].astype(jnp.float32)
    own_density_ref[...] = density_ref[...]
    own_forces_ref[...] = forces_ref[...]


def design_kernel(count_load, *refs):
    marks_ref = refs[0]
    density_refs = refs[1 : 1 + count_load]
    out_ref = refs[-1]
    load = lax.axis_index("load")
    own_rows = density_refs[0].shape[1]
    for step in range(count_load):
        start = pl.multiple_of(partner(load, step, count_load) * own_rows, own_rows)
        out_ref[0, :, pl.ds(start, own_rows)] = density_refs[step][...]
    out_ref[1] = marks_ref[...]


def sum_kernel(rows, *refs):
    sum_ref, first_ref, second_ref = refs[-3:]
    total = refs[0][...]
    for ref in refs[1:-3]:
        total = total + ref[...]
    sum_ref[...] = total
    end = total.shape[0] - 8
    top, bottom, share = total[end - rows : end], total[:rows], total[end:]
    even = lax.axis_index("gz") % 2 == 0
    first_ref[:rows] = jnp.where(even, top, bottom)
    first_ref[rows:] = share
    second_ref[...] = jnp.where(even, bottom, top)


def update_kernel(count_gz, *refs):
    sum_ref, first_ref, second_ref = refs[:3]
    share_refs = refs[3:-5]
    rec_ref, density_ref, marks_ref, new_ref, filt_ref = refs[-5:]
    layers, own_rows, columns = density_ref.shape
    rows = marks_ref.shape[1]
    load = lax.axis_index("load")
    even = lax.axis_index("gz") % 2 == 0
    first, second = first_ref[:rows], second_ref[...]
    numers = [jnp.where(even, second, first)]
    numers += [sum_ref[layer * rows : (layer + 1) * rows] for layer in range(layers)]
    numers += [jnp.where(even, first, second)]
    for layer, numer in enumerate(filter_layers(numers)):
        filt_ref[layer] = numer * rec_ref[layer]
    total = sum_ref[layers * rows :] + first_ref[rows:]
    for ref in share_refs:
        total = total + ref[...]
    mean = jnp.sum(total, keepdims=True) * (1.0 / (count_gz * layers * rows * columns))
    mean = jnp.broadcast_to(mean, (own_rows, columns))
    start = pl.multiple_of(load * own_rows, own_rows)
    for layer in range(layers):
        density = density_ref[layer]
        candidate = density * jnp.sqrt(filt_ref[layer, pl.ds(start, own_rows)] / mean)
        lower = jnp.maximum(density - MOVE_LIMIT, FLOOR_DENSITY)
        upper = jnp.minimum(density + MOVE_LIMIT, 1.0)
        updated = jnp.minimum(jnp.maximum(candidate, lower), upper)
        new_ref[layer] = jnp.where(marks_ref[layer, pl.ds(start, own_rows)] == 2.0, 1.0, updated)


def partner(index, step, count):
    if count & (count - 1) == 0:
        return index ^ step
    return (index + step) % count


def met(block, axis, step):
    count = lax.axis_size(axis)
    return lax.ppermute(block, axis, [(partner(i, step, count), i) for i in range(count)])


def swapped(block, axis, distance, odd):
    count = lax.axis_size(axis)
    low = [i for i in range(count - distance) if i // distance % 2 == odd]
    return lax.ppermute(block, axis, [(i, i + distance) for i in low] + [(i + distance, i) for i in low])


def on_device(density, labels, forces, case_weights):
    count_gz, count_load = lax.axis_size("gz"), lax.axis_size("load")
    cases, _, layers, rows, columns = forces.shape
    nodes = layers + 2 * SWEEPS + 1
    hops = -(-(SWEEPS + 1) // layers)
    vmem = pl.BlockSpec(memory_space=pltpu.VMEM)
    plane = (rows, columns)
    f32 = jnp.float32
    plane_bytes = rows * columns * 4

    def call(kernel, out, scratch, planes, cost, *args):
        return pl.pallas_call(
            kernel,
            out_shape=out,
            in_specs=[vmem] * len(args),
            out_specs=vmem if not isinstance(out, tuple) else (vmem,) * len(out),
            scratch_shapes=[pltpu.VMEM(shape, f32) for shape in scratch],
            compiler_params=pltpu.CompilerParams(vmem_limit_bytes=planes * plane_bytes + (4 << 20)),
            cost_estimate=pl.CostEstimate(flops=cost, bytes_accessed=cost // 10, transcendentals=0),
        )(*args)

    def along_gz(block):
        return [swapped(block, "gz", far, odd) for far in range(1, hops + 1) for odd in range(2)]

    shape = jax.ShapeDtypeStruct
    marks, own_density, own_forces = call(
        stage_kernel,
        (shape(labels.shape, f32), shape(density.shape, f32), shape(forces.shape, f32)),
        [],
        6 * layers + 4 * cases * 3 * layers,
        1_000_000,
        labels,
        density,
        forces,
    )
    force_swaps = along_gz(forces)
    early = force_swaps[-2:]
    design = pl.pallas_call(
        functools.partial(design_kernel, count_load),
        out_shape=shape((2, layers) + plane, f32),
        in_specs=[vmem] * (1 + count_load) + [pl.BlockSpec(memory_space=pl.ANY)] * len(early),
        out_specs=vmem,
        cost_estimate=pl.CostEstimate(flops=1_000_000, bytes_accessed=100_000, transcendentals=0),
    )(marks, own_density, *[met(density, "load", step) for step in range(1, count_load)], *early)
    design_blocks = [design] + along_gz(design)

    hbm = pl.BlockSpec(memory_space=pltpu.HBM)
    smooth_planes = nodes * 8 + 3 * (layers + 1) + 24 + 24 + layers
    smooth_planes += 2 * len(design_blocks) * (cases * 3 + 2) * layers + 8 * cases * layers
    displacement, sens, rec = pl.pallas_call(
        functools.partial(smooth_kernel, hops, count_gz),
        out_shape=(
            shape(forces.shape, f32),
            shape((layers * rows + 8, columns), f32),
            shape((layers,) + plane, f32),
        ),
        in_specs=[pl.BlockSpec(memory_space=pltpu.SMEM)] + [vmem] * (2 * len(design_blocks)),
        out_specs=(hbm, vmem, vmem),
        scratch_shapes=[
            pltpu.VMEM((nodes - 1,) + plane, f32),
            pltpu.VMEM((nodes,) + plane, f32),
            pltpu.VMEM((3, nodes) + plane, f32),
            pltpu.VMEM((3, nodes) + plane, f32),
            pltpu.VMEM((3, layers + 1) + plane, f32),
            pltpu.VMEM((2, 12) + plane, f32),
            pltpu.VMEM((12,) + plane, f32),
            pltpu.VMEM((12 + layers,) + plane, f32),
            pltpu.VMEM(forces.shape, f32),
            pltpu.VMEM((layers,) + plane, f32),
            pltpu.SemaphoreType.DMA((cases,)),
        ],
        compiler_params=pltpu.CompilerParams(vmem_limit_bytes=smooth_planes * plane_bytes + (4 << 20)),
        cost_estimate=pl.CostEstimate(flops=60_000_000, bytes_accessed=2_000_000, transcendentals=0),
    )(case_weights, *design_blocks, own_forces, *force_swaps)

    whole, first, second = call(
        functools.partial(sum_kernel, rows),
        (shape(sens.shape, f32), shape((rows + 8, columns), f32), shape(plane, f32)),
        [],
        2 * (count_load + 3) * (layers + 1),
        1_000_000,
        sens,
        *[met(sens, "load", step) for step in range(1, count_load)],
    )
    share = whole[layers * rows :]
    new_density = call(
        functools.partial(update_kernel, count_gz),
        shape(density.shape, f32),
        [(layers,) + plane],
        10 * layers + 4 + count_gz,
        1_000_000,
        whole,
        swapped(first, "gz", 1, 0),
        swapped(second, "gz", 1, 1),
        *[met(share, "gz", step) for step in range(2, count_gz)],
        rec,
        own_density,
        marks,
    )
    return (new_density, displacement)


def solution(mesh):
    return jax.shard_map(
        on_device,
        mesh=mesh,
        in_specs=(
            P("gz", "load", None),
            P("gz", None, None),
            P("load", None, "gz", None, None),
            P(),
        ),
        out_specs=(P("gz", "load", None), P("load", None, "gz", None, None)),
        check_vma=False,
    )
```

time: 246 us -> 66 us (0.27); the launches traced: 243 us -> 65.5 us
  local copies, waits for them, and re-layouts: 62.6 us -> 7.02 us
  blocking collectives: 52.1 us -> 0 us
  other arithmetic: 22.1 us -> 0 us
  starting transfers between devices: 52.1 us -> 34 us
  waiting for transfers between devices: 30.1 us -> 15.3 us
  between operations: 15.6 us -> 0.81 us
  Pallas kernels: 0 us -> 8.37 us
  matrix products: 8.21 us -> 0 us
    concatenate x7 -> x0, local copies, waits for them, and re-layouts: 42.9 us -> none  [element_forces(): stacked = jnp.concatenate(views, axis=1)]
    psum x1 -> x0, blocking collectives: 42.3 us -> none  [on_device(): total = lax.psum(jnp.sum(filtered), ('load', 'gz'))]
    reduce_scatter x1 -> x0, waiting for transfers between devices: 19.8 us -> none  [on_device(): lax.psum_scatter(term_local, 'load', scatter_dimension=1, tiled=True)]
    ppermute x22, starting transfers between devices: 52.1 us -> 34 us  [the longest x12 18 us: met(): lax.ppermute(block, axis, [(partner(i, step, count), i) for i in range(co...]
    slice x25 -> x1, local copies, waits for them, and re-layouts: 14.2 us -> 0.01 us  [on_device(): share = whole[layers * rows:]]
    all_gather x1 -> x0, blocking collectives: 9.83 us -> none  [on_device(): dense_full = lax.all_gather(density, 'load', axis=1, tiled=True)]
    pallas_call x0 -> x5, Pallas kernels: none -> 8.37 us  [the longest x1 6.16 us: on_device(): pl.pallas_call(functools.partial(smooth_kernel, hops, count_gz), out_shap...]
    dot_general x7 -> x0, matrix products: 8.21 us -> none  [element_forces(): jnp.einsum('ij,bjzyx->bizyx', stiffness, stacked, precision=lax.Precision...]
  transfers between devices with their start and end apart: 23 -> 22, of which waited for: 5 -> 12; matrix products, arithmetic and copies ran while one was open for 31% -> 0% of each run, Pallas kernels for 0% -> 2%
where the time goes in v1:
time: 66 us; the launch traced here: 65.5 us
  starting transfers between devices  34 us (52%)
  waiting for transfers between devices  15.3 us (23%)
  Pallas kernels  8.37 us (13%)
  local copies, waits for them, and re-layouts  7.02 us (11%)
  between operations  0.81 us (1%)
    ppermute x12, starting transfers between devices, met(): lax.ppermute(block, axis, [(partner(i, step, count), i) for i in range(co...  18 us
    ppermute x10, starting transfers between devices, swapped(): lax.ppermute(block, axis, [(i, i + distance) for i in low] + [(i + distan...  16.1 us
    ppermute x12, waiting for transfers between devices, met(): lax.ppermute(block, axis, [(partner(i, step, count), i) for i in range(co...  14.1 us
    unnamed x32, local copies, waits for them, and re-layouts  7.01 us
    pallas_call x1, Pallas kernels, on_device(): pl.pallas_call(functools.partial(smooth_kernel, hops, count_gz), out_shap...  6.16 us
    pallas_call x1, Pallas kernels, on_device(): pl.pallas_call(functools.partial(design_kernel, count_load), out_shape=sh...  1.43 us
  transfers between devices with their start and end apart: 22, of which 12 were waited for; matrix products, arithmetic and copies ran while one was open for 0% of the time, Pallas kernels for 2%

profile of v1, /device:TPU:0, one launch (start us, length us, event | category | flops | bytes accessed | tf_op | source)
XLA Modules:
  0.0 65.5 jit_solution(15012410099184725490)
XLA Ops:
  0.6 0.7 %collective-permute-start.4 = (f32[2,3,2,32,128]{4,3,2,1,0:T(8,128)}, f32[2,3,2,32,128]{4,3,2,1,0:T(8,128)S(1)}, u32[]{:S(2)}, u32[]{:S(2)}) collective-permute-start(f32[2,3,2,32,128]{4,3,2,1,0:T(8,128)} %forces_ref.1), channel_id=1, source_target_pairs={{2,4},{3,5},{4,2},{5,3},{10,12},{11,13},{12,10},{13,11},{18,20},{1... | collective-permute-start | bytes 589832 | tf_op jit(solution)/shard_map/ppermute | solution.py:374
  1.3 5.9 %collective-permute-start.3 = (f32[2,3,2,32,128]{4,3,2,1,0:T(8,128)}, f32[2,3,2,32,128]{4,3,2,1,0:T(8,128)S(1)}, u32[]{:S(2)}, u32[]{:S(2)}) collective-permute-start(f32[2,3,2,32,128]{4,3,2,1,0:T(8,128)} %forces_ref.1), channel_id=1, source_target_pairs={{0,2},{1,3},{4,6},{5,7},{2,0},{3,1},{6,4},{7,5},{8,10},{9,11},{12,... | collective-permute-start | bytes 589832 | tf_op jit(solution)/shard_map/ppermute | solution.py:374
  7.2 0.7 %collective-permute-start.10 = (f32[2,3,2,32,128]{4,3,2,1,0:T(8,128)}, f32[2,3,2,32,128]{4,3,2,1,0:T(8,128)S(1)}, u32[]{:S(2)}, u32[]{:S(2)}) collective-permute-start(f32[2,3,2,32,128]{4,3,2,1,0:T(8,128)} %forces_ref.1), channel_id=1, source_target_pairs={{1,2},{3,4},{5,6},{2,1},{4,3},{6,5},{9,10},{11,12},{13,14},{10,9},... | collective-permute-start | bytes 589832 | tf_op jit(solution)/shard_map/ppermute | solution.py:374
  7.9 1.4 %collective-permute-start.9 = (f32[2,3,2,32,128]{4,3,2,1,0:T(8,128)}, f32[2,3,2,32,128]{4,3,2,1,0:T(8,128)S(1)}, u32[]{:S(2)}, u32[]{:S(2)}) collective-permute-start(f32[2,3,2,32,128]{4,3,2,1,0:T(8,128)} %forces_ref.1), channel_id=1, source_target_pairs={{0,1},{2,3},{4,5},{6,7},{1,0},{3,2},{5,4},{7,6},{8,9},{10,11},{12,... | collective-permute-start | bytes 589832 | tf_op jit(solution)/shard_map/ppermute | solution.py:374
  9.3 1.5 %collective-permute-start = (f32[2,8,128]{2,1,0:T(8,128)}, f32[2,8,128]{2,1,0:T(8,128)S(1)}, u32[]{:S(2)}, u32[]{:S(2)}) collective-permute-start(f32[2,8,128]{2,1,0:T(8,128)} %density_ref.1), channel_id=1, source_target_pairs={{8,0},{0,8},{24,16},{16,24},{9,1},{1,9},{25,17},{17,25},{10,2},{2,... | collective-permute-start | bytes 24584 | tf_op jit(solution)/shard_map/ppermute | solution.py:368
  10.8 2.4 %collective-permute-done.refs_2_ = f32[2,8,128]{2,1,0:T(8,128)S(1)} collective-permute-done((f32[2,8,128]{2,1,0:T(8,128)}, f32[2,8,128]{2,1,0:T(8,128)S(1)}, u32[]{:S(2)}, u32[]{:S(2)}) %collective-permute-start) | collective-permute-done | bytes 8224 | tf_op jit(solution)/shard_map/ppermute | solution.py:368
  13.2 2.4 %collective-permute-start.2 = (f32[2,8,128]{2,1,0:T(8,128)}, f32[2,8,128]{2,1,0:T(8,128)S(1)}, u32[]{:S(2)}, u32[]{:S(2)}) collective-permute-start(f32[2,8,128]{2,1,0:T(8,128)} %density_ref.1), channel_id=1, source_target_pairs={{24,0},{16,8},{8,16},{0,24},{25,1},{17,9},{9,17},{1,25},{26,2},{18... | collective-permute-start | bytes 24584 | tf_op jit(solution)/shard_map/ppermute | solution.py:368
  15.6 2.3 %collective-permute-done.2.refs_4_ = f32[2,8,128]{2,1,0:T(8,128)S(1)} collective-permute-done((f32[2,8,128]{2,1,0:T(8,128)}, f32[2,8,128]{2,1,0:T(8,128)S(1)}, u32[]{:S(2)}, u32[]{:S(2)}) %collective-permute-start.2) | collective-permute-done | bytes 8224 | tf_op jit(solution)/shard_map/ppermute | solution.py:368
  17.9 1.5 %collective-permute-start.1 = (f32[2,8,128]{2,1,0:T(8,128)}, f32[2,8,128]{2,1,0:T(8,128)S(1)}, u32[]{:S(2)}, u32[]{:S(2)}) collective-permute-start(f32[2,8,128]{2,1,0:T(8,128)} %density_ref.1), channel_id=1, source_target_pairs={{16,0},{24,8},{0,16},{8,24},{17,1},{25,9},{1,17},{9,25},{18,2},{26... | collective-permute-start | bytes 24584 | tf_op jit(solution)/shard_map/ppermute | solution.py:368
  19.5 0.9 %copy-done.5 = f32[2,3,2,32,128]{4,3,2,1,0:T(8,128)S(1)} copy-done((f32[2,3,2,32,128]{4,3,2,1,0:T(8,128)S(1)}, f32[2,3,2,32,128]{4,3,2,1,0:T(8,128)}, u32[]{:S(2)}) %copy-start.5) | copy-done | bytes 196632
  20.4 0.8 %copy-done.10 = s32[2,32,128]{2,1,0:T(8,128)S(1)} copy-done((s32[2,32,128]{2,1,0:T(8,128)S(1)}, s32[2,32,128]{2,1,0:T(8,128)}, u32[]{:S(2)}) %copy-start.10) | copy-done | bytes 32792
  21.2 0.7 %copy-done.11 = f32[2,8,128]{2,1,0:T(8,128)S(1)} copy-done((f32[2,8,128]{2,1,0:T(8,128)S(1)}, f32[2,8,128]{2,1,0:T(8,128)}, u32[]{:S(2)}) %copy-start.11) | copy-done | bytes 8216
  21.9 0.0 copy-done.13
  21.9 0.0 copy-done.14
  21.9 0.0 copy-start.6
  21.9 0.6 copy-done.6
  22.5 0.6 copy-done.8
  23.1 0.0 collective-permute-done.1.refs_3_
  23.1 0.0 collective-permute-done.4.refs_6_.refs_10_
  23.1 0.0 collective-permute-done.3.refs_5_.refs_9_
  23.1 0.0 copy-start.2
  23.1 0.6 copy-done.15
  23.7 0.1 copy-done
  23.8 0.1 copy-done.2
  23.9 1.4 %shard_map.60.refs_1_ = f32[2,2,32,128]{3,2,1,0:T(8,128)} custom-call(f32[2,32,128]{2,1,0:T(8,128)} %copy-done.6, f32[2,8,128]{2,1,0:T(8,128)} %copy-done.8, f32[2,8,128]{2,1,0:T(8,128)} %copy-done.13, f32[2,8,128]{2,1,0:T(8,128)} %copy-done.15, f32[2,8,128]{2,1,0:T(8,128)} %copy-done.14, f32[2,3,2,32,128]{4,3,2,1,0:T(8,128)} %copy-done.2, ...), custom_call_target="tpu_custom_call" | custom-call | flops 1000000 | bytes 100000 | tf_op jit(solution)/shard_map/pallas_call | solution.py:414
  25.3 0.8 %collective-permute-start.8 = (f32[2,2,32,128]{3,2,1,0:T(8,128)}, f32[2,2,32,128]{3,2,1,0:T(8,128)S(1)}, u32[]{:S(2)}, u32[]{:S(2)}) collective-permute-start(f32[2,2,32,128]{3,2,1,0:T(8,128)} %shard_map.60.refs_1_), channel_id=1, source_target_pairs={{2,4},{3,5},{4,2},{5,3},{10,12},{11,13},{12,10},{13,11},{18,20},{1... | collective-permute-start | bytes 196616 | tf_op jit(solution)/shard_map/ppermute | solution.py:374
  26.1 3.8 %collective-permute-start.7 = (f32[2,2,32,128]{3,2,1,0:T(8,128)}, f32[2,2,32,128]{3,2,1,0:T(8,128)S(1)}, u32[]{:S(2)}, u32[]{:S(2)}) collective-permute-start(f32[2,2,32,128]{3,2,1,0:T(8,128)} %shard_map.60.refs_1_), channel_id=1, source_target_pairs={{0,2},{1,3},{4,6},{5,7},{2,0},{3,1},{6,4},{7,5},{8,10},{9,11},{12,... | collective-permute-start | bytes 196616 | tf_op jit(solution)/shard_map/ppermute | solution.py:374
  29.8 0.7 collective-permute-start.6
  30.5 0.0 collective-permute-done.10.refs_8_
  30.5 1.4 %collective-permute-start.5 = (f32[2,2,32,128]{3,2,1,0:T(8,128)}, f32[2,2,32,128]{3,2,1,0:T(8,128)S(1)}, u32[]{:S(2)}, u32[]{:S(2)}) collective-permute-start(f32[2,2,32,128]{3,2,1,0:T(8,128)} %shard_map.60.refs_1_), channel_id=1, source_target_pairs={{0,1},{2,3},{4,5},{6,7},{1,0},{3,2},{5,4},{7,6},{8,9},{10,11},{12,... | collective-permute-start | bytes 196616 | tf_op jit(solution)/shard_map/ppermute | solution.py:374
  32.0 0.0 collective-permute-done.9.refs_7_
  32.0 0.0 collective-permute-done.8.refs_5_
  32.0 0.3 collective-permute-done.7.refs_4_
  32.3 0.0 collective-permute-done.6.refs_3_
  32.3 0.8 %collective-permute-done.5.refs_2_ = f32[2,2,32,128]{3,2,1,0:T(8,128)S(1)} collective-permute-done((f32[2,2,32,128]{3,2,1,0:T(8,128)}, f32[2,2,32,128]{3,2,1,0:T(8,128)S(1)}, u32[]{:S(2)}, u32[]{:S(2)}) %collective-permute-start.5) | collective-permute-done | bytes 65568 | tf_op jit(solution)/shard_map/ppermute | solution.py:374
  33.1 0.9 %copy-done.1 = f32[2,3,2,32,128]{4,3,2,1,0:T(8,128)S(1)} copy-done((f32[2,3,2,32,128]{4,3,2,1,0:T(8,128)S(1)}, f32[2,3,2,32,128]{4,3,2,1,0:T(8,128)}, u32[]{:S(2)}) %copy-start.1) | copy-done | bytes 196632
  34.0 0.9 %copy-done.3 = f32[2,3,2,32,128]{4,3,2,1,0:T(8,128)S(1)} copy-done((f32[2,3,2,32,128]{4,3,2,1,0:T(8,128)S(1)}, f32[2,3,2,32,128]{4,3,2,1,0:T(8,128)}, u32[]{:S(2)}) %copy-start.3) | copy-done | bytes 196632
  34.9 0.8 %copy-done.4 = f32[2,2,32,128]{3,2,1,0:T(8,128)S(1)} copy-done((f32[2,2,32,128]{3,2,1,0:T(8,128)S(1)}, f32[2,2,32,128]{3,2,1,0:T(8,128)}, u32[]{:S(2)}) %copy-start.4) | copy-done | bytes 65560
  35.8 6.2 %shard_map.61 = (f32[2,3,2,32,128]{4,3,2,1,0:T(8,128)}, f32[72,128]{1,0:T(8,128)S(1)}, f32[2,32,128]{2,1,0:T(8,128)S(1)}) custom-call(s32[8]{0:T(128)S(1)} %copy-done.12, f32[2,2,32,128]{3,2,1,0:T(8,128)S(1)} %copy-done.4, f32[2,2,32,128]{3,2,1,0:T(8,128)S(1)} %collective-permute-done.5.refs_2_, f32[2,2,32,128]{3,2,1,0:T(8,128)S(1)} %collective-permute-done.6.refs_3_, ...), custom_call_target="tpu_custom_call" | custom-call | flops 60000000 | bytes 2000000 | tf_op jit(solution)/shard_map/pallas_call | solution.py:426
  41.9 1.5 %collective-permute-start.13 = (f32[72,128]{1,0:T(8,128)S(1)}, f32[72,128]{1,0:T(8,128)S(1)}, u32[]{:S(2)}, u32[]{:S(2)}) collective-permute-start(f32[72,128]{1,0:T(8,128)S(1)} %get-tuple-element.14.refs_0_), channel_id=1, source_target_pairs={{24,0},{16,8},{8,16},{0,24},{25,1},{17,9},{9,17},{1,25},{26,2},{18... | collective-permute-start | bytes 110600 | tf_op jit(solution)/shard_map/ppermute | solution.py:368
  43.4 1.5 %collective-permute-start.12 = (f32[72,128]{1,0:T(8,128)S(1)}, f32[72,128]{1,0:T(8,128)S(1)}, u32[]{:S(2)}, u32[]{:S(2)}) collective-permute-start(f32[72,128]{1,0:T(8,128)S(1)} %get-tuple-element.14.refs_0_), channel_id=1, source_target_pairs={{16,0},{24,8},{0,16},{8,24},{17,1},{25,9},{1,17},{9,25},{18,2},{26... | collective-permute-start | bytes 110600 | tf_op jit(solution)/shard_map/ppermute | solution.py:368
  45.0 0.5 collective-permute-start.11
  45.5 1.8 %collective-permute-done.13.refs_3_ = f32[72,128]{1,0:T(8,128)S(1)} collective-permute-done((f32[72,128]{1,0:T(8,128)S(1)}, f32[72,128]{1,0:T(8,128)S(1)}, u32[]{:S(2)}, u32[]{:S(2)}) %collective-permute-start.13) | collective-permute-done | bytes 36896 | tf_op jit(solution)/shard_map/ppermute | solution.py:368
  47.3 0.7 %collective-permute-done.12.refs_2_ = f32[72,128]{1,0:T(8,128)S(1)} collective-permute-done((f32[72,128]{1,0:T(8,128)S(1)}, f32[72,128]{1,0:T(8,128)S(1)}, u32[]{:S(2)}, u32[]{:S(2)}) %collective-permute-start.12) | collective-permute-done | bytes 36896 | tf_op jit(solution)/shard_map/ppermute | solution.py:368
  48.0 0.9 %collective-permute-done.11.refs_1_ = f32[72,128]{1,0:T(8,128)S(1)} collective-permute-done((f32[72,128]{1,0:T(8,128)S(1)}, f32[72,128]{1,0:T(8,128)S(1)}, u32[]{:S(2)}, u32[]{:S(2)}) %collective-permute-start.11) | collective-permute-done | bytes 36896 | tf_op jit(solution)/shard_map/ppermute | solution.py:368
  48.9 0.0 copy-start.9
  49.0 0.1 collective-permute-start.14
  49.0 0.7 %collective-permute-start.15 = (f32[32,128]{1,0:T(8,128)S(1)}, f32[32,128]{1,0:T(8,128)S(1)}, u32[]{:S(2)}, u32[]{:S(2)}) collective-permute-start(f32[32,128]{1,0:T(8,128)S(1)} %get-tuple-element.17), channel_id=1, source_target_pairs={{1,2},{3,4},{5,6},{2,1},{4,3},{6,5},{9,10},{11,12},{13,14},{10,9},... | collective-permute-start | bytes 49160 | tf_op jit(solution)/shard_map/ppermute | solution.py:374
  49.7 4.0 %collective-permute-start.21 = (f32[8,128]{1,0:T(8,128)S(1)}, f32[8,128]{1,0:T(8,128)S(1)}, u32[]{:S(2)}, u32[]{:S(2)}) collective-permute-start(f32[8,128]{1,0:T(8,128)S(1)} %slice.3), channel_id=1, source_target_pairs={{7,0},{6,1},{5,2},{4,3},{3,4},{2,5},{1,6},{0,7},{15,8},{14,9},{13,... | collective-permute-start | bytes 12296 | tf_op jit(solution)/shard_map/ppermute | solution.py:368
  53.7 3.4 %collective-permute-start.20 = (f32[8,128]{1,0:T(8,128)S(1)}, f32[8,128]{1,0:T(8,128)S(1)}, u32[]{:S(2)}, u32[]{:S(2)}) collective-permute-start(f32[8,128]{1,0:T(8,128)S(1)} %slice.3), channel_id=1, source_target_pairs={{6,0},{7,1},{4,2},{5,3},{2,4},{3,5},{0,6},{1,7},{14,8},{15,9},{12,... | collective-permute-start | bytes 12296 | tf_op jit(solution)/shard_map/ppermute | solution.py:368
  57.2 0.0 collective-permute-start.19
  57.2 0.0 collective-permute-done.21.refs_8_
  57.2 1.0 %collective-permute-start.18 = (f32[8,128]{1,0:T(8,128)S(1)}, f32[8,128]{1,0:T(8,128)S(1)}, u32[]{:S(2)}, u32[]{:S(2)}) collective-permute-start(f32[8,128]{1,0:T(8,128)S(1)} %slice.3), channel_id=1, source_target_pairs={{4,0},{5,1},{6,2},{7,3},{0,4},{1,5},{2,6},{3,7},{12,8},{13,9},{14,... | collective-permute-start | bytes 12296 | tf_op jit(solution)/shard_map/ppermute | solution.py:368
  58.2 1.0 %collective-permute-done.20.refs_7_ = f32[8,128]{1,0:T(8,128)S(1)} collective-permute-done((f32[8,128]{1,0:T(8,128)S(1)}, f32[8,128]{1,0:T(8,128)S(1)}, u32[]{:S(2)}, u32[]{:S(2)}) %collective-permute-start.20) | collective-permute-done | bytes 4128 | tf_op jit(solution)/shard_map/ppermute | solution.py:368
  59.1 0.0 collective-permute-start.17
  59.2 1.9 %collective-permute-done.19.refs_6_ = f32[8,128]{1,0:T(8,128)S(1)} collective-permute-done((f32[8,128]{1,0:T(8,128)S(1)}, f32[8,128]{1,0:T(8,128)S(1)}, u32[]{:S(2)}, u32[]{:S(2)}) %collective-permute-start.19) | collective-permute-done | bytes 4128 | tf_op jit(solution)/shard_map/ppermute | solution.py:368
  61.1 0.5 collective-permute-start.16
  61.6 0.1 collective-permute-done.18.refs_5_
  61.7 0.5 collective-permute-done.17.refs_4_
  62.2 2.5 %collective-permute-done.16.refs_3_ = f32[8,128]{1,0:T(8,128)S(1)} collective-permute-done((f32[8,128]{1,0:T(8,128)S(1)}, f32[8,128]{1,0:T(8,128)S(1)}, u32[]{:S(2)}, u32[]{:S(2)}) %collective-permute-start.16) | collective-permute-done | bytes 4128 | tf_op jit(solution)/shard_map/ppermute | solution.py:368
  64.7 0.0 collective-permute-done.15.refs_2_
  64.7 0.0 collective-permute-done.14.refs_1_
  64.7 0.0 copy-done.7
  64.7 0.7 %shard_map.63 = f32[2,8,128]{2,1,0:T(8,128)} custom-call(f32[72,128]{1,0:T(8,128)S(1)} %get-tuple-element.15.refs_0_, f32[40,128]{1,0:T(8,128)S(1)} %collective-permute-done.14.refs_1_, f32[32,128]{1,0:T(8,128)S(1)} %collective-permute-done.15.refs_2_, f32[8,128]{1,0:T(8,128)S(1)} %collective-permute-done.16.refs_3_, ...), custom_call_target="tpu_custom_call" | custom-call | flops 1000000 | bytes 100000 | tf_op jit(solution)/shard_map/pallas_call | solution.py:388
  (18 shorter events, 0.1 us)
Async XLA Ops:
  0.6 22.5 %collective-permute-start.4 = (f32[2,3,2,32,128]{4,3,2,1,0:T(8,128)}, f32[2,3,2,32,128]{4,3,2,1,0:T(8,128)S(1)}, u32[]{:S(2)}, u32[]{:S(2)}) collective-permute-start(f32[2,3,2,32,128]{4,3,2,1,0:T(8,128)} %forces_ref.1), channel_id=1, source_target_pairs={{2,4},{3,5},{4,2},{5,3},{10,12},{11,13},{12,10},{13,11},{18,20},{1... | collective-permute-start | bytes 589832 | tf_op jit(solution)/shard_map/ppermute | solution.py:374
  1.3 21.8 %collective-permute-start.3 = (f32[2,3,2,32,128]{4,3,2,1,0:T(8,128)}, f32[2,3,2,32,128]{4,3,2,1,0:T(8,128)S(1)}, u32[]{:S(2)}, u32[]{:S(2)}) collective-permute-start(f32[2,3,2,32,128]{4,3,2,1,0:T(8,128)} %forces_ref.1), channel_id=1, source_target_pairs={{0,2},{1,3},{4,6},{5,7},{2,0},{3,1},{6,4},{7,5},{8,10},{9,11},{12,... | collective-permute-start | bytes 589832 | tf_op jit(solution)/shard_map/ppermute | solution.py:374
  7.2 23.3 %collective-permute-start.10 = (f32[2,3,2,32,128]{4,3,2,1,0:T(8,128)}, f32[2,3,2,32,128]{4,3,2,1,0:T(8,128)S(1)}, u32[]{:S(2)}, u32[]{:S(2)}) collective-permute-start(f32[2,3,2,32,128]{4,3,2,1,0:T(8,128)} %forces_ref.1), channel_id=1, source_target_pairs={{1,2},{3,4},{5,6},{2,1},{4,3},{6,5},{9,10},{11,12},{13,14},{10,9},... | collective-permute-start | bytes 589832 | tf_op jit(solution)/shard_map/ppermute | solution.py:374
  7.9 24.1 %collective-permute-start.9 = (f32[2,3,2,32,128]{4,3,2,1,0:T(8,128)}, f32[2,3,2,32,128]{4,3,2,1,0:T(8,128)S(1)}, u32[]{:S(2)}, u32[]{:S(2)}) collective-permute-start(f32[2,3,2,32,128]{4,3,2,1,0:T(8,128)} %forces_ref.1), channel_id=1, source_target_pairs={{0,1},{2,3},{4,5},{6,7},{1,0},{3,2},{5,4},{7,6},{8,9},{10,11},{12,... | collective-permute-start | bytes 589832 | tf_op jit(solution)/shard_map/ppermute | solution.py:374
  9.3 3.9 %collective-permute-start = (f32[2,8,128]{2,1,0:T(8,128)}, f32[2,8,128]{2,1,0:T(8,128)S(1)}, u32[]{:S(2)}, u32[]{:S(2)}) collective-permute-start(f32[2,8,128]{2,1,0:T(8,128)} %density_ref.1), channel_id=1, source_target_pairs={{8,0},{0,8},{24,16},{16,24},{9,1},{1,9},{25,17},{17,25},{10,2},{2,... | collective-permute-start | bytes 24584 | tf_op jit(solution)/shard_map/ppermute | solution.py:368
  13.2 8.7 %copy-start.13 = (f32[2,8,128]{2,1,0:T(8,128)}, f32[2,8,128]{2,1,0:T(8,128)S(1)}, u32[]{:S(2)}) copy-start(f32[2,8,128]{2,1,0:T(8,128)S(1)} %collective-permute-done.refs_2_) | copy-start | bytes 24580
  13.2 4.8 %collective-permute-start.2 = (f32[2,8,128]{2,1,0:T(8,128)}, f32[2,8,128]{2,1,0:T(8,128)S(1)}, u32[]{:S(2)}, u32[]{:S(2)}) collective-permute-start(f32[2,8,128]{2,1,0:T(8,128)} %density_ref.1), channel_id=1, source_target_pairs={{24,0},{16,8},{8,16},{0,24},{25,1},{17,9},{9,17},{1,25},{26,2},{18... | collective-permute-start | bytes 24584 | tf_op jit(solution)/shard_map/ppermute | solution.py:368
  17.9 3.9 %copy-start.14 = (f32[2,8,128]{2,1,0:T(8,128)}, f32[2,8,128]{2,1,0:T(8,128)S(1)}, u32[]{:S(2)}) copy-start(f32[2,8,128]{2,1,0:T(8,128)S(1)} %collective-permute-done.2.refs_4_) | copy-start | bytes 24580
  17.9 5.2 %collective-permute-start.1 = (f32[2,8,128]{2,1,0:T(8,128)}, f32[2,8,128]{2,1,0:T(8,128)S(1)}, u32[]{:S(2)}, u32[]{:S(2)}) collective-permute-start(f32[2,8,128]{2,1,0:T(8,128)} %density_ref.1), channel_id=1, source_target_pairs={{16,0},{24,8},{0,16},{8,24},{17,1},{25,9},{1,17},{9,25},{18,2},{26... | collective-permute-start | bytes 24584 | tf_op jit(solution)/shard_map/ppermute | solution.py:368
  19.5 0.9 %copy-start.5 = (f32[2,3,2,32,128]{4,3,2,1,0:T(8,128)S(1)}, f32[2,3,2,32,128]{4,3,2,1,0:T(8,128)}, u32[]{:S(2)}) copy-start(f32[2,3,2,32,128]{4,3,2,1,0:T(8,128)} %forces_ref.1) | copy-start | bytes 589828
  20.4 0.8 %copy-start.10 = (s32[2,32,128]{2,1,0:T(8,128)S(1)}, s32[2,32,128]{2,1,0:T(8,128)}, u32[]{:S(2)}) copy-start(s32[2,32,128]{2,1,0:T(8,128)} %labels_ref.1) | copy-start | bytes 98308
  21.2 0.7 %copy-start.11 = (f32[2,8,128]{2,1,0:T(8,128)S(1)}, f32[2,8,128]{2,1,0:T(8,128)}, u32[]{:S(2)}) copy-start(f32[2,8,128]{2,1,0:T(8,128)} %density_ref.1) | copy-start | bytes 24580
  21.9 0.6 copy-start.6
  22.5 0.6 copy-start.8
  23.1 0.6 copy-start.15
  23.1 0.7 %copy-start = (f32[2,3,2,32,128]{4,3,2,1,0:T(8,128)}, f32[2,3,2,32,128]{4,3,2,1,0:T(8,128)S(1)}, u32[]{:S(2)}) copy-start(f32[2,3,2,32,128]{4,3,2,1,0:T(8,128)S(1)} %collective-permute-done.4.refs_6_.refs_10_) | copy-start | bytes 589828
  23.1 0.7 %copy-start.2 = (f32[2,3,2,32,128]{4,3,2,1,0:T(8,128)}, f32[2,3,2,32,128]{4,3,2,1,0:T(8,128)S(1)}, u32[]{:S(2)}) copy-start(f32[2,3,2,32,128]{4,3,2,1,0:T(8,128)S(1)} %collective-permute-done.3.refs_5_.refs_9_) | copy-start | bytes 589828
  25.3 7.8 %copy-start.12 = (s32[8]{0:T(128)S(1)}, s32[8]{0:T(128)}, u32[]{:S(2)}) copy-start(s32[8]{0:T(128)} %refs_0_.1) | copy-start | bytes 100
  25.3 6.7 %collective-permute-start.8 = (f32[2,2,32,128]{3,2,1,0:T(8,128)}, f32[2,2,32,128]{3,2,1,0:T(8,128)S(1)}, u32[]{:S(2)}, u32[]{:S(2)}) collective-permute-start(f32[2,2,32,128]{3,2,1,0:T(8,128)} %shard_map.60.refs_1_), channel_id=1, source_target_pairs={{2,4},{3,5},{4,2},{5,3},{10,12},{11,13},{12,10},{13,11},{18,20},{1... | collective-permute-start | bytes 196616 | tf_op jit(solution)/shard_map/ppermute | solution.py:374
  26.1 6.2 %collective-permute-start.7 = (f32[2,2,32,128]{3,2,1,0:T(8,128)}, f32[2,2,32,128]{3,2,1,0:T(8,128)S(1)}, u32[]{:S(2)}, u32[]{:S(2)}) collective-permute-start(f32[2,2,32,128]{3,2,1,0:T(8,128)} %shard_map.60.refs_1_), channel_id=1, source_target_pairs={{0,2},{1,3},{4,6},{5,7},{2,0},{3,1},{6,4},{7,5},{8,10},{9,11},{12,... | collective-permute-start | bytes 196616 | tf_op jit(solution)/shard_map/ppermute | solution.py:374
  29.8 2.5 %collective-permute-start.6 = (f32[2,2,32,128]{3,2,1,0:T(8,128)}, f32[2,2,32,128]{3,2,1,0:T(8,128)S(1)}, u32[]{:S(2)}, u32[]{:S(2)}) collective-permute-start(f32[2,2,32,128]{3,2,1,0:T(8,128)} %shard_map.60.refs_1_), channel_id=1, source_target_pairs={{1,2},{3,4},{5,6},{2,1},{4,3},{6,5},{9,10},{11,12},{13,14},{10,9},... | collective-permute-start | bytes 196616 | tf_op jit(solution)/shard_map/ppermute | solution.py:374
  30.5 2.6 %collective-permute-start.5 = (f32[2,2,32,128]{3,2,1,0:T(8,128)}, f32[2,2,32,128]{3,2,1,0:T(8,128)S(1)}, u32[]{:S(2)}, u32[]{:S(2)}) collective-permute-start(f32[2,2,32,128]{3,2,1,0:T(8,128)} %shard_map.60.refs_1_), channel_id=1, source_target_pairs={{0,1},{2,3},{4,5},{6,7},{1,0},{3,2},{5,4},{7,6},{8,9},{10,11},{12,... | collective-permute-start | bytes 196616 | tf_op jit(solution)/shard_map/ppermute | solution.py:374
  33.1 0.9 %copy-start.1 = (f32[2,3,2,32,128]{4,3,2,1,0:T(8,128)S(1)}, f32[2,3,2,32,128]{4,3,2,1,0:T(8,128)}, u32[]{:S(2)}) copy-start(f32[2,3,2,32,128]{4,3,2,1,0:T(8,128)} %copy-done) | copy-start | bytes 589828
  34.0 0.9 %copy-start.3 = (f32[2,3,2,32,128]{4,3,2,1,0:T(8,128)S(1)}, f32[2,3,2,32,128]{4,3,2,1,0:T(8,128)}, u32[]{:S(2)}) copy-start(f32[2,3,2,32,128]{4,3,2,1,0:T(8,128)} %copy-done.2) | copy-start | bytes 589828
  34.9 0.8 %copy-start.4 = (f32[2,2,32,128]{3,2,1,0:T(8,128)S(1)}, f32[2,2,32,128]{3,2,1,0:T(8,128)}, u32[]{:S(2)}) copy-start(f32[2,2,32,128]{3,2,1,0:T(8,128)} %shard_map.60.refs_1_) | copy-start | bytes 196612
  41.9 5.4 %collective-permute-start.13 = (f32[72,128]{1,0:T(8,128)S(1)}, f32[72,128]{1,0:T(8,128)S(1)}, u32[]{:S(2)}, u32[]{:S(2)}) collective-permute-start(f32[72,128]{1,0:T(8,128)S(1)} %get-tuple-element.14.refs_0_), channel_id=1, source_target_pairs={{24,0},{16,8},{8,16},{0,24},{25,1},{17,9},{9,17},{1,25},{26,2},{18... | collective-permute-start | bytes 110600 | tf_op jit(solution)/shard_map/ppermute | solution.py:368
  43.4 4.6 %collective-permute-start.12 = (f32[72,128]{1,0:T(8,128)S(1)}, f32[72,128]{1,0:T(8,128)S(1)}, u32[]{:S(2)}, u32[]{:S(2)}) collective-permute-start(f32[72,128]{1,0:T(8,128)S(1)} %get-tuple-element.14.refs_0_), channel_id=1, source_target_pairs={{16,0},{24,8},{0,16},{8,24},{17,1},{25,9},{1,17},{9,25},{18,2},{26... | collective-permute-start | bytes 110600 | tf_op jit(solution)/shard_map/ppermute | solution.py:368
  45.0 4.0 %collective-permute-start.11 = (f32[72,128]{1,0:T(8,128)S(1)}, f32[72,128]{1,0:T(8,128)S(1)}, u32[]{:S(2)}, u32[]{:S(2)}) collective-permute-start(f32[72,128]{1,0:T(8,128)S(1)} %get-tuple-element.14.refs_0_), channel_id=1, source_target_pairs={{8,0},{0,8},{24,16},{16,24},{9,1},{1,9},{25,17},{17,25},{10,2},{2,... | collective-permute-start | bytes 110600 | tf_op jit(solution)/shard_map/ppermute | solution.py:368
  48.9 15.8 %copy-start.7 = (f32[2,32,128]{2,1,0:T(8,128)S(1)}, f32[2,32,128]{2,1,0:T(8,128)}, u32[]{:S(2)}) copy-start(f32[2,32,128]{2,1,0:T(8,128)} %copy-done.6) | copy-start | bytes 98308
  48.9 15.8 %copy-start.9 = (f32[2,8,128]{2,1,0:T(8,128)S(1)}, f32[2,8,128]{2,1,0:T(8,128)}, u32[]{:S(2)}) copy-start(f32[2,8,128]{2,1,0:T(8,128)} %copy-done.8) | copy-start | bytes 24580
  49.0 15.7 %collective-permute-start.14 = (f32[40,128]{1,0:T(8,128)S(1)}, f32[40,128]{1,0:T(8,128)S(1)}, u32[]{:S(2)}, u32[]{:S(2)}) collective-permute-start(f32[40,128]{1,0:T(8,128)S(1)} %get-tuple-element.16), channel_id=1, source_target_pairs={{0,1},{2,3},{4,5},{6,7},{1,0},{3,2},{5,4},{7,6},{8,9},{10,11},{12,... | collective-permute-start | bytes 61448 | tf_op jit(solution)/shard_map/ppermute | solution.py:374
  49.0 15.7 %collective-permute-start.15 = (f32[32,128]{1,0:T(8,128)S(1)}, f32[32,128]{1,0:T(8,128)S(1)}, u32[]{:S(2)}, u32[]{:S(2)}) collective-permute-start(f32[32,128]{1,0:T(8,128)S(1)} %get-tuple-element.17), channel_id=1, source_target_pairs={{1,2},{3,4},{5,6},{2,1},{4,3},{6,5},{9,10},{11,12},{13,14},{10,9},... | collective-permute-start | bytes 49160 | tf_op jit(solution)/shard_map/ppermute | solution.py:374
  49.7 7.4 %collective-permute-start.21 = (f32[8,128]{1,0:T(8,128)S(1)}, f32[8,128]{1,0:T(8,128)S(1)}, u32[]{:S(2)}, u32[]{:S(2)}) collective-permute-start(f32[8,128]{1,0:T(8,128)S(1)} %slice.3), channel_id=1, source_target_pairs={{7,0},{6,1},{5,2},{4,3},{3,4},{2,5},{1,6},{0,7},{15,8},{14,9},{13,... | collective-permute-start | bytes 12296 | tf_op jit(solution)/shard_map/ppermute | solution.py:368
  53.7 5.4 %collective-permute-start.20 = (f32[8,128]{1,0:T(8,128)S(1)}, f32[8,128]{1,0:T(8,128)S(1)}, u32[]{:S(2)}, u32[]{:S(2)}) collective-permute-start(f32[8,128]{1,0:T(8,128)S(1)} %slice.3), channel_id=1, source_target_pairs={{6,0},{7,1},{4,2},{5,3},{2,4},{3,5},{0,6},{1,7},{14,8},{15,9},{12,... | collective-permute-start | bytes 12296 | tf_op jit(solution)/shard_map/ppermute | solution.py:368
  57.2 3.9 %collective-permute-start.19 = (f32[8,128]{1,0:T(8,128)S(1)}, f32[8,128]{1,0:T(8,128)S(1)}, u32[]{:S(2)}, u32[]{:S(2)}) collective-permute-start(f32[8,128]{1,0:T(8,128)S(1)} %slice.3), channel_id=1, source_target_pairs={{5,0},{4,1},{7,2},{6,3},{1,4},{0,5},{3,6},{2,7},{13,8},{12,9},{15,... | collective-permute-start | bytes 12296 | tf_op jit(solution)/shard_map/ppermute | solution.py:368
  57.2 4.5 %collective-permute-start.18 = (f32[8,128]{1,0:T(8,128)S(1)}, f32[8,128]{1,0:T(8,128)S(1)}, u32[]{:S(2)}, u32[]{:S(2)}) collective-permute-start(f32[8,128]{1,0:T(8,128)S(1)} %slice.3), channel_id=1, source_target_pairs={{4,0},{5,1},{6,2},{7,3},{0,4},{1,5},{2,6},{3,7},{12,8},{13,9},{14,... | collective-permute-start | bytes 12296 | tf_op jit(solution)/shard_map/ppermute | solution.py:368
  59.1 3.0 %collective-permute-start.17 = (f32[8,128]{1,0:T(8,128)S(1)}, f32[8,128]{1,0:T(8,128)S(1)}, u32[]{:S(2)}, u32[]{:S(2)}) collective-permute-start(f32[8,128]{1,0:T(8,128)S(1)} %slice.3), channel_id=1, source_target_pairs={{3,0},{2,1},{1,2},{0,3},{7,4},{6,5},{5,6},{4,7},{11,8},{10,9},{9,1... | collective-permute-start | bytes 12296 | tf_op jit(solution)/shard_map/ppermute | solution.py:368
  61.1 3.6 %collective-permute-start.16 = (f32[8,128]{1,0:T(8,128)S(1)}, f32[8,128]{1,0:T(8,128)S(1)}, u32[]{:S(2)}, u32[]{:S(2)}) collective-permute-start(f32[8,128]{1,0:T(8,128)S(1)} %slice.3), channel_id=1, source_target_pairs={{2,0},{3,1},{0,2},{1,3},{6,4},{7,5},{4,6},{5,7},{10,8},{11,9},{8,1... | collective-permute-start | bytes 12296 | tf_op jit(solution)/shard_map/ppermute | solution.py:368

commit v2 on v1

v2 whole, which is shorter than its diff:
```python
import functools

import jax
import jax.numpy as jnp
from jax import lax
from jax.experimental import pallas as pl
from jax.experimental.pallas import tpu as pltpu
from jax.sharding import PartitionSpec as P

SWEEPS = 3
EMIN = 0.001
LOWER_EIG = 0.1
UPPER_EIG = 2.5
MOVE_LIMIT = 0.2
FLOOR_DENSITY = 0.001
POISSON = 0.3
LAME = POISSON / ((1 + POISSON) * (1 - 2 * POISSON))
SHEAR = 1.0 / (2 * (1 + POISSON))
KE_DIAG = (LAME + 4 * SHEAR) / 9
EDGE = 1.5 - 2.0**0.5
PLANE = ("ss", "sd", "ds", "dd")


def chunks_of(rows):
    return [pl.ds(at, 8) for at in range(0, rows, 8)]


def next_x(a):
    lanes = a.shape[1]
    lane = lax.broadcasted_iota(jnp.int32, a.shape, 1)
    return jnp.where(lane == lanes - 1, 0.0, pltpu.roll(a, lanes - 1, 1))


def last_x(a):
    lane = lax.broadcasted_iota(jnp.int32, a.shape, 1)
    return jnp.where(lane == 0, 0.0, pltpu.roll(a, 1, 1))


def next_y(plane):
    row = lax.broadcasted_iota(jnp.int32, plane[0].shape, 0)
    rolled = [pltpu.roll(a, 7, 0) for a in plane] + [jnp.zeros_like(plane[0])]
    return [jnp.where(row == 7, rolled[at + 1], rolled[at]) for at in range(len(plane))]


def last_y(plane):
    row = lax.broadcasted_iota(jnp.int32, plane[0].shape, 0)
    rolled = [jnp.zeros_like(plane[0])] + [pltpu.roll(a, 1, 0) for a in plane]
    return [jnp.where(row == 0, rolled[at], rolled[at + 1]) for at in range(len(plane))]


def add(*planes):
    return [sum(chunks[1:], chunks[0]) for chunks in zip(*planes)]


def sub(one, other):
    return [a - b for a, b in zip(one, other)]


def to_modes_xy(u):
    ux = [next_x(a) for a in u]
    s, d = add(ux, u), sub(ux, u)
    sy, dy = next_y(s), next_y(d)
    return add(sy, s), sub(sy, s), add(dy, d), sub(dy, d)


def from_modes_xy(ss, sd, ds, dd):
    s = add(sub(ss, sd), last_y(add(ss, sd)))
    d = add(sub(ds, dd), last_y(add(ds, dd)))
    return add(sub(s, d), [last_x(a) for a in add(s, d)])


def modes_z(low, high):
    modes = []
    for comp in range(3):
        one = {}
        for pq in PLANE:
            if pq != "ss":
                one[pq + "s"] = high[comp][pq] + low[comp][pq]
            one[pq + "d"] = high[comp][pq] - low[comp][pq]
        modes.append(one)
    return modes


NORMAL = ((0, "dss"), (1, "sds"), (2, "ssd"))
BENDS = (((1, "dds"), (2, "dsd")), ((0, "dds"), (2, "sdd")), ((0, "dsd"), (1, "sdd")))
SHEARS = (((0, "sds"), (1, "dss")), ((0, "ssd"), (2, "dss")), ((1, "ssd"), (2, "sds")))
STIFF = (SHEAR / 16, SHEAR / 48, (LAME + 4 * SHEAR) / 144, SHEAR / 8)
TWIST = ((0, "sdd"), (1, "dsd"), (2, "dds"))


def mode_forces(modes, e1, e2, e3, e4):
    m = lambda key: modes[key[0]][key[1]]
    out = [{}, {}, {}]

    def put(key, value):
        out[key[0]][key[1]] = value

    trace = (LAME / (2 * SHEAR)) * (m(NORMAL[0]) + m(NORMAL[1]) + m(NORMAL[2]))
    for key in NORMAL:
        put(key, e4 * (trace + m(key)))
    for a, b in BENDS:
        t = (LAME / (3 * SHEAR)) * (m(a) + m(b))
        put(a, e1 * (t + m(a)))
        put(b, e1 * (t + m(b)))
    for a, b in SHEARS:
        f = e1 * (m(a) + m(b))
        put(a, f)
        put(b, f)
    t = m(TWIST[0]) + m(TWIST[1]) + m(TWIST[2])
    for key in TWIST:
        put(key, e2 * (t + m(key)))
    for comp in range(3):
        put((comp, "ddd"), e3 * modes[comp]["ddd"])
    return out


def mode_energy(modes):
    m = lambda key: modes[key[0]][key[1]]
    sq = lambda v: v * v
    n = [m(key) for key in NORMAL]
    total = (3 * LAME / SHEAR) * sq(n[0] + n[1] + n[2]) + 6.0 * (sq(n[0]) + sq(n[1]) + sq(n[2]))
    shear = None
    for a, b in SHEARS:
        t = sq(m(a) + m(b))
        shear = t if shear is None else shear + t
    total = total + 3.0 * shear
    sums, own = None, None
    for a, b in BENDS:
        t = sq(m(a) + m(b))
        o = sq(m(a)) + sq(m(b))
        sums = t if sums is None else sums + t
        own = o if own is None else own + o
    total = total + (LAME / SHEAR) * sums + 3.0 * own
    a, b, c = (m(key) for key in TWIST)
    total = total + (sq(a + b) + sq(a + c) + sq(b + c))
    bulk = sq(modes[0]["ddd"]) + sq(modes[1]["ddd"]) + sq(modes[2]["ddd"])
    return total + ((LAME + 4 * SHEAR) / (3 * SHEAR)) * bulk


def filter_planes(plane):
    x = [last_x(a) + next_x(a) for a in plane]
    cross = add(x, add(last_y(plane), next_y(plane)))
    diagonal = add(last_y(x), next_y(x))
    near = [1.5 * a + 0.5 * c + EDGE * d for a, c, d in zip(plane, cross, diagonal)]
    return near, [0.5 * a + EDGE * c for a, c in zip(plane, cross)]


def filter_layers(layers):
    pairs = [filter_planes(plane) for plane in layers]
    return [
        add(pairs[at][0], add(pairs[at - 1][1], pairs[at + 1][1])) for at in range(1, len(layers) - 1)
    ]


def partner(index, step):
    return index ^ step


def smooth_kernel(hops, count_gz, *refs):
    blocks = 1 + 2 * hops
    weights_ref = refs[0]
    pack_refs = refs[1 : 1 + blocks]
    disp_hbm, own_ref = refs[1 + blocks : 3 + blocks]
    slot_refs = refs[3 + blocks : -11]
    stiff_ref, inv_ref, res_ref, step_ref, sol_ref, mode_ref, node_ref = refs[-11:-4]
    disp_ref, weight_ref, energy_ref, disp_sem = refs[-4:]

    cases, _, layers, rows, columns = disp_ref.shape
    nodes = layers + 2 * SWEEPS + 1
    chunks = chunks_of(rows)
    gz = lax.axis_index("gz")
    load = lax.axis_index("load")
    even = gz % 2 == 0

    def packed(layer, group, kind):
        hop = layer // layers
        plane = pack_plane(cases, layers, group, kind, layer - hop * layers)
        if hop == 0:
            return [pack_refs[0][plane, chunk] for chunk in chunks]
        far = abs(hop)
        beside, across = pack_refs[2 * far - 1], pack_refs[2 * far]
        by_sibling = even == (hop > 0)
        return [jnp.where(by_sibling, beside[plane, chunk], across[plane, chunk]) for chunk in chunks]

    def inside(layer):
        owner = gz + layer // layers
        return jnp.logical_and(owner >= 0, owner < count_gz)

    below = None
    for at in range(nodes + 1):
        layer = at - SWEEPS - 1
        live = jnp.where(inside(layer), 1.0, 0.0)
        marks = packed(layer, cases, 1)
        moduli = []
        for chunk_at, (dense, mark) in enumerate(zip(packed(layer, cases, 0), marks)):
            solid = jnp.where(mark == 2.0, 1.0, dense)
            modulus = (EMIN + (1.0 - EMIN) * solid * solid * solid) * live
            moduli.append(modulus)
            if 0 <= layer < layers:
                weight = (3.0 * (1.0 - EMIN)) * solid * solid * dense
                weight_ref[layer, pl.ds(8 + 8 * chunk_at, 8)] = weight
            if 1 <= at < nodes:
                for kind, factor in enumerate(STIFF):
                    stiff_ref[kind, at - 1, chunks[chunk_at]] = modulus * factor
        spread = add(moduli, [last_x(a) for a in moduli])
        spread = add(spread, last_y(spread))
        if at > 0:
            for chunk, mark, low, high in zip(chunks, marks, below, spread):
                free = jnp.logical_and(mark != 1.0, inside(layer))
                diag = jnp.where(free, KE_DIAG * (low + high), 1.0)
                inv_ref[at - 1, chunk] = jnp.where(free, 1.0 / diag, 0.0)
        below = spread

    theta = 0.5 * (UPPER_EIG + LOWER_EIG)
    delta = 0.5 * (UPPER_EIG - LOWER_EIG)
    sigma = theta / delta

    def load_modes(node, chunk):
        return [
            {pq: mode_ref[node, comp * 4 + i, chunk] for i, pq in enumerate(PLANE)}
            for comp in range(3)
        ]

    def store_modes(node, comp, field):
        for i, plane in enumerate(to_modes_xy(field)):
            for chunk, a in zip(chunks, plane):
                mode_ref[node, comp * 4 + i, chunk] = a

    def one_case(case, carry):
        for at in range(nodes):
            for comp in range(3):
                field = []
                for chunk, force in zip(chunks, packed(at - SWEEPS, case, comp)):
                    step = inv_ref[at, chunk] * force * (1.0 / theta)
                    field.append(step)
                    if 1 <= at < nodes - 1:
                        step_ref[comp, at, chunk] = step
                    if SWEEPS <= at <= SWEEPS + layers:
                        sol_ref[comp, at - SWEEPS, chunk] = step
                store_modes(at, comp, field)

        factor = 1.0 / sigma
        for sweep in range(1, SWEEPS + 1):
            factor_next = 1.0 / (2.0 * sigma - factor)
            keep, take = factor_next * factor, 2.0 * factor_next / delta
            first, end = sweep - 1, nodes - sweep
            if sweep > 1:
                for node in range(first, end + 1):
                    for comp in range(3):
                        store_modes(node, comp, [step_ref[comp, node, chunk] for chunk in chunks])
            for chunk in chunks:
                low = load_modes(first, chunk)
                up = None
                for element in range(first, end):
                    high = load_modes(element + 1, chunk)
                    stiff = [stiff_ref[kind, element, chunk] for kind in range(4)]
                    f = mode_forces(modes_z(low, high), *stiff)
                    ups = []
                    for comp in range(3):
                        for i, pq in enumerate(PLANE):
                            diff = f[comp][pq + "d"]
                            at = comp * 4 + i
                            if pq == "ss":
                                ups.append(diff)
                                if up:
                                    node_ref[element, at, chunk] = up[at] - diff
                            else:
                                both = f[comp][pq + "s"]
                                ups.append(both + diff)
                                if up:
                                    node_ref[element, at, chunk] = up[at] + (both - diff)
                    low, up = high, ups
            for node in range(first + 1, end):
                for comp in range(3):
                    g = [[node_ref[node, comp * 4 + i, chunk] for chunk in chunks] for i in range(4)]
                    if sweep == 1:
                        before = packed(node - SWEEPS, case, comp)
                    else:
                        before = [res_ref[comp, node, chunk] for chunk in chunks]
                    for chunk, res in zip(chunks, sub(before, from_modes_xy(*g))):
                        step = keep * step_ref[comp, node, chunk] + take * (inv_ref[node, chunk] * res)
                        if sweep < SWEEPS:
                            res_ref[comp, node, chunk] = res
                            step_ref[comp, node, chunk] = step
                        if SWEEPS <= node <= SWEEPS + layers:
                            sol = sol_ref[comp, node - SWEEPS, chunk] + step
                            sol_ref[comp, node - SWEEPS, chunk] = sol
                            if sweep == SWEEPS and node < SWEEPS + layers:
                                disp_ref[case, comp, node - SWEEPS, chunk] = sol
            factor = factor_next
        pltpu.make_async_copy(disp_ref.at[case], disp_hbm.at[case], disp_sem.at[case]).start()

        weight = weights_ref[load * cases + case].astype(jnp.float32)
        for node in range(layers + 1):
            for comp in range(3):
                store_modes(node, comp, [sol_ref[comp, node, chunk] for chunk in chunks])
        for chunk in chunks:
            low = load_modes(0, chunk)
            for layer in range(layers):
                high = load_modes(layer + 1, chunk)
                energy = weight * mode_energy(modes_z(low, high))
                before = jnp.where(case == 0, 0.0, energy_ref[layer, chunk])
                energy_ref[layer, chunk] = before + energy
                low = high
        return carry

    lax.fori_loop(0, cases, one_case, 0)
    weight_sum = weights_ref[0]
    for at in range(1, weights_ref.shape[0]):
        weight_sum = weight_sum + weights_ref[at]
    weight_sum = jnp.full((8, columns), weight_sum.astype(jnp.float32))
    scale = (SHEAR / 48) / weight_sum

    spans = filter_layers([packed(layer, cases, 0) for layer in range(-2, layers + 2)])
    recs = [
        [jnp.where(inside(layer), 1.0 / jnp.where(inside(layer), a, 1.0), 0.0) for a in span]
        for layer, span in zip(range(-1, layers + 1), spans)
    ]
    shares = filter_layers(recs)
    total = jnp.zeros((8, columns), jnp.float32)
    own_rows = own_ref.shape[2]
    own = pl.ds(pl.multiple_of(load * own_rows, own_rows), own_rows)
    for layer in range(layers):
        for kind in range(2):
            own_ref[1 + kind, layer] = pack_refs[0][pack_plane(cases, layers, cases, kind, layer), own]
        for at, chunk in enumerate(chunks):
            inner = pl.ds(8 + 8 * at, 8)
            sens = weight_ref[layer, inner] * (energy_ref[layer, chunk] * scale)
            weight_ref[layer, inner] = sens
            total = total + sens * shares[layer][at]
            energy_ref[layer, chunk] = recs[layer + 1][at]
        own_ref[0, layer] = energy_ref[layer, own]
        weight_ref[layer, :8] = jnp.zeros((8, columns), jnp.float32)
        weight_ref[layer, 8 + rows :] = jnp.zeros((8, columns), jnp.float32)
    share = jnp.sum(total, axis=0, keepdims=True)
    wide = own_rows + 2
    for step, slot_ref in enumerate(slot_refs):
        start = pl.multiple_of(partner(load, step) * own_rows, own_rows)
        for layer in range(layers):
            window = weight_ref[layer, pl.ds(start, own_rows + 16)]
            slot_ref[layer * wide : (layer + 1) * wide] = window[7 : 7 + wide]
        slot_ref[layers * wide : layers * wide + 1] = share
    for case in range(cases):
        pltpu.make_async_copy(disp_ref.at[case], disp_hbm.at[case], disp_sem.at[case]).wait()


def pack_plane(cases, layers, group, kind, layer):
    return (group * 3 + kind) * layers + layer


def stage_kernel(labels_ref, forces_ref, pack_ref):
    cases, _, layers, _, _ = forces_ref.shape
    for case in range(cases):
        for comp in range(3):
            for layer in range(layers):
                pack_ref[pack_plane(cases, layers, case, comp, layer)] = forces_ref[case, comp, layer]
    for layer in range(layers):
        marks = labels_ref[layer].astype(jnp.float32)
        pack_ref[pack_plane(cases, layers, cases, 1, layer)] = marks


def design_kernel(cases, *refs):
    density_refs, pack_ref = refs[1:-1], refs[-1]
    layers, own_rows, _ = density_refs[0].shape
    load = lax.axis_index("load")
    for step, density_ref in enumerate(density_refs):
        start = pl.multiple_of(partner(load, step) * own_rows, own_rows)
        for layer in range(layers):
            plane = pack_plane(cases, layers, cases, 0, layer)
            pack_ref[plane, pl.ds(start, own_rows)] = density_ref[layer]


def sum_kernel(*refs):
    total = refs[0][...]
    for ref in refs[1:-1]:
        total = total + ref[...]
    refs[-1][...] = total


def forward_kernel(layers, wide, sum_ref, beside_ref, out_ref):
    even = lax.axis_index("gz") % 2 == 0
    end = layers * wide
    out_ref[:wide] = jnp.where(even, beside_ref[end - wide : end], beside_ref[:wide])
    out_ref[wide : wide + 1] = sum_ref[end : end + 1] + beside_ref[end : end + 1]


def share_kernel(wide, mine_ref, other_ref, out_ref):
    out_ref[...] = mine_ref[...]
    out_ref[wide : wide + 1] = mine_ref[wide : wide + 1] + other_ref[wide : wide + 1]


def chip_masks(count_gz):
    masks = []
    while 2 ** (len(masks) + 1) < count_gz:
        masks.append(2 ** (len(masks) + 1) - 1)
    return masks


def update_kernel(cells, masks, *refs):
    sum_ref, beside_ref, mine_ref = refs[:3]
    other_refs = refs[3:-2]
    own_ref, new_ref = refs[-2:]
    _, layers, own_rows, columns = own_ref.shape
    wide = own_rows + 2
    gz = lax.axis_index("gz")
    even, chip = gz % 2 == 0, gz // 2
    beside = jnp.where(even, beside_ref[:wide], beside_ref[(layers - 1) * wide : layers * wide])
    across = jnp.zeros((wide, columns), jnp.float32)
    for mask, other_ref in zip(masks, other_refs):
        borders = (chip ^ mask) == jnp.where(even, chip - 1, chip + 1)
        across = jnp.where(borders, other_ref[:wide], across)
    numers = [jnp.where(even, across, beside)]
    numers += [sum_ref[layer * wide : (layer + 1) * wide] for layer in range(layers)]
    numers += [jnp.where(even, beside, across)]
    near, far = [], []
    for numer in numers:
        back, mid, front = (numer[at : at + own_rows] for at in range(3))
        sides = back + front
        cross = sides + (last_x(mid) + next_x(mid))
        near.append(1.5 * mid + 0.5 * cross + EDGE * (last_x(sides) + next_x(sides)))
        far.append(0.5 * mid + EDGE * cross)
    total = mine_ref[wide : wide + 1] + other_refs[-1][wide : wide + 1]
    mean = jnp.sum(total, keepdims=True) * (1.0 / cells)
    mean = jnp.broadcast_to(mean, (own_rows, columns))
    for layer in range(layers):
        numer = near[layer + 1] + (far[layer] + far[layer + 2])
        filtered = numer * own_ref[0, layer]
        density = own_ref[1, layer]
        candidate = density * jnp.sqrt(filtered / mean)
        lower = jnp.maximum(density - MOVE_LIMIT, FLOOR_DENSITY)
        upper = jnp.minimum(density + MOVE_LIMIT, 1.0)
        updated = jnp.minimum(jnp.maximum(candidate, lower), upper)
        new_ref[layer] = jnp.where(own_ref[2, layer] == 2.0, 1.0, updated)


def met(block, axis, step):
    count = lax.axis_size(axis)
    return lax.ppermute(block, axis, [(partner(i, step), i) for i in range(count)])


def swapped_across(block, count):
    low = range(1, count - 1, 2)
    return lax.ppermute(block, "gz", [(i, i + 1) for i in low] + [(i + 1, i) for i in low])


def from_neighbours(pack, hops, count):
    beside, across = met(pack, "gz", 1), swapped_across(pack, count)
    blocks = [beside, across]
    for far in range(2, hops + 1):
        beside = met(across, "gz", 1)
        up = [(i - far, i) for i in range(0, count, 2) if i - far >= 0]
        down = [(i + far, i) for i in range(1, count, 2) if i + far < count]
        across = lax.ppermute(pack, "gz", up + down)
        blocks += [beside, across]
    return blocks


def on_device(density, labels, forces, case_weights):
    count_gz, count_load = lax.axis_size("gz"), lax.axis_size("load")
    cases, _, layers, rows, columns = forces.shape
    own_rows = density.shape[1]
    nodes = layers + 2 * SWEEPS + 1
    hops = -(-(SWEEPS + 1) // layers)
    wide = own_rows + 2
    f32 = jnp.float32
    plane = (rows, columns)
    plane_bytes = rows * columns * 4
    vmem = pl.BlockSpec(memory_space=pltpu.VMEM)
    smem = pl.BlockSpec(memory_space=pltpu.SMEM)

    def shape(*dims):
        return jax.ShapeDtypeStruct(dims, f32)

    def call(kernel, out, args, planes, flops, in_specs=None, scratch=(), **more):
        limit = planes * plane_bytes + (2 << 20)
        return pl.pallas_call(
            kernel,
            out_shape=out,
            in_specs=in_specs or [vmem] * len(args),
            out_specs=more.pop("out_specs", vmem),
            scratch_shapes=scratch,
            compiler_params=pltpu.CompilerParams(vmem_limit_bytes=limit),
            cost_estimate=pl.CostEstimate(flops=flops, bytes_accessed=flops // 10, transcendentals=0),
            **more,
        )(*args)

    planes = (cases * 3 + 2) * layers
    pack = call(stage_kernel, shape(planes, rows, columns), (labels, forces), 2 * planes, 1_000_000)
    densities = [density] + [met(density, "load", step) for step in range(1, count_load)]
    pack = call(
        functools.partial(design_kernel, cases),
        shape(planes, rows, columns),
        (pack, *densities),
        2 * planes + 2 * layers,
        100_000,
        input_output_aliases={0: 0},
    )
    packs = [pack] + from_neighbours(pack, hops, count_gz)

    slot_rows = -(-(layers * wide + 1) // 8) * 8
    scratch = [
        pltpu.VMEM((4, nodes - 1) + plane, f32),
        pltpu.VMEM((nodes,) + plane, f32),
        pltpu.VMEM((3, nodes) + plane, f32),
        pltpu.VMEM((3, nodes) + plane, f32),
        pltpu.VMEM((3, layers + 1) + plane, f32),
        pltpu.VMEM((nodes, 12) + plane, f32),
        pltpu.VMEM((nodes, 12) + plane, f32),
        pltpu.VMEM(forces.shape, f32),
        pltpu.VMEM((layers, rows + 16, columns), f32),
        pltpu.VMEM((layers,) + plane, f32),
        pltpu.SemaphoreType.DMA((cases,)),
    ]
    smooth_planes = nodes * 35 + 3 * (layers + 1) + 4 * layers
    smooth_planes += len(packs) * planes + cases * 3 * layers + 8 * layers
    displacement, own, *slots = call(
        functools.partial(smooth_kernel, hops, count_gz),
        (shape(*forces.shape), shape(3, layers, own_rows, columns))
        + (shape(slot_rows, columns),) * count_load,
        (case_weights, *packs),
        smooth_planes,
        60_000_000,
        in_specs=[smem] + [vmem] * len(packs),
        out_specs=(pl.BlockSpec(memory_space=pltpu.HBM),) + (vmem,) * (1 + count_load),
        scratch=scratch,
    )

    received = [met(slots[step], "load", step) for step in range(1, count_load)]
    whole = call(sum_kernel, shape(slot_rows, columns), (slots[0], *received), 2 * count_load, 100_000)
    beside = met(whole, "gz", 1)
    forward_rows = -(-(wide + 1) // 8) * 8
    mine = call(
        functools.partial(forward_kernel, layers, wide),
        shape(forward_rows, columns),
        (whole, beside),
        4 * layers,
        10_000,
    )
    others = []
    masks = chip_masks(count_gz)
    for mask in masks:
        if others:
            mine = call(
                functools.partial(share_kernel, wide),
                shape(forward_rows, columns),
                (mine, others[-1]),
                4,
                10_000,
            )
        others.append(met(mine, "gz", 2 * mask))
    new_density = call(
        functools.partial(update_kernel, float(count_gz * layers * rows * columns), masks),
        shape(*density.shape),
        (whole, beside, mine, *others, own),
        8 * layers,
        100_000,
    )
    return (new_density, displacement)


def solution(mesh):
    return jax.shard_map(
        on_device,
        mesh=mesh,
        in_specs=(
            P("gz", "load", None),
            P("gz", None, None),
            P("load", None, "gz", None, None),
            P(),
        ),
        out_specs=(P("gz", "load", None), P("load", None, "gz", None, None)),
        check_vma=False,
    )
```

time: 66 us -> 43 us (0.65)
  starting transfers between devices: 34 us -> 22.3 us
  local copies, waits for them, and re-layouts: 7.02 us -> 1.69 us
  waiting for transfers between devices: 15.3 us -> 11.6 us
  Pallas kernels: 8.37 us -> 6.49 us
    ppermute x22 -> x13, starting transfers between devices: 34 us -> 22.3 us  [the longest x11 16.9 us: met(): lax.ppermute(block, axis, [(partner(i, step), i) for i in range(count)])]
    unnamed x32 -> x8, local copies, waits for them, and re-layouts: 7.01 us -> 1.69 us
    ppermute x22 -> x13, waiting for transfers between devices: 15.3 us -> 11.6 us  [the longest x11 9.62 us: met(): lax.ppermute(block, axis, [(partner(i, step), i) for i in range(count)])]
    pallas_call x5 -> x7, Pallas kernels: 8.37 us -> 6.49 us  [call(): pl.pallas_call(kernel, out_shape=out, in_specs=in_specs or [vmem] * len(a...]
  transfers between devices with their start and end apart: 22 -> 13, of which waited for: 12 -> 9; matrix products, arithmetic and copies ran while one was open for 0% -> 0% of each run, Pallas kernels for 2% -> 0%
where the time goes in v2:
time: 43 us; the launch traced here: 42.7 us
  starting transfers between devices  22.3 us (52%)
  waiting for transfers between devices  11.6 us (27%)
  Pallas kernels  6.49 us (15%)
  local copies, waits for them, and re-layouts  1.69 us (4%)
  between operations  0.71 us (2%)
    ppermute x11, starting transfers between devices, met(): lax.ppermute(block, axis, [(partner(i, step), i) for i in range(count)])  16.9 us
    ppermute x11, waiting for transfers between devices, met(): lax.ppermute(block, axis, [(partner(i, step), i) for i in range(count)])  9.62 us
    pallas_call x7, Pallas kernels, call(): pl.pallas_call(kernel, out_shape=out, in_specs=in_specs or [vmem] * len(a...  6.49 us
    ppermute x1, starting transfers between devices, from_neighbours(): across = lax.ppermute(pack, 'gz', up + down)  4.74 us
    ppermute x1, waiting for transfers between devices, from_neighbours(): across = lax.ppermute(pack, 'gz', up + down)  1.95 us
    unnamed x8, local copies, waits for them, and re-layouts  1.69 us
  transfers between devices with their start and end apart: 13, of which 9 were waited for; matrix products, arithmetic and copies ran while one was open for 0% of the time, Pallas kernels for 0%

profile of v2, /device:TPU:0, one launch (start us, length us, event | category | flops | bytes accessed | tf_op | source)
XLA Modules:
  0.0 42.7 jit_solution(12592420762000011052)
XLA Ops:
  0.6 3.0 %collective-permute-start.1 = (f32[2,8,128]{2,1,0:T(8,128)}, f32[2,8,128]{2,1,0:T(8,128)S(1)}, u32[]{:S(2)}, u32[]{:S(2)}) collective-permute-start(f32[2,8,128]{2,1,0:T(8,128)} %refs_1_.1), channel_id=1, source_target_pairs={{16,0},{24,8},{0,16},{8,24},{17,1},{25,9},{1,17},{9,25},{18,2},{26... | collective-permute-start | bytes 24584 | tf_op jit(solution)/shard_map/ppermute | solution.py:438
  3.7 1.5 %collective-permute-start = (f32[2,8,128]{2,1,0:T(8,128)}, f32[2,8,128]{2,1,0:T(8,128)S(1)}, u32[]{:S(2)}, u32[]{:S(2)}) collective-permute-start(f32[2,8,128]{2,1,0:T(8,128)} %refs_1_.1), channel_id=1, source_target_pairs={{8,0},{0,8},{24,16},{16,24},{9,1},{1,9},{25,17},{17,25},{10,2},{2,... | collective-permute-start | bytes 24584 | tf_op jit(solution)/shard_map/ppermute | solution.py:438
  5.2 0.0 collective-permute-start.2
  5.2 0.0 copy-start
  5.2 0.9 %copy-done = f32[2,3,2,32,128]{4,3,2,1,0:T(8,128)S(1)} copy-done((f32[2,3,2,32,128]{4,3,2,1,0:T(8,128)S(1)}, f32[2,3,2,32,128]{4,3,2,1,0:T(8,128)}, u32[]{:S(2)}) %copy-start) | copy-done | bytes 196632
  6.1 0.0 copy-start.1
  6.1 0.8 %copy-done.1 = s32[2,32,128]{2,1,0:T(8,128)S(1)} copy-done((s32[2,32,128]{2,1,0:T(8,128)S(1)}, s32[2,32,128]{2,1,0:T(8,128)}, u32[]{:S(2)}) %copy-start.1) | copy-done | bytes 32792
  6.9 0.0 copy-start.2
  6.9 0.0 copy-start.3
  6.9 0.0 collective-permute-done.1.refs_3_
  6.9 0.6 %collective-permute-done.refs_2_ = f32[2,8,128]{2,1,0:T(8,128)S(1)} collective-permute-done((f32[2,8,128]{2,1,0:T(8,128)}, f32[2,8,128]{2,1,0:T(8,128)S(1)}, u32[]{:S(2)}, u32[]{:S(2)}) %collective-permute-start) | collective-permute-done | bytes 8224 | tf_op jit(solution)/shard_map/ppermute | solution.py:438
  7.5 2.4 %collective-permute-done.2.refs_4_ = f32[2,8,128]{2,1,0:T(8,128)S(1)} collective-permute-done((f32[2,8,128]{2,1,0:T(8,128)}, f32[2,8,128]{2,1,0:T(8,128)S(1)}, u32[]{:S(2)}, u32[]{:S(2)}) %collective-permute-start.2) | collective-permute-done | bytes 8224 | tf_op jit(solution)/shard_map/ppermute | solution.py:438
  9.9 0.0 copy-done.2
  9.9 0.7 %collective-permute-start.4 = (f32[16,32,128]{2,1,0:T(8,128)S(1)}, f32[16,32,128]{2,1,0:T(8,128)S(1)}, u32[]{:S(2)}, u32[]{:S(2)}) collective-permute-start(f32[16,32,128]{2,1,0:T(8,128)S(1)} %shard_map.60.refs_1_), channel_id=1, source_target_pairs={{1,2},{3,4},{5,6},{2,1},{4,3},{6,5},{9,10},{11,12},{13,14},{10,9},... | collective-permute-start | bytes 786440 | tf_op jit(solution)/shard_map/ppermute | solution.py:443
  10.6 4.7 %collective-permute-start.6 = (f32[16,32,128]{2,1,0:T(8,128)S(1)}, f32[16,32,128]{2,1,0:T(8,128)S(1)}, u32[]{:S(2)}, u32[]{:S(2)}) collective-permute-start(f32[16,32,128]{2,1,0:T(8,128)S(1)} %shard_map.60.refs_1_), channel_id=1, source_target_pairs={{0,2},{2,4},{4,6},{3,1},{5,3},{7,5},{8,10},{10,12},{12,14},{11,9},... | collective-permute-start | bytes 786440 | tf_op jit(solution)/shard_map/ppermute | solution.py:453
  15.4 0.1 collective-permute-start.3
  15.4 0.0 collective-permute-done.4.refs_3_
  15.4 2.1 %collective-permute-start.5 = (f32[16,32,128]{2,1,0:T(8,128)S(1)}, f32[16,32,128]{2,1,0:T(8,128)S(1)}, u32[]{:S(2)}, u32[]{:S(2)}) collective-permute-start(f32[16,32,128]{2,1,0:T(8,128)S(1)} %collective-permute-done.4.refs_3_), channel_id=1, source_target_pairs={{1,0},{0,1},{3,2},{2,3},{5,4},{4,5},{7,6},{6,7},{9,8},{8,9},{11,10... | collective-permute-start | bytes 786440 | tf_op jit(solution)/shard_map/ppermute | solution.py:438
  17.6 1.9 %collective-permute-done.6.refs_5_ = f32[16,32,128]{2,1,0:T(8,128)S(1)} collective-permute-done((f32[16,32,128]{2,1,0:T(8,128)S(1)}, f32[16,32,128]{2,1,0:T(8,128)S(1)}, u32[]{:S(2)}, u32[]{:S(2)}) %collective-permute-start.6) | collective-permute-done | bytes 262176 | tf_op jit(solution)/shard_map/ppermute | solution.py:453
  19.5 0.0 collective-permute-done.3.refs_2_
  19.5 0.0 collective-permute-done.5.refs_4_
  19.5 0.0 copy-done.3
  19.5 5.7 %shard_map.61 = (f32[2,3,2,32,128]{4,3,2,1,0:T(8,128)}, f32[3,2,8,128]{3,2,1,0:T(8,128)S(1)}, f32[24,128]{1,0:T(8,128)S(1)}, f32[24,128]{1,0:T(8,128)S(1)}, f32[...) custom-call(s32[8]{0:T(128)S(1)} %copy-done.3, f32[16,32,128]{2,1,0:T(8,128)S(1)} %shard_map.60.refs_1_, ...), custom_call_target="tpu_custom_call" | custom-call | flops 60000000 | bytes 6000000 | tf_op jit(solution)/shard_map/pallas_call | solution.py:476
  25.3 0.6 %collective-permute-start.7 = (f32[24,128]{1,0:T(8,128)S(1)}, f32[24,128]{1,0:T(8,128)S(1)}, u32[]{:S(2)}, u32[]{:S(2)}) collective-permute-start(f32[24,128]{1,0:T(8,128)S(1)} %get-tuple-element.9), channel_id=1, source_target_pairs={{8,0},{0,8},{24,16},{16,24},{9,1},{1,9},{25,17},{17,25},{10,2},{2,... | collective-permute-start | bytes 36872 | tf_op jit(solution)/shard_map/ppermute | solution.py:438
  25.9 0.6 %collective-permute-start.8 = (f32[24,128]{1,0:T(8,128)S(1)}, f32[24,128]{1,0:T(8,128)S(1)}, u32[]{:S(2)}, u32[]{:S(2)}) collective-permute-start(f32[24,128]{1,0:T(8,128)S(1)} %get-tuple-element.10), channel_id=1, source_target_pairs={{16,0},{24,8},{0,16},{8,24},{17,1},{25,9},{1,17},{9,25},{18,2},{26... | collective-permute-start | bytes 36872 | tf_op jit(solution)/shard_map/ppermute | solution.py:438
  26.4 2.4 %collective-permute-start.9 = (f32[24,128]{1,0:T(8,128)S(1)}, f32[24,128]{1,0:T(8,128)S(1)}, u32[]{:S(2)}, u32[]{:S(2)}) collective-permute-start(f32[24,128]{1,0:T(8,128)S(1)} %get-tuple-element.11), channel_id=1, source_target_pairs={{24,0},{16,8},{8,16},{0,24},{25,1},{17,9},{9,17},{1,25},{26,2},{18... | collective-permute-start | bytes 36872 | tf_op jit(solution)/shard_map/ppermute | solution.py:438
  28.8 0.2 collective-permute-done.7.refs_1_
  29.0 0.5 %collective-permute-done.8.refs_2_ = f32[24,128]{1,0:T(8,128)S(1)} collective-permute-done((f32[24,128]{1,0:T(8,128)S(1)}, f32[24,128]{1,0:T(8,128)S(1)}, u32[]{:S(2)}, u32[]{:S(2)}) %collective-permute-start.8) | collective-permute-done | bytes 12320 | tf_op jit(solution)/shard_map/ppermute | solution.py:438
  29.6 1.4 %collective-permute-done.9.refs_3_ = f32[24,128]{1,0:T(8,128)S(1)} collective-permute-done((f32[24,128]{1,0:T(8,128)S(1)}, f32[24,128]{1,0:T(8,128)S(1)}, u32[]{:S(2)}, u32[]{:S(2)}) %collective-permute-start.9) | collective-permute-done | bytes 12320 | tf_op jit(solution)/shard_map/ppermute | solution.py:438
  31.0 0.0 collective-permute-start.10
  31.0 1.2 %collective-permute-done.10.beside_ref.refs_1_ = f32[24,128]{1,0:T(8,128)S(1)} collective-permute-done((f32[24,128]{1,0:T(8,128)S(1)}, f32[24,128]{1,0:T(8,128)S(1)}, u32[]{:S(2)}, u32[]{:S(2)}) %collective-permute-start.10) | collective-permute-done | bytes 12320 | tf_op jit(solution)/shard_map/ppermute | solution.py:438
  32.2 2.5 %collective-permute-start.11 = (f32[16,128]{1,0:T(8,128)S(1)}, f32[16,128]{1,0:T(8,128)S(1)}, u32[]{:S(2)}, u32[]{:S(2)}) collective-permute-start(f32[16,128]{1,0:T(8,128)S(1)} %shard_map.63.mine_ref), channel_id=1, source_target_pairs={{2,0},{3,1},{0,2},{1,3},{6,4},{7,5},{4,6},{5,7},{10,8},{11,9},{8,1... | collective-permute-start | bytes 24584 | tf_op jit(solution)/shard_map/ppermute | solution.py:438
  34.7 1.6 %collective-permute-done.11.other_ref.refs_3_ = f32[16,128]{1,0:T(8,128)S(1)} collective-permute-done((f32[16,128]{1,0:T(8,128)S(1)}, f32[16,128]{1,0:T(8,128)S(1)}, u32[]{:S(2)}, u32[]{:S(2)}) %collective-permute-start.11) | collective-permute-done | bytes 8224 | tf_op jit(solution)/shard_map/ppermute | solution.py:438
  36.3 4.0 %collective-permute-start.12 = (f32[16,128]{1,0:T(8,128)S(1)}, f32[16,128]{1,0:T(8,128)S(1)}, u32[]{:S(2)}, u32[]{:S(2)}) collective-permute-start(f32[16,128]{1,0:T(8,128)S(1)} %shard_map.64.refs_2_), channel_id=1, source_target_pairs={{6,0},{7,1},{4,2},{5,3},{2,4},{3,5},{0,6},{1,7},{14,8},{15,9},{12,... | collective-permute-start | bytes 24584 | tf_op jit(solution)/shard_map/ppermute | solution.py:438
  40.4 1.6 %collective-permute-done.12.refs_4_ = f32[16,128]{1,0:T(8,128)S(1)} collective-permute-done((f32[16,128]{1,0:T(8,128)S(1)}, f32[16,128]{1,0:T(8,128)S(1)}, u32[]{:S(2)}, u32[]{:S(2)}) %collective-permute-start.12) | collective-permute-done | bytes 8224 | tf_op jit(solution)/shard_map/ppermute | solution.py:438
  42.0 0.7 %shard_map.65 = f32[2,8,128]{2,1,0:T(8,128)} custom-call(f32[24,128]{1,0:T(8,128)S(1)} %shard_map.62.sum_ref.refs_0_, f32[24,128]{1,0:T(8,128)S(1)} %collective-permute-done.10.beside_ref.refs_1_, f32[16,128]{1,0:T(8,128)S(1)} %shard_map.64.refs_2_, f32[16,128]{1,0:T(8,128)S(1)} %collective-permute-done.11.other_ref.refs_3_, ...), custom_call_target="tpu_custom_call" | custom-call | flops 100000 | bytes 10000 | tf_op jit(solution)/shard_map/pallas_call | solution.py:476
  (5 shorter events, 0.0 us)
Async XLA Ops:
  0.6 6.3 %collective-permute-start.1 = (f32[2,8,128]{2,1,0:T(8,128)}, f32[2,8,128]{2,1,0:T(8,128)S(1)}, u32[]{:S(2)}, u32[]{:S(2)}) collective-permute-start(f32[2,8,128]{2,1,0:T(8,128)} %refs_1_.1), channel_id=1, source_target_pairs={{16,0},{24,8},{0,16},{8,24},{17,1},{25,9},{1,17},{9,25},{18,2},{26... | collective-permute-start | bytes 24584 | tf_op jit(solution)/shard_map/ppermute | solution.py:438
  3.7 3.9 %collective-permute-start = (f32[2,8,128]{2,1,0:T(8,128)}, f32[2,8,128]{2,1,0:T(8,128)S(1)}, u32[]{:S(2)}, u32[]{:S(2)}) collective-permute-start(f32[2,8,128]{2,1,0:T(8,128)} %refs_1_.1), channel_id=1, source_target_pairs={{8,0},{0,8},{24,16},{16,24},{9,1},{1,9},{25,17},{17,25},{10,2},{2,... | collective-permute-start | bytes 24584 | tf_op jit(solution)/shard_map/ppermute | solution.py:438
  5.2 4.8 %collective-permute-start.2 = (f32[2,8,128]{2,1,0:T(8,128)}, f32[2,8,128]{2,1,0:T(8,128)S(1)}, u32[]{:S(2)}, u32[]{:S(2)}) collective-permute-start(f32[2,8,128]{2,1,0:T(8,128)} %refs_1_.1), channel_id=1, source_target_pairs={{24,0},{16,8},{8,16},{0,24},{25,1},{17,9},{9,17},{1,25},{26,2},{18... | collective-permute-start | bytes 24584 | tf_op jit(solution)/shard_map/ppermute | solution.py:438
  5.2 0.9 %copy-start = (f32[2,3,2,32,128]{4,3,2,1,0:T(8,128)S(1)}, f32[2,3,2,32,128]{4,3,2,1,0:T(8,128)}, u32[]{:S(2)}) copy-start(f32[2,3,2,32,128]{4,3,2,1,0:T(8,128)} %forces_ref.1) | copy-start | bytes 589828
  6.1 0.8 %copy-start.1 = (s32[2,32,128]{2,1,0:T(8,128)S(1)}, s32[2,32,128]{2,1,0:T(8,128)}, u32[]{:S(2)}) copy-start(s32[2,32,128]{2,1,0:T(8,128)} %labels_ref.1) | copy-start | bytes 98308
  6.9 3.0 %copy-start.2 = (f32[2,8,128]{2,1,0:T(8,128)S(1)}, f32[2,8,128]{2,1,0:T(8,128)}, u32[]{:S(2)}) copy-start(f32[2,8,128]{2,1,0:T(8,128)} %refs_1_.1) | copy-start | bytes 24580
  6.9 12.6 %copy-start.3 = (s32[8]{0:T(128)S(1)}, s32[8]{0:T(128)}, u32[]{:S(2)}) copy-start(s32[8]{0:T(128)} %refs_0_.1) | copy-start | bytes 100
  9.9 5.5 %collective-permute-start.4 = (f32[16,32,128]{2,1,0:T(8,128)S(1)}, f32[16,32,128]{2,1,0:T(8,128)S(1)}, u32[]{:S(2)}, u32[]{:S(2)}) collective-permute-start(f32[16,32,128]{2,1,0:T(8,128)S(1)} %shard_map.60.refs_1_), channel_id=1, source_target_pairs={{1,2},{3,4},{5,6},{2,1},{4,3},{6,5},{9,10},{11,12},{13,14},{10,9},... | collective-permute-start | bytes 786440 | tf_op jit(solution)/shard_map/ppermute | solution.py:443
  10.6 8.9 %collective-permute-start.6 = (f32[16,32,128]{2,1,0:T(8,128)S(1)}, f32[16,32,128]{2,1,0:T(8,128)S(1)}, u32[]{:S(2)}, u32[]{:S(2)}) collective-permute-start(f32[16,32,128]{2,1,0:T(8,128)S(1)} %shard_map.60.refs_1_), channel_id=1, source_target_pairs={{0,2},{2,4},{4,6},{3,1},{5,3},{7,5},{8,10},{10,12},{12,14},{11,9},... | collective-permute-start | bytes 786440 | tf_op jit(solution)/shard_map/ppermute | solution.py:453
  15.4 4.2 %collective-permute-start.3 = (f32[16,32,128]{2,1,0:T(8,128)S(1)}, f32[16,32,128]{2,1,0:T(8,128)S(1)}, u32[]{:S(2)}, u32[]{:S(2)}) collective-permute-start(f32[16,32,128]{2,1,0:T(8,128)S(1)} %shard_map.60.refs_1_), channel_id=1, source_target_pairs={{1,0},{0,1},{3,2},{2,3},{5,4},{4,5},{7,6},{6,7},{9,8},{8,9},{11,10... | collective-permute-start | bytes 786440 | tf_op jit(solution)/shard_map/ppermute | solution.py:438
  15.4 4.1 %collective-permute-start.5 = (f32[16,32,128]{2,1,0:T(8,128)S(1)}, f32[16,32,128]{2,1,0:T(8,128)S(1)}, u32[]{:S(2)}, u32[]{:S(2)}) collective-permute-start(f32[16,32,128]{2,1,0:T(8,128)S(1)} %collective-permute-done.4.refs_3_), channel_id=1, source_target_pairs={{1,0},{0,1},{3,2},{2,3},{5,4},{4,5},{7,6},{6,7},{9,8},{8,9},{11,10... | collective-permute-start | bytes 786440 | tf_op jit(solution)/shard_map/ppermute | solution.py:438
  25.3 3.8 %collective-permute-start.7 = (f32[24,128]{1,0:T(8,128)S(1)}, f32[24,128]{1,0:T(8,128)S(1)}, u32[]{:S(2)}, u32[]{:S(2)}) collective-permute-start(f32[24,128]{1,0:T(8,128)S(1)} %get-tuple-element.9), channel_id=1, source_target_pairs={{8,0},{0,8},{24,16},{16,24},{9,1},{1,9},{25,17},{17,25},{10,2},{2,... | collective-permute-start | bytes 36872 | tf_op jit(solution)/shard_map/ppermute | solution.py:438
  25.9 3.7 %collective-permute-start.8 = (f32[24,128]{1,0:T(8,128)S(1)}, f32[24,128]{1,0:T(8,128)S(1)}, u32[]{:S(2)}, u32[]{:S(2)}) collective-permute-start(f32[24,128]{1,0:T(8,128)S(1)} %get-tuple-element.10), channel_id=1, source_target_pairs={{16,0},{24,8},{0,16},{8,24},{17,1},{25,9},{1,17},{9,25},{18,2},{26... | collective-permute-start | bytes 36872 | tf_op jit(solution)/shard_map/ppermute | solution.py:438
  26.4 4.6 %collective-permute-start.9 = (f32[24,128]{1,0:T(8,128)S(1)}, f32[24,128]{1,0:T(8,128)S(1)}, u32[]{:S(2)}, u32[]{:S(2)}) collective-permute-start(f32[24,128]{1,0:T(8,128)S(1)} %get-tuple-element.11), channel_id=1, source_target_pairs={{24,0},{16,8},{8,16},{0,24},{25,1},{17,9},{9,17},{1,25},{26,2},{18... | collective-permute-start | bytes 36872 | tf_op jit(solution)/shard_map/ppermute | solution.py:438
  31.0 1.2 %collective-permute-start.10 = (f32[24,128]{1,0:T(8,128)S(1)}, f32[24,128]{1,0:T(8,128)S(1)}, u32[]{:S(2)}, u32[]{:S(2)}) collective-permute-start(f32[24,128]{1,0:T(8,128)S(1)} %shard_map.62.sum_ref.refs_0_), channel_id=1, source_target_pairs={{1,0},{0,1},{3,2},{2,3},{5,4},{4,5},{7,6},{6,7},{9,8},{8,9},{11,10... | collective-permute-start | bytes 36872 | tf_op jit(solution)/shard_map/ppermute | solution.py:438
  32.2 4.1 %collective-permute-start.11 = (f32[16,128]{1,0:T(8,128)S(1)}, f32[16,128]{1,0:T(8,128)S(1)}, u32[]{:S(2)}, u32[]{:S(2)}) collective-permute-start(f32[16,128]{1,0:T(8,128)S(1)} %shard_map.63.mine_ref), channel_id=1, source_target_pairs={{2,0},{3,1},{0,2},{1,3},{6,4},{7,5},{4,6},{5,7},{10,8},{11,9},{8,1... | collective-permute-start | bytes 24584 | tf_op jit(solution)/shard_map/ppermute | solution.py:438
  36.3 5.7 %collective-permute-start.12 = (f32[16,128]{1,0:T(8,128)S(1)}, f32[16,128]{1,0:T(8,128)S(1)}, u32[]{:S(2)}, u32[]{:S(2)}) collective-permute-start(f32[16,128]{1,0:T(8,128)S(1)} %shard_map.64.refs_2_), channel_id=1, source_target_pairs={{6,0},{7,1},{4,2},{5,3},{2,4},{3,5},{0,6},{1,7},{14,8},{15,9},{12,... | collective-permute-start | bytes 24584 | tf_op jit(solution)/shard_map/ppermute | solution.py:438

commit v3 on v2

--- a/solution.py
+++ b/solution.py
@@ -160,8 +160,7 @@
     blocks = 1 + 2 * hops
     weights_ref = refs[0]
     pack_refs = refs[1 : 1 + blocks]
-    disp_hbm, own_ref = refs[1 + blocks : 3 + blocks]
-    slot_refs = refs[3 + blocks : -11]
+    disp_hbm, own_ref, keep_ref, send_ref = refs[1 + blocks : -11]
     stiff_ref, inv_ref, res_ref, step_ref, sol_ref, mode_ref, node_ref = refs[-11:-4]
     disp_ref, weight_ref, energy_ref, disp_sem = refs[-4:]
 
@@ -334,12 +333,15 @@
         weight_ref[layer, 8 + rows :] = jnp.zeros((8, columns), jnp.float32)
     share = jnp.sum(total, axis=0, keepdims=True)
     wide = own_rows + 2
-    for step, slot_ref in enumerate(slot_refs):
+    count_load = rows // own_rows
+    for step in range(count_load):
         start = pl.multiple_of(partner(load, step) * own_rows, own_rows)
+        slot_ref, base = (keep_ref, 0) if step < count_load // 2 else (send_ref, count_load // 2)
+        at = (step - base) * (slot_ref.shape[0] * 2 // count_load)
         for layer in range(layers):
             window = weight_ref[layer, pl.ds(start, own_rows + 16)]
-            slot_ref[layer * wide : (layer + 1) * wide] = window[7 : 7 + wide]
-        slot_ref[layers * wide : layers * wide + 1] = share
+            slot_ref[at + layer * wide : at + (layer + 1) * wide] = window[7 : 7 + wide]
+        slot_ref[at + layers * wide : at + layers * wide + 1] = share
     for case in range(cases):
         pltpu.make_async_copy(disp_ref.at[case], disp_hbm.at[case], disp_sem.at[case]).wait()
 
@@ -359,22 +361,31 @@
         pack_ref[pack_plane(cases, layers, cases, 1, layer)] = marks
 
 
-def design_kernel(cases, *refs):
-    density_refs, pack_ref = refs[1:-1], refs[-1]
-    layers, own_rows, _ = density_refs[0].shape
+def join_kernel(one_ref, other_ref, out_ref):
+    count = one_ref.shape[0]
+    out_ref[:count] = one_ref[...]
+    out_ref[count:] = other_ref[...]
+
+
+def design_kernel(cases, pack_in_ref, near_ref, far_ref, pack_ref):
+    count, layers, own_rows, _ = near_ref.shape
     load = lax.axis_index("load")
-    for step, density_ref in enumerate(density_refs):
+    for step in range(2 * count):
         start = pl.multiple_of(partner(load, step) * own_rows, own_rows)
+        density_ref = near_ref if step < count else far_ref
         for layer in range(layers):
             plane = pack_plane(cases, layers, cases, 0, layer)
-            pack_ref[plane, pl.ds(start, own_rows)] = density_ref[layer]
-
-
-def sum_kernel(*refs):
-    total = refs[0][...]
-    for ref in refs[1:-1]:
-        total = total + ref[...]
-    refs[-1][...] = total
+            pack_ref[plane, pl.ds(start, own_rows)] = density_ref[step % count, layer]
+
+
+def halve_kernel(keep_ref, other_ref, keep_out_ref, send_out_ref):
+    half = keep_out_ref.shape[0]
+    keep_out_ref[...] = keep_ref[:half] + other_ref[:half]
+    send_out_ref[...] = keep_ref[half:] + other_ref[half:]
+
+
+def sum_kernel(keep_ref, other_ref, out_ref):
+    out_ref[...] = keep_ref[...] + other_ref[...]
 
 
 def forward_kernel(layers, wide, sum_ref, beside_ref, out_ref):
@@ -384,19 +395,28 @@
     out_ref[wide : wide + 1] = sum_ref[end : end + 1] + beside_ref[end : end + 1]
 
 
-def share_kernel(wide, mine_ref, other_ref, out_ref):
+def share_kernel(wide, mine_ref, *refs):
+    out_ref = refs[-1]
     out_ref[...] = mine_ref[...]
-    out_ref[wide : wide + 1] = mine_ref[wide : wide + 1] + other_ref[wide : wide + 1]
-
-
-def chip_masks(count_gz):
-    masks = []
-    while 2 ** (len(masks) + 1) < count_gz:
-        masks.append(2 ** (len(masks) + 1) - 1)
-    return masks
-
-
-def update_kernel(cells, masks, *refs):
+    out_ref[wide : wide + 1] = share_sum(wide, mine_ref, *refs[:-1])
+
+
+def share_sum(wide, *refs):
+    total = refs[0][wide : wide + 1]
+    for ref in refs[1:]:
+        total = total + ref[wide : wide + 1]
+    return total
+
+
+def chip_rounds(count_gz):
+    edges = []
+    while 2 ** (len(edges) + 1) < count_gz:
+        edges.append(2 ** (len(edges) + 1) - 1)
+    pairs = [edges[at : at + 2] for at in range(0, len(edges), 2)]
+    return [pair + [pair[0] ^ pair[1]] if len(pair) == 2 else pair for pair in pairs]
+
+
+def update_kernel(cells, rounds, *refs):
     sum_ref, beside_ref, mine_ref = refs[:3]
     other_refs = refs[3:-2]
     own_ref, new_ref = refs[-2:]
@@ -406,7 +426,7 @@
     even, chip = gz % 2 == 0, gz // 2
     beside = jnp.where(even, beside_ref[:wide], beside_ref[(layers - 1) * wide : layers * wide])
     across = jnp.zeros((wide, columns), jnp.float32)
-    for mask, other_ref in zip(masks, other_refs):
+    for mask, other_ref in zip(sum(rounds, []), other_refs):
         borders = (chip ^ mask) == jnp.where(even, chip - 1, chip + 1)
         across = jnp.where(borders, other_ref[:wide], across)
     numers = [jnp.where(even, across, beside)]
@@ -419,7 +439,7 @@
         cross = sides + (last_x(mid) + next_x(mid))
         near.append(1.5 * mid + 0.5 * cross + EDGE * (last_x(sides) + next_x(sides)))
         far.append(0.5 * mid + EDGE * cross)
-    total = mine_ref[wide : wide + 1] + other_refs[-1][wide : wide + 1]
+    total = share_sum(wide, mine_ref, *other_refs[-len(rounds[-1]) :])
     mean = jnp.sum(total, keepdims=True) * (1.0 / cells)
     mean = jnp.broadcast_to(mean, (own_rows, columns))
     for layer in range(layers):
@@ -486,11 +506,16 @@
 
     planes = (cases * 3 + 2) * layers
     pack = call(stage_kernel, shape(planes, rows, columns), (labels, forces), 2 * planes, 1_000_000)
-    densities = [density] + [met(density, "load", step) for step in range(1, count_load)]
+    near = density[None]
+    far = met(near, "load", 1)
+    while 2 * near.shape[0] < count_load:
+        count = near.shape[0]
+        near = call(join_kernel, shape(2 * count, *density.shape), (near, far), 8 * layers, 10_000)
+        far = met(near, "load", 2 * count)
     pack = call(
         functools.partial(design_kernel, cases),
         shape(planes, rows, columns),
-        (pack, *densities),
+        (pack, near, far),
         2 * planes + 2 * layers,
         100_000,
         input_output_aliases={0: 0},
@@ -513,20 +538,32 @@
     ]
     smooth_planes = nodes * 35 + 3 * (layers + 1) + 4 * layers
     smooth_planes += len(packs) * planes + cases * 3 * layers + 8 * layers
-    displacement, own, *slots = call(
+    displacement, own, kept, sent = call(
         functools.partial(smooth_kernel, hops, count_gz),
         (shape(*forces.shape), shape(3, layers, own_rows, columns))
-        + (shape(slot_rows, columns),) * count_load,
+        + (shape(count_load // 2 * slot_rows, columns),) * 2,
         (case_weights, *packs),
         smooth_planes,
         60_000_000,
         in_specs=[smem] + [vmem] * len(packs),
-        out_specs=(pl.BlockSpec(memory_space=pltpu.HBM),) + (vmem,) * (1 + count_load),
+        out_specs=(pl.BlockSpec(memory_space=pltpu.HBM),) + (vmem,) * 3,
         scratch=scratch,
     )
 
-    received = [met(slots[step], "load", step) for step in range(1, count_load)]
-    whole = call(sum_kernel, shape(slot_rows, columns), (slots[0], *received), 2 * count_load, 100_000)
+    step = count_load // 2
+    other = met(sent, "load", step)
+    while step > 1:
+        step //= 2
+        kept, sent = call(
+            halve_kernel,
+            (shape(step * slot_rows, columns),) * 2,
+            (kept, other),
+            2 * count_load,
+            10_000,
+            out_specs=(vmem, vmem),
+        )
+        other = met(sent, "load", step)
+    whole = call(sum_kernel, shape(slot_rows, columns), (kept, other), 4, 10_000)
     beside = met(whole, "gz", 1)
     forward_rows = -(-(wide + 1) // 8) * 8
     mine = call(
@@ -537,19 +574,19 @@
         10_000,
     )
     others = []
-    masks = chip_masks(count_gz)
-    for mask in masks:
-        if others:
+    rounds = chip_rounds(count_gz)
+    for at, masks in enumerate(rounds):
+        if at > 0:
             mine = call(
                 functools.partial(share_kernel, wide),
                 shape(forward_rows, columns),
-                (mine, others[-1]),
-                4,
+                (mine, *others[-len(rounds[at - 1]) :]),
+                8,
                 10_000,
             )
-        others.append(met(mine, "gz", 2 * mask))
+        others += [met(mine, "gz", 2 * mask) for mask in masks]
     new_density = call(
-        functools.partial(update_kernel, float(count_gz * layers * rows * columns), masks),
+        functools.partial(update_kernel, float(count_gz * layers * rows * columns), rounds),
         shape(*density.shape),
         (whole, beside, mine, *others, own),
         8 * layers,

time: 43 us -> 44.5 us (1.035)
  waiting for transfers between devices: 11.6 us -> 14.2 us
  starting transfers between devices: 22.3 us -> 21.2 us
    ppermute x11 -> x10, waiting for transfers between devices: 9.62 us -> 12.3 us  [met(): lax.ppermute(block, axis, [(partner(i, step), i) for i in range(count)])]
    ppermute x11 -> x10, starting transfers between devices: 16.9 us -> 15.3 us  [met(): lax.ppermute(block, axis, [(partner(i, step), i) for i in range(count)])]
    ppermute x1, starting transfers between devices: 4.74 us -> 5.24 us  [from_neighbours(): across = lax.ppermute(pack, 'gz', up + down)]
    pallas_call x7 -> x8, Pallas kernels: 6.49 us -> 6.5 us  [call(): pl.pallas_call(kernel, out_shape=out, in_specs=in_specs or [vmem] * len(a...]
  transfers between devices with their start and end apart: 13 -> 12, of which waited for: 9 -> 7; matrix products, arithmetic and copies ran while one was open for 0% -> 0% of each run, Pallas kernels for 0% -> 0%
where the time goes in v3:
time: 44.5 us; the launch traced here: 44.3 us
  starting transfers between devices  21.2 us (48%)
  waiting for transfers between devices  14.2 us (32%)
  Pallas kernels  6.5 us (15%)
  local copies, waits for them, and re-layouts  1.63 us (4%)
  between operations  0.71 us (2%)
    ppermute x10, starting transfers between devices, met(): lax.ppermute(block, axis, [(partner(i, step), i) for i in range(count)])  15.3 us
    ppermute x10, waiting for transfers between devices, met(): lax.ppermute(block, axis, [(partner(i, step), i) for i in range(count)])  12.3 us
    pallas_call x8, Pallas kernels, call(): pl.pallas_call(kernel, out_shape=out, in_specs=in_specs or [vmem] * len(a...  6.5 us
    ppermute x1, starting transfers between devices, from_neighbours(): across = lax.ppermute(pack, 'gz', up + down)  5.24 us
    ppermute x1, waiting for transfers between devices, from_neighbours(): across = lax.ppermute(pack, 'gz', up + down)  1.95 us
    unnamed x8, local copies, waits for them, and re-layouts  1.63 us
  transfers between devices with their start and end apart: 12, of which 7 were waited for; matrix products, arithmetic and copies ran while one was open for 0% of the time, Pallas kernels for 0%

profile of v3, /device:TPU:0, one launch (start us, length us, event | category | flops | bytes accessed | tf_op | source)
XLA Modules:
  0.0 44.3 jit_solution(15238268032280159057)
XLA Ops:
  0.6 0.0 copy-start.1
  0.6 3.0 %collective-permute-start = (f32[1,2,8,128]{3,2,1,0:T(8,128)}, f32[1,2,8,128]{3,2,1,0:T(8,128)S(1)}, u32[]{:S(2)}, u32[]{:S(2)}) collective-permute-start(f32[1,2,8,128]{3,2,1,0:T(8,128)} %bitcast.1), channel_id=1, source_target_pairs={{8,0},{0,8},{24,16},{16,24},{9,1},{1,9},{25,17},{17,25},{10,2},{2,... | collective-permute-start | bytes 24584 | tf_op jit(solution)/shard_map/ppermute | solution.py:458
  3.6 1.8 %collective-permute-done.other_ref = f32[1,2,8,128]{3,2,1,0:T(8,128)S(1)} collective-permute-done((f32[1,2,8,128]{3,2,1,0:T(8,128)}, f32[1,2,8,128]{3,2,1,0:T(8,128)S(1)}, u32[]{:S(2)}, u32[]{:S(2)}) %collective-permute-start) | collective-permute-done | bytes 8224 | tf_op jit(solution)/shard_map/ppermute | solution.py:458
  5.5 0.0 copy-start.2
  5.5 0.7 %copy-done.2 = f32[2,8,128]{2,1,0:T(8,128)S(1)} copy-done((f32[2,8,128]{2,1,0:T(8,128)S(1)}, f32[2,8,128]{2,1,0:T(8,128)}, u32[]{:S(2)}) %copy-start.2) | copy-done | bytes 8216
  6.2 2.0 %collective-permute-start.1 = (f32[2,2,8,128]{3,2,1,0:T(8,128)S(1)}, f32[2,2,8,128]{3,2,1,0:T(8,128)S(1)}, u32[]{:S(2)}, u32[]{:S(2)}) collective-permute-start(f32[2,2,8,128]{3,2,1,0:T(8,128)S(1)} %shard_map.60.near_ref), channel_id=1, source_target_pairs={{16,0},{24,8},{0,16},{8,24},{17,1},{25,9},{1,17},{9,25},{18,2},{26... | collective-permute-start | bytes 49160 | tf_op jit(solution)/shard_map/ppermute | solution.py:458
  8.2 0.0 copy-done.1
  8.2 0.0 copy-start
  8.2 0.9 %copy-done = f32[2,3,2,32,128]{4,3,2,1,0:T(8,128)S(1)} copy-done((f32[2,3,2,32,128]{4,3,2,1,0:T(8,128)S(1)}, f32[2,3,2,32,128]{4,3,2,1,0:T(8,128)}, u32[]{:S(2)}) %copy-start) | copy-done | bytes 196632
  9.2 0.0 copy-start.3
  9.2 0.8 %collective-permute-done.1.far_ref = f32[2,2,8,128]{3,2,1,0:T(8,128)S(1)} collective-permute-done((f32[2,2,8,128]{3,2,1,0:T(8,128)S(1)}, f32[2,2,8,128]{3,2,1,0:T(8,128)S(1)}, u32[]{:S(2)}, u32[]{:S(2)}) %collective-permute-start.1) | collective-permute-done | bytes 16416 | tf_op jit(solution)/shard_map/ppermute | solution.py:458
  10.0 0.7 %collective-permute-start.3 = (f32[16,32,128]{2,1,0:T(8,128)S(1)}, f32[16,32,128]{2,1,0:T(8,128)S(1)}, u32[]{:S(2)}, u32[]{:S(2)}) collective-permute-start(f32[16,32,128]{2,1,0:T(8,128)S(1)} %shard_map.61.refs_1_), channel_id=1, source_target_pairs={{1,2},{3,4},{5,6},{2,1},{4,3},{6,5},{9,10},{11,12},{13,14},{10,9},... | collective-permute-start | bytes 786440 | tf_op jit(solution)/shard_map/ppermute | solution.py:463
  10.6 5.2 %collective-permute-start.5 = (f32[16,32,128]{2,1,0:T(8,128)S(1)}, f32[16,32,128]{2,1,0:T(8,128)S(1)}, u32[]{:S(2)}, u32[]{:S(2)}) collective-permute-start(f32[16,32,128]{2,1,0:T(8,128)S(1)} %shard_map.61.refs_1_), channel_id=1, source_target_pairs={{0,2},{2,4},{4,6},{3,1},{5,3},{7,5},{8,10},{10,12},{12,14},{11,9},... | collective-permute-start | bytes 786440 | tf_op jit(solution)/shard_map/ppermute | solution.py:473
  15.9 0.1 collective-permute-start.2
  16.0 0.0 collective-permute-done.3.refs_3_
  16.0 2.1 %collective-permute-start.4 = (f32[16,32,128]{2,1,0:T(8,128)S(1)}, f32[16,32,128]{2,1,0:T(8,128)S(1)}, u32[]{:S(2)}, u32[]{:S(2)}) collective-permute-start(f32[16,32,128]{2,1,0:T(8,128)S(1)} %collective-permute-done.3.refs_3_), channel_id=1, source_target_pairs={{1,0},{0,1},{3,2},{2,3},{5,4},{4,5},{7,6},{6,7},{9,8},{8,9},{11,10... | collective-permute-start | bytes 786440 | tf_op jit(solution)/shard_map/ppermute | solution.py:458
  18.1 1.9 %collective-permute-done.5.refs_5_ = f32[16,32,128]{2,1,0:T(8,128)S(1)} collective-permute-done((f32[16,32,128]{2,1,0:T(8,128)S(1)}, f32[16,32,128]{2,1,0:T(8,128)S(1)}, u32[]{:S(2)}, u32[]{:S(2)}) %collective-permute-start.5) | collective-permute-done | bytes 262176 | tf_op jit(solution)/shard_map/ppermute | solution.py:473
  20.0 0.0 collective-permute-done.2.refs_2_
  20.0 0.0 collective-permute-done.4.refs_4_
  20.0 0.0 copy-done.3
  20.1 5.7 %shard_map.62 = (f32[2,3,2,32,128]{4,3,2,1,0:T(8,128)}, f32[3,2,8,128]{3,2,1,0:T(8,128)S(1)}, f32[48,128]{1,0:T(8,128)S(1)}, f32[48,128]{1,0:T(8,128)S(1)}) custom-call(s32[8]{0:T(128)S(1)} %copy-done.3, f32[16,32,128]{2,1,0:T(8,128)S(1)} %shard_map.61.refs_1_, f32[16,32,128]{2,1,0:T(8,128)S(1)} %collective-permute-done.2.refs_2_, ...), custom_call_target="tpu_custom_call" | custom-call | flops 60000000 | bytes 6000000 | tf_op jit(solution)/shard_map/pallas_call | solution.py:496
  25.8 1.6 %collective-permute-start.6 = (f32[48,128]{1,0:T(8,128)S(1)}, f32[48,128]{1,0:T(8,128)S(1)}, u32[]{:S(2)}, u32[]{:S(2)}) collective-permute-start(f32[48,128]{1,0:T(8,128)S(1)} %get-tuple-element.9), channel_id=1, source_target_pairs={{16,0},{24,8},{0,16},{8,24},{17,1},{25,9},{1,17},{9,25},{18,2},{26... | collective-permute-start | bytes 73736 | tf_op jit(solution)/shard_map/ppermute | solution.py:458
  27.4 2.4 %collective-permute-done.6.other_ref = f32[48,128]{1,0:T(8,128)S(1)} collective-permute-done((f32[48,128]{1,0:T(8,128)S(1)}, f32[48,128]{1,0:T(8,128)S(1)}, u32[]{:S(2)}, u32[]{:S(2)}) %collective-permute-start.6) | collective-permute-done | bytes 24608 | tf_op jit(solution)/shard_map/ppermute | solution.py:458
  29.8 1.5 %collective-permute-start.7 = (f32[24,128]{1,0:T(8,128)S(1)}, f32[24,128]{1,0:T(8,128)S(1)}, u32[]{:S(2)}, u32[]{:S(2)}) collective-permute-start(f32[24,128]{1,0:T(8,128)S(1)} %get-tuple-element.11), channel_id=1, source_target_pairs={{8,0},{0,8},{24,16},{16,24},{9,1},{1,9},{25,17},{17,25},{10,2},{2,... | collective-permute-start | bytes 36872 | tf_op jit(solution)/shard_map/ppermute | solution.py:458
  31.3 2.2 %collective-permute-done.7.other_ref = f32[24,128]{1,0:T(8,128)S(1)} collective-permute-done((f32[24,128]{1,0:T(8,128)S(1)}, f32[24,128]{1,0:T(8,128)S(1)}, u32[]{:S(2)}, u32[]{:S(2)}) %collective-permute-start.7) | collective-permute-done | bytes 12320 | tf_op jit(solution)/shard_map/ppermute | solution.py:458
  33.5 0.0 collective-permute-start.8
  33.5 1.2 %collective-permute-done.8.beside_ref.refs_1_ = f32[24,128]{1,0:T(8,128)S(1)} collective-permute-done((f32[24,128]{1,0:T(8,128)S(1)}, f32[24,128]{1,0:T(8,128)S(1)}, u32[]{:S(2)}, u32[]{:S(2)}) %collective-permute-start.8) | collective-permute-done | bytes 12320 | tf_op jit(solution)/shard_map/ppermute | solution.py:458
  34.7 3.4 %collective-permute-start.11 = (f32[16,128]{1,0:T(8,128)S(1)}, f32[16,128]{1,0:T(8,128)S(1)}, u32[]{:S(2)}, u32[]{:S(2)}) collective-permute-start(f32[16,128]{1,0:T(8,128)S(1)} %shard_map.65.refs_2_), channel_id=1, source_target_pairs={{4,0},{5,1},{6,2},{7,3},{0,4},{1,5},{2,6},{3,7},{12,8},{13,9},{14,... | collective-permute-start | bytes 24584 | tf_op jit(solution)/shard_map/ppermute | solution.py:458
  38.1 1.3 %collective-permute-start.10 = (f32[16,128]{1,0:T(8,128)S(1)}, f32[16,128]{1,0:T(8,128)S(1)}, u32[]{:S(2)}, u32[]{:S(2)}) collective-permute-start(f32[16,128]{1,0:T(8,128)S(1)} %shard_map.65.refs_2_), channel_id=1, source_target_pairs={{6,0},{7,1},{4,2},{5,3},{2,4},{3,5},{0,6},{1,7},{14,8},{15,9},{12,... | collective-permute-start | bytes 24584 | tf_op jit(solution)/shard_map/ppermute | solution.py:458
  39.4 0.2 collective-permute-start.9
  39.6 0.0 collective-permute-done.11.refs_5_
  39.7 3.8 %collective-permute-done.10.refs_4_ = f32[16,128]{1,0:T(8,128)S(1)} collective-permute-done((f32[16,128]{1,0:T(8,128)S(1)}, f32[16,128]{1,0:T(8,128)S(1)}, u32[]{:S(2)}, u32[]{:S(2)}) %collective-permute-start.10) | collective-permute-done | bytes 8224 | tf_op jit(solution)/shard_map/ppermute | solution.py:458
  43.5 0.0 collective-permute-done.9.refs_3_
  43.5 0.7 %shard_map.66 = f32[2,8,128]{2,1,0:T(8,128)} custom-call(f32[24,128]{1,0:T(8,128)S(1)} %shard_map.64.sum_ref.refs_0_, f32[24,128]{1,0:T(8,128)S(1)} %collective-permute-done.8.beside_ref.refs_1_, f32[16,128]{1,0:T(8,128)S(1)} %shard_map.65.refs_2_, f32[16,128]{1,0:T(8,128)S(1)} %collective-permute-done.9.refs_3_, ...), custom_call_target="tpu_custom_call" | custom-call | flops 100000 | bytes 10000 | tf_op jit(solution)/shard_map/pallas_call | solution.py:496
  (6 shorter events, 0.0 us)
Async XLA Ops:
  0.6 7.6 %copy-start.1 = (s32[2,32,128]{2,1,0:T(8,128)S(1)}, s32[2,32,128]{2,1,0:T(8,128)}, u32[]{:S(2)}) copy-start(s32[2,32,128]{2,1,0:T(8,128)} %labels_ref.1) | copy-start | bytes 98308
  0.6 4.8 %collective-permute-start = (f32[1,2,8,128]{3,2,1,0:T(8,128)}, f32[1,2,8,128]{3,2,1,0:T(8,128)S(1)}, u32[]{:S(2)}, u32[]{:S(2)}) collective-permute-start(f32[1,2,8,128]{3,2,1,0:T(8,128)} %bitcast.1), channel_id=1, source_target_pairs={{8,0},{0,8},{24,16},{16,24},{9,1},{1,9},{25,17},{17,25},{10,2},{2,... | collective-permute-start | bytes 24584 | tf_op jit(solution)/shard_map/ppermute | solution.py:458
  5.5 0.7 %copy-start.2 = (f32[2,8,128]{2,1,0:T(8,128)S(1)}, f32[2,8,128]{2,1,0:T(8,128)}, u32[]{:S(2)}) copy-start(f32[2,8,128]{2,1,0:T(8,128)} %param.4) | copy-start | bytes 24580
  6.2 3.8 %collective-permute-start.1 = (f32[2,2,8,128]{3,2,1,0:T(8,128)S(1)}, f32[2,2,8,128]{3,2,1,0:T(8,128)S(1)}, u32[]{:S(2)}, u32[]{:S(2)}) collective-permute-start(f32[2,2,8,128]{3,2,1,0:T(8,128)S(1)} %shard_map.60.near_ref), channel_id=1, source_target_pairs={{16,0},{24,8},{0,16},{8,24},{17,1},{25,9},{1,17},{9,25},{18,2},{26... | collective-permute-start | bytes 49160 | tf_op jit(solution)/shard_map/ppermute | solution.py:458
  8.2 0.9 %copy-start = (f32[2,3,2,32,128]{4,3,2,1,0:T(8,128)S(1)}, f32[2,3,2,32,128]{4,3,2,1,0:T(8,128)}, u32[]{:S(2)}) copy-start(f32[2,3,2,32,128]{4,3,2,1,0:T(8,128)} %forces_ref.1) | copy-start | bytes 589828
  9.2 10.9 %copy-start.3 = (s32[8]{0:T(128)S(1)}, s32[8]{0:T(128)}, u32[]{:S(2)}) copy-start(s32[8]{0:T(128)} %refs_0_.1) | copy-start | bytes 100
  10.0 6.0 %collective-permute-start.3 = (f32[16,32,128]{2,1,0:T(8,128)S(1)}, f32[16,32,128]{2,1,0:T(8,128)S(1)}, u32[]{:S(2)}, u32[]{:S(2)}) collective-permute-start(f32[16,32,128]{2,1,0:T(8,128)S(1)} %shard_map.61.refs_1_), channel_id=1, source_target_pairs={{1,2},{3,4},{5,6},{2,1},{4,3},{6,5},{9,10},{11,12},{13,14},{10,9},... | collective-permute-start | bytes 786440 | tf_op jit(solution)/shard_map/ppermute | solution.py:463
  10.6 9.4 %collective-permute-start.5 = (f32[16,32,128]{2,1,0:T(8,128)S(1)}, f32[16,32,128]{2,1,0:T(8,128)S(1)}, u32[]{:S(2)}, u32[]{:S(2)}) collective-permute-start(f32[16,32,128]{2,1,0:T(8,128)S(1)} %shard_map.61.refs_1_), channel_id=1, source_target_pairs={{0,2},{2,4},{4,6},{3,1},{5,3},{7,5},{8,10},{10,12},{12,14},{11,9},... | collective-permute-start | bytes 786440 | tf_op jit(solution)/shard_map/ppermute | solution.py:473
  15.9 4.2 %collective-permute-start.2 = (f32[16,32,128]{2,1,0:T(8,128)S(1)}, f32[16,32,128]{2,1,0:T(8,128)S(1)}, u32[]{:S(2)}, u32[]{:S(2)}) collective-permute-start(f32[16,32,128]{2,1,0:T(8,128)S(1)} %shard_map.61.refs_1_), channel_id=1, source_target_pairs={{1,0},{0,1},{3,2},{2,3},{5,4},{4,5},{7,6},{6,7},{9,8},{8,9},{11,10... | collective-permute-start | bytes 786440 | tf_op jit(solution)/shard_map/ppermute | solution.py:458
  16.0 4.1 %collective-permute-start.4 = (f32[16,32,128]{2,1,0:T(8,128)S(1)}, f32[16,32,128]{2,1,0:T(8,128)S(1)}, u32[]{:S(2)}, u32[]{:S(2)}) collective-permute-start(f32[16,32,128]{2,1,0:T(8,128)S(1)} %collective-permute-done.3.refs_3_), channel_id=1, source_target_pairs={{1,0},{0,1},{3,2},{2,3},{5,4},{4,5},{7,6},{6,7},{9,8},{8,9},{11,10... | collective-permute-start | bytes 786440 | tf_op jit(solution)/shard_map/ppermute | solution.py:458
  25.8 4.0 %collective-permute-start.6 = (f32[48,128]{1,0:T(8,128)S(1)}, f32[48,128]{1,0:T(8,128)S(1)}, u32[]{:S(2)}, u32[]{:S(2)}) collective-permute-start(f32[48,128]{1,0:T(8,128)S(1)} %get-tuple-element.9), channel_id=1, source_target_pairs={{16,0},{24,8},{0,16},{8,24},{17,1},{25,9},{1,17},{9,25},{18,2},{26... | collective-permute-start | bytes 73736 | tf_op jit(solution)/shard_map/ppermute | solution.py:458
  29.8 3.7 %collective-permute-start.7 = (f32[24,128]{1,0:T(8,128)S(1)}, f32[24,128]{1,0:T(8,128)S(1)}, u32[]{:S(2)}, u32[]{:S(2)}) collective-permute-start(f32[24,128]{1,0:T(8,128)S(1)} %get-tuple-element.11), channel_id=1, source_target_pairs={{8,0},{0,8},{24,16},{16,24},{9,1},{1,9},{25,17},{17,25},{10,2},{2,... | collective-permute-start | bytes 36872 | tf_op jit(solution)/shard_map/ppermute | solution.py:458
  33.5 1.2 %collective-permute-start.8 = (f32[24,128]{1,0:T(8,128)S(1)}, f32[24,128]{1,0:T(8,128)S(1)}, u32[]{:S(2)}, u32[]{:S(2)}) collective-permute-start(f32[24,128]{1,0:T(8,128)S(1)} %shard_map.64.sum_ref.refs_0_), channel_id=1, source_target_pairs={{1,0},{0,1},{3,2},{2,3},{5,4},{4,5},{7,6},{6,7},{9,8},{8,9},{11,10... | collective-permute-start | bytes 36872 | tf_op jit(solution)/shard_map/ppermute | solution.py:458
  34.7 5.0 %collective-permute-start.11 = (f32[16,128]{1,0:T(8,128)S(1)}, f32[16,128]{1,0:T(8,128)S(1)}, u32[]{:S(2)}, u32[]{:S(2)}) collective-permute-start(f32[16,128]{1,0:T(8,128)S(1)} %shard_map.65.refs_2_), channel_id=1, source_target_pairs={{4,0},{5,1},{6,2},{7,3},{0,4},{1,5},{2,6},{3,7},{12,8},{13,9},{14,... | collective-permute-start | bytes 24584 | tf_op jit(solution)/shard_map/ppermute | solution.py:458
  38.1 5.4 %collective-permute-start.10 = (f32[16,128]{1,0:T(8,128)S(1)}, f32[16,128]{1,0:T(8,128)S(1)}, u32[]{:S(2)}, u32[]{:S(2)}) collective-permute-start(f32[16,128]{1,0:T(8,128)S(1)} %shard_map.65.refs_2_), channel_id=1, source_target_pairs={{6,0},{7,1},{4,2},{5,3},{2,4},{3,5},{0,6},{1,7},{14,8},{15,9},{12,... | collective-permute-start | bytes 24584 | tf_op jit(solution)/shard_map/ppermute | solution.py:458
  39.4 4.1 %collective-permute-start.9 = (f32[16,128]{1,0:T(8,128)S(1)}, f32[16,128]{1,0:T(8,128)S(1)}, u32[]{:S(2)}, u32[]{:S(2)}) collective-permute-start(f32[16,128]{1,0:T(8,128)S(1)} %shard_map.65.refs_2_), channel_id=1, source_target_pairs={{2,0},{3,1},{0,2},{1,3},{6,4},{7,5},{4,6},{5,7},{10,8},{11,9},{8,1... | collective-permute-start | bytes 24584 | tf_op jit(solution)/shard_map/ppermute | solution.py:458

commit v4 on v2

--- a/solution.py
+++ b/solution.py
@@ -311,7 +311,9 @@
     weight_sum = jnp.full((8, columns), weight_sum.astype(jnp.float32))
     scale = (SHEAR / 48) / weight_sum
 
-    spans = filter_layers([packed(layer, cases, 0) for layer in range(-2, layers + 2)])
+    spans = filter_layers(
+        [[jnp.where(inside(at), a, 0.0) for a in packed(at, cases, 0)] for at in range(-2, layers + 2)]
+    )
     recs = [
         [jnp.where(inside(layer), 1.0 / jnp.where(inside(layer), a, 1.0), 0.0) for a in span]
         for layer, span in zip(range(-1, layers + 1), spans)
@@ -384,19 +386,28 @@
     out_ref[wide : wide + 1] = sum_ref[end : end + 1] + beside_ref[end : end + 1]
 
 
-def share_kernel(wide, mine_ref, other_ref, out_ref):
+def share_kernel(wide, mine_ref, *refs):
+    out_ref = refs[-1]
     out_ref[...] = mine_ref[...]
-    out_ref[wide : wide + 1] = mine_ref[wide : wide + 1] + other_ref[wide : wide + 1]
-
-
-def chip_masks(count_gz):
-    masks = []
-    while 2 ** (len(masks) + 1) < count_gz:
-        masks.append(2 ** (len(masks) + 1) - 1)
-    return masks
-
-
-def update_kernel(cells, masks, *refs):
+    out_ref[wide : wide + 1] = share_sum(wide, mine_ref, *refs[:-1])
+
+
+def share_sum(wide, *refs):
+    total = refs[0][wide : wide + 1]
+    for ref in refs[1:]:
+        total = total + ref[wide : wide + 1]
+    return total
+
+
+def chip_rounds(count_gz):
+    edges = []
+    while 2 ** (len(edges) + 1) < count_gz:
+        edges.append(2 ** (len(edges) + 1) - 1)
+    pairs = [edges[at : at + 2] for at in range(0, len(edges), 2)]
+    return [pair + [pair[0] ^ pair[1]] if len(pair) == 2 else pair for pair in pairs]
+
+
+def update_kernel(cells, rounds, *refs):
     sum_ref, beside_ref, mine_ref = refs[:3]
     other_refs = refs[3:-2]
     own_ref, new_ref = refs[-2:]
@@ -406,7 +417,7 @@
     even, chip = gz % 2 == 0, gz // 2
     beside = jnp.where(even, beside_ref[:wide], beside_ref[(layers - 1) * wide : layers * wide])
     across = jnp.zeros((wide, columns), jnp.float32)
-    for mask, other_ref in zip(masks, other_refs):
+    for mask, other_ref in zip(sum(rounds, []), other_refs):
         borders = (chip ^ mask) == jnp.where(even, chip - 1, chip + 1)
         across = jnp.where(borders, other_ref[:wide], across)
     numers = [jnp.where(even, across, beside)]
@@ -419,7 +430,7 @@
         cross = sides + (last_x(mid) + next_x(mid))
         near.append(1.5 * mid + 0.5 * cross + EDGE * (last_x(sides) + next_x(sides)))
         far.append(0.5 * mid + EDGE * cross)
-    total = mine_ref[wide : wide + 1] + other_refs[-1][wide : wide + 1]
+    total = share_sum(wide, mine_ref, *other_refs[-len(rounds[-1]) :])
     mean = jnp.sum(total, keepdims=True) * (1.0 / cells)
     mean = jnp.broadcast_to(mean, (own_rows, columns))
     for layer in range(layers):
@@ -438,19 +449,18 @@
     return lax.ppermute(block, axis, [(partner(i, step), i) for i in range(count)])
 
 
-def swapped_across(block, count):
+def from_neighbours(pack, hops, count):
     low = range(1, count - 1, 2)
-    return lax.ppermute(block, "gz", [(i, i + 1) for i in low] + [(i + 1, i) for i in low])
-
-
-def from_neighbours(pack, hops, count):
-    beside, across = met(pack, "gz", 1), swapped_across(pack, count)
+    pairs = [(i, i + 1) for i in low] + [(i + 1, i) for i in low] + [(0, 0), (count - 1, count - 1)]
+    beside, across = met(pack, "gz", 1), lax.ppermute(pack, "gz", pairs)
     blocks = [beside, across]
     for far in range(2, hops + 1):
         beside = met(across, "gz", 1)
         up = [(i - far, i) for i in range(0, count, 2) if i - far >= 0]
         down = [(i + far, i) for i in range(1, count, 2) if i + far < count]
-        across = lax.ppermute(pack, "gz", up + down)
+        free = [i for i in range(count) if i not in dict(up + down)]
+        empty = [i for i in range(count) if i not in dict(up + down).values()]
+        across = lax.ppermute(pack, "gz", up + down + list(zip(free, empty)))
         blocks += [beside, across]
     return blocks
 
@@ -537,19 +547,19 @@
         10_000,
     )
     others = []
-    masks = chip_masks(count_gz)
-    for mask in masks:
-        if others:
+    rounds = chip_rounds(count_gz)
+    for at, masks in enumerate(rounds):
+        if at > 0:
             mine = call(
                 functools.partial(share_kernel, wide),
                 shape(forward_rows, columns),
-                (mine, others[-1]),
-                4,
+                (mine, *others[-len(rounds[at - 1]) :]),
+                8,
                 10_000,
             )
-        others.append(met(mine, "gz", 2 * mask))
+        others += [met(mine, "gz", 2 * mask) for mask in masks]
     new_density = call(
-        functools.partial(update_kernel, float(count_gz * layers * rows * columns), masks),
+        functools.partial(update_kernel, float(count_gz * layers * rows * columns), rounds),
         shape(*density.shape),
         (whole, beside, mine, *others, own),
         8 * layers,

time: 43 us -> 43.1 us (level)
    ppermute x11 -> x12, starting transfers between devices: 16.9 us -> 19.1 us  [met(): lax.ppermute(block, axis, [(partner(i, step), i) for i in range(count)])]
    ppermute x2, starting transfers between devices: 5.42 us -> 3.51 us  [the longest x1 2.84 us: from_neighbours(): across = lax.ppermute(pack, 'gz', up + down + list(zip(free, empty)))]
    ppermute x2, waiting for transfers between devices: 1.95 us -> 0.37 us  [the longest x1 0.37 us: from_neighbours(): across = lax.ppermute(pack, 'gz', up + down + list(zip(free, empty)))]
    ppermute x11 -> x12, waiting for transfers between devices: 9.62 us -> 11 us  [met(): lax.ppermute(block, axis, [(partner(i, step), i) for i in range(count)])]
    pallas_call x7 -> x6, Pallas kernels: 6.49 us -> 6.52 us  [call(): pl.pallas_call(kernel, out_shape=out, in_specs=in_specs or [vmem] * len(a...]
  transfers between devices with their start and end apart: 13 -> 14, of which waited for: 9 -> 9; matrix products, arithmetic and copies ran while one was open for 0% -> 0% of each run, Pallas kernels for 0% -> 0%
where the time goes in v4:
time: 43.1 us; the launch traced here: 42.9 us
  starting transfers between devices  22.6 us (52%)
  waiting for transfers between devices  11.4 us (26%)
  Pallas kernels  6.52 us (15%)
  local copies, waits for them, and re-layouts  1.69 us (4%)
  between operations  0.69 us (2%)
    ppermute x12, starting transfers between devices, met(): lax.ppermute(block, axis, [(partner(i, step), i) for i in range(count)])  19.1 us
    ppermute x12, waiting for transfers between devices, met(): lax.ppermute(block, axis, [(partner(i, step), i) for i in range(count)])  11 us
    pallas_call x6, Pallas kernels, call(): pl.pallas_call(kernel, out_shape=out, in_specs=in_specs or [vmem] * len(a...  6.52 us
    ppermute x1, starting transfers between devices, from_neighbours(): across = lax.ppermute(pack, 'gz', up + down + list(zip(free, empty)))  2.84 us
    unnamed x8, local copies, waits for them, and re-layouts  1.69 us
  transfers between devices with their start and end apart: 14, of which 9 were waited for; matrix products, arithmetic and copies ran while one was open for 0% of the time, Pallas kernels for 0%

profile of v4, /device:TPU:0, one launch (start us, length us, event | category | flops | bytes accessed | tf_op | source)
XLA Modules:
  0.0 42.9 jit_solution(15995375503460331586)
XLA Ops:
  0.6 3.0 %collective-permute-start.1 = (f32[2,8,128]{2,1,0:T(8,128)}, f32[2,8,128]{2,1,0:T(8,128)S(1)}, u32[]{:S(2)}, u32[]{:S(2)}) collective-permute-start(f32[2,8,128]{2,1,0:T(8,128)} %refs_1_.1), channel_id=1, source_target_pairs={{16,0},{24,8},{0,16},{8,24},{17,1},{25,9},{1,17},{9,25},{18,2},{26... | collective-permute-start | bytes 24584 | tf_op jit(solution)/shard_map/ppermute | solution.py:449
  3.7 1.5 %collective-permute-start = (f32[2,8,128]{2,1,0:T(8,128)}, f32[2,8,128]{2,1,0:T(8,128)S(1)}, u32[]{:S(2)}, u32[]{:S(2)}) collective-permute-start(f32[2,8,128]{2,1,0:T(8,128)} %refs_1_.1), channel_id=1, source_target_pairs={{8,0},{0,8},{24,16},{16,24},{9,1},{1,9},{25,17},{17,25},{10,2},{2,... | collective-permute-start | bytes 24584 | tf_op jit(solution)/shard_map/ppermute | solution.py:449
  5.2 0.0 collective-permute-start.2
  5.2 0.0 copy-start
  5.2 0.9 %copy-done = f32[2,3,2,32,128]{4,3,2,1,0:T(8,128)S(1)} copy-done((f32[2,3,2,32,128]{4,3,2,1,0:T(8,128)S(1)}, f32[2,3,2,32,128]{4,3,2,1,0:T(8,128)}, u32[]{:S(2)}) %copy-start) | copy-done | bytes 196632
  6.1 0.0 copy-start.1
  6.1 0.8 %copy-done.1 = s32[2,32,128]{2,1,0:T(8,128)S(1)} copy-done((s32[2,32,128]{2,1,0:T(8,128)S(1)}, s32[2,32,128]{2,1,0:T(8,128)}, u32[]{:S(2)}) %copy-start.1) | copy-done | bytes 32792
  6.9 0.0 copy-start.2
  6.9 0.0 copy-start.3
  6.9 0.0 collective-permute-done.1.refs_3_
  6.9 0.6 %collective-permute-done.refs_2_ = f32[2,8,128]{2,1,0:T(8,128)S(1)} collective-permute-done((f32[2,8,128]{2,1,0:T(8,128)}, f32[2,8,128]{2,1,0:T(8,128)S(1)}, u32[]{:S(2)}, u32[]{:S(2)}) %collective-permute-start) | collective-permute-done | bytes 8224 | tf_op jit(solution)/shard_map/ppermute | solution.py:449
  7.5 2.4 %collective-permute-done.2.refs_4_ = f32[2,8,128]{2,1,0:T(8,128)S(1)} collective-permute-done((f32[2,8,128]{2,1,0:T(8,128)}, f32[2,8,128]{2,1,0:T(8,128)S(1)}, u32[]{:S(2)}, u32[]{:S(2)}) %collective-permute-start.2) | collective-permute-done | bytes 8224 | tf_op jit(solution)/shard_map/ppermute | solution.py:449
  9.9 0.0 copy-done.2
  9.9 0.7 %collective-permute-start.4 = (f32[16,32,128]{2,1,0:T(8,128)S(1)}, f32[16,32,128]{2,1,0:T(8,128)S(1)}, u32[]{:S(2)}, u32[]{:S(2)}) collective-permute-start(f32[16,32,128]{2,1,0:T(8,128)S(1)} %shard_map.60.refs_1_), channel_id=1, source_target_pairs={{1,2},{3,4},{5,6},{2,1},{4,3},{6,5},{0,0},{7,7},{9,10},{11,12},{13... | collective-permute-start | bytes 786440 | tf_op jit(solution)/shard_map/ppermute | solution.py:455
  10.6 2.8 %collective-permute-start.6 = (f32[16,32,128]{2,1,0:T(8,128)S(1)}, f32[16,32,128]{2,1,0:T(8,128)S(1)}, u32[]{:S(2)}, u32[]{:S(2)}) collective-permute-start(f32[16,32,128]{2,1,0:T(8,128)S(1)} %shard_map.60.refs_1_), channel_id=1, source_target_pairs={{0,2},{2,4},{4,6},{3,1},{5,3},{7,5},{1,0},{6,7},{8,10},{10,12},{12... | collective-permute-start | bytes 786440 | tf_op jit(solution)/shard_map/ppermute | solution.py:463
  13.4 0.2 collective-permute-start.3
  13.6 0.0 collective-permute-done.4.refs_3_
  13.6 5.5 %collective-permute-start.5 = (f32[16,32,128]{2,1,0:T(8,128)S(1)}, f32[16,32,128]{2,1,0:T(8,128)S(1)}, u32[]{:S(2)}, u32[]{:S(2)}) collective-permute-start(f32[16,32,128]{2,1,0:T(8,128)S(1)} %collective-permute-done.4.refs_3_), channel_id=1, source_target_pairs={{1,0},{0,1},{3,2},{2,3},{5,4},{4,5},{7,6},{6,7},{9,8},{8,9},{11,10... | collective-permute-start | bytes 786440 | tf_op jit(solution)/shard_map/ppermute | solution.py:449
  19.2 0.4 collective-permute-done.6.refs_5_
  19.5 0.0 collective-permute-done.3.refs_2_
  19.5 0.8 %collective-permute-done.5.refs_4_ = f32[16,32,128]{2,1,0:T(8,128)S(1)} collective-permute-done((f32[16,32,128]{2,1,0:T(8,128)S(1)}, f32[16,32,128]{2,1,0:T(8,128)S(1)}, u32[]{:S(2)}, u32[]{:S(2)}) %collective-permute-start.5) | collective-permute-done | bytes 262176 | tf_op jit(solution)/shard_map/ppermute | solution.py:449
  20.3 0.0 copy-done.3
  20.3 5.7 %shard_map.61 = (f32[2,3,2,32,128]{4,3,2,1,0:T(8,128)}, f32[3,2,8,128]{3,2,1,0:T(8,128)S(1)}, f32[24,128]{1,0:T(8,128)S(1)}, f32[24,128]{1,0:T(8,128)S(1)}, f32[...) custom-call(s32[8]{0:T(128)S(1)} %copy-done.3, f32[16,32,128]{2,1,0:T(8,128)S(1)} %shard_map.60.refs_1_, ...), custom_call_target="tpu_custom_call" | custom-call | flops 60000000 | bytes 6000000 | tf_op jit(solution)/shard_map/pallas_call | solution.py:486
  26.1 0.6 %collective-permute-start.7 = (f32[24,128]{1,0:T(8,128)S(1)}, f32[24,128]{1,0:T(8,128)S(1)}, u32[]{:S(2)}, u32[]{:S(2)}) collective-permute-start(f32[24,128]{1,0:T(8,128)S(1)} %get-tuple-element.9), channel_id=1, source_target_pairs={{8,0},{0,8},{24,16},{16,24},{9,1},{1,9},{25,17},{17,25},{10,2},{2,... | collective-permute-start | bytes 36872 | tf_op jit(solution)/shard_map/ppermute | solution.py:449
  26.7 0.6 %collective-permute-start.8 = (f32[24,128]{1,0:T(8,128)S(1)}, f32[24,128]{1,0:T(8,128)S(1)}, u32[]{:S(2)}, u32[]{:S(2)}) collective-permute-start(f32[24,128]{1,0:T(8,128)S(1)} %get-tuple-element.10), channel_id=1, source_target_pairs={{16,0},{24,8},{0,16},{8,24},{17,1},{25,9},{1,17},{9,25},{18,2},{26... | collective-permute-start | bytes 36872 | tf_op jit(solution)/shard_map/ppermute | solution.py:449
  27.2 2.4 %collective-permute-start.9 = (f32[24,128]{1,0:T(8,128)S(1)}, f32[24,128]{1,0:T(8,128)S(1)}, u32[]{:S(2)}, u32[]{:S(2)}) collective-permute-start(f32[24,128]{1,0:T(8,128)S(1)} %get-tuple-element.11), channel_id=1, source_target_pairs={{24,0},{16,8},{8,16},{0,24},{25,1},{17,9},{9,17},{1,25},{26,2},{18... | collective-permute-start | bytes 36872 | tf_op jit(solution)/shard_map/ppermute | solution.py:449
  29.6 0.2 collective-permute-done.7.refs_1_
  29.8 0.5 %collective-permute-done.8.refs_2_ = f32[24,128]{1,0:T(8,128)S(1)} collective-permute-done((f32[24,128]{1,0:T(8,128)S(1)}, f32[24,128]{1,0:T(8,128)S(1)}, u32[]{:S(2)}, u32[]{:S(2)}) %collective-permute-start.8) | collective-permute-done | bytes 12320 | tf_op jit(solution)/shard_map/ppermute | solution.py:449
  30.4 1.5 %collective-permute-done.9.refs_3_ = f32[24,128]{1,0:T(8,128)S(1)} collective-permute-done((f32[24,128]{1,0:T(8,128)S(1)}, f32[24,128]{1,0:T(8,128)S(1)}, u32[]{:S(2)}, u32[]{:S(2)}) %collective-permute-start.9) | collective-permute-done | bytes 12320 | tf_op jit(solution)/shard_map/ppermute | solution.py:449
  31.8 0.0 collective-permute-start.10
  31.9 1.2 %collective-permute-done.10.beside_ref.refs_1_ = f32[24,128]{1,0:T(8,128)S(1)} collective-permute-done((f32[24,128]{1,0:T(8,128)S(1)}, f32[24,128]{1,0:T(8,128)S(1)}, u32[]{:S(2)}, u32[]{:S(2)}) %collective-permute-start.10) | collective-permute-done | bytes 12320 | tf_op jit(solution)/shard_map/ppermute | solution.py:449
  33.0 3.6 %collective-permute-start.13 = (f32[16,128]{1,0:T(8,128)S(1)}, f32[16,128]{1,0:T(8,128)S(1)}, u32[]{:S(2)}, u32[]{:S(2)}) collective-permute-start(f32[16,128]{1,0:T(8,128)S(1)} %shard_map.63.refs_2_), channel_id=1, source_target_pairs={{4,0},{5,1},{6,2},{7,3},{0,4},{1,5},{2,6},{3,7},{12,8},{13,9},{14,... | collective-permute-start | bytes 24584 | tf_op jit(solution)/shard_map/ppermute | solution.py:449
  36.7 1.3 %collective-permute-start.12 = (f32[16,128]{1,0:T(8,128)S(1)}, f32[16,128]{1,0:T(8,128)S(1)}, u32[]{:S(2)}, u32[]{:S(2)}) collective-permute-start(f32[16,128]{1,0:T(8,128)S(1)} %shard_map.63.refs_2_), channel_id=1, source_target_pairs={{6,0},{7,1},{4,2},{5,3},{2,4},{3,5},{0,6},{1,7},{14,8},{15,9},{12,... | collective-permute-start | bytes 24584 | tf_op jit(solution)/shard_map/ppermute | solution.py:449
  38.0 0.2 collective-permute-start.11
  38.3 0.0 collective-permute-done.13.refs_5_
  38.3 3.8 %collective-permute-done.12.refs_4_ = f32[16,128]{1,0:T(8,128)S(1)} collective-permute-done((f32[16,128]{1,0:T(8,128)S(1)}, f32[16,128]{1,0:T(8,128)S(1)}, u32[]{:S(2)}, u32[]{:S(2)}) %collective-permute-start.12) | collective-permute-done | bytes 8224 | tf_op jit(solution)/shard_map/ppermute | solution.py:449
  42.1 0.0 collective-permute-done.11.refs_3_
  42.1 0.7 %shard_map.64 = f32[2,8,128]{2,1,0:T(8,128)} custom-call(f32[24,128]{1,0:T(8,128)S(1)} %shard_map.62.sum_ref.refs_0_, f32[24,128]{1,0:T(8,128)S(1)} %collective-permute-done.10.beside_ref.refs_1_, f32[16,128]{1,0:T(8,128)S(1)} %shard_map.63.refs_2_, f32[16,128]{1,0:T(8,128)S(1)} %collective-permute-done.11.refs_3_, ...), custom_call_target="tpu_custom_call" | custom-call | flops 100000 | bytes 10000 | tf_op jit(solution)/shard_map/pallas_call | solution.py:486
  (4 shorter events, 0.0 us)
Async XLA Ops:
  0.6 6.3 %collective-permute-start.1 = (f32[2,8,128]{2,1,0:T(8,128)}, f32[2,8,128]{2,1,0:T(8,128)S(1)}, u32[]{:S(2)}, u32[]{:S(2)}) collective-permute-start(f32[2,8,128]{2,1,0:T(8,128)} %refs_1_.1), channel_id=1, source_target_pairs={{16,0},{24,8},{0,16},{8,24},{17,1},{25,9},{1,17},{9,25},{18,2},{26... | collective-permute-start | bytes 24584 | tf_op jit(solution)/shard_map/ppermute | solution.py:449
  3.7 3.9 %collective-permute-start = (f32[2,8,128]{2,1,0:T(8,128)}, f32[2,8,128]{2,1,0:T(8,128)S(1)}, u32[]{:S(2)}, u32[]{:S(2)}) collective-permute-start(f32[2,8,128]{2,1,0:T(8,128)} %refs_1_.1), channel_id=1, source_target_pairs={{8,0},{0,8},{24,16},{16,24},{9,1},{1,9},{25,17},{17,25},{10,2},{2,... | collective-permute-start | bytes 24584 | tf_op jit(solution)/shard_map/ppermute | solution.py:449
  5.2 4.8 %collective-permute-start.2 = (f32[2,8,128]{2,1,0:T(8,128)}, f32[2,8,128]{2,1,0:T(8,128)S(1)}, u32[]{:S(2)}, u32[]{:S(2)}) collective-permute-start(f32[2,8,128]{2,1,0:T(8,128)} %refs_1_.1), channel_id=1, source_target_pairs={{24,0},{16,8},{8,16},{0,24},{25,1},{17,9},{9,17},{1,25},{26,2},{18... | collective-permute-start | bytes 24584 | tf_op jit(solution)/shard_map/ppermute | solution.py:449
  5.2 0.9 %copy-start = (f32[2,3,2,32,128]{4,3,2,1,0:T(8,128)S(1)}, f32[2,3,2,32,128]{4,3,2,1,0:T(8,128)}, u32[]{:S(2)}) copy-start(f32[2,3,2,32,128]{4,3,2,1,0:T(8,128)} %forces_ref.1) | copy-start | bytes 589828
  6.1 0.8 %copy-start.1 = (s32[2,32,128]{2,1,0:T(8,128)S(1)}, s32[2,32,128]{2,1,0:T(8,128)}, u32[]{:S(2)}) copy-start(s32[2,32,128]{2,1,0:T(8,128)} %labels_ref.1) | copy-start | bytes 98308
  6.9 3.0 %copy-start.2 = (f32[2,8,128]{2,1,0:T(8,128)S(1)}, f32[2,8,128]{2,1,0:T(8,128)}, u32[]{:S(2)}) copy-start(f32[2,8,128]{2,1,0:T(8,128)} %refs_1_.1) | copy-start | bytes 24580
  6.9 13.4 %copy-start.3 = (s32[8]{0:T(128)S(1)}, s32[8]{0:T(128)}, u32[]{:S(2)}) copy-start(s32[8]{0:T(128)} %refs_0_.1) | copy-start | bytes 100
  9.9 3.7 %collective-permute-start.4 = (f32[16,32,128]{2,1,0:T(8,128)S(1)}, f32[16,32,128]{2,1,0:T(8,128)S(1)}, u32[]{:S(2)}, u32[]{:S(2)}) collective-permute-start(f32[16,32,128]{2,1,0:T(8,128)S(1)} %shard_map.60.refs_1_), channel_id=1, source_target_pairs={{1,2},{3,4},{5,6},{2,1},{4,3},{6,5},{0,0},{7,7},{9,10},{11,12},{13... | collective-permute-start | bytes 786440 | tf_op jit(solution)/shard_map/ppermute | solution.py:455
  10.6 8.9 %collective-permute-start.6 = (f32[16,32,128]{2,1,0:T(8,128)S(1)}, f32[16,32,128]{2,1,0:T(8,128)S(1)}, u32[]{:S(2)}, u32[]{:S(2)}) collective-permute-start(f32[16,32,128]{2,1,0:T(8,128)S(1)} %shard_map.60.refs_1_), channel_id=1, source_target_pairs={{0,2},{2,4},{4,6},{3,1},{5,3},{7,5},{1,0},{6,7},{8,10},{10,12},{12... | collective-permute-start | bytes 786440 | tf_op jit(solution)/shard_map/ppermute | solution.py:463
  13.4 6.1 %collective-permute-start.3 = (f32[16,32,128]{2,1,0:T(8,128)S(1)}, f32[16,32,128]{2,1,0:T(8,128)S(1)}, u32[]{:S(2)}, u32[]{:S(2)}) collective-permute-start(f32[16,32,128]{2,1,0:T(8,128)S(1)} %shard_map.60.refs_1_), channel_id=1, source_target_pairs={{1,0},{0,1},{3,2},{2,3},{5,4},{4,5},{7,6},{6,7},{9,8},{8,9},{11,10... | collective-permute-start | bytes 786440 | tf_op jit(solution)/shard_map/ppermute | solution.py:449
  13.6 6.7 %collective-permute-start.5 = (f32[16,32,128]{2,1,0:T(8,128)S(1)}, f32[16,32,128]{2,1,0:T(8,128)S(1)}, u32[]{:S(2)}, u32[]{:S(2)}) collective-permute-start(f32[16,32,128]{2,1,0:T(8,128)S(1)} %collective-permute-done.4.refs_3_), channel_id=1, source_target_pairs={{1,0},{0,1},{3,2},{2,3},{5,4},{4,5},{7,6},{6,7},{9,8},{8,9},{11,10... | collective-permute-start | bytes 786440 | tf_op jit(solution)/shard_map/ppermute | solution.py:449
  26.1 3.8 %collective-permute-start.7 = (f32[24,128]{1,0:T(8,128)S(1)}, f32[24,128]{1,0:T(8,128)S(1)}, u32[]{:S(2)}, u32[]{:S(2)}) collective-permute-start(f32[24,128]{1,0:T(8,128)S(1)} %get-tuple-element.9), channel_id=1, source_target_pairs={{8,0},{0,8},{24,16},{16,24},{9,1},{1,9},{25,17},{17,25},{10,2},{2,... | collective-permute-start | bytes 36872 | tf_op jit(solution)/shard_map/ppermute | solution.py:449
  26.7 3.7 %collective-permute-start.8 = (f32[24,128]{1,0:T(8,128)S(1)}, f32[24,128]{1,0:T(8,128)S(1)}, u32[]{:S(2)}, u32[]{:S(2)}) collective-permute-start(f32[24,128]{1,0:T(8,128)S(1)} %get-tuple-element.10), channel_id=1, source_target_pairs={{16,0},{24,8},{0,16},{8,24},{17,1},{25,9},{1,17},{9,25},{18,2},{26... | collective-permute-start | bytes 36872 | tf_op jit(solution)/shard_map/ppermute | solution.py:449
  27.2 4.6 %collective-permute-start.9 = (f32[24,128]{1,0:T(8,128)S(1)}, f32[24,128]{1,0:T(8,128)S(1)}, u32[]{:S(2)}, u32[]{:S(2)}) collective-permute-start(f32[24,128]{1,0:T(8,128)S(1)} %get-tuple-element.11), channel_id=1, source_target_pairs={{24,0},{16,8},{8,16},{0,24},{25,1},{17,9},{9,17},{1,25},{26,2},{18... | collective-permute-start | bytes 36872 | tf_op jit(solution)/shard_map/ppermute | solution.py:449
  31.8 1.2 %collective-permute-start.10 = (f32[24,128]{1,0:T(8,128)S(1)}, f32[24,128]{1,0:T(8,128)S(1)}, u32[]{:S(2)}, u32[]{:S(2)}) collective-permute-start(f32[24,128]{1,0:T(8,128)S(1)} %shard_map.62.sum_ref.refs_0_), channel_id=1, source_target_pairs={{1,0},{0,1},{3,2},{2,3},{5,4},{4,5},{7,6},{6,7},{9,8},{8,9},{11,10... | collective-permute-start | bytes 36872 | tf_op jit(solution)/shard_map/ppermute | solution.py:449
  33.0 5.3 %collective-permute-start.13 = (f32[16,128]{1,0:T(8,128)S(1)}, f32[16,128]{1,0:T(8,128)S(1)}, u32[]{:S(2)}, u32[]{:S(2)}) collective-permute-start(f32[16,128]{1,0:T(8,128)S(1)} %shard_map.63.refs_2_), channel_id=1, source_target_pairs={{4,0},{5,1},{6,2},{7,3},{0,4},{1,5},{2,6},{3,7},{12,8},{13,9},{14,... | collective-permute-start | bytes 24584 | tf_op jit(solution)/shard_map/ppermute | solution.py:449
  36.7 5.4 %collective-permute-start.12 = (f32[16,128]{1,0:T(8,128)S(1)}, f32[16,128]{1,0:T(8,128)S(1)}, u32[]{:S(2)}, u32[]{:S(2)}) collective-permute-start(f32[16,128]{1,0:T(8,128)S(1)} %shard_map.63.refs_2_), channel_id=1, source_target_pairs={{6,0},{7,1},{4,2},{5,3},{2,4},{3,5},{0,6},{1,7},{14,8},{15,9},{12,... | collective-permute-start | bytes 24584 | tf_op jit(solution)/shard_map/ppermute | solution.py:449
  38.0 4.1 %collective-permute-start.11 = (f32[16,128]{1,0:T(8,128)S(1)}, f32[16,128]{1,0:T(8,128)S(1)}, u32[]{:S(2)}, u32[]{:S(2)}) collective-permute-start(f32[16,128]{1,0:T(8,128)S(1)} %shard_map.63.refs_2_), channel_id=1, source_target_pairs={{2,0},{3,1},{0,2},{1,3},{6,4},{7,5},{4,6},{5,7},{10,8},{11,9},{8,1... | collective-permute-start | bytes 24584 | tf_op jit(solution)/shard_map/ppermute | solution.py:449

commit v5 on v4

--- a/solution.py
+++ b/solution.py
@@ -157,7 +157,7 @@
 
 
 def smooth_kernel(hops, count_gz, *refs):
-    blocks = 1 + 2 * hops
+    blocks = 1 + 3 * hops
     weights_ref = refs[0]
     pack_refs = refs[1 : 1 + blocks]
     disp_hbm, own_ref = refs[1 + blocks : 3 + blocks]
@@ -174,13 +174,18 @@
 
     def packed(layer, group, kind):
         hop = layer // layers
-        plane = pack_plane(cases, layers, group, kind, layer - hop * layers)
+        plane = pack_plane(cases, layers, cases if group is None else group, kind, layer - hop * layers)
         if hop == 0:
             return [pack_refs[0][plane, chunk] for chunk in chunks]
-        far = abs(hop)
-        beside, across = pack_refs[2 * far - 1], pack_refs[2 * far]
+        beside_ref, design_ref, force_ref = pack_refs[3 * abs(hop) - 2 : 3 * abs(hop) + 1]
+        if group is not None:
+            across = [force_ref[group, kind, layer - hop * layers, chunk] for chunk in chunks]
+        else:
+            across = [design_ref[kind * layers + layer - hop * layers, chunk] for chunk in chunks]
         by_sibling = even == (hop > 0)
-        return [jnp.where(by_sibling, beside[plane, chunk], across[plane, chunk]) for chunk in chunks]
+        return [
+            jnp.where(by_sibling, beside_ref[plane, chunk], a) for chunk, a in zip(chunks, across)
+        ]
 
     def inside(layer):
         owner = gz + layer // layers
@@ -190,9 +195,9 @@
     for at in range(nodes + 1):
         layer = at - SWEEPS - 1
         live = jnp.where(inside(layer), 1.0, 0.0)
-        marks = packed(layer, cases, 1)
+        marks = packed(layer, None, 1)
         moduli = []
-        for chunk_at, (dense, mark) in enumerate(zip(packed(layer, cases, 0), marks)):
+        for chunk_at, (dense, mark) in enumerate(zip(packed(layer, None, 0), marks)):
             solid = jnp.where(mark == 2.0, 1.0, dense)
             modulus = (EMIN + (1.0 - EMIN) * solid * solid * solid) * live
             moduli.append(modulus)
@@ -312,7 +317,7 @@
     scale = (SHEAR / 48) / weight_sum
 
     spans = filter_layers(
-        [[jnp.where(inside(at), a, 0.0) for a in packed(at, cases, 0)] for at in range(-2, layers + 2)]
+        [[jnp.where(inside(at), a, 0.0) for a in packed(at, None, 0)] for at in range(-2, layers + 2)]
     )
     recs = [
         [jnp.where(inside(layer), 1.0 / jnp.where(inside(layer), a, 1.0), 0.0) for a in span]
@@ -361,8 +366,9 @@
         pack_ref[pack_plane(cases, layers, cases, 1, layer)] = marks
 
 
-def design_kernel(cases, *refs):
-    density_refs, pack_ref = refs[1:-1], refs[-1]
+def design_kernel(cases, count_load, *refs):
+    density_refs = refs[1 : 1 + count_load]
+    pack_ref, design_ref = refs[-2:]
     layers, own_rows, _ = density_refs[0].shape
     load = lax.axis_index("load")
     for step, density_ref in enumerate(density_refs):
@@ -370,6 +376,17 @@
         for layer in range(layers):
             plane = pack_plane(cases, layers, cases, 0, layer)
             pack_ref[plane, pl.ds(start, own_rows)] = density_ref[layer]
+    design_ref[...] = pack_ref[cases * 3 * layers :]
+
+
+def join_kernel(force_ref, design_ref, *refs):
+    pack_ref = refs[-1]
+    cases, _, layers, _, _ = force_ref.shape
+    for case in range(cases):
+        for comp in range(3):
+            for layer in range(layers):
+                pack_ref[pack_plane(cases, layers, case, comp, layer)] = force_ref[case, comp, layer]
+    pack_ref[cases * 3 * layers :] = design_ref[...]
 
 
 def sum_kernel(*refs):
@@ -449,20 +466,12 @@
     return lax.ppermute(block, axis, [(partner(i, step), i) for i in range(count)])
 
 
-def from_neighbours(pack, hops, count):
-    low = range(1, count - 1, 2)
-    pairs = [(i, i + 1) for i in low] + [(i + 1, i) for i in low] + [(0, 0), (count - 1, count - 1)]
-    beside, across = met(pack, "gz", 1), lax.ppermute(pack, "gz", pairs)
-    blocks = [beside, across]
-    for far in range(2, hops + 1):
-        beside = met(across, "gz", 1)
-        up = [(i - far, i) for i in range(0, count, 2) if i - far >= 0]
-        down = [(i + far, i) for i in range(1, count, 2) if i + far < count]
-        free = [i for i in range(count) if i not in dict(up + down)]
-        empty = [i for i in range(count) if i not in dict(up + down).values()]
-        across = lax.ppermute(pack, "gz", up + down + list(zip(free, empty)))
-        blocks += [beside, across]
-    return blocks
+def across_pairs(far, count):
+    up = [(i - far, i) for i in range(0, count, 2) if i - far >= 0]
+    down = [(i + far, i) for i in range(1, count, 2) if i + far < count]
+    free = [i for i in range(count) if i not in dict(up + down)]
+    empty = [i for i in range(count) if i not in dict(up + down).values()]
+    return up + down + list(zip(free, empty))
 
 
 def on_device(density, labels, forces, case_weights):
@@ -495,17 +504,37 @@
         )(*args)
 
     planes = (cases * 3 + 2) * layers
+    far_forces = [
+        lax.ppermute(forces, "gz", across_pairs(far, count_gz)) for far in range(1, hops + 1)
+    ]
     pack = call(stage_kernel, shape(planes, rows, columns), (labels, forces), 2 * planes, 1_000_000)
     densities = [density] + [met(density, "load", step) for step in range(1, count_load)]
-    pack = call(
-        functools.partial(design_kernel, cases),
-        shape(planes, rows, columns),
-        (pack, *densities),
-        2 * planes + 2 * layers,
+    pack, design = call(
+        functools.partial(design_kernel, cases, count_load),
+        (shape(planes, rows, columns), shape(2 * layers, rows, columns)),
+        (pack, *densities, *far_forces),
+        2 * planes + 6 * layers,
         100_000,
+        in_specs=[vmem] * (1 + count_load) + [pl.BlockSpec(memory_space=pl.ANY)] * hops,
+        out_specs=(vmem, vmem),
         input_output_aliases={0: 0},
     )
-    packs = [pack] + from_neighbours(pack, hops, count_gz)
+    far_designs = [
+        lax.ppermute(design, "gz", across_pairs(far, count_gz)) for far in range(1, hops + 1)
+    ]
+    beside, packs = pack, [pack]
+    for at in range(hops):
+        packs += [met(beside, "gz", 1), far_designs[at], far_forces[at]]
+        if at < hops - 1:
+            later = far_designs[at + 1 :]
+            beside = call(
+                join_kernel,
+                shape(planes, rows, columns),
+                (far_forces[at], far_designs[at], *later),
+                2 * planes,
+                100_000,
+                in_specs=[vmem] * 2 + [pl.BlockSpec(memory_space=pl.ANY)] * len(later),
+            )
 
     slot_rows = -(-(layers * wide + 1) // 8) * 8
     scratch = [
@@ -522,7 +551,7 @@
         pltpu.SemaphoreType.DMA((cases,)),
     ]
     smooth_planes = nodes * 35 + 3 * (layers + 1) + 4 * layers
-    smooth_planes += len(packs) * planes + cases * 3 * layers + 8 * layers
+    smooth_planes += (1 + 2 * hops) * planes + cases * 3 * layers + 8 * layers
     displacement, own, *slots = call(
         functools.partial(smooth_kernel, hops, count_gz),
         (shape(*forces.shape), shape(3, layers, own_rows, columns))

time: 43.1 us -> 43.5 us (level)
  starting transfers between devices: 22.6 us -> 23.6 us
  waiting for transfers between devices: 11.4 us -> 10.7 us
    ppermute x2 -> x4, starting transfers between devices: 3.51 us -> 7.27 us  [the longest x2 4.61 us: on_device(): lax.ppermute(forces, 'gz', across_pairs(far, count_gz))]
    ppermute x12, starting transfers between devices: 19.1 us -> 16.3 us  [met(): lax.ppermute(block, axis, [(partner(i, step), i) for i in range(count)])]
    pallas_call x6 -> x7, Pallas kernels: 6.52 us -> 6.53 us  [call(): pl.pallas_call(kernel, out_shape=out, in_specs=in_specs or [vmem] * len(a...]
  transfers between devices with their start and end apart: 14 -> 16, of which waited for: 9 -> 10; matrix products, arithmetic and copies ran while one was open for 0% -> 0% of each run, Pallas kernels for 0% -> 0%
where the time goes in v5:
time: 43.5 us; the launch traced here: 43.3 us
  starting transfers between devices  23.6 us (54%)
  waiting for transfers between devices  10.7 us (25%)
  Pallas kernels  6.53 us (15%)
  local copies, waits for them, and re-layouts  1.69 us (4%)
  between operations  0.7 us (2%)
    ppermute x12, starting transfers between devices, met(): lax.ppermute(block, axis, [(partner(i, step), i) for i in range(count)])  16.3 us
    ppermute x12, waiting for transfers between devices, met(): lax.ppermute(block, axis, [(partner(i, step), i) for i in range(count)])  10.7 us
    pallas_call x7, Pallas kernels, call(): pl.pallas_call(kernel, out_shape=out, in_specs=in_specs or [vmem] * len(a...  6.53 us
    ppermute x2, starting transfers between devices, on_device(): lax.ppermute(forces, 'gz', across_pairs(far, count_gz))  4.61 us
    ppermute x2, starting transfers between devices, on_device(): lax.ppermute(design, 'gz', across_pairs(far, count_gz))  2.65 us
    unnamed x8, local copies, waits for them, and re-layouts  1.69 us
  transfers between devices with their start and end apart: 16, of which 10 were waited for; matrix products, arithmetic and copies ran while one was open for 0% of the time, Pallas kernels for 0%

profile of v5, /device:TPU:0, one launch (start us, length us, event | category | flops | bytes accessed | tf_op | source)
XLA Modules:
  0.0 43.3 jit_solution(15611631070115563234)
XLA Ops:
  0.6 3.0 %collective-permute-start.4 = (f32[2,3,2,32,128]{4,3,2,1,0:T(8,128)}, f32[2,3,2,32,128]{4,3,2,1,0:T(8,128)S(1)}, u32[]{:S(2)}, u32[]{:S(2)}) collective-permute-start(f32[2,3,2,32,128]{4,3,2,1,0:T(8,128)} %forces_ref.1), channel_id=1, source_target_pairs={{0,2},{2,4},{4,6},{3,1},{5,3},{7,5},{1,0},{6,7},{8,10},{10,12},{12... | collective-permute-start | bytes 589832 | tf_op jit(solution)/shard_map/ppermute | solution.py:508
  3.7 1.6 %collective-permute-start.3 = (f32[2,3,2,32,128]{4,3,2,1,0:T(8,128)}, f32[2,3,2,32,128]{4,3,2,1,0:T(8,128)S(1)}, u32[]{:S(2)}, u32[]{:S(2)}) collective-permute-start(f32[2,3,2,32,128]{4,3,2,1,0:T(8,128)} %forces_ref.1), channel_id=1, source_target_pairs={{1,2},{3,4},{5,6},{2,1},{4,3},{6,5},{0,0},{7,7},{9,10},{11,12},{13... | collective-permute-start | bytes 589832 | tf_op jit(solution)/shard_map/ppermute | solution.py:508
  5.2 1.5 %collective-permute-start.1 = (f32[2,8,128]{2,1,0:T(8,128)}, f32[2,8,128]{2,1,0:T(8,128)S(1)}, u32[]{:S(2)}, u32[]{:S(2)}) collective-permute-start(f32[2,8,128]{2,1,0:T(8,128)} %refs_1_.1), channel_id=1, source_target_pairs={{16,0},{24,8},{0,16},{8,24},{17,1},{25,9},{1,17},{9,25},{18,2},{26... | collective-permute-start | bytes 24584 | tf_op jit(solution)/shard_map/ppermute | solution.py:466
  6.8 1.5 %collective-permute-start = (f32[2,8,128]{2,1,0:T(8,128)}, f32[2,8,128]{2,1,0:T(8,128)S(1)}, u32[]{:S(2)}, u32[]{:S(2)}) collective-permute-start(f32[2,8,128]{2,1,0:T(8,128)} %refs_1_.1), channel_id=1, source_target_pairs={{8,0},{0,8},{24,16},{16,24},{9,1},{1,9},{25,17},{17,25},{10,2},{2,... | collective-permute-start | bytes 24584 | tf_op jit(solution)/shard_map/ppermute | solution.py:466
  8.3 0.5 %collective-permute-start.2 = (f32[2,8,128]{2,1,0:T(8,128)}, f32[2,8,128]{2,1,0:T(8,128)S(1)}, u32[]{:S(2)}, u32[]{:S(2)}) collective-permute-start(f32[2,8,128]{2,1,0:T(8,128)} %refs_1_.1), channel_id=1, source_target_pairs={{24,0},{16,8},{8,16},{0,24},{25,1},{17,9},{9,17},{1,25},{26,2},{18... | collective-permute-start | bytes 24584 | tf_op jit(solution)/shard_map/ppermute | solution.py:466
  8.7 0.0 copy-start
  8.7 0.9 %copy-done = f32[2,3,2,32,128]{4,3,2,1,0:T(8,128)S(1)} copy-done((f32[2,3,2,32,128]{4,3,2,1,0:T(8,128)S(1)}, f32[2,3,2,32,128]{4,3,2,1,0:T(8,128)}, u32[]{:S(2)}) %copy-start) | copy-done | bytes 196632
  9.7 0.0 copy-start.1
  9.7 0.8 %copy-done.1 = s32[2,32,128]{2,1,0:T(8,128)S(1)} copy-done((s32[2,32,128]{2,1,0:T(8,128)S(1)}, s32[2,32,128]{2,1,0:T(8,128)}, u32[]{:S(2)}) %copy-start.1) | copy-done | bytes 32792
  10.4 0.0 copy-start.2
  10.4 0.0 collective-permute-done.1.refs_3_
  10.5 0.2 collective-permute-done.refs_2_
  10.6 2.4 %collective-permute-done.2.refs_4_ = f32[2,8,128]{2,1,0:T(8,128)S(1)} collective-permute-done((f32[2,8,128]{2,1,0:T(8,128)}, f32[2,8,128]{2,1,0:T(8,128)S(1)}, u32[]{:S(2)}, u32[]{:S(2)}) %collective-permute-start.2) | collective-permute-done | bytes 8224 | tf_op jit(solution)/shard_map/ppermute | solution.py:466
  13.0 0.0 collective-permute-done.4.refs_6_.refs_7_
  13.0 0.0 collective-permute-done.3.refs_5_.force_ref.refs_4_
  13.0 0.0 copy-done.2
  13.1 2.0 %collective-permute-start.7 = (f32[4,32,128]{2,1,0:T(8,128)S(1)}, f32[4,32,128]{2,1,0:T(8,128)S(1)}, u32[]{:S(2)}, u32[]{:S(2)}) collective-permute-start(f32[4,32,128]{2,1,0:T(8,128)S(1)} %get-tuple-element.11), channel_id=1, source_target_pairs={{0,2},{2,4},{4,6},{3,1},{5,3},{7,5},{1,0},{6,7},{8,10},{10,12},{12... | collective-permute-start | bytes 196616 | tf_op jit(solution)/shard_map/ppermute | solution.py:523
  15.1 0.7 %collective-permute-start.6 = (f32[4,32,128]{2,1,0:T(8,128)S(1)}, f32[4,32,128]{2,1,0:T(8,128)S(1)}, u32[]{:S(2)}, u32[]{:S(2)}) collective-permute-start(f32[4,32,128]{2,1,0:T(8,128)S(1)} %get-tuple-element.11), channel_id=1, source_target_pairs={{1,2},{3,4},{5,6},{2,1},{4,3},{6,5},{0,0},{7,7},{9,10},{11,12},{13... | collective-permute-start | bytes 196616 | tf_op jit(solution)/shard_map/ppermute | solution.py:523
  15.7 0.0 copy-start.3
  15.7 3.0 %collective-permute-start.5 = (f32[16,32,128]{2,1,0:T(8,128)S(1)}, f32[16,32,128]{2,1,0:T(8,128)S(1)}, u32[]{:S(2)}, u32[]{:S(2)}) collective-permute-start(f32[16,32,128]{2,1,0:T(8,128)S(1)} %get-tuple-element.10.refs_1_), channel_id=1, source_target_pairs={{1,0},{0,1},{3,2},{2,3},{5,4},{4,5},{7,6},{6,7},{9,8},{8,9},{11,10... | collective-permute-start | bytes 786440 | tf_op jit(solution)/shard_map/ppermute | solution.py:466
  18.7 0.0 collective-permute-done.7.refs_0_.refs_6_
  18.7 0.0 collective-permute-done.6.design_ref.refs_3_
  18.8 1.9 %collective-permute-start.8 = (f32[16,32,128]{2,1,0:T(8,128)S(1)}, f32[16,32,128]{2,1,0:T(8,128)S(1)}, u32[]{:S(2)}, u32[]{:S(2)}) collective-permute-start(f32[16,32,128]{2,1,0:T(8,128)S(1)} %shard_map.61), channel_id=1, source_target_pairs={{1,0},{0,1},{3,2},{2,3},{5,4},{4,5},{7,6},{6,7},{9,8},{8,9},{11,10... | collective-permute-start | bytes 786440 | tf_op jit(solution)/shard_map/ppermute | solution.py:466
  20.7 0.0 collective-permute-done.5.refs_2_
  20.7 1.2 %collective-permute-done.8.refs_5_ = f32[16,32,128]{2,1,0:T(8,128)S(1)} collective-permute-done((f32[16,32,128]{2,1,0:T(8,128)S(1)}, f32[16,32,128]{2,1,0:T(8,128)S(1)}, u32[]{:S(2)}, u32[]{:S(2)}) %collective-permute-start.8) | collective-permute-done | bytes 262176 | tf_op jit(solution)/shard_map/ppermute | solution.py:466
  21.8 0.0 copy-done.3
  21.8 5.7 %shard_map.62 = (f32[2,3,2,32,128]{4,3,2,1,0:T(8,128)}, f32[3,2,8,128]{3,2,1,0:T(8,128)S(1)}, f32[24,128]{1,0:T(8,128)S(1)}, f32[24,128]{1,0:T(8,128)S(1)}, f32[...) custom-call(s32[8]{0:T(128)S(1)} %copy-done.3, f32[16,32,128]{2,1,0:T(8,128)S(1)} %get-tuple-element.10.refs_1_, ...), custom_call_target="tpu_custom_call" | custom-call | flops 60000000 | bytes 6000000 | tf_op jit(solution)/shard_map/pallas_call | solution.py:495
  27.6 0.6 %collective-permute-start.9 = (f32[24,128]{1,0:T(8,128)S(1)}, f32[24,128]{1,0:T(8,128)S(1)}, u32[]{:S(2)}, u32[]{:S(2)}) collective-permute-start(f32[24,128]{1,0:T(8,128)S(1)} %get-tuple-element.13), channel_id=1, source_target_pairs={{8,0},{0,8},{24,16},{16,24},{9,1},{1,9},{25,17},{17,25},{10,2},{2,... | collective-permute-start | bytes 36872 | tf_op jit(solution)/shard_map/ppermute | solution.py:466
  28.2 0.5 %collective-permute-start.10 = (f32[24,128]{1,0:T(8,128)S(1)}, f32[24,128]{1,0:T(8,128)S(1)}, u32[]{:S(2)}, u32[]{:S(2)}) collective-permute-start(f32[24,128]{1,0:T(8,128)S(1)} %get-tuple-element.14), channel_id=1, source_target_pairs={{16,0},{24,8},{0,16},{8,24},{17,1},{25,9},{1,17},{9,25},{18,2},{26... | collective-permute-start | bytes 36872 | tf_op jit(solution)/shard_map/ppermute | solution.py:466
  28.7 2.4 %collective-permute-start.11 = (f32[24,128]{1,0:T(8,128)S(1)}, f32[24,128]{1,0:T(8,128)S(1)}, u32[]{:S(2)}, u32[]{:S(2)}) collective-permute-start(f32[24,128]{1,0:T(8,128)S(1)} %get-tuple-element.15), channel_id=1, source_target_pairs={{24,0},{16,8},{8,16},{0,24},{25,1},{17,9},{9,17},{1,25},{26,2},{18... | collective-permute-start | bytes 36872 | tf_op jit(solution)/shard_map/ppermute | solution.py:466
  31.1 0.2 collective-permute-done.9.refs_1_
  31.3 0.5 %collective-permute-done.10.refs_2_ = f32[24,128]{1,0:T(8,128)S(1)} collective-permute-done((f32[24,128]{1,0:T(8,128)S(1)}, f32[24,128]{1,0:T(8,128)S(1)}, u32[]{:S(2)}, u32[]{:S(2)}) %collective-permute-start.10) | collective-permute-done | bytes 12320 | tf_op jit(solution)/shard_map/ppermute | solution.py:466
  31.9 1.4 %collective-permute-done.11.refs_3_ = f32[24,128]{1,0:T(8,128)S(1)} collective-permute-done((f32[24,128]{1,0:T(8,128)S(1)}, f32[24,128]{1,0:T(8,128)S(1)}, u32[]{:S(2)}, u32[]{:S(2)}) %collective-permute-start.11) | collective-permute-done | bytes 12320 | tf_op jit(solution)/shard_map/ppermute | solution.py:466
  33.3 0.0 collective-permute-start.12
  33.3 1.2 %collective-permute-done.12.beside_ref.refs_1_ = f32[24,128]{1,0:T(8,128)S(1)} collective-permute-done((f32[24,128]{1,0:T(8,128)S(1)}, f32[24,128]{1,0:T(8,128)S(1)}, u32[]{:S(2)}, u32[]{:S(2)}) %collective-permute-start.12) | collective-permute-done | bytes 12320 | tf_op jit(solution)/shard_map/ppermute | solution.py:466
  34.5 2.1 %collective-permute-start.15 = (f32[16,128]{1,0:T(8,128)S(1)}, f32[16,128]{1,0:T(8,128)S(1)}, u32[]{:S(2)}, u32[]{:S(2)}) collective-permute-start(f32[16,128]{1,0:T(8,128)S(1)} %shard_map.64.refs_2_), channel_id=1, source_target_pairs={{4,0},{5,1},{6,2},{7,3},{0,4},{1,5},{2,6},{3,7},{12,8},{13,9},{14,... | collective-permute-start | bytes 24584 | tf_op jit(solution)/shard_map/ppermute | solution.py:466
  36.6 2.3 %collective-permute-start.14 = (f32[16,128]{1,0:T(8,128)S(1)}, f32[16,128]{1,0:T(8,128)S(1)}, u32[]{:S(2)}, u32[]{:S(2)}) collective-permute-start(f32[16,128]{1,0:T(8,128)S(1)} %shard_map.64.refs_2_), channel_id=1, source_target_pairs={{6,0},{7,1},{4,2},{5,3},{2,4},{3,5},{0,6},{1,7},{14,8},{15,9},{12,... | collective-permute-start | bytes 24584 | tf_op jit(solution)/shard_map/ppermute | solution.py:466
  38.9 0.0 collective-permute-start.13
  38.9 0.2 collective-permute-done.15.refs_5_
  39.1 3.0 %collective-permute-done.14.refs_4_ = f32[16,128]{1,0:T(8,128)S(1)} collective-permute-done((f32[16,128]{1,0:T(8,128)S(1)}, f32[16,128]{1,0:T(8,128)S(1)}, u32[]{:S(2)}, u32[]{:S(2)}) %collective-permute-start.14) | collective-permute-done | bytes 8224 | tf_op jit(solution)/shard_map/ppermute | solution.py:466
  42.0 0.5 %collective-permute-done.13.refs_3_ = f32[16,128]{1,0:T(8,128)S(1)} collective-permute-done((f32[16,128]{1,0:T(8,128)S(1)}, f32[16,128]{1,0:T(8,128)S(1)}, u32[]{:S(2)}, u32[]{:S(2)}) %collective-permute-start.13) | collective-permute-done | bytes 8224 | tf_op jit(solution)/shard_map/ppermute | solution.py:466
  42.5 0.7 %shard_map.65 = f32[2,8,128]{2,1,0:T(8,128)} custom-call(f32[24,128]{1,0:T(8,128)S(1)} %shard_map.63.sum_ref.refs_0_, f32[24,128]{1,0:T(8,128)S(1)} %collective-permute-done.12.beside_ref.refs_1_, f32[16,128]{1,0:T(8,128)S(1)} %shard_map.64.refs_2_, f32[16,128]{1,0:T(8,128)S(1)} %collective-permute-done.13.refs_3_, ...), custom_call_target="tpu_custom_call" | custom-call | flops 100000 | bytes 10000 | tf_op jit(solution)/shard_map/pallas_call | solution.py:495
  (5 shorter events, 0.1 us)
Async XLA Ops:
  0.6 12.4 %collective-permute-start.4 = (f32[2,3,2,32,128]{4,3,2,1,0:T(8,128)}, f32[2,3,2,32,128]{4,3,2,1,0:T(8,128)S(1)}, u32[]{:S(2)}, u32[]{:S(2)}) collective-permute-start(f32[2,3,2,32,128]{4,3,2,1,0:T(8,128)} %forces_ref.1), channel_id=1, source_target_pairs={{0,2},{2,4},{4,6},{3,1},{5,3},{7,5},{1,0},{6,7},{8,10},{10,12},{12... | collective-permute-start | bytes 589832 | tf_op jit(solution)/shard_map/ppermute | solution.py:508
  3.7 9.4 %collective-permute-start.3 = (f32[2,3,2,32,128]{4,3,2,1,0:T(8,128)}, f32[2,3,2,32,128]{4,3,2,1,0:T(8,128)S(1)}, u32[]{:S(2)}, u32[]{:S(2)}) collective-permute-start(f32[2,3,2,32,128]{4,3,2,1,0:T(8,128)} %forces_ref.1), channel_id=1, source_target_pairs={{1,2},{3,4},{5,6},{2,1},{4,3},{6,5},{0,0},{7,7},{9,10},{11,12},{13... | collective-permute-start | bytes 589832 | tf_op jit(solution)/shard_map/ppermute | solution.py:508
  5.2 5.2 %collective-permute-start.1 = (f32[2,8,128]{2,1,0:T(8,128)}, f32[2,8,128]{2,1,0:T(8,128)S(1)}, u32[]{:S(2)}, u32[]{:S(2)}) collective-permute-start(f32[2,8,128]{2,1,0:T(8,128)} %refs_1_.1), channel_id=1, source_target_pairs={{16,0},{24,8},{0,16},{8,24},{17,1},{25,9},{1,17},{9,25},{18,2},{26... | collective-permute-start | bytes 24584 | tf_op jit(solution)/shard_map/ppermute | solution.py:466
  6.8 3.9 %collective-permute-start = (f32[2,8,128]{2,1,0:T(8,128)}, f32[2,8,128]{2,1,0:T(8,128)S(1)}, u32[]{:S(2)}, u32[]{:S(2)}) collective-permute-start(f32[2,8,128]{2,1,0:T(8,128)} %refs_1_.1), channel_id=1, source_target_pairs={{8,0},{0,8},{24,16},{16,24},{9,1},{1,9},{25,17},{17,25},{10,2},{2,... | collective-permute-start | bytes 24584 | tf_op jit(solution)/shard_map/ppermute | solution.py:466
  8.3 4.8 %collective-permute-start.2 = (f32[2,8,128]{2,1,0:T(8,128)}, f32[2,8,128]{2,1,0:T(8,128)S(1)}, u32[]{:S(2)}, u32[]{:S(2)}) collective-permute-start(f32[2,8,128]{2,1,0:T(8,128)} %refs_1_.1), channel_id=1, source_target_pairs={{24,0},{16,8},{8,16},{0,24},{25,1},{17,9},{9,17},{1,25},{26,2},{18... | collective-permute-start | bytes 24584 | tf_op jit(solution)/shard_map/ppermute | solution.py:466
  8.7 0.9 %copy-start = (f32[2,3,2,32,128]{4,3,2,1,0:T(8,128)S(1)}, f32[2,3,2,32,128]{4,3,2,1,0:T(8,128)}, u32[]{:S(2)}) copy-start(f32[2,3,2,32,128]{4,3,2,1,0:T(8,128)} %forces_ref.1) | copy-start | bytes 589828
  9.7 0.8 %copy-start.1 = (s32[2,32,128]{2,1,0:T(8,128)S(1)}, s32[2,32,128]{2,1,0:T(8,128)}, u32[]{:S(2)}) copy-start(s32[2,32,128]{2,1,0:T(8,128)} %labels_ref.1) | copy-start | bytes 98308
  10.4 2.6 %copy-start.2 = (f32[2,8,128]{2,1,0:T(8,128)S(1)}, f32[2,8,128]{2,1,0:T(8,128)}, u32[]{:S(2)}) copy-start(f32[2,8,128]{2,1,0:T(8,128)} %refs_1_.1) | copy-start | bytes 24580
  13.1 5.7 %collective-permute-start.7 = (f32[4,32,128]{2,1,0:T(8,128)S(1)}, f32[4,32,128]{2,1,0:T(8,128)S(1)}, u32[]{:S(2)}, u32[]{:S(2)}) collective-permute-start(f32[4,32,128]{2,1,0:T(8,128)S(1)} %get-tuple-element.11), channel_id=1, source_target_pairs={{0,2},{2,4},{4,6},{3,1},{5,3},{7,5},{1,0},{6,7},{8,10},{10,12},{12... | collective-permute-start | bytes 196616 | tf_op jit(solution)/shard_map/ppermute | solution.py:523
  15.1 3.7 %collective-permute-start.6 = (f32[4,32,128]{2,1,0:T(8,128)S(1)}, f32[4,32,128]{2,1,0:T(8,128)S(1)}, u32[]{:S(2)}, u32[]{:S(2)}) collective-permute-start(f32[4,32,128]{2,1,0:T(8,128)S(1)} %get-tuple-element.11), channel_id=1, source_target_pairs={{1,2},{3,4},{5,6},{2,1},{4,3},{6,5},{0,0},{7,7},{9,10},{11,12},{13... | collective-permute-start | bytes 196616 | tf_op jit(solution)/shard_map/ppermute | solution.py:523
  15.7 6.1 %copy-start.3 = (s32[8]{0:T(128)S(1)}, s32[8]{0:T(128)}, u32[]{:S(2)}) copy-start(s32[8]{0:T(128)} %refs_0_.1) | copy-start | bytes 100
  15.7 4.9 %collective-permute-start.5 = (f32[16,32,128]{2,1,0:T(8,128)S(1)}, f32[16,32,128]{2,1,0:T(8,128)S(1)}, u32[]{:S(2)}, u32[]{:S(2)}) collective-permute-start(f32[16,32,128]{2,1,0:T(8,128)S(1)} %get-tuple-element.10.refs_1_), channel_id=1, source_target_pairs={{1,0},{0,1},{3,2},{2,3},{5,4},{4,5},{7,6},{6,7},{9,8},{8,9},{11,10... | collective-permute-start | bytes 786440 | tf_op jit(solution)/shard_map/ppermute | solution.py:466
  18.8 3.1 %collective-permute-start.8 = (f32[16,32,128]{2,1,0:T(8,128)S(1)}, f32[16,32,128]{2,1,0:T(8,128)S(1)}, u32[]{:S(2)}, u32[]{:S(2)}) collective-permute-start(f32[16,32,128]{2,1,0:T(8,128)S(1)} %shard_map.61), channel_id=1, source_target_pairs={{1,0},{0,1},{3,2},{2,3},{5,4},{4,5},{7,6},{6,7},{9,8},{8,9},{11,10... | collective-permute-start | bytes 786440 | tf_op jit(solution)/shard_map/ppermute | solution.py:466
  27.6 3.8 %collective-permute-start.9 = (f32[24,128]{1,0:T(8,128)S(1)}, f32[24,128]{1,0:T(8,128)S(1)}, u32[]{:S(2)}, u32[]{:S(2)}) collective-permute-start(f32[24,128]{1,0:T(8,128)S(1)} %get-tuple-element.13), channel_id=1, source_target_pairs={{8,0},{0,8},{24,16},{16,24},{9,1},{1,9},{25,17},{17,25},{10,2},{2,... | collective-permute-start | bytes 36872 | tf_op jit(solution)/shard_map/ppermute | solution.py:466
  28.2 3.7 %collective-permute-start.10 = (f32[24,128]{1,0:T(8,128)S(1)}, f32[24,128]{1,0:T(8,128)S(1)}, u32[]{:S(2)}, u32[]{:S(2)}) collective-permute-start(f32[24,128]{1,0:T(8,128)S(1)} %get-tuple-element.14), channel_id=1, source_target_pairs={{16,0},{24,8},{0,16},{8,24},{17,1},{25,9},{1,17},{9,25},{18,2},{26... | collective-permute-start | bytes 36872 | tf_op jit(solution)/shard_map/ppermute | solution.py:466
  28.7 4.6 %collective-permute-start.11 = (f32[24,128]{1,0:T(8,128)S(1)}, f32[24,128]{1,0:T(8,128)S(1)}, u32[]{:S(2)}, u32[]{:S(2)}) collective-permute-start(f32[24,128]{1,0:T(8,128)S(1)} %get-tuple-element.15), channel_id=1, source_target_pairs={{24,0},{16,8},{8,16},{0,24},{25,1},{17,9},{9,17},{1,25},{26,2},{18... | collective-permute-start | bytes 36872 | tf_op jit(solution)/shard_map/ppermute | solution.py:466
  33.3 1.2 %collective-permute-start.12 = (f32[24,128]{1,0:T(8,128)S(1)}, f32[24,128]{1,0:T(8,128)S(1)}, u32[]{:S(2)}, u32[]{:S(2)}) collective-permute-start(f32[24,128]{1,0:T(8,128)S(1)} %shard_map.63.sum_ref.refs_0_), channel_id=1, source_target_pairs={{1,0},{0,1},{3,2},{2,3},{5,4},{4,5},{7,6},{6,7},{9,8},{8,9},{11,10... | collective-permute-start | bytes 36872 | tf_op jit(solution)/shard_map/ppermute | solution.py:466
  34.5 4.5 %collective-permute-start.15 = (f32[16,128]{1,0:T(8,128)S(1)}, f32[16,128]{1,0:T(8,128)S(1)}, u32[]{:S(2)}, u32[]{:S(2)}) collective-permute-start(f32[16,128]{1,0:T(8,128)S(1)} %shard_map.64.refs_2_), channel_id=1, source_target_pairs={{4,0},{5,1},{6,2},{7,3},{0,4},{1,5},{2,6},{3,7},{12,8},{13,9},{14,... | collective-permute-start | bytes 24584 | tf_op jit(solution)/shard_map/ppermute | solution.py:466
  36.6 5.4 %collective-permute-start.14 = (f32[16,128]{1,0:T(8,128)S(1)}, f32[16,128]{1,0:T(8,128)S(1)}, u32[]{:S(2)}, u32[]{:S(2)}) collective-permute-start(f32[16,128]{1,0:T(8,128)S(1)} %shard_map.64.refs_2_), channel_id=1, source_target_pairs={{6,0},{7,1},{4,2},{5,3},{2,4},{3,5},{0,6},{1,7},{14,8},{15,9},{12,... | collective-permute-start | bytes 24584 | tf_op jit(solution)/shard_map/ppermute | solution.py:466
  38.9 3.7 %collective-permute-start.13 = (f32[16,128]{1,0:T(8,128)S(1)}, f32[16,128]{1,0:T(8,128)S(1)}, u32[]{:S(2)}, u32[]{:S(2)}) collective-permute-start(f32[16,128]{1,0:T(8,128)S(1)} %shard_map.64.refs_2_), channel_id=1, source_target_pairs={{2,0},{3,1},{0,2},{1,3},{6,4},{7,5},{4,6},{5,7},{10,8},{11,9},{8,1... | collective-permute-start | bytes 24584 | tf_op jit(solution)/shard_map/ppermute | solution.py:466

commit v6 on v4

--- a/solution.py
+++ b/solution.py
@@ -244,10 +244,6 @@
             factor_next = 1.0 / (2.0 * sigma - factor)
             keep, take = factor_next * factor, 2.0 * factor_next / delta
             first, end = sweep - 1, nodes - sweep
-            if sweep > 1:
-                for node in range(first, end + 1):
-                    for comp in range(3):
-                        store_modes(node, comp, [step_ref[comp, node, chunk] for chunk in chunks])
             for chunk in chunks:
                 low = load_modes(first, chunk)
                 up = None
@@ -277,27 +273,29 @@
                         before = packed(node - SWEEPS, case, comp)
                     else:
                         before = [res_ref[comp, node, chunk] for chunk in chunks]
+                    steps, sols = [], []
                     for chunk, res in zip(chunks, sub(before, from_modes_xy(*g))):
                         step = keep * step_ref[comp, node, chunk] + take * (inv_ref[node, chunk] * res)
+                        steps.append(step)
                         if sweep < SWEEPS:
                             res_ref[comp, node, chunk] = res
                             step_ref[comp, node, chunk] = step
                         if SWEEPS <= node <= SWEEPS + layers:
                             sol = sol_ref[comp, node - SWEEPS, chunk] + step
-                            sol_ref[comp, node - SWEEPS, chunk] = sol
-                            if sweep == SWEEPS and node < SWEEPS + layers:
+                            sols.append(sol)
+                            if sweep < SWEEPS:
+                                sol_ref[comp, node - SWEEPS, chunk] = sol
+                            elif node < SWEEPS + layers:
                                 disp_ref[case, comp, node - SWEEPS, chunk] = sol
+                    store_modes(node, comp, steps if sweep < SWEEPS else sols)
             factor = factor_next
         pltpu.make_async_copy(disp_ref.at[case], disp_hbm.at[case], disp_sem.at[case]).start()
 
         weight = weights_ref[load * cases + case].astype(jnp.float32)
-        for node in range(layers + 1):
-            for comp in range(3):
-                store_modes(node, comp, [sol_ref[comp, node, chunk] for chunk in chunks])
         for chunk in chunks:
-            low = load_modes(0, chunk)
+            low = load_modes(SWEEPS, chunk)
             for layer in range(layers):
-                high = load_modes(layer + 1, chunk)
+                high = load_modes(SWEEPS + layer + 1, chunk)
                 energy = weight * mode_energy(modes_z(low, high))
                 before = jnp.where(case == 0, 0.0, energy_ref[layer, chunk])
                 energy_ref[layer, chunk] = before + energy
@@ -361,11 +359,11 @@
         pack_ref[pack_plane(cases, layers, cases, 1, layer)] = marks
 
 
-def design_kernel(cases, *refs):
+def design_kernel(cases, steps, *refs):
     density_refs, pack_ref = refs[1:-1], refs[-1]
     layers, own_rows, _ = density_refs[0].shape
     load = lax.axis_index("load")
-    for step, density_ref in enumerate(density_refs):
+    for step, density_ref in zip(steps, density_refs):
         start = pl.multiple_of(partner(load, step) * own_rows, own_rows)
         for layer in range(layers):
             plane = pack_plane(cases, layers, cases, 0, layer)
@@ -404,7 +402,7 @@
     while 2 ** (len(edges) + 1) < count_gz:
         edges.append(2 ** (len(edges) + 1) - 1)
     pairs = [edges[at : at + 2] for at in range(0, len(edges), 2)]
-    return [pair + [pair[0] ^ pair[1]] if len(pair) == 2 else pair for pair in pairs]
+    return [[pair[0], pair[0] ^ pair[1], pair[1]] if len(pair) == 2 else pair for pair in pairs]
 
 
 def update_kernel(cells, rounds, *refs):
@@ -496,9 +494,10 @@
 
     planes = (cases * 3 + 2) * layers
     pack = call(stage_kernel, shape(planes, rows, columns), (labels, forces), 2 * planes, 1_000_000)
-    densities = [density] + [met(density, "load", step) for step in range(1, count_load)]
+    steps = [0] + list(range(2, count_load)) + [1]
+    densities = [density] + [met(density, "load", step) for step in steps[1:]]
     pack = call(
-        functools.partial(design_kernel, cases),
+        functools.partial(design_kernel, cases, steps),
         shape(planes, rows, columns),
         (pack, *densities),
         2 * planes + 2 * layers,
@@ -535,7 +534,7 @@
         scratch=scratch,
     )
 
-    received = [met(slots[step], "load", step) for step in range(1, count_load)]
+    received = [met(slots[step], "load", step) for step in range(count_load - 1, 0, -1)]
     whole = call(sum_kernel, shape(slot_rows, columns), (slots[0], *received), 2 * count_load, 100_000)
     beside = met(whole, "gz", 1)
     forward_rows = -(-(wide + 1) // 8) * 8

time: 43.1 us -> 42.5 us (0.986)
  waiting for transfers between devices: 11.4 us -> 10.5 us
    ppermute x12, waiting for transfers between devices: 11 us -> 10.1 us  [met(): lax.ppermute(block, axis, [(partner(i, step), i) for i in range(count)])]
  transfers between devices with their start and end apart: 14 -> 14, of which waited for: 9 -> 10; matrix products, arithmetic and copies ran while one was open for 0% -> 0% of each run, Pallas kernels for 0% -> 0%
where the time goes in v6:
time: 42.5 us; the launch traced here: 42.2 us
  starting transfers between devices  22.7 us (53%)
  waiting for transfers between devices  10.5 us (25%)
  Pallas kernels  6.72 us (16%)
  local copies, waits for them, and re-layouts  1.69 us (4%)
  between operations  0.69 us (2%)
    ppermute x12, starting transfers between devices, met(): lax.ppermute(block, axis, [(partner(i, step), i) for i in range(count)])  19.2 us
    ppermute x12, waiting for transfers between devices, met(): lax.ppermute(block, axis, [(partner(i, step), i) for i in range(count)])  10.1 us
    pallas_call x6, Pallas kernels, call(): pl.pallas_call(kernel, out_shape=out, in_specs=in_specs or [vmem] * len(a...  6.72 us
    ppermute x1, starting transfers between devices, from_neighbours(): across = lax.ppermute(pack, 'gz', up + down + list(zip(free, empty)))  2.84 us
    unnamed x8, local copies, waits for them, and re-layouts  1.69 us
  transfers between devices with their start and end apart: 14, of which 10 were waited for; matrix products, arithmetic and copies ran while one was open for 0% of the time, Pallas kernels for 0%

profile of v6, /device:TPU:0, one launch (start us, length us, event | category | flops | bytes accessed | tf_op | source)
XLA Modules:
  0.0 42.2 jit_solution(14954713838918525929)
XLA Ops:
  0.6 4.0 %collective-permute-start.1 = (f32[2,8,128]{2,1,0:T(8,128)}, f32[2,8,128]{2,1,0:T(8,128)S(1)}, u32[]{:S(2)}, u32[]{:S(2)}) collective-permute-start(f32[2,8,128]{2,1,0:T(8,128)} %refs_1_.1), channel_id=1, source_target_pairs={{24,0},{16,8},{8,16},{0,24},{25,1},{17,9},{9,17},{1,25},{26,2},{18... | collective-permute-start | bytes 24584 | tf_op jit(solution)/shard_map/ppermute | solution.py:447
  4.6 0.5 %collective-permute-start = (f32[2,8,128]{2,1,0:T(8,128)}, f32[2,8,128]{2,1,0:T(8,128)S(1)}, u32[]{:S(2)}, u32[]{:S(2)}) collective-permute-start(f32[2,8,128]{2,1,0:T(8,128)} %refs_1_.1), channel_id=1, source_target_pairs={{16,0},{24,8},{0,16},{8,24},{17,1},{25,9},{1,17},{9,25},{18,2},{26... | collective-permute-start | bytes 24584 | tf_op jit(solution)/shard_map/ppermute | solution.py:447
  5.1 0.1 collective-permute-start.2
  5.2 0.0 copy-start
  5.2 0.9 %copy-done = f32[2,3,2,32,128]{4,3,2,1,0:T(8,128)S(1)} copy-done((f32[2,3,2,32,128]{4,3,2,1,0:T(8,128)S(1)}, f32[2,3,2,32,128]{4,3,2,1,0:T(8,128)}, u32[]{:S(2)}) %copy-start) | copy-done | bytes 196632
  6.2 0.0 copy-start.1
  6.2 0.8 %copy-done.1 = s32[2,32,128]{2,1,0:T(8,128)S(1)} copy-done((s32[2,32,128]{2,1,0:T(8,128)S(1)}, s32[2,32,128]{2,1,0:T(8,128)}, u32[]{:S(2)}) %copy-start.1) | copy-done | bytes 32792
  6.9 0.0 copy-start.2
  6.9 0.0 copy-start.3
  7.0 0.0 collective-permute-done.1.refs_3_
  7.0 1.5 %collective-permute-done.refs_2_ = f32[2,8,128]{2,1,0:T(8,128)S(1)} collective-permute-done((f32[2,8,128]{2,1,0:T(8,128)}, f32[2,8,128]{2,1,0:T(8,128)S(1)}, u32[]{:S(2)}, u32[]{:S(2)}) %collective-permute-start) | collective-permute-done | bytes 8224 | tf_op jit(solution)/shard_map/ppermute | solution.py:447
  8.5 0.5 %collective-permute-done.2.refs_4_ = f32[2,8,128]{2,1,0:T(8,128)S(1)} collective-permute-done((f32[2,8,128]{2,1,0:T(8,128)}, f32[2,8,128]{2,1,0:T(8,128)S(1)}, u32[]{:S(2)}, u32[]{:S(2)}) %collective-permute-start.2) | collective-permute-done | bytes 8224 | tf_op jit(solution)/shard_map/ppermute | solution.py:447
  9.0 0.0 copy-done.2
  9.0 0.7 %collective-permute-start.4 = (f32[16,32,128]{2,1,0:T(8,128)S(1)}, f32[16,32,128]{2,1,0:T(8,128)S(1)}, u32[]{:S(2)}, u32[]{:S(2)}) collective-permute-start(f32[16,32,128]{2,1,0:T(8,128)S(1)} %shard_map.60.refs_1_), channel_id=1, source_target_pairs={{1,2},{3,4},{5,6},{2,1},{4,3},{6,5},{0,0},{7,7},{9,10},{11,12},{13... | collective-permute-start | bytes 786440 | tf_op jit(solution)/shard_map/ppermute | solution.py:453
  9.7 2.8 %collective-permute-start.6 = (f32[16,32,128]{2,1,0:T(8,128)S(1)}, f32[16,32,128]{2,1,0:T(8,128)S(1)}, u32[]{:S(2)}, u32[]{:S(2)}) collective-permute-start(f32[16,32,128]{2,1,0:T(8,128)S(1)} %shard_map.60.refs_1_), channel_id=1, source_target_pairs={{0,2},{2,4},{4,6},{3,1},{5,3},{7,5},{1,0},{6,7},{8,10},{10,12},{12... | collective-permute-start | bytes 786440 | tf_op jit(solution)/shard_map/ppermute | solution.py:461
  12.5 0.2 collective-permute-start.3
  12.7 0.0 collective-permute-done.4.refs_3_
  12.7 5.5 %collective-permute-start.5 = (f32[16,32,128]{2,1,0:T(8,128)S(1)}, f32[16,32,128]{2,1,0:T(8,128)S(1)}, u32[]{:S(2)}, u32[]{:S(2)}) collective-permute-start(f32[16,32,128]{2,1,0:T(8,128)S(1)} %collective-permute-done.4.refs_3_), channel_id=1, source_target_pairs={{1,0},{0,1},{3,2},{2,3},{5,4},{4,5},{7,6},{6,7},{9,8},{8,9},{11,10... | collective-permute-start | bytes 786440 | tf_op jit(solution)/shard_map/ppermute | solution.py:447
  18.2 0.4 collective-permute-done.6.refs_5_
  18.6 0.0 collective-permute-done.3.refs_2_
  18.6 0.8 %collective-permute-done.5.refs_4_ = f32[16,32,128]{2,1,0:T(8,128)S(1)} collective-permute-done((f32[16,32,128]{2,1,0:T(8,128)S(1)}, f32[16,32,128]{2,1,0:T(8,128)S(1)}, u32[]{:S(2)}, u32[]{:S(2)}) %collective-permute-start.5) | collective-permute-done | bytes 262176 | tf_op jit(solution)/shard_map/ppermute | solution.py:447
  19.4 0.0 copy-done.3
  19.4 5.9 %shard_map.61 = (f32[2,3,2,32,128]{4,3,2,1,0:T(8,128)}, f32[3,2,8,128]{3,2,1,0:T(8,128)S(1)}, f32[24,128]{1,0:T(8,128)S(1)}, f32[24,128]{1,0:T(8,128)S(1)}, f32[...) custom-call(s32[8]{0:T(128)S(1)} %copy-done.3, f32[16,32,128]{2,1,0:T(8,128)S(1)} %shard_map.60.refs_1_, ...), custom_call_target="tpu_custom_call" | custom-call | flops 60000000 | bytes 6000000 | tf_op jit(solution)/shard_map/pallas_call | solution.py:484
  25.3 1.6 %collective-permute-start.7 = (f32[24,128]{1,0:T(8,128)S(1)}, f32[24,128]{1,0:T(8,128)S(1)}, u32[]{:S(2)}, u32[]{:S(2)}) collective-permute-start(f32[24,128]{1,0:T(8,128)S(1)} %get-tuple-element.9), channel_id=1, source_target_pairs={{24,0},{16,8},{8,16},{0,24},{25,1},{17,9},{9,17},{1,25},{26,2},{18... | collective-permute-start | bytes 36872 | tf_op jit(solution)/shard_map/ppermute | solution.py:447
  26.9 0.5 %collective-permute-start.8 = (f32[24,128]{1,0:T(8,128)S(1)}, f32[24,128]{1,0:T(8,128)S(1)}, u32[]{:S(2)}, u32[]{:S(2)}) collective-permute-start(f32[24,128]{1,0:T(8,128)S(1)} %get-tuple-element.10), channel_id=1, source_target_pairs={{16,0},{24,8},{0,16},{8,24},{17,1},{25,9},{1,17},{9,25},{18,2},{26... | collective-permute-start | bytes 36872 | tf_op jit(solution)/shard_map/ppermute | solution.py:447
  27.4 1.5 %collective-permute-start.9 = (f32[24,128]{1,0:T(8,128)S(1)}, f32[24,128]{1,0:T(8,128)S(1)}, u32[]{:S(2)}, u32[]{:S(2)}) collective-permute-start(f32[24,128]{1,0:T(8,128)S(1)} %get-tuple-element.11), channel_id=1, source_target_pairs={{8,0},{0,8},{24,16},{16,24},{9,1},{1,9},{25,17},{17,25},{10,2},{2,... | collective-permute-start | bytes 36872 | tf_op jit(solution)/shard_map/ppermute | solution.py:447
  28.9 1.1 %collective-permute-done.7.refs_1_ = f32[24,128]{1,0:T(8,128)S(1)} collective-permute-done((f32[24,128]{1,0:T(8,128)S(1)}, f32[24,128]{1,0:T(8,128)S(1)}, u32[]{:S(2)}, u32[]{:S(2)}) %collective-permute-start.7) | collective-permute-done | bytes 12320 | tf_op jit(solution)/shard_map/ppermute | solution.py:447
  30.0 0.6 %collective-permute-done.8.refs_2_ = f32[24,128]{1,0:T(8,128)S(1)} collective-permute-done((f32[24,128]{1,0:T(8,128)S(1)}, f32[24,128]{1,0:T(8,128)S(1)}, u32[]{:S(2)}, u32[]{:S(2)}) %collective-permute-start.8) | collective-permute-done | bytes 12320 | tf_op jit(solution)/shard_map/ppermute | solution.py:447
  30.6 0.5 %collective-permute-done.9.refs_3_ = f32[24,128]{1,0:T(8,128)S(1)} collective-permute-done((f32[24,128]{1,0:T(8,128)S(1)}, f32[24,128]{1,0:T(8,128)S(1)}, u32[]{:S(2)}, u32[]{:S(2)}) %collective-permute-start.9) | collective-permute-done | bytes 12320 | tf_op jit(solution)/shard_map/ppermute | solution.py:447
  31.1 0.0 collective-permute-start.10
  31.1 1.2 %collective-permute-done.10.beside_ref.refs_1_ = f32[24,128]{1,0:T(8,128)S(1)} collective-permute-done((f32[24,128]{1,0:T(8,128)S(1)}, f32[24,128]{1,0:T(8,128)S(1)}, u32[]{:S(2)}, u32[]{:S(2)}) %collective-permute-start.10) | collective-permute-done | bytes 12320 | tf_op jit(solution)/shard_map/ppermute | solution.py:447
  32.3 4.7 %collective-permute-start.13 = (f32[16,128]{1,0:T(8,128)S(1)}, f32[16,128]{1,0:T(8,128)S(1)}, u32[]{:S(2)}, u32[]{:S(2)}) collective-permute-start(f32[16,128]{1,0:T(8,128)S(1)} %shard_map.63.refs_2_), channel_id=1, source_target_pairs={{6,0},{7,1},{4,2},{5,3},{2,4},{3,5},{0,6},{1,7},{14,8},{15,9},{12,... | collective-permute-start | bytes 24584 | tf_op jit(solution)/shard_map/ppermute | solution.py:447
  36.9 0.0 collective-permute-start.12
  36.9 0.6 %collective-permute-start.11 = (f32[16,128]{1,0:T(8,128)S(1)}, f32[16,128]{1,0:T(8,128)S(1)}, u32[]{:S(2)}, u32[]{:S(2)}) collective-permute-start(f32[16,128]{1,0:T(8,128)S(1)} %shard_map.63.refs_2_), channel_id=1, source_target_pairs={{2,0},{3,1},{0,2},{1,3},{6,4},{7,5},{4,6},{5,7},{10,8},{11,9},{8,1... | collective-permute-start | bytes 24584 | tf_op jit(solution)/shard_map/ppermute | solution.py:447
  37.6 1.0 %collective-permute-done.13.refs_5_ = f32[16,128]{1,0:T(8,128)S(1)} collective-permute-done((f32[16,128]{1,0:T(8,128)S(1)}, f32[16,128]{1,0:T(8,128)S(1)}, u32[]{:S(2)}, u32[]{:S(2)}) %collective-permute-start.13) | collective-permute-done | bytes 8224 | tf_op jit(solution)/shard_map/ppermute | solution.py:447
  38.6 2.9 %collective-permute-done.12.refs_4_ = f32[16,128]{1,0:T(8,128)S(1)} collective-permute-done((f32[16,128]{1,0:T(8,128)S(1)}, f32[16,128]{1,0:T(8,128)S(1)}, u32[]{:S(2)}, u32[]{:S(2)}) %collective-permute-start.12) | collective-permute-done | bytes 8224 | tf_op jit(solution)/shard_map/ppermute | solution.py:447
  41.5 0.0 collective-permute-done.11.refs_3_
  41.5 0.7 %shard_map.64 = f32[2,8,128]{2,1,0:T(8,128)} custom-call(f32[24,128]{1,0:T(8,128)S(1)} %shard_map.62.sum_ref.refs_0_, f32[24,128]{1,0:T(8,128)S(1)} %collective-permute-done.10.beside_ref.refs_1_, f32[16,128]{1,0:T(8,128)S(1)} %shard_map.63.refs_2_, f32[16,128]{1,0:T(8,128)S(1)} %collective-permute-done.11.refs_3_, ...), custom_call_target="tpu_custom_call" | custom-call | flops 100000 | bytes 10000 | tf_op jit(solution)/shard_map/pallas_call | solution.py:484
  (4 shorter events, 0.0 us)
Async XLA Ops:
  0.6 6.3 %collective-permute-start.1 = (f32[2,8,128]{2,1,0:T(8,128)}, f32[2,8,128]{2,1,0:T(8,128)S(1)}, u32[]{:S(2)}, u32[]{:S(2)}) collective-permute-start(f32[2,8,128]{2,1,0:T(8,128)} %refs_1_.1), channel_id=1, source_target_pairs={{24,0},{16,8},{8,16},{0,24},{25,1},{17,9},{9,17},{1,25},{26,2},{18... | collective-permute-start | bytes 24584 | tf_op jit(solution)/shard_map/ppermute | solution.py:447
  4.6 3.9 %collective-permute-start = (f32[2,8,128]{2,1,0:T(8,128)}, f32[2,8,128]{2,1,0:T(8,128)S(1)}, u32[]{:S(2)}, u32[]{:S(2)}) collective-permute-start(f32[2,8,128]{2,1,0:T(8,128)} %refs_1_.1), channel_id=1, source_target_pairs={{16,0},{24,8},{0,16},{8,24},{17,1},{25,9},{1,17},{9,25},{18,2},{26... | collective-permute-start | bytes 24584 | tf_op jit(solution)/shard_map/ppermute | solution.py:447
  5.1 3.9 %collective-permute-start.2 = (f32[2,8,128]{2,1,0:T(8,128)}, f32[2,8,128]{2,1,0:T(8,128)S(1)}, u32[]{:S(2)}, u32[]{:S(2)}) collective-permute-start(f32[2,8,128]{2,1,0:T(8,128)} %refs_1_.1), channel_id=1, source_target_pairs={{8,0},{0,8},{24,16},{16,24},{9,1},{1,9},{25,17},{17,25},{10,2},{2,... | collective-permute-start | bytes 24584 | tf_op jit(solution)/shard_map/ppermute | solution.py:447
  5.2 0.9 %copy-start = (f32[2,3,2,32,128]{4,3,2,1,0:T(8,128)S(1)}, f32[2,3,2,32,128]{4,3,2,1,0:T(8,128)}, u32[]{:S(2)}) copy-start(f32[2,3,2,32,128]{4,3,2,1,0:T(8,128)} %forces_ref.1) | copy-start | bytes 589828
  6.2 0.8 %copy-start.1 = (s32[2,32,128]{2,1,0:T(8,128)S(1)}, s32[2,32,128]{2,1,0:T(8,128)}, u32[]{:S(2)}) copy-start(s32[2,32,128]{2,1,0:T(8,128)} %labels_ref.1) | copy-start | bytes 98308
  6.9 2.0 %copy-start.2 = (f32[2,8,128]{2,1,0:T(8,128)S(1)}, f32[2,8,128]{2,1,0:T(8,128)}, u32[]{:S(2)}) copy-start(f32[2,8,128]{2,1,0:T(8,128)} %refs_1_.1) | copy-start | bytes 24580
  6.9 12.4 %copy-start.3 = (s32[8]{0:T(128)S(1)}, s32[8]{0:T(128)}, u32[]{:S(2)}) copy-start(s32[8]{0:T(128)} %refs_0_.1) | copy-start | bytes 100
  9.0 3.7 %collective-permute-start.4 = (f32[16,32,128]{2,1,0:T(8,128)S(1)}, f32[16,32,128]{2,1,0:T(8,128)S(1)}, u32[]{:S(2)}, u32[]{:S(2)}) collective-permute-start(f32[16,32,128]{2,1,0:T(8,128)S(1)} %shard_map.60.refs_1_), channel_id=1, source_target_pairs={{1,2},{3,4},{5,6},{2,1},{4,3},{6,5},{0,0},{7,7},{9,10},{11,12},{13... | collective-permute-start | bytes 786440 | tf_op jit(solution)/shard_map/ppermute | solution.py:453
  9.7 8.9 %collective-permute-start.6 = (f32[16,32,128]{2,1,0:T(8,128)S(1)}, f32[16,32,128]{2,1,0:T(8,128)S(1)}, u32[]{:S(2)}, u32[]{:S(2)}) collective-permute-start(f32[16,32,128]{2,1,0:T(8,128)S(1)} %shard_map.60.refs_1_), channel_id=1, source_target_pairs={{0,2},{2,4},{4,6},{3,1},{5,3},{7,5},{1,0},{6,7},{8,10},{10,12},{12... | collective-permute-start | bytes 786440 | tf_op jit(solution)/shard_map/ppermute | solution.py:461
  12.5 6.1 %collective-permute-start.3 = (f32[16,32,128]{2,1,0:T(8,128)S(1)}, f32[16,32,128]{2,1,0:T(8,128)S(1)}, u32[]{:S(2)}, u32[]{:S(2)}) collective-permute-start(f32[16,32,128]{2,1,0:T(8,128)S(1)} %shard_map.60.refs_1_), channel_id=1, source_target_pairs={{1,0},{0,1},{3,2},{2,3},{5,4},{4,5},{7,6},{6,7},{9,8},{8,9},{11,10... | collective-permute-start | bytes 786440 | tf_op jit(solution)/shard_map/ppermute | solution.py:447
  12.7 6.7 %collective-permute-start.5 = (f32[16,32,128]{2,1,0:T(8,128)S(1)}, f32[16,32,128]{2,1,0:T(8,128)S(1)}, u32[]{:S(2)}, u32[]{:S(2)}) collective-permute-start(f32[16,32,128]{2,1,0:T(8,128)S(1)} %collective-permute-done.4.refs_3_), channel_id=1, source_target_pairs={{1,0},{0,1},{3,2},{2,3},{5,4},{4,5},{7,6},{6,7},{9,8},{8,9},{11,10... | collective-permute-start | bytes 786440 | tf_op jit(solution)/shard_map/ppermute | solution.py:447
  25.3 4.7 %collective-permute-start.7 = (f32[24,128]{1,0:T(8,128)S(1)}, f32[24,128]{1,0:T(8,128)S(1)}, u32[]{:S(2)}, u32[]{:S(2)}) collective-permute-start(f32[24,128]{1,0:T(8,128)S(1)} %get-tuple-element.9), channel_id=1, source_target_pairs={{24,0},{16,8},{8,16},{0,24},{25,1},{17,9},{9,17},{1,25},{26,2},{18... | collective-permute-start | bytes 36872 | tf_op jit(solution)/shard_map/ppermute | solution.py:447
  26.9 3.7 %collective-permute-start.8 = (f32[24,128]{1,0:T(8,128)S(1)}, f32[24,128]{1,0:T(8,128)S(1)}, u32[]{:S(2)}, u32[]{:S(2)}) collective-permute-start(f32[24,128]{1,0:T(8,128)S(1)} %get-tuple-element.10), channel_id=1, source_target_pairs={{16,0},{24,8},{0,16},{8,24},{17,1},{25,9},{1,17},{9,25},{18,2},{26... | collective-permute-start | bytes 36872 | tf_op jit(solution)/shard_map/ppermute | solution.py:447
  27.4 3.7 %collective-permute-start.9 = (f32[24,128]{1,0:T(8,128)S(1)}, f32[24,128]{1,0:T(8,128)S(1)}, u32[]{:S(2)}, u32[]{:S(2)}) collective-permute-start(f32[24,128]{1,0:T(8,128)S(1)} %get-tuple-element.11), channel_id=1, source_target_pairs={{8,0},{0,8},{24,16},{16,24},{9,1},{1,9},{25,17},{17,25},{10,2},{2,... | collective-permute-start | bytes 36872 | tf_op jit(solution)/shard_map/ppermute | solution.py:447
  31.1 1.2 %collective-permute-start.10 = (f32[24,128]{1,0:T(8,128)S(1)}, f32[24,128]{1,0:T(8,128)S(1)}, u32[]{:S(2)}, u32[]{:S(2)}) collective-permute-start(f32[24,128]{1,0:T(8,128)S(1)} %shard_map.62.sum_ref.refs_0_), channel_id=1, source_target_pairs={{1,0},{0,1},{3,2},{2,3},{5,4},{4,5},{7,6},{6,7},{9,8},{8,9},{11,10... | collective-permute-start | bytes 36872 | tf_op jit(solution)/shard_map/ppermute | solution.py:447
  32.3 6.3 %collective-permute-start.13 = (f32[16,128]{1,0:T(8,128)S(1)}, f32[16,128]{1,0:T(8,128)S(1)}, u32[]{:S(2)}, u32[]{:S(2)}) collective-permute-start(f32[16,128]{1,0:T(8,128)S(1)} %shard_map.63.refs_2_), channel_id=1, source_target_pairs={{6,0},{7,1},{4,2},{5,3},{2,4},{3,5},{0,6},{1,7},{14,8},{15,9},{12,... | collective-permute-start | bytes 24584 | tf_op jit(solution)/shard_map/ppermute | solution.py:447
  36.9 4.5 %collective-permute-start.12 = (f32[16,128]{1,0:T(8,128)S(1)}, f32[16,128]{1,0:T(8,128)S(1)}, u32[]{:S(2)}, u32[]{:S(2)}) collective-permute-start(f32[16,128]{1,0:T(8,128)S(1)} %shard_map.63.refs_2_), channel_id=1, source_target_pairs={{4,0},{5,1},{6,2},{7,3},{0,4},{1,5},{2,6},{3,7},{12,8},{13,9},{14,... | collective-permute-start | bytes 24584 | tf_op jit(solution)/shard_map/ppermute | solution.py:447
  36.9 4.5 %collective-permute-start.11 = (f32[16,128]{1,0:T(8,128)S(1)}, f32[16,128]{1,0:T(8,128)S(1)}, u32[]{:S(2)}, u32[]{:S(2)}) collective-permute-start(f32[16,128]{1,0:T(8,128)S(1)} %shard_map.63.refs_2_), channel_id=1, source_target_pairs={{2,0},{3,1},{0,2},{1,3},{6,4},{7,5},{4,6},{5,7},{10,8},{11,9},{8,1... | collective-permute-start | bytes 24584 | tf_op jit(solution)/shard_map/ppermute | solution.py:447

commit v7 on v5

--- a/solution.py
+++ b/solution.py
@@ -366,12 +366,12 @@
         pack_ref[pack_plane(cases, layers, cases, 1, layer)] = marks
 
 
-def design_kernel(cases, count_load, *refs):
-    density_refs = refs[1 : 1 + count_load]
+def design_kernel(cases, steps, *refs):
+    density_refs = refs[1 : 1 + len(steps)]
     pack_ref, design_ref = refs[-2:]
     layers, own_rows, _ = density_refs[0].shape
     load = lax.axis_index("load")
-    for step, density_ref in enumerate(density_refs):
+    for step, density_ref in zip(steps, density_refs):
         start = pl.multiple_of(partner(load, step) * own_rows, own_rows)
         for layer in range(layers):
             plane = pack_plane(cases, layers, cases, 0, layer)
@@ -421,7 +421,7 @@
     while 2 ** (len(edges) + 1) < count_gz:
         edges.append(2 ** (len(edges) + 1) - 1)
     pairs = [edges[at : at + 2] for at in range(0, len(edges), 2)]
-    return [pair + [pair[0] ^ pair[1]] if len(pair) == 2 else pair for pair in pairs]
+    return [[pair[0], pair[0] ^ pair[1], pair[1]] if len(pair) == 2 else pair for pair in pairs]
 
 
 def update_kernel(cells, rounds, *refs):
@@ -508,9 +508,10 @@
         lax.ppermute(forces, "gz", across_pairs(far, count_gz)) for far in range(1, hops + 1)
     ]
     pack = call(stage_kernel, shape(planes, rows, columns), (labels, forces), 2 * planes, 1_000_000)
-    densities = [density] + [met(density, "load", step) for step in range(1, count_load)]
+    steps = [0] + list(range(2, count_load)) + [1]
+    densities = [density] + [met(density, "load", step) for step in steps[1:]]
     pack, design = call(
-        functools.partial(design_kernel, cases, count_load),
+        functools.partial(design_kernel, cases, steps),
         (shape(planes, rows, columns), shape(2 * layers, rows, columns)),
         (pack, *densities, *far_forces),
         2 * planes + 6 * layers,
@@ -564,7 +565,7 @@
         scratch=scratch,
     )
 
-    received = [met(slots[step], "load", step) for step in range(1, count_load)]
+    received = [met(slots[step], "load", step) for step in range(count_load - 1, 0, -1)]
     whole = call(sum_kernel, shape(slot_rows, columns), (slots[0], *received), 2 * count_load, 100_000)
     beside = met(whole, "gz", 1)
     forward_rows = -(-(wide + 1) // 8) * 8

time: 43.5 us -> 41.7 us (0.959)
  waiting for transfers between devices: 10.7 us -> 8.86 us
    ppermute x12, waiting for transfers between devices: 10.7 us -> 8.85 us  [met(): lax.ppermute(block, axis, [(partner(i, step), i) for i in range(count)])]
where the time goes in v7:
time: 41.7 us; the launch traced here: 41.4 us
  starting transfers between devices  23.6 us (57%)
  waiting for transfers between devices  8.86 us (21%)
  Pallas kernels  6.53 us (16%)
  local copies, waits for them, and re-layouts  1.69 us (4%)
  between operations  0.7 us (2%)
    ppermute x12, starting transfers between devices, met(): lax.ppermute(block, axis, [(partner(i, step), i) for i in range(count)])  16.4 us
    ppermute x12, waiting for transfers between devices, met(): lax.ppermute(block, axis, [(partner(i, step), i) for i in range(count)])  8.85 us
    pallas_call x7, Pallas kernels, call(): pl.pallas_call(kernel, out_shape=out, in_specs=in_specs or [vmem] * len(a...  6.53 us
    ppermute x2, starting transfers between devices, on_device(): lax.ppermute(forces, 'gz', across_pairs(far, count_gz))  4.61 us
    ppermute x2, starting transfers between devices, on_device(): lax.ppermute(design, 'gz', across_pairs(far, count_gz))  2.65 us
    unnamed x8, local copies, waits for them, and re-layouts  1.69 us
  transfers between devices with their start and end apart: 16, of which 10 were waited for; matrix products, arithmetic and copies ran while one was open for 0% of the time, Pallas kernels for 0%

profile of v7, /device:TPU:0, one launch (start us, length us, event | category | flops | bytes accessed | tf_op | source)
XLA Modules:
  0.0 41.4 jit_solution(4440138442982753664)
XLA Ops:
  0.6 3.0 %collective-permute-start.4 = (f32[2,3,2,32,128]{4,3,2,1,0:T(8,128)}, f32[2,3,2,32,128]{4,3,2,1,0:T(8,128)S(1)}, u32[]{:S(2)}, u32[]{:S(2)}) collective-permute-start(f32[2,3,2,32,128]{4,3,2,1,0:T(8,128)} %forces_ref.1), channel_id=1, source_target_pairs={{0,2},{2,4},{4,6},{3,1},{5,3},{7,5},{1,0},{6,7},{8,10},{10,12},{12... | collective-permute-start | bytes 589832 | tf_op jit(solution)/shard_map/ppermute | solution.py:508
  3.7 1.6 %collective-permute-start.3 = (f32[2,3,2,32,128]{4,3,2,1,0:T(8,128)}, f32[2,3,2,32,128]{4,3,2,1,0:T(8,128)S(1)}, u32[]{:S(2)}, u32[]{:S(2)}) collective-permute-start(f32[2,3,2,32,128]{4,3,2,1,0:T(8,128)} %forces_ref.1), channel_id=1, source_target_pairs={{1,2},{3,4},{5,6},{2,1},{4,3},{6,5},{0,0},{7,7},{9,10},{11,12},{13... | collective-permute-start | bytes 589832 | tf_op jit(solution)/shard_map/ppermute | solution.py:508
  5.2 2.4 %collective-permute-start.1 = (f32[2,8,128]{2,1,0:T(8,128)}, f32[2,8,128]{2,1,0:T(8,128)S(1)}, u32[]{:S(2)}, u32[]{:S(2)}) collective-permute-start(f32[2,8,128]{2,1,0:T(8,128)} %refs_1_.1), channel_id=1, source_target_pairs={{24,0},{16,8},{8,16},{0,24},{25,1},{17,9},{9,17},{1,25},{26,2},{18... | collective-permute-start | bytes 24584 | tf_op jit(solution)/shard_map/ppermute | solution.py:466
  7.7 0.5 %collective-permute-start = (f32[2,8,128]{2,1,0:T(8,128)}, f32[2,8,128]{2,1,0:T(8,128)S(1)}, u32[]{:S(2)}, u32[]{:S(2)}) collective-permute-start(f32[2,8,128]{2,1,0:T(8,128)} %refs_1_.1), channel_id=1, source_target_pairs={{16,0},{24,8},{0,16},{8,24},{17,1},{25,9},{1,17},{9,25},{18,2},{26... | collective-permute-start | bytes 24584 | tf_op jit(solution)/shard_map/ppermute | solution.py:466
  8.2 0.5 %collective-permute-start.2 = (f32[2,8,128]{2,1,0:T(8,128)}, f32[2,8,128]{2,1,0:T(8,128)S(1)}, u32[]{:S(2)}, u32[]{:S(2)}) collective-permute-start(f32[2,8,128]{2,1,0:T(8,128)} %refs_1_.1), channel_id=1, source_target_pairs={{8,0},{0,8},{24,16},{16,24},{9,1},{1,9},{25,17},{17,25},{10,2},{2,... | collective-permute-start | bytes 24584 | tf_op jit(solution)/shard_map/ppermute | solution.py:466
  8.7 0.0 copy-start
  8.7 0.9 %copy-done = f32[2,3,2,32,128]{4,3,2,1,0:T(8,128)S(1)} copy-done((f32[2,3,2,32,128]{4,3,2,1,0:T(8,128)S(1)}, f32[2,3,2,32,128]{4,3,2,1,0:T(8,128)}, u32[]{:S(2)}) %copy-start) | copy-done | bytes 196632
  9.7 0.0 copy-start.1
  9.7 0.8 %copy-done.1 = s32[2,32,128]{2,1,0:T(8,128)S(1)} copy-done((s32[2,32,128]{2,1,0:T(8,128)S(1)}, s32[2,32,128]{2,1,0:T(8,128)}, u32[]{:S(2)}) %copy-start.1) | copy-done | bytes 32792
  10.4 0.0 copy-start.2
  10.4 0.0 collective-permute-done.1.refs_3_
  10.5 1.1 %collective-permute-done.refs_2_ = f32[2,8,128]{2,1,0:T(8,128)S(1)} collective-permute-done((f32[2,8,128]{2,1,0:T(8,128)}, f32[2,8,128]{2,1,0:T(8,128)S(1)}, u32[]{:S(2)}, u32[]{:S(2)}) %collective-permute-start) | collective-permute-done | bytes 8224 | tf_op jit(solution)/shard_map/ppermute | solution.py:466
  11.6 0.5 %collective-permute-done.2.refs_4_ = f32[2,8,128]{2,1,0:T(8,128)S(1)} collective-permute-done((f32[2,8,128]{2,1,0:T(8,128)}, f32[2,8,128]{2,1,0:T(8,128)S(1)}, u32[]{:S(2)}, u32[]{:S(2)}) %collective-permute-start.2) | collective-permute-done | bytes 8224 | tf_op jit(solution)/shard_map/ppermute | solution.py:466
  12.1 0.0 collective-permute-done.4.refs_6_.refs_7_
  12.1 0.0 collective-permute-done.3.refs_5_.force_ref.refs_4_
  12.1 0.0 copy-done.2
  12.1 2.0 %collective-permute-start.7 = (f32[4,32,128]{2,1,0:T(8,128)S(1)}, f32[4,32,128]{2,1,0:T(8,128)S(1)}, u32[]{:S(2)}, u32[]{:S(2)}) collective-permute-start(f32[4,32,128]{2,1,0:T(8,128)S(1)} %get-tuple-element.11), channel_id=1, source_target_pairs={{0,2},{2,4},{4,6},{3,1},{5,3},{7,5},{1,0},{6,7},{8,10},{10,12},{12... | collective-permute-start | bytes 196616 | tf_op jit(solution)/shard_map/ppermute | solution.py:524
  14.1 0.7 %collective-permute-start.6 = (f32[4,32,128]{2,1,0:T(8,128)S(1)}, f32[4,32,128]{2,1,0:T(8,128)S(1)}, u32[]{:S(2)}, u32[]{:S(2)}) collective-permute-start(f32[4,32,128]{2,1,0:T(8,128)S(1)} %get-tuple-element.11), channel_id=1, source_target_pairs={{1,2},{3,4},{5,6},{2,1},{4,3},{6,5},{0,0},{7,7},{9,10},{11,12},{13... | collective-permute-start | bytes 196616 | tf_op jit(solution)/shard_map/ppermute | solution.py:524
  14.8 0.0 copy-start.3
  14.8 3.0 %collective-permute-start.5 = (f32[16,32,128]{2,1,0:T(8,128)S(1)}, f32[16,32,128]{2,1,0:T(8,128)S(1)}, u32[]{:S(2)}, u32[]{:S(2)}) collective-permute-start(f32[16,32,128]{2,1,0:T(8,128)S(1)} %get-tuple-element.10.refs_1_), channel_id=1, source_target_pairs={{1,0},{0,1},{3,2},{2,3},{5,4},{4,5},{7,6},{6,7},{9,8},{8,9},{11,10... | collective-permute-start | bytes 786440 | tf_op jit(solution)/shard_map/ppermute | solution.py:466
  17.8 0.0 collective-permute-done.7.refs_0_.refs_6_
  17.8 0.0 collective-permute-done.6.design_ref.refs_3_
  17.8 1.9 %collective-permute-start.8 = (f32[16,32,128]{2,1,0:T(8,128)S(1)}, f32[16,32,128]{2,1,0:T(8,128)S(1)}, u32[]{:S(2)}, u32[]{:S(2)}) collective-permute-start(f32[16,32,128]{2,1,0:T(8,128)S(1)} %shard_map.61), channel_id=1, source_target_pairs={{1,0},{0,1},{3,2},{2,3},{5,4},{4,5},{7,6},{6,7},{9,8},{8,9},{11,10... | collective-permute-start | bytes 786440 | tf_op jit(solution)/shard_map/ppermute | solution.py:466
  19.7 0.0 collective-permute-done.5.refs_2_
  19.7 1.2 %collective-permute-done.8.refs_5_ = f32[16,32,128]{2,1,0:T(8,128)S(1)} collective-permute-done((f32[16,32,128]{2,1,0:T(8,128)S(1)}, f32[16,32,128]{2,1,0:T(8,128)S(1)}, u32[]{:S(2)}, u32[]{:S(2)}) %collective-permute-start.8) | collective-permute-done | bytes 262176 | tf_op jit(solution)/shard_map/ppermute | solution.py:466
  20.9 0.0 copy-done.3
  20.9 5.7 %shard_map.62 = (f32[2,3,2,32,128]{4,3,2,1,0:T(8,128)}, f32[3,2,8,128]{3,2,1,0:T(8,128)S(1)}, f32[24,128]{1,0:T(8,128)S(1)}, f32[24,128]{1,0:T(8,128)S(1)}, f32[...) custom-call(s32[8]{0:T(128)S(1)} %copy-done.3, f32[16,32,128]{2,1,0:T(8,128)S(1)} %get-tuple-element.10.refs_1_, ...), custom_call_target="tpu_custom_call" | custom-call | flops 60000000 | bytes 6000000 | tf_op jit(solution)/shard_map/pallas_call | solution.py:495
  26.6 1.6 %collective-permute-start.9 = (f32[24,128]{1,0:T(8,128)S(1)}, f32[24,128]{1,0:T(8,128)S(1)}, u32[]{:S(2)}, u32[]{:S(2)}) collective-permute-start(f32[24,128]{1,0:T(8,128)S(1)} %get-tuple-element.13), channel_id=1, source_target_pairs={{24,0},{16,8},{8,16},{0,24},{25,1},{17,9},{9,17},{1,25},{26,2},{18... | collective-permute-start | bytes 36872 | tf_op jit(solution)/shard_map/ppermute | solution.py:466
  28.2 0.5 %collective-permute-start.10 = (f32[24,128]{1,0:T(8,128)S(1)}, f32[24,128]{1,0:T(8,128)S(1)}, u32[]{:S(2)}, u32[]{:S(2)}) collective-permute-start(f32[24,128]{1,0:T(8,128)S(1)} %get-tuple-element.14), channel_id=1, source_target_pairs={{16,0},{24,8},{0,16},{8,24},{17,1},{25,9},{1,17},{9,25},{18,2},{26... | collective-permute-start | bytes 36872 | tf_op jit(solution)/shard_map/ppermute | solution.py:466
  28.7 1.5 %collective-permute-start.11 = (f32[24,128]{1,0:T(8,128)S(1)}, f32[24,128]{1,0:T(8,128)S(1)}, u32[]{:S(2)}, u32[]{:S(2)}) collective-permute-start(f32[24,128]{1,0:T(8,128)S(1)} %get-tuple-element.15), channel_id=1, source_target_pairs={{8,0},{0,8},{24,16},{16,24},{9,1},{1,9},{25,17},{17,25},{10,2},{2,... | collective-permute-start | bytes 36872 | tf_op jit(solution)/shard_map/ppermute | solution.py:466
  30.2 1.1 %collective-permute-done.9.refs_1_ = f32[24,128]{1,0:T(8,128)S(1)} collective-permute-done((f32[24,128]{1,0:T(8,128)S(1)}, f32[24,128]{1,0:T(8,128)S(1)}, u32[]{:S(2)}, u32[]{:S(2)}) %collective-permute-start.9) | collective-permute-done | bytes 12320 | tf_op jit(solution)/shard_map/ppermute | solution.py:466
  31.3 0.6 %collective-permute-done.10.refs_2_ = f32[24,128]{1,0:T(8,128)S(1)} collective-permute-done((f32[24,128]{1,0:T(8,128)S(1)}, f32[24,128]{1,0:T(8,128)S(1)}, u32[]{:S(2)}, u32[]{:S(2)}) %collective-permute-start.10) | collective-permute-done | bytes 12320 | tf_op jit(solution)/shard_map/ppermute | solution.py:466
  31.9 0.5 %collective-permute-done.11.refs_3_ = f32[24,128]{1,0:T(8,128)S(1)} collective-permute-done((f32[24,128]{1,0:T(8,128)S(1)}, f32[24,128]{1,0:T(8,128)S(1)}, u32[]{:S(2)}, u32[]{:S(2)}) %collective-permute-start.11) | collective-permute-done | bytes 12320 | tf_op jit(solution)/shard_map/ppermute | solution.py:466
  32.4 0.0 collective-permute-start.12
  32.4 1.2 %collective-permute-done.12.beside_ref.refs_1_ = f32[24,128]{1,0:T(8,128)S(1)} collective-permute-done((f32[24,128]{1,0:T(8,128)S(1)}, f32[24,128]{1,0:T(8,128)S(1)}, u32[]{:S(2)}, u32[]{:S(2)}) %collective-permute-start.12) | collective-permute-done | bytes 12320 | tf_op jit(solution)/shard_map/ppermute | solution.py:466
  33.6 1.7 %collective-permute-start.15 = (f32[16,128]{1,0:T(8,128)S(1)}, f32[16,128]{1,0:T(8,128)S(1)}, u32[]{:S(2)}, u32[]{:S(2)}) collective-permute-start(f32[16,128]{1,0:T(8,128)S(1)} %shard_map.64.refs_2_), channel_id=1, source_target_pairs={{6,0},{7,1},{4,2},{5,3},{2,4},{3,5},{0,6},{1,7},{14,8},{15,9},{12,... | collective-permute-start | bytes 24584 | tf_op jit(solution)/shard_map/ppermute | solution.py:466
  35.3 1.7 %collective-permute-start.14 = (f32[16,128]{1,0:T(8,128)S(1)}, f32[16,128]{1,0:T(8,128)S(1)}, u32[]{:S(2)}, u32[]{:S(2)}) collective-permute-start(f32[16,128]{1,0:T(8,128)S(1)} %shard_map.64.refs_2_), channel_id=1, source_target_pairs={{4,0},{5,1},{6,2},{7,3},{0,4},{1,5},{2,6},{3,7},{12,8},{13,9},{14,... | collective-permute-start | bytes 24584 | tf_op jit(solution)/shard_map/ppermute | solution.py:466
  37.0 0.9 %collective-permute-start.13 = (f32[16,128]{1,0:T(8,128)S(1)}, f32[16,128]{1,0:T(8,128)S(1)}, u32[]{:S(2)}, u32[]{:S(2)}) collective-permute-start(f32[16,128]{1,0:T(8,128)S(1)} %shard_map.64.refs_2_), channel_id=1, source_target_pairs={{2,0},{3,1},{0,2},{1,3},{6,4},{7,5},{4,6},{5,7},{10,8},{11,9},{8,1... | collective-permute-start | bytes 24584 | tf_op jit(solution)/shard_map/ppermute | solution.py:466
  38.0 1.1 %collective-permute-done.15.refs_5_ = f32[16,128]{1,0:T(8,128)S(1)} collective-permute-done((f32[16,128]{1,0:T(8,128)S(1)}, f32[16,128]{1,0:T(8,128)S(1)}, u32[]{:S(2)}, u32[]{:S(2)}) %collective-permute-start.15) | collective-permute-done | bytes 8224 | tf_op jit(solution)/shard_map/ppermute | solution.py:466
  39.0 0.8 %collective-permute-done.14.refs_4_ = f32[16,128]{1,0:T(8,128)S(1)} collective-permute-done((f32[16,128]{1,0:T(8,128)S(1)}, f32[16,128]{1,0:T(8,128)S(1)}, u32[]{:S(2)}, u32[]{:S(2)}) %collective-permute-start.14) | collective-permute-done | bytes 8224 | tf_op jit(solution)/shard_map/ppermute | solution.py:466
  39.9 0.8 %collective-permute-done.13.refs_3_ = f32[16,128]{1,0:T(8,128)S(1)} collective-permute-done((f32[16,128]{1,0:T(8,128)S(1)}, f32[16,128]{1,0:T(8,128)S(1)}, u32[]{:S(2)}, u32[]{:S(2)}) %collective-permute-start.13) | collective-permute-done | bytes 8224 | tf_op jit(solution)/shard_map/ppermute | solution.py:466
  40.7 0.7 %shard_map.65 = f32[2,8,128]{2,1,0:T(8,128)} custom-call(f32[24,128]{1,0:T(8,128)S(1)} %shard_map.63.sum_ref.refs_0_, f32[24,128]{1,0:T(8,128)S(1)} %collective-permute-done.12.beside_ref.refs_1_, f32[16,128]{1,0:T(8,128)S(1)} %shard_map.64.refs_2_, f32[16,128]{1,0:T(8,128)S(1)} %collective-permute-done.13.refs_3_, ...), custom_call_target="tpu_custom_call" | custom-call | flops 100000 | bytes 10000 | tf_op jit(solution)/shard_map/pallas_call | solution.py:495
  (5 shorter events, 0.1 us)
Async XLA Ops:
  0.6 11.4 %collective-permute-start.4 = (f32[2,3,2,32,128]{4,3,2,1,0:T(8,128)}, f32[2,3,2,32,128]{4,3,2,1,0:T(8,128)S(1)}, u32[]{:S(2)}, u32[]{:S(2)}) collective-permute-start(f32[2,3,2,32,128]{4,3,2,1,0:T(8,128)} %forces_ref.1), channel_id=1, source_target_pairs={{0,2},{2,4},{4,6},{3,1},{5,3},{7,5},{1,0},{6,7},{8,10},{10,12},{12... | collective-permute-start | bytes 589832 | tf_op jit(solution)/shard_map/ppermute | solution.py:508
  3.7 8.4 %collective-permute-start.3 = (f32[2,3,2,32,128]{4,3,2,1,0:T(8,128)}, f32[2,3,2,32,128]{4,3,2,1,0:T(8,128)S(1)}, u32[]{:S(2)}, u32[]{:S(2)}) collective-permute-start(f32[2,3,2,32,128]{4,3,2,1,0:T(8,128)} %forces_ref.1), channel_id=1, source_target_pairs={{1,2},{3,4},{5,6},{2,1},{4,3},{6,5},{0,0},{7,7},{9,10},{11,12},{13... | collective-permute-start | bytes 589832 | tf_op jit(solution)/shard_map/ppermute | solution.py:508
  5.2 5.2 %collective-permute-start.1 = (f32[2,8,128]{2,1,0:T(8,128)}, f32[2,8,128]{2,1,0:T(8,128)S(1)}, u32[]{:S(2)}, u32[]{:S(2)}) collective-permute-start(f32[2,8,128]{2,1,0:T(8,128)} %refs_1_.1), channel_id=1, source_target_pairs={{24,0},{16,8},{8,16},{0,24},{25,1},{17,9},{9,17},{1,25},{26,2},{18... | collective-permute-start | bytes 24584 | tf_op jit(solution)/shard_map/ppermute | solution.py:466
  7.7 3.9 %collective-permute-start = (f32[2,8,128]{2,1,0:T(8,128)}, f32[2,8,128]{2,1,0:T(8,128)S(1)}, u32[]{:S(2)}, u32[]{:S(2)}) collective-permute-start(f32[2,8,128]{2,1,0:T(8,128)} %refs_1_.1), channel_id=1, source_target_pairs={{16,0},{24,8},{0,16},{8,24},{17,1},{25,9},{1,17},{9,25},{18,2},{26... | collective-permute-start | bytes 24584 | tf_op jit(solution)/shard_map/ppermute | solution.py:466
  8.2 3.9 %collective-permute-start.2 = (f32[2,8,128]{2,1,0:T(8,128)}, f32[2,8,128]{2,1,0:T(8,128)S(1)}, u32[]{:S(2)}, u32[]{:S(2)}) collective-permute-start(f32[2,8,128]{2,1,0:T(8,128)} %refs_1_.1), channel_id=1, source_target_pairs={{8,0},{0,8},{24,16},{16,24},{9,1},{1,9},{25,17},{17,25},{10,2},{2,... | collective-permute-start | bytes 24584 | tf_op jit(solution)/shard_map/ppermute | solution.py:466
  8.7 0.9 %copy-start = (f32[2,3,2,32,128]{4,3,2,1,0:T(8,128)S(1)}, f32[2,3,2,32,128]{4,3,2,1,0:T(8,128)}, u32[]{:S(2)}) copy-start(f32[2,3,2,32,128]{4,3,2,1,0:T(8,128)} %forces_ref.1) | copy-start | bytes 589828
  9.7 0.8 %copy-start.1 = (s32[2,32,128]{2,1,0:T(8,128)S(1)}, s32[2,32,128]{2,1,0:T(8,128)}, u32[]{:S(2)}) copy-start(s32[2,32,128]{2,1,0:T(8,128)} %labels_ref.1) | copy-start | bytes 98308
  10.4 1.6 %copy-start.2 = (f32[2,8,128]{2,1,0:T(8,128)S(1)}, f32[2,8,128]{2,1,0:T(8,128)}, u32[]{:S(2)}) copy-start(f32[2,8,128]{2,1,0:T(8,128)} %refs_1_.1) | copy-start | bytes 24580
  12.1 5.7 %collective-permute-start.7 = (f32[4,32,128]{2,1,0:T(8,128)S(1)}, f32[4,32,128]{2,1,0:T(8,128)S(1)}, u32[]{:S(2)}, u32[]{:S(2)}) collective-permute-start(f32[4,32,128]{2,1,0:T(8,128)S(1)} %get-tuple-element.11), channel_id=1, source_target_pairs={{0,2},{2,4},{4,6},{3,1},{5,3},{7,5},{1,0},{6,7},{8,10},{10,12},{12... | collective-permute-start | bytes 196616 | tf_op jit(solution)/shard_map/ppermute | solution.py:524
  14.1 3.7 %collective-permute-start.6 = (f32[4,32,128]{2,1,0:T(8,128)S(1)}, f32[4,32,128]{2,1,0:T(8,128)S(1)}, u32[]{:S(2)}, u32[]{:S(2)}) collective-permute-start(f32[4,32,128]{2,1,0:T(8,128)S(1)} %get-tuple-element.11), channel_id=1, source_target_pairs={{1,2},{3,4},{5,6},{2,1},{4,3},{6,5},{0,0},{7,7},{9,10},{11,12},{13... | collective-permute-start | bytes 196616 | tf_op jit(solution)/shard_map/ppermute | solution.py:524
  14.8 6.1 %copy-start.3 = (s32[8]{0:T(128)S(1)}, s32[8]{0:T(128)}, u32[]{:S(2)}) copy-start(s32[8]{0:T(128)} %refs_0_.1) | copy-start | bytes 100
  14.8 4.9 %collective-permute-start.5 = (f32[16,32,128]{2,1,0:T(8,128)S(1)}, f32[16,32,128]{2,1,0:T(8,128)S(1)}, u32[]{:S(2)}, u32[]{:S(2)}) collective-permute-start(f32[16,32,128]{2,1,0:T(8,128)S(1)} %get-tuple-element.10.refs_1_), channel_id=1, source_target_pairs={{1,0},{0,1},{3,2},{2,3},{5,4},{4,5},{7,6},{6,7},{9,8},{8,9},{11,10... | collective-permute-start | bytes 786440 | tf_op jit(solution)/shard_map/ppermute | solution.py:466
  17.8 3.1 %collective-permute-start.8 = (f32[16,32,128]{2,1,0:T(8,128)S(1)}, f32[16,32,128]{2,1,0:T(8,128)S(1)}, u32[]{:S(2)}, u32[]{:S(2)}) collective-permute-start(f32[16,32,128]{2,1,0:T(8,128)S(1)} %shard_map.61), channel_id=1, source_target_pairs={{1,0},{0,1},{3,2},{2,3},{5,4},{4,5},{7,6},{6,7},{9,8},{8,9},{11,10... | collective-permute-start | bytes 786440 | tf_op jit(solution)/shard_map/ppermute | solution.py:466
  26.6 4.7 %collective-permute-start.9 = (f32[24,128]{1,0:T(8,128)S(1)}, f32[24,128]{1,0:T(8,128)S(1)}, u32[]{:S(2)}, u32[]{:S(2)}) collective-permute-start(f32[24,128]{1,0:T(8,128)S(1)} %get-tuple-element.13), channel_id=1, source_target_pairs={{24,0},{16,8},{8,16},{0,24},{25,1},{17,9},{9,17},{1,25},{26,2},{18... | collective-permute-start | bytes 36872 | tf_op jit(solution)/shard_map/ppermute | solution.py:466
  28.2 3.7 %collective-permute-start.10 = (f32[24,128]{1,0:T(8,128)S(1)}, f32[24,128]{1,0:T(8,128)S(1)}, u32[]{:S(2)}, u32[]{:S(2)}) collective-permute-start(f32[24,128]{1,0:T(8,128)S(1)} %get-tuple-element.14), channel_id=1, source_target_pairs={{16,0},{24,8},{0,16},{8,24},{17,1},{25,9},{1,17},{9,25},{18,2},{26... | collective-permute-start | bytes 36872 | tf_op jit(solution)/shard_map/ppermute | solution.py:466
  28.7 3.7 %collective-permute-start.11 = (f32[24,128]{1,0:T(8,128)S(1)}, f32[24,128]{1,0:T(8,128)S(1)}, u32[]{:S(2)}, u32[]{:S(2)}) collective-permute-start(f32[24,128]{1,0:T(8,128)S(1)} %get-tuple-element.15), channel_id=1, source_target_pairs={{8,0},{0,8},{24,16},{16,24},{9,1},{1,9},{25,17},{17,25},{10,2},{2,... | collective-permute-start | bytes 36872 | tf_op jit(solution)/shard_map/ppermute | solution.py:466
  32.4 1.2 %collective-permute-start.12 = (f32[24,128]{1,0:T(8,128)S(1)}, f32[24,128]{1,0:T(8,128)S(1)}, u32[]{:S(2)}, u32[]{:S(2)}) collective-permute-start(f32[24,128]{1,0:T(8,128)S(1)} %shard_map.63.sum_ref.refs_0_), channel_id=1, source_target_pairs={{1,0},{0,1},{3,2},{2,3},{5,4},{4,5},{7,6},{6,7},{9,8},{8,9},{11,10... | collective-permute-start | bytes 36872 | tf_op jit(solution)/shard_map/ppermute | solution.py:466
  33.6 5.5 %collective-permute-start.15 = (f32[16,128]{1,0:T(8,128)S(1)}, f32[16,128]{1,0:T(8,128)S(1)}, u32[]{:S(2)}, u32[]{:S(2)}) collective-permute-start(f32[16,128]{1,0:T(8,128)S(1)} %shard_map.64.refs_2_), channel_id=1, source_target_pairs={{6,0},{7,1},{4,2},{5,3},{2,4},{3,5},{0,6},{1,7},{14,8},{15,9},{12,... | collective-permute-start | bytes 24584 | tf_op jit(solution)/shard_map/ppermute | solution.py:466
  35.3 4.5 %collective-permute-start.14 = (f32[16,128]{1,0:T(8,128)S(1)}, f32[16,128]{1,0:T(8,128)S(1)}, u32[]{:S(2)}, u32[]{:S(2)}) collective-permute-start(f32[16,128]{1,0:T(8,128)S(1)} %shard_map.64.refs_2_), channel_id=1, source_target_pairs={{4,0},{5,1},{6,2},{7,3},{0,4},{1,5},{2,6},{3,7},{12,8},{13,9},{14,... | collective-permute-start | bytes 24584 | tf_op jit(solution)/shard_map/ppermute | solution.py:466
  37.0 3.7 %collective-permute-start.13 = (f32[16,128]{1,0:T(8,128)S(1)}, f32[16,128]{1,0:T(8,128)S(1)}, u32[]{:S(2)}, u32[]{:S(2)}) collective-permute-start(f32[16,128]{1,0:T(8,128)S(1)} %shard_map.64.refs_2_), channel_id=1, source_target_pairs={{2,0},{3,1},{0,2},{1,3},{6,4},{7,5},{4,6},{5,7},{10,8},{11,9},{8,1... | collective-permute-start | bytes 24584 | tf_op jit(solution)/shard_map/ppermute | solution.py:466

commit v8 on v7

--- a/solution.py
+++ b/solution.py
@@ -157,7 +157,7 @@
 
 
 def smooth_kernel(hops, count_gz, *refs):
-    blocks = 1 + 3 * hops
+    blocks = 4 * hops
     weights_ref = refs[0]
     pack_refs = refs[1 : 1 + blocks]
     disp_hbm, own_ref = refs[1 + blocks : 3 + blocks]
@@ -174,18 +174,24 @@
 
     def packed(layer, group, kind):
         hop = layer // layers
-        plane = pack_plane(cases, layers, cases if group is None else group, kind, layer - hop * layers)
+        inner = layer - hop * layers
+        plane = pack_plane(cases, layers, cases if group is None else group, kind, inner)
         if hop == 0:
             return [pack_refs[0][plane, chunk] for chunk in chunks]
-        beside_ref, design_ref, force_ref = pack_refs[3 * abs(hop) - 2 : 3 * abs(hop) + 1]
-        if group is not None:
-            across = [force_ref[group, kind, layer - hop * layers, chunk] for chunk in chunks]
+
+        def pick(design_ref, force_ref):
+            if group is None:
+                return [design_ref[kind * layers + inner, chunk] for chunk in chunks]
+            return [force_ref[group, kind, inner, chunk] for chunk in chunks]
+
+        at = 4 * abs(hop) - 2
+        across = pick(*pack_refs[at : at + 2])
+        if abs(hop) == 1:
+            beside = [pack_refs[1][plane, chunk] for chunk in chunks]
         else:
-            across = [design_ref[kind * layers + layer - hop * layers, chunk] for chunk in chunks]
+            beside = pick(*pack_refs[at - 2 : at])
         by_sibling = even == (hop > 0)
-        return [
-            jnp.where(by_sibling, beside_ref[plane, chunk], a) for chunk, a in zip(chunks, across)
-        ]
+        return [jnp.where(by_sibling, one, other) for one, other in zip(beside, across)]
 
     def inside(layer):
         owner = gz + layer // layers
@@ -379,16 +385,6 @@
     design_ref[...] = pack_ref[cases * 3 * layers :]
 
 
-def join_kernel(force_ref, design_ref, *refs):
-    pack_ref = refs[-1]
-    cases, _, layers, _, _ = force_ref.shape
-    for case in range(cases):
-        for comp in range(3):
-            for layer in range(layers):
-                pack_ref[pack_plane(cases, layers, case, comp, layer)] = force_ref[case, comp, layer]
-    pack_ref[cases * 3 * layers :] = design_ref[...]
-
-
 def sum_kernel(*refs):
     total = refs[0][...]
     for ref in refs[1:-1]:
@@ -466,12 +462,12 @@
     return lax.ppermute(block, axis, [(partner(i, step), i) for i in range(count)])
 
 
-def across_pairs(far, count):
-    up = [(i - far, i) for i in range(0, count, 2) if i - far >= 0]
-    down = [(i + far, i) for i in range(1, count, 2) if i + far < count]
-    free = [i for i in range(count) if i not in dict(up + down)]
-    empty = [i for i in range(count) if i not in dict(up + down).values()]
-    return up + down + list(zip(free, empty))
+def far_pairs(far, count, across):
+    pairs = [(i - far if (i % 2 == 0) == across else i + far, i) for i in range(count)]
+    pairs = [(source, i) for source, i in pairs if 0 <= source < count]
+    free = [i for i in range(count) if i not in dict(pairs)]
+    empty = [i for i in range(count) if i not in dict(pairs).values()]
+    return pairs + list(zip(free, empty))
 
 
 def on_device(density, labels, forces, case_weights):
@@ -505,7 +501,7 @@
 
     planes = (cases * 3 + 2) * layers
     far_forces = [
-        lax.ppermute(forces, "gz", across_pairs(far, count_gz)) for far in range(1, hops + 1)
+        lax.ppermute(forces, "gz", far_pairs(far, count_gz, True)) for far in range(1, hops + 1)
     ]
     pack = call(stage_kernel, shape(planes, rows, columns), (labels, forces), 2 * planes, 1_000_000)
     steps = [0] + list(range(2, count_load)) + [1]
@@ -520,22 +516,12 @@
         out_specs=(vmem, vmem),
         input_output_aliases={0: 0},
     )
-    far_designs = [
-        lax.ppermute(design, "gz", across_pairs(far, count_gz)) for far in range(1, hops + 1)
-    ]
-    beside, packs = pack, [pack]
-    for at in range(hops):
-        packs += [met(beside, "gz", 1), far_designs[at], far_forces[at]]
-        if at < hops - 1:
-            later = far_designs[at + 1 :]
-            beside = call(
-                join_kernel,
-                shape(planes, rows, columns),
-                (far_forces[at], far_designs[at], *later),
-                2 * planes,
-                100_000,
-                in_specs=[vmem] * 2 + [pl.BlockSpec(memory_space=pl.ANY)] * len(later),
-            )
+    packs = [pack, met(pack, "gz", 1)]
+    for far, forces_far in enumerate(far_forces, 1):
+        if far > 1:
+            packs.append(lax.ppermute(design, "gz", far_pairs(far, count_gz, False)))
+            packs.append(met(far_forces[far - 2], "gz", 1))
+        packs += [lax.ppermute(design, "gz", far_pairs(far, count_gz, True)), forces_far]
 
     slot_rows = -(-(layers * wide + 1) // 8) * 8
     scratch = [

time: 41.7 us -> 41.5 us (level)
  starting transfers between devices: 23.6 us -> 19.8 us
  waiting for transfers between devices: 8.86 us -> 12.5 us
    ppermute x12, starting transfers between devices: 16.4 us -> 12.5 us  [met(): lax.ppermute(block, axis, [(partner(i, step), i) for i in range(count)])]
    ppermute x4 -> x5, waiting for transfers between devices: 0.01 us -> 3.61 us  [the longest x1 2.36 us: on_device(): packs.append(lax.ppermute(design, 'gz', far_pairs(far, count_gz, False)))]
    ppermute x4 -> x5, starting transfers between devices: 7.27 us -> 7.25 us  [the longest x2 4.61 us: on_device(): lax.ppermute(forces, 'gz', far_pairs(far, count_gz, True))]
    pallas_call x7 -> x6, Pallas kernels: 6.53 us -> 6.52 us  [call(): pl.pallas_call(kernel, out_shape=out, in_specs=in_specs or [vmem] * len(a...]
  transfers between devices with their start and end apart: 16 -> 17, of which waited for: 10 -> 11; matrix products, arithmetic and copies ran while one was open for 0% -> 0% of each run, Pallas kernels for 0% -> 0%
where the time goes in v8:
time: 41.5 us; the launch traced here: 41.2 us
  starting transfers between devices  19.8 us (48%)
  waiting for transfers between devices  12.5 us (30%)
  Pallas kernels  6.52 us (16%)
  local copies, waits for them, and re-layouts  1.69 us (4%)
  between operations  0.7 us (2%)
    ppermute x12, starting transfers between devices, met(): lax.ppermute(block, axis, [(partner(i, step), i) for i in range(count)])  12.5 us
    ppermute x12, waiting for transfers between devices, met(): lax.ppermute(block, axis, [(partner(i, step), i) for i in range(count)])  8.9 us
    pallas_call x6, Pallas kernels, call(): pl.pallas_call(kernel, out_shape=out, in_specs=in_specs or [vmem] * len(a...  6.52 us
    ppermute x2, starting transfers between devices, on_device(): lax.ppermute(forces, 'gz', far_pairs(far, count_gz, True))  4.61 us
    ppermute x2, starting transfers between devices, on_device(): lax.ppermute(design, 'gz', far_pairs(far, count_gz, True))  2.64 us
    ppermute x1, waiting for transfers between devices, on_device(): packs.append(lax.ppermute(design, 'gz', far_pairs(far, count_gz, False)))  2.36 us
    unnamed x8, local copies, waits for them, and re-layouts  1.69 us
    ppermute x2, waiting for transfers between devices, on_device(): lax.ppermute(design, 'gz', far_pairs(far, count_gz, True))  1.24 us
  transfers between devices with their start and end apart: 17, of which 11 were waited for; matrix products, arithmetic and copies ran while one was open for 0% of the time, Pallas kernels for 0%

profile of v8, /device:TPU:0, one launch (start us, length us, event | category | flops | bytes accessed | tf_op | source)
XLA Modules:
  0.0 41.2 jit_solution(12387701743118847105)
XLA Ops:
  0.6 3.0 %collective-permute-start.4 = (f32[2,3,2,32,128]{4,3,2,1,0:T(8,128)}, f32[2,3,2,32,128]{4,3,2,1,0:T(8,128)S(1)}, u32[]{:S(2)}, u32[]{:S(2)}) collective-permute-start(f32[2,3,2,32,128]{4,3,2,1,0:T(8,128)} %forces_ref.1), channel_id=1, source_target_pairs={{3,1},{0,2},{5,3},{2,4},{7,5},{4,6},{1,0},{6,7},{11,9},{8,10},{13,... | collective-permute-start | bytes 589832 | tf_op jit(solution)/shard_map/ppermute | solution.py:504
  3.7 1.6 %collective-permute-start.3 = (f32[2,3,2,32,128]{4,3,2,1,0:T(8,128)}, f32[2,3,2,32,128]{4,3,2,1,0:T(8,128)S(1)}, u32[]{:S(2)}, u32[]{:S(2)}) collective-permute-start(f32[2,3,2,32,128]{4,3,2,1,0:T(8,128)} %forces_ref.1), channel_id=1, source_target_pairs={{2,1},{1,2},{4,3},{3,4},{6,5},{5,6},{0,0},{7,7},{10,9},{9,10},{12,... | collective-permute-start | bytes 589832 | tf_op jit(solution)/shard_map/ppermute | solution.py:504
  5.2 2.4 %collective-permute-start.1 = (f32[2,8,128]{2,1,0:T(8,128)}, f32[2,8,128]{2,1,0:T(8,128)S(1)}, u32[]{:S(2)}, u32[]{:S(2)}) collective-permute-start(f32[2,8,128]{2,1,0:T(8,128)} %refs_1_.1), channel_id=1, source_target_pairs={{24,0},{16,8},{8,16},{0,24},{25,1},{17,9},{9,17},{1,25},{26,2},{18... | collective-permute-start | bytes 24584 | tf_op jit(solution)/shard_map/ppermute | solution.py:462
  7.7 0.5 %collective-permute-start = (f32[2,8,128]{2,1,0:T(8,128)}, f32[2,8,128]{2,1,0:T(8,128)S(1)}, u32[]{:S(2)}, u32[]{:S(2)}) collective-permute-start(f32[2,8,128]{2,1,0:T(8,128)} %refs_1_.1), channel_id=1, source_target_pairs={{16,0},{24,8},{0,16},{8,24},{17,1},{25,9},{1,17},{9,25},{18,2},{26... | collective-permute-start | bytes 24584 | tf_op jit(solution)/shard_map/ppermute | solution.py:462
  8.2 0.5 %collective-permute-start.2 = (f32[2,8,128]{2,1,0:T(8,128)}, f32[2,8,128]{2,1,0:T(8,128)S(1)}, u32[]{:S(2)}, u32[]{:S(2)}) collective-permute-start(f32[2,8,128]{2,1,0:T(8,128)} %refs_1_.1), channel_id=1, source_target_pairs={{8,0},{0,8},{24,16},{16,24},{9,1},{1,9},{25,17},{17,25},{10,2},{2,... | collective-permute-start | bytes 24584 | tf_op jit(solution)/shard_map/ppermute | solution.py:462
  8.7 0.0 copy-start
  8.7 0.9 %copy-done = f32[2,3,2,32,128]{4,3,2,1,0:T(8,128)S(1)} copy-done((f32[2,3,2,32,128]{4,3,2,1,0:T(8,128)S(1)}, f32[2,3,2,32,128]{4,3,2,1,0:T(8,128)}, u32[]{:S(2)}) %copy-start) | copy-done | bytes 196632
  9.7 0.0 copy-start.1
  9.7 0.8 %copy-done.1 = s32[2,32,128]{2,1,0:T(8,128)S(1)} copy-done((s32[2,32,128]{2,1,0:T(8,128)S(1)}, s32[2,32,128]{2,1,0:T(8,128)}, u32[]{:S(2)}) %copy-start.1) | copy-done | bytes 32792
  10.4 0.0 copy-start.2
  10.4 0.0 collective-permute-done.1.refs_3_
  10.5 1.1 %collective-permute-done.refs_2_ = f32[2,8,128]{2,1,0:T(8,128)S(1)} collective-permute-done((f32[2,8,128]{2,1,0:T(8,128)}, f32[2,8,128]{2,1,0:T(8,128)S(1)}, u32[]{:S(2)}, u32[]{:S(2)}) %collective-permute-start) | collective-permute-done | bytes 8224 | tf_op jit(solution)/shard_map/ppermute | solution.py:462
  11.6 0.5 %collective-permute-done.2.refs_4_ = f32[2,8,128]{2,1,0:T(8,128)S(1)} collective-permute-done((f32[2,8,128]{2,1,0:T(8,128)}, f32[2,8,128]{2,1,0:T(8,128)S(1)}, u32[]{:S(2)}, u32[]{:S(2)}) %collective-permute-start.2) | collective-permute-done | bytes 8224 | tf_op jit(solution)/shard_map/ppermute | solution.py:462
  12.1 0.0 collective-permute-done.4.refs_6_.refs_8_
  12.1 0.0 collective-permute-done.3.refs_5_.refs_4_
  12.1 0.0 copy-done.2
  12.1 0.0 copy-start.3
  12.1 0.4 %collective-permute-start.5 = (f32[16,32,128]{2,1,0:T(8,128)S(1)}, f32[16,32,128]{2,1,0:T(8,128)S(1)}, u32[]{:S(2)}, u32[]{:S(2)}) collective-permute-start(f32[16,32,128]{2,1,0:T(8,128)S(1)} %get-tuple-element.10.refs_1_), channel_id=1, source_target_pairs={{1,0},{0,1},{3,2},{2,3},{5,4},{4,5},{7,6},{6,7},{9,8},{8,9},{11,10... | collective-permute-start | bytes 786440 | tf_op jit(solution)/shard_map/ppermute | solution.py:462
  12.6 0.1 collective-permute-start.8
  12.7 2.0 %collective-permute-start.9 = (f32[4,32,128]{2,1,0:T(8,128)S(1)}, f32[4,32,128]{2,1,0:T(8,128)S(1)}, u32[]{:S(2)}, u32[]{:S(2)}) collective-permute-start(f32[4,32,128]{2,1,0:T(8,128)S(1)} %get-tuple-element.11), channel_id=1, source_target_pairs={{3,1},{0,2},{5,3},{2,4},{7,5},{4,6},{1,0},{6,7},{11,9},{8,10},{13,... | collective-permute-start | bytes 196616 | tf_op jit(solution)/shard_map/ppermute | solution.py:524
  14.7 0.0 collective-permute-start.7
  14.7 0.7 %collective-permute-start.6 = (f32[4,32,128]{2,1,0:T(8,128)S(1)}, f32[4,32,128]{2,1,0:T(8,128)S(1)}, u32[]{:S(2)}, u32[]{:S(2)}) collective-permute-start(f32[4,32,128]{2,1,0:T(8,128)S(1)} %get-tuple-element.11), channel_id=1, source_target_pairs={{2,1},{1,2},{4,3},{3,4},{6,5},{5,6},{0,0},{7,7},{10,9},{9,10},{12,... | collective-permute-start | bytes 196616 | tf_op jit(solution)/shard_map/ppermute | solution.py:524
  15.3 1.2 %collective-permute-done.9.refs_7_ = f32[4,32,128]{2,1,0:T(8,128)S(1)} collective-permute-done((f32[4,32,128]{2,1,0:T(8,128)S(1)}, f32[4,32,128]{2,1,0:T(8,128)S(1)}, u32[]{:S(2)}, u32[]{:S(2)}) %collective-permute-start.9) | collective-permute-done | bytes 65568 | tf_op jit(solution)/shard_map/ppermute | solution.py:524
  16.6 2.4 %collective-permute-done.7.refs_5_ = f32[4,32,128]{2,1,0:T(8,128)S(1)} collective-permute-done((f32[4,32,128]{2,1,0:T(8,128)S(1)}, f32[4,32,128]{2,1,0:T(8,128)S(1)}, u32[]{:S(2)}, u32[]{:S(2)}) %collective-permute-start.7) | collective-permute-done | bytes 65568 | tf_op jit(solution)/shard_map/ppermute | solution.py:522
  18.9 0.0 collective-permute-done.6.refs_3_
  18.9 0.0 collective-permute-done.8.refs_6_
  18.9 0.0 collective-permute-done.5.refs_2_
  19.0 0.0 copy-done.3
  19.0 5.7 %shard_map.61 = (f32[2,3,2,32,128]{4,3,2,1,0:T(8,128)}, f32[3,2,8,128]{3,2,1,0:T(8,128)S(1)}, f32[24,128]{1,0:T(8,128)S(1)}, f32[24,128]{1,0:T(8,128)S(1)}, f32[...) custom-call(s32[8]{0:T(128)S(1)} %copy-done.3, f32[16,32,128]{2,1,0:T(8,128)S(1)} %get-tuple-element.10.refs_1_, ...), custom_call_target="tpu_custom_call" | custom-call | flops 60000000 | bytes 6000000 | tf_op jit(solution)/shard_map/pallas_call | solution.py:491
  24.7 1.9 %collective-permute-start.10 = (f32[24,128]{1,0:T(8,128)S(1)}, f32[24,128]{1,0:T(8,128)S(1)}, u32[]{:S(2)}, u32[]{:S(2)}) collective-permute-start(f32[24,128]{1,0:T(8,128)S(1)} %get-tuple-element.13), channel_id=1, source_target_pairs={{24,0},{16,8},{8,16},{0,24},{25,1},{17,9},{9,17},{1,25},{26,2},{18... | collective-permute-start | bytes 36872 | tf_op jit(solution)/shard_map/ppermute | solution.py:462
  26.6 0.5 %collective-permute-start.11 = (f32[24,128]{1,0:T(8,128)S(1)}, f32[24,128]{1,0:T(8,128)S(1)}, u32[]{:S(2)}, u32[]{:S(2)}) collective-permute-start(f32[24,128]{1,0:T(8,128)S(1)} %get-tuple-element.14), channel_id=1, source_target_pairs={{16,0},{24,8},{0,16},{8,24},{17,1},{25,9},{1,17},{9,25},{18,2},{26... | collective-permute-start | bytes 36872 | tf_op jit(solution)/shard_map/ppermute | solution.py:462
  27.1 1.1 %collective-permute-start.12 = (f32[24,128]{1,0:T(8,128)S(1)}, f32[24,128]{1,0:T(8,128)S(1)}, u32[]{:S(2)}, u32[]{:S(2)}) collective-permute-start(f32[24,128]{1,0:T(8,128)S(1)} %get-tuple-element.15), channel_id=1, source_target_pairs={{8,0},{0,8},{24,16},{16,24},{9,1},{1,9},{25,17},{17,25},{10,2},{2,... | collective-permute-start | bytes 36872 | tf_op jit(solution)/shard_map/ppermute | solution.py:462
  28.2 1.1 %collective-permute-done.10.refs_1_ = f32[24,128]{1,0:T(8,128)S(1)} collective-permute-done((f32[24,128]{1,0:T(8,128)S(1)}, f32[24,128]{1,0:T(8,128)S(1)}, u32[]{:S(2)}, u32[]{:S(2)}) %collective-permute-start.10) | collective-permute-done | bytes 12320 | tf_op jit(solution)/shard_map/ppermute | solution.py:462
  29.4 1.0 %collective-permute-done.11.refs_2_ = f32[24,128]{1,0:T(8,128)S(1)} collective-permute-done((f32[24,128]{1,0:T(8,128)S(1)}, f32[24,128]{1,0:T(8,128)S(1)}, u32[]{:S(2)}, u32[]{:S(2)}) %collective-permute-start.11) | collective-permute-done | bytes 12320 | tf_op jit(solution)/shard_map/ppermute | solution.py:462
  30.3 0.5 %collective-permute-done.12.refs_3_ = f32[24,128]{1,0:T(8,128)S(1)} collective-permute-done((f32[24,128]{1,0:T(8,128)S(1)}, f32[24,128]{1,0:T(8,128)S(1)}, u32[]{:S(2)}, u32[]{:S(2)}) %collective-permute-start.12) | collective-permute-done | bytes 12320 | tf_op jit(solution)/shard_map/ppermute | solution.py:462
  30.9 0.1 collective-permute-start.13
  31.0 1.0 %collective-permute-done.13.beside_ref.refs_1_ = f32[24,128]{1,0:T(8,128)S(1)} collective-permute-done((f32[24,128]{1,0:T(8,128)S(1)}, f32[24,128]{1,0:T(8,128)S(1)}, u32[]{:S(2)}, u32[]{:S(2)}) %collective-permute-start.13) | collective-permute-done | bytes 12320 | tf_op jit(solution)/shard_map/ppermute | solution.py:462
  32.0 3.5 %collective-permute-start.16 = (f32[16,128]{1,0:T(8,128)S(1)}, f32[16,128]{1,0:T(8,128)S(1)}, u32[]{:S(2)}, u32[]{:S(2)}) collective-permute-start(f32[16,128]{1,0:T(8,128)S(1)} %shard_map.63.refs_2_), channel_id=1, source_target_pairs={{6,0},{7,1},{4,2},{5,3},{2,4},{3,5},{0,6},{1,7},{14,8},{15,9},{12,... | collective-permute-start | bytes 24584 | tf_op jit(solution)/shard_map/ppermute | solution.py:462
  35.5 1.3 %collective-permute-start.15 = (f32[16,128]{1,0:T(8,128)S(1)}, f32[16,128]{1,0:T(8,128)S(1)}, u32[]{:S(2)}, u32[]{:S(2)}) collective-permute-start(f32[16,128]{1,0:T(8,128)S(1)} %shard_map.63.refs_2_), channel_id=1, source_target_pairs={{4,0},{5,1},{6,2},{7,3},{0,4},{1,5},{2,6},{3,7},{12,8},{13,9},{14,... | collective-permute-start | bytes 24584 | tf_op jit(solution)/shard_map/ppermute | solution.py:462
  36.8 0.0 collective-permute-start.14
  36.8 0.7 %collective-permute-done.16.refs_5_ = f32[16,128]{1,0:T(8,128)S(1)} collective-permute-done((f32[16,128]{1,0:T(8,128)S(1)}, f32[16,128]{1,0:T(8,128)S(1)}, u32[]{:S(2)}, u32[]{:S(2)}) %collective-permute-start.16) | collective-permute-done | bytes 8224 | tf_op jit(solution)/shard_map/ppermute | solution.py:462
  37.5 2.6 %collective-permute-done.15.refs_4_ = f32[16,128]{1,0:T(8,128)S(1)} collective-permute-done((f32[16,128]{1,0:T(8,128)S(1)}, f32[16,128]{1,0:T(8,128)S(1)}, u32[]{:S(2)}, u32[]{:S(2)}) %collective-permute-start.15) | collective-permute-done | bytes 8224 | tf_op jit(solution)/shard_map/ppermute | solution.py:462
  40.1 0.4 collective-permute-done.14.refs_3_
  40.5 0.7 %shard_map.64 = f32[2,8,128]{2,1,0:T(8,128)} custom-call(f32[24,128]{1,0:T(8,128)S(1)} %shard_map.62.sum_ref.refs_0_, f32[24,128]{1,0:T(8,128)S(1)} %collective-permute-done.13.beside_ref.refs_1_, f32[16,128]{1,0:T(8,128)S(1)} %shard_map.63.refs_2_, f32[16,128]{1,0:T(8,128)S(1)} %collective-permute-done.14.refs_3_, ...), custom_call_target="tpu_custom_call" | custom-call | flops 100000 | bytes 10000 | tf_op jit(solution)/shard_map/pallas_call | solution.py:491
  (4 shorter events, 0.1 us)
Async XLA Ops:
  0.6 11.4 %collective-permute-start.4 = (f32[2,3,2,32,128]{4,3,2,1,0:T(8,128)}, f32[2,3,2,32,128]{4,3,2,1,0:T(8,128)S(1)}, u32[]{:S(2)}, u32[]{:S(2)}) collective-permute-start(f32[2,3,2,32,128]{4,3,2,1,0:T(8,128)} %forces_ref.1), channel_id=1, source_target_pairs={{3,1},{0,2},{5,3},{2,4},{7,5},{4,6},{1,0},{6,7},{11,9},{8,10},{13,... | collective-permute-start | bytes 589832 | tf_op jit(solution)/shard_map/ppermute | solution.py:504
  3.7 8.4 %collective-permute-start.3 = (f32[2,3,2,32,128]{4,3,2,1,0:T(8,128)}, f32[2,3,2,32,128]{4,3,2,1,0:T(8,128)S(1)}, u32[]{:S(2)}, u32[]{:S(2)}) collective-permute-start(f32[2,3,2,32,128]{4,3,2,1,0:T(8,128)} %forces_ref.1), channel_id=1, source_target_pairs={{2,1},{1,2},{4,3},{3,4},{6,5},{5,6},{0,0},{7,7},{10,9},{9,10},{12,... | collective-permute-start | bytes 589832 | tf_op jit(solution)/shard_map/ppermute | solution.py:504
  5.2 5.2 %collective-permute-start.1 = (f32[2,8,128]{2,1,0:T(8,128)}, f32[2,8,128]{2,1,0:T(8,128)S(1)}, u32[]{:S(2)}, u32[]{:S(2)}) collective-permute-start(f32[2,8,128]{2,1,0:T(8,128)} %refs_1_.1), channel_id=1, source_target_pairs={{24,0},{16,8},{8,16},{0,24},{25,1},{17,9},{9,17},{1,25},{26,2},{18... | collective-permute-start | bytes 24584 | tf_op jit(solution)/shard_map/ppermute | solution.py:462
  7.7 3.9 %collective-permute-start = (f32[2,8,128]{2,1,0:T(8,128)}, f32[2,8,128]{2,1,0:T(8,128)S(1)}, u32[]{:S(2)}, u32[]{:S(2)}) collective-permute-start(f32[2,8,128]{2,1,0:T(8,128)} %refs_1_.1), channel_id=1, source_target_pairs={{16,0},{24,8},{0,16},{8,24},{17,1},{25,9},{1,17},{9,25},{18,2},{26... | collective-permute-start | bytes 24584 | tf_op jit(solution)/shard_map/ppermute | solution.py:462
  8.2 3.9 %collective-permute-start.2 = (f32[2,8,128]{2,1,0:T(8,128)}, f32[2,8,128]{2,1,0:T(8,128)S(1)}, u32[]{:S(2)}, u32[]{:S(2)}) collective-permute-start(f32[2,8,128]{2,1,0:T(8,128)} %refs_1_.1), channel_id=1, source_target_pairs={{8,0},{0,8},{24,16},{16,24},{9,1},{1,9},{25,17},{17,25},{10,2},{2,... | collective-permute-start | bytes 24584 | tf_op jit(solution)/shard_map/ppermute | solution.py:462
  8.7 0.9 %copy-start = (f32[2,3,2,32,128]{4,3,2,1,0:T(8,128)S(1)}, f32[2,3,2,32,128]{4,3,2,1,0:T(8,128)}, u32[]{:S(2)}) copy-start(f32[2,3,2,32,128]{4,3,2,1,0:T(8,128)} %forces_ref.1) | copy-start | bytes 589828
  9.7 0.8 %copy-start.1 = (s32[2,32,128]{2,1,0:T(8,128)S(1)}, s32[2,32,128]{2,1,0:T(8,128)}, u32[]{:S(2)}) copy-start(s32[2,32,128]{2,1,0:T(8,128)} %labels_ref.1) | copy-start | bytes 98308
  10.4 1.6 %copy-start.2 = (f32[2,8,128]{2,1,0:T(8,128)S(1)}, f32[2,8,128]{2,1,0:T(8,128)}, u32[]{:S(2)}) copy-start(f32[2,8,128]{2,1,0:T(8,128)} %refs_1_.1) | copy-start | bytes 24580
  12.1 6.9 %copy-start.3 = (s32[8]{0:T(128)S(1)}, s32[8]{0:T(128)}, u32[]{:S(2)}) copy-start(s32[8]{0:T(128)} %refs_0_.1) | copy-start | bytes 100
  12.1 6.8 %collective-permute-start.5 = (f32[16,32,128]{2,1,0:T(8,128)S(1)}, f32[16,32,128]{2,1,0:T(8,128)S(1)}, u32[]{:S(2)}, u32[]{:S(2)}) collective-permute-start(f32[16,32,128]{2,1,0:T(8,128)S(1)} %get-tuple-element.10.refs_1_), channel_id=1, source_target_pairs={{1,0},{0,1},{3,2},{2,3},{5,4},{4,5},{7,6},{6,7},{9,8},{8,9},{11,10... | collective-permute-start | bytes 786440 | tf_op jit(solution)/shard_map/ppermute | solution.py:462
  12.6 6.4 %collective-permute-start.8 = (f32[2,3,2,32,128]{4,3,2,1,0:T(8,128)S(1)}, f32[2,3,2,32,128]{4,3,2,1,0:T(8,128)S(1)}, u32[]{:S(2)}, u32[]{:S(2)}) collective-permute-start(f32[2,3,2,32,128]{4,3,2,1,0:T(8,128)S(1)} %collective-permute-done.3.refs_5_.refs_4_), channel_id=1, source_target_pairs={{1,0},{0,1},{3,2},{2,3},{5,4},{4,5},{7,6},{6,7},{9,8},{8,9},{11,10... | collective-permute-start | bytes 589832 | tf_op jit(solution)/shard_map/ppermute | solution.py:462
  12.7 3.9 %collective-permute-start.9 = (f32[4,32,128]{2,1,0:T(8,128)S(1)}, f32[4,32,128]{2,1,0:T(8,128)S(1)}, u32[]{:S(2)}, u32[]{:S(2)}) collective-permute-start(f32[4,32,128]{2,1,0:T(8,128)S(1)} %get-tuple-element.11), channel_id=1, source_target_pairs={{3,1},{0,2},{5,3},{2,4},{7,5},{4,6},{1,0},{6,7},{11,9},{8,10},{13,... | collective-permute-start | bytes 196616 | tf_op jit(solution)/shard_map/ppermute | solution.py:524
  14.7 4.3 %collective-permute-start.7 = (f32[4,32,128]{2,1,0:T(8,128)S(1)}, f32[4,32,128]{2,1,0:T(8,128)S(1)}, u32[]{:S(2)}, u32[]{:S(2)}) collective-permute-start(f32[4,32,128]{2,1,0:T(8,128)S(1)} %get-tuple-element.11), channel_id=1, source_target_pairs={{2,0},{4,2},{1,3},{6,4},{3,5},{5,7},{0,1},{7,6},{10,8},{12,10},{9,... | collective-permute-start | bytes 196616 | tf_op jit(solution)/shard_map/ppermute | solution.py:522
  14.7 4.3 %collective-permute-start.6 = (f32[4,32,128]{2,1,0:T(8,128)S(1)}, f32[4,32,128]{2,1,0:T(8,128)S(1)}, u32[]{:S(2)}, u32[]{:S(2)}) collective-permute-start(f32[4,32,128]{2,1,0:T(8,128)S(1)} %get-tuple-element.11), channel_id=1, source_target_pairs={{2,1},{1,2},{4,3},{3,4},{6,5},{5,6},{0,0},{7,7},{10,9},{9,10},{12,... | collective-permute-start | bytes 196616 | tf_op jit(solution)/shard_map/ppermute | solution.py:524
  24.7 4.7 %collective-permute-start.10 = (f32[24,128]{1,0:T(8,128)S(1)}, f32[24,128]{1,0:T(8,128)S(1)}, u32[]{:S(2)}, u32[]{:S(2)}) collective-permute-start(f32[24,128]{1,0:T(8,128)S(1)} %get-tuple-element.13), channel_id=1, source_target_pairs={{24,0},{16,8},{8,16},{0,24},{25,1},{17,9},{9,17},{1,25},{26,2},{18... | collective-permute-start | bytes 36872 | tf_op jit(solution)/shard_map/ppermute | solution.py:462
  26.6 3.7 %collective-permute-start.11 = (f32[24,128]{1,0:T(8,128)S(1)}, f32[24,128]{1,0:T(8,128)S(1)}, u32[]{:S(2)}, u32[]{:S(2)}) collective-permute-start(f32[24,128]{1,0:T(8,128)S(1)} %get-tuple-element.14), channel_id=1, source_target_pairs={{16,0},{24,8},{0,16},{8,24},{17,1},{25,9},{1,17},{9,25},{18,2},{26... | collective-permute-start | bytes 36872 | tf_op jit(solution)/shard_map/ppermute | solution.py:462
  27.1 3.7 %collective-permute-start.12 = (f32[24,128]{1,0:T(8,128)S(1)}, f32[24,128]{1,0:T(8,128)S(1)}, u32[]{:S(2)}, u32[]{:S(2)}) collective-permute-start(f32[24,128]{1,0:T(8,128)S(1)} %get-tuple-element.15), channel_id=1, source_target_pairs={{8,0},{0,8},{24,16},{16,24},{9,1},{1,9},{25,17},{17,25},{10,2},{2,... | collective-permute-start | bytes 36872 | tf_op jit(solution)/shard_map/ppermute | solution.py:462
  30.9 1.2 %collective-permute-start.13 = (f32[24,128]{1,0:T(8,128)S(1)}, f32[24,128]{1,0:T(8,128)S(1)}, u32[]{:S(2)}, u32[]{:S(2)}) collective-permute-start(f32[24,128]{1,0:T(8,128)S(1)} %shard_map.62.sum_ref.refs_0_), channel_id=1, source_target_pairs={{1,0},{0,1},{3,2},{2,3},{5,4},{4,5},{7,6},{6,7},{9,8},{8,9},{11,10... | collective-permute-start | bytes 36872 | tf_op jit(solution)/shard_map/ppermute | solution.py:462
  32.0 5.4 %collective-permute-start.16 = (f32[16,128]{1,0:T(8,128)S(1)}, f32[16,128]{1,0:T(8,128)S(1)}, u32[]{:S(2)}, u32[]{:S(2)}) collective-permute-start(f32[16,128]{1,0:T(8,128)S(1)} %shard_map.63.refs_2_), channel_id=1, source_target_pairs={{6,0},{7,1},{4,2},{5,3},{2,4},{3,5},{0,6},{1,7},{14,8},{15,9},{12,... | collective-permute-start | bytes 24584 | tf_op jit(solution)/shard_map/ppermute | solution.py:462
  35.5 4.5 %collective-permute-start.15 = (f32[16,128]{1,0:T(8,128)S(1)}, f32[16,128]{1,0:T(8,128)S(1)}, u32[]{:S(2)}, u32[]{:S(2)}) collective-permute-start(f32[16,128]{1,0:T(8,128)S(1)} %shard_map.63.refs_2_), channel_id=1, source_target_pairs={{4,0},{5,1},{6,2},{7,3},{0,4},{1,5},{2,6},{3,7},{12,8},{13,9},{14,... | collective-permute-start | bytes 24584 | tf_op jit(solution)/shard_map/ppermute | solution.py:462
  36.8 3.7 %collective-permute-start.14 = (f32[16,128]{1,0:T(8,128)S(1)}, f32[16,128]{1,0:T(8,128)S(1)}, u32[]{:S(2)}, u32[]{:S(2)}) collective-permute-start(f32[16,128]{1,0:T(8,128)S(1)} %shard_map.63.refs_2_), channel_id=1, source_target_pairs={{2,0},{3,1},{0,2},{1,3},{6,4},{7,5},{4,6},{5,7},{10,8},{11,9},{8,1... | collective-permute-start | bytes 24584 | tf_op jit(solution)/shard_map/ppermute | solution.py:462

commit v9 on v8

--- a/solution.py
+++ b/solution.py
@@ -88,30 +88,45 @@
 TWIST = ((0, "sdd"), (1, "dsd"), (2, "dds"))
 
 
-def mode_forces(modes, e1, e2, e3, e4):
-    m = lambda key: modes[key[0]][key[1]]
-    out = [{}, {}, {}]
-
-    def put(key, value):
-        out[key[0]][key[1]] = value
-
-    trace = (LAME / (2 * SHEAR)) * (m(NORMAL[0]) + m(NORMAL[1]) + m(NORMAL[2]))
-    for key in NORMAL:
-        put(key, e4 * (trace + m(key)))
-    for a, b in BENDS:
-        t = (LAME / (3 * SHEAR)) * (m(a) + m(b))
-        put(a, e1 * (t + m(a)))
-        put(b, e1 * (t + m(b)))
-    for a, b in SHEARS:
-        f = e1 * (m(a) + m(b))
-        put(a, f)
-        put(b, f)
-    t = m(TWIST[0]) + m(TWIST[1]) + m(TWIST[2])
-    for key in TWIST:
-        put(key, e2 * (t + m(key)))
-    for comp in range(3):
-        put((comp, "ddd"), e3 * modes[comp]["ddd"])
-    return out
+def mode_forces(mode, e1, e2, e3, e4, give):
+    def normal():
+        m = [mode(*key) for key in NORMAL]
+        trace = (LAME / (2 * SHEAR)) * (m[0] + m[1] + m[2])
+        for key, a in zip(NORMAL, m):
+            give(*key, e4 * (trace + a))
+
+    def bend(at):
+        m = [mode(*key) for key in BENDS[at]]
+        t = (LAME / (3 * SHEAR)) * (m[0] + m[1])
+        for key, a in zip(BENDS[at], m):
+            give(*key, e1 * (t + a))
+
+    def shear(at):
+        m = [mode(*key) for key in SHEARS[at]]
+        f = e1 * (m[0] + m[1])
+        for key in SHEARS[at]:
+            give(*key, f)
+
+    def twist():
+        m = [mode(*key) for key in TWIST]
+        t = m[0] + m[1] + m[2]
+        for key, a in zip(TWIST, m):
+            give(*key, e2 * (t + a))
+
+    def bulk(comp):
+        give(comp, "ddd", e3 * mode(comp, "ddd"))
+
+    shear(0)
+    twist()
+    normal()
+    bend(2)
+    bend(0)
+    bulk(1)
+    shear(1)
+    bend(1)
+    bulk(0)
+    shear(2)
+    bulk(2)
 
 
 def mode_energy(modes):
@@ -260,27 +275,31 @@
                     for comp in range(3):
                         store_modes(node, comp, [step_ref[comp, node, chunk] for chunk in chunks])
             for chunk in chunks:
-                low = load_modes(first, chunk)
-                up = None
+                up = {}
                 for element in range(first, end):
-                    high = load_modes(element + 1, chunk)
+                    carried, up = up, {}
+                    forces = {}
+
+                    def mode(comp, name):
+                        at = comp * 4 + PLANE.index(name[:2])
+                        low, high = mode_ref[element, at, chunk], mode_ref[element + 1, at, chunk]
+                        return high + low if name[2] == "s" else high - low
+
+                    def give(comp, name, force):
+                        pq, at = name[:2], comp * 4 + PLANE.index(name[:2])
+                        forces[comp, name] = force
+                        diff, both = forces.get((comp, pq + "d")), forces.get((comp, pq + "s"))
+                        if pq == "ss":
+                            up[at] = diff
+                            if carried:
+                                node_ref[element, at, chunk] = carried[at] - diff
+                        elif diff is not None and both is not None:
+                            up[at] = both + diff
+                            if carried:
+                                node_ref[element, at, chunk] = carried[at] + (both - diff)
+
                     stiff = [stiff_ref[kind, element, chunk] for kind in range(4)]
-                    f = mode_forces(modes_z(low, high), *stiff)
-                    ups = []
-                    for comp in range(3):
-                        for i, pq in enumerate(PLANE):
-                            diff = f[comp][pq + "d"]
-                            at = comp * 4 + i
-                            if pq == "ss":
-                                ups.append(diff)
-                                if up:
-                                    node_ref[element, at, chunk] = up[at] - diff
-                            else:
-                                both = f[comp][pq + "s"]
-                                ups.append(both + diff)
-                                if up:
-                                    node_ref[element, at, chunk] = up[at] + (both - diff)
-                    low, up = high, ups
+                    mode_forces(mode, *stiff, give)
             for node in range(first + 1, end):
                 for comp in range(3):
                     g = [[node_ref[node, comp * 4 + i, chunk] for chunk in chunks] for i in range(4)]

time: 41.5 us -> 41.5 us (level)
  no operation moved by 1% of the time
where the time goes in v9:
time: 41.5 us; the launch traced here: 41.2 us
  starting transfers between devices  19.8 us (48%)
  waiting for transfers between devices  12.5 us (30%)
  Pallas kernels  6.54 us (16%)
  local copies, waits for them, and re-layouts  1.69 us (4%)
  between operations  0.7 us (2%)
    ppermute x12, starting transfers between devices, met(): lax.ppermute(block, axis, [(partner(i, step), i) for i in range(count)])  12.5 us
    ppermute x12, waiting for transfers between devices, met(): lax.ppermute(block, axis, [(partner(i, step), i) for i in range(count)])  8.9 us
    pallas_call x6, Pallas kernels, call(): pl.pallas_call(kernel, out_shape=out, in_specs=in_specs or [vmem] * len(a...  6.54 us
    ppermute x2, starting transfers between devices, on_device(): lax.ppermute(forces, 'gz', far_pairs(far, count_gz, True))  4.61 us
    ppermute x2, starting transfers between devices, on_device(): lax.ppermute(design, 'gz', far_pairs(far, count_gz, True))  2.64 us
    ppermute x1, waiting for transfers between devices, on_device(): packs.append(lax.ppermute(design, 'gz', far_pairs(far, count_gz, False)))  2.36 us
    unnamed x8, local copies, waits for them, and re-layouts  1.69 us
    ppermute x2, waiting for transfers between devices, on_device(): lax.ppermute(design, 'gz', far_pairs(far, count_gz, True))  1.24 us
  transfers between devices with their start and end apart: 17, of which 11 were waited for; matrix products, arithmetic and copies ran while one was open for 0% of the time, Pallas kernels for 0%

profile of v9, /device:TPU:0, one launch (start us, length us, event | category | flops | bytes accessed | tf_op | source)
XLA Modules:
  0.0 41.2 jit_solution(17804700608551544163)
XLA Ops:
  0.6 3.0 %collective-permute-start.4 = (f32[2,3,2,32,128]{4,3,2,1,0:T(8,128)}, f32[2,3,2,32,128]{4,3,2,1,0:T(8,128)S(1)}, u32[]{:S(2)}, u32[]{:S(2)}) collective-permute-start(f32[2,3,2,32,128]{4,3,2,1,0:T(8,128)} %forces_ref.1), channel_id=1, source_target_pairs={{3,1},{0,2},{5,3},{2,4},{7,5},{4,6},{1,0},{6,7},{11,9},{8,10},{13,... | collective-permute-start | bytes 589832 | tf_op jit(solution)/shard_map/ppermute | solution.py:523
  3.7 1.6 %collective-permute-start.3 = (f32[2,3,2,32,128]{4,3,2,1,0:T(8,128)}, f32[2,3,2,32,128]{4,3,2,1,0:T(8,128)S(1)}, u32[]{:S(2)}, u32[]{:S(2)}) collective-permute-start(f32[2,3,2,32,128]{4,3,2,1,0:T(8,128)} %forces_ref.1), channel_id=1, source_target_pairs={{2,1},{1,2},{4,3},{3,4},{6,5},{5,6},{0,0},{7,7},{10,9},{9,10},{12,... | collective-permute-start | bytes 589832 | tf_op jit(solution)/shard_map/ppermute | solution.py:523
  5.2 2.4 %collective-permute-start.1 = (f32[2,8,128]{2,1,0:T(8,128)}, f32[2,8,128]{2,1,0:T(8,128)S(1)}, u32[]{:S(2)}, u32[]{:S(2)}) collective-permute-start(f32[2,8,128]{2,1,0:T(8,128)} %refs_1_.1), channel_id=1, source_target_pairs={{24,0},{16,8},{8,16},{0,24},{25,1},{17,9},{9,17},{1,25},{26,2},{18... | collective-permute-start | bytes 24584 | tf_op jit(solution)/shard_map/ppermute | solution.py:481
  7.7 0.5 %collective-permute-start = (f32[2,8,128]{2,1,0:T(8,128)}, f32[2,8,128]{2,1,0:T(8,128)S(1)}, u32[]{:S(2)}, u32[]{:S(2)}) collective-permute-start(f32[2,8,128]{2,1,0:T(8,128)} %refs_1_.1), channel_id=1, source_target_pairs={{16,0},{24,8},{0,16},{8,24},{17,1},{25,9},{1,17},{9,25},{18,2},{26... | collective-permute-start | bytes 24584 | tf_op jit(solution)/shard_map/ppermute | solution.py:481
  8.2 0.5 %collective-permute-start.2 = (f32[2,8,128]{2,1,0:T(8,128)}, f32[2,8,128]{2,1,0:T(8,128)S(1)}, u32[]{:S(2)}, u32[]{:S(2)}) collective-permute-start(f32[2,8,128]{2,1,0:T(8,128)} %refs_1_.1), channel_id=1, source_target_pairs={{8,0},{0,8},{24,16},{16,24},{9,1},{1,9},{25,17},{17,25},{10,2},{2,... | collective-permute-start | bytes 24584 | tf_op jit(solution)/shard_map/ppermute | solution.py:481
  8.7 0.0 copy-start
  8.7 0.9 %copy-done = f32[2,3,2,32,128]{4,3,2,1,0:T(8,128)S(1)} copy-done((f32[2,3,2,32,128]{4,3,2,1,0:T(8,128)S(1)}, f32[2,3,2,32,128]{4,3,2,1,0:T(8,128)}, u32[]{:S(2)}) %copy-start) | copy-done | bytes 196632
  9.7 0.0 copy-start.1
  9.7 0.8 %copy-done.1 = s32[2,32,128]{2,1,0:T(8,128)S(1)} copy-done((s32[2,32,128]{2,1,0:T(8,128)S(1)}, s32[2,32,128]{2,1,0:T(8,128)}, u32[]{:S(2)}) %copy-start.1) | copy-done | bytes 32792
  10.4 0.0 copy-start.2
  10.4 0.0 collective-permute-done.1.refs_3_
  10.5 1.1 %collective-permute-done.refs_2_ = f32[2,8,128]{2,1,0:T(8,128)S(1)} collective-permute-done((f32[2,8,128]{2,1,0:T(8,128)}, f32[2,8,128]{2,1,0:T(8,128)S(1)}, u32[]{:S(2)}, u32[]{:S(2)}) %collective-permute-start) | collective-permute-done | bytes 8224 | tf_op jit(solution)/shard_map/ppermute | solution.py:481
  11.6 0.5 %collective-permute-done.2.refs_4_ = f32[2,8,128]{2,1,0:T(8,128)S(1)} collective-permute-done((f32[2,8,128]{2,1,0:T(8,128)}, f32[2,8,128]{2,1,0:T(8,128)S(1)}, u32[]{:S(2)}, u32[]{:S(2)}) %collective-permute-start.2) | collective-permute-done | bytes 8224 | tf_op jit(solution)/shard_map/ppermute | solution.py:481
  12.1 0.0 collective-permute-done.4.refs_6_.refs_8_
  12.1 0.0 collective-permute-done.3.refs_5_.refs_4_
  12.1 0.0 copy-done.2
  12.1 0.0 copy-start.3
  12.1 0.4 %collective-permute-start.5 = (f32[16,32,128]{2,1,0:T(8,128)S(1)}, f32[16,32,128]{2,1,0:T(8,128)S(1)}, u32[]{:S(2)}, u32[]{:S(2)}) collective-permute-start(f32[16,32,128]{2,1,0:T(8,128)S(1)} %get-tuple-element.10.refs_1_), channel_id=1, source_target_pairs={{1,0},{0,1},{3,2},{2,3},{5,4},{4,5},{7,6},{6,7},{9,8},{8,9},{11,10... | collective-permute-start | bytes 786440 | tf_op jit(solution)/shard_map/ppermute | solution.py:481
  12.6 0.1 collective-permute-start.8
  12.7 2.0 %collective-permute-start.9 = (f32[4,32,128]{2,1,0:T(8,128)S(1)}, f32[4,32,128]{2,1,0:T(8,128)S(1)}, u32[]{:S(2)}, u32[]{:S(2)}) collective-permute-start(f32[4,32,128]{2,1,0:T(8,128)S(1)} %get-tuple-element.11), channel_id=1, source_target_pairs={{3,1},{0,2},{5,3},{2,4},{7,5},{4,6},{1,0},{6,7},{11,9},{8,10},{13,... | collective-permute-start | bytes 196616 | tf_op jit(solution)/shard_map/ppermute | solution.py:543
  14.7 0.0 collective-permute-start.7
  14.7 0.7 %collective-permute-start.6 = (f32[4,32,128]{2,1,0:T(8,128)S(1)}, f32[4,32,128]{2,1,0:T(8,128)S(1)}, u32[]{:S(2)}, u32[]{:S(2)}) collective-permute-start(f32[4,32,128]{2,1,0:T(8,128)S(1)} %get-tuple-element.11), channel_id=1, source_target_pairs={{2,1},{1,2},{4,3},{3,4},{6,5},{5,6},{0,0},{7,7},{10,9},{9,10},{12,... | collective-permute-start | bytes 196616 | tf_op jit(solution)/shard_map/ppermute | solution.py:543
  15.3 1.2 %collective-permute-done.9.refs_7_ = f32[4,32,128]{2,1,0:T(8,128)S(1)} collective-permute-done((f32[4,32,128]{2,1,0:T(8,128)S(1)}, f32[4,32,128]{2,1,0:T(8,128)S(1)}, u32[]{:S(2)}, u32[]{:S(2)}) %collective-permute-start.9) | collective-permute-done | bytes 65568 | tf_op jit(solution)/shard_map/ppermute | solution.py:543
  16.6 2.4 %collective-permute-done.7.refs_5_ = f32[4,32,128]{2,1,0:T(8,128)S(1)} collective-permute-done((f32[4,32,128]{2,1,0:T(8,128)S(1)}, f32[4,32,128]{2,1,0:T(8,128)S(1)}, u32[]{:S(2)}, u32[]{:S(2)}) %collective-permute-start.7) | collective-permute-done | bytes 65568 | tf_op jit(solution)/shard_map/ppermute | solution.py:541
  18.9 0.0 collective-permute-done.6.refs_3_
  18.9 0.0 collective-permute-done.8.refs_6_
  18.9 0.0 collective-permute-done.5.refs_2_
  19.0 0.0 copy-done.3
  19.0 5.7 %shard_map.61 = (f32[2,3,2,32,128]{4,3,2,1,0:T(8,128)}, f32[3,2,8,128]{3,2,1,0:T(8,128)S(1)}, f32[24,128]{1,0:T(8,128)S(1)}, f32[24,128]{1,0:T(8,128)S(1)}, f32[...) custom-call(s32[8]{0:T(128)S(1)} %copy-done.3, f32[16,32,128]{2,1,0:T(8,128)S(1)} %get-tuple-element.10.refs_1_, ...), custom_call_target="tpu_custom_call" | custom-call | flops 60000000 | bytes 6000000 | tf_op jit(solution)/shard_map/pallas_call | solution.py:510
  24.7 1.9 %collective-permute-start.10 = (f32[24,128]{1,0:T(8,128)S(1)}, f32[24,128]{1,0:T(8,128)S(1)}, u32[]{:S(2)}, u32[]{:S(2)}) collective-permute-start(f32[24,128]{1,0:T(8,128)S(1)} %get-tuple-element.13), channel_id=1, source_target_pairs={{24,0},{16,8},{8,16},{0,24},{25,1},{17,9},{9,17},{1,25},{26,2},{18... | collective-permute-start | bytes 36872 | tf_op jit(solution)/shard_map/ppermute | solution.py:481
  26.7 0.5 %collective-permute-start.11 = (f32[24,128]{1,0:T(8,128)S(1)}, f32[24,128]{1,0:T(8,128)S(1)}, u32[]{:S(2)}, u32[]{:S(2)}) collective-permute-start(f32[24,128]{1,0:T(8,128)S(1)} %get-tuple-element.14), channel_id=1, source_target_pairs={{16,0},{24,8},{0,16},{8,24},{17,1},{25,9},{1,17},{9,25},{18,2},{26... | collective-permute-start | bytes 36872 | tf_op jit(solution)/shard_map/ppermute | solution.py:481
  27.2 1.1 %collective-permute-start.12 = (f32[24,128]{1,0:T(8,128)S(1)}, f32[24,128]{1,0:T(8,128)S(1)}, u32[]{:S(2)}, u32[]{:S(2)}) collective-permute-start(f32[24,128]{1,0:T(8,128)S(1)} %get-tuple-element.15), channel_id=1, source_target_pairs={{8,0},{0,8},{24,16},{16,24},{9,1},{1,9},{25,17},{17,25},{10,2},{2,... | collective-permute-start | bytes 36872 | tf_op jit(solution)/shard_map/ppermute | solution.py:481
  28.3 1.1 %collective-permute-done.10.refs_1_ = f32[24,128]{1,0:T(8,128)S(1)} collective-permute-done((f32[24,128]{1,0:T(8,128)S(1)}, f32[24,128]{1,0:T(8,128)S(1)}, u32[]{:S(2)}, u32[]{:S(2)}) %collective-permute-start.10) | collective-permute-done | bytes 12320 | tf_op jit(solution)/shard_map/ppermute | solution.py:481
  29.4 1.0 %collective-permute-done.11.refs_2_ = f32[24,128]{1,0:T(8,128)S(1)} collective-permute-done((f32[24,128]{1,0:T(8,128)S(1)}, f32[24,128]{1,0:T(8,128)S(1)}, u32[]{:S(2)}, u32[]{:S(2)}) %collective-permute-start.11) | collective-permute-done | bytes 12320 | tf_op jit(solution)/shard_map/ppermute | solution.py:481
  30.4 0.5 %collective-permute-done.12.refs_3_ = f32[24,128]{1,0:T(8,128)S(1)} collective-permute-done((f32[24,128]{1,0:T(8,128)S(1)}, f32[24,128]{1,0:T(8,128)S(1)}, u32[]{:S(2)}, u32[]{:S(2)}) %collective-permute-start.12) | collective-permute-done | bytes 12320 | tf_op jit(solution)/shard_map/ppermute | solution.py:481
  30.9 0.1 collective-permute-start.13
  31.0 1.0 %collective-permute-done.13.beside_ref.refs_1_ = f32[24,128]{1,0:T(8,128)S(1)} collective-permute-done((f32[24,128]{1,0:T(8,128)S(1)}, f32[24,128]{1,0:T(8,128)S(1)}, u32[]{:S(2)}, u32[]{:S(2)}) %collective-permute-start.13) | collective-permute-done | bytes 12320 | tf_op jit(solution)/shard_map/ppermute | solution.py:481
  32.1 3.5 %collective-permute-start.16 = (f32[16,128]{1,0:T(8,128)S(1)}, f32[16,128]{1,0:T(8,128)S(1)}, u32[]{:S(2)}, u32[]{:S(2)}) collective-permute-start(f32[16,128]{1,0:T(8,128)S(1)} %shard_map.63.refs_2_), channel_id=1, source_target_pairs={{6,0},{7,1},{4,2},{5,3},{2,4},{3,5},{0,6},{1,7},{14,8},{15,9},{12,... | collective-permute-start | bytes 24584 | tf_op jit(solution)/shard_map/ppermute | solution.py:481
  35.6 1.3 %collective-permute-start.15 = (f32[16,128]{1,0:T(8,128)S(1)}, f32[16,128]{1,0:T(8,128)S(1)}, u32[]{:S(2)}, u32[]{:S(2)}) collective-permute-start(f32[16,128]{1,0:T(8,128)S(1)} %shard_map.63.refs_2_), channel_id=1, source_target_pairs={{4,0},{5,1},{6,2},{7,3},{0,4},{1,5},{2,6},{3,7},{12,8},{13,9},{14,... | collective-permute-start | bytes 24584 | tf_op jit(solution)/shard_map/ppermute | solution.py:481
  36.8 0.0 collective-permute-start.14
  36.8 0.7 %collective-permute-done.16.refs_5_ = f32[16,128]{1,0:T(8,128)S(1)} collective-permute-done((f32[16,128]{1,0:T(8,128)S(1)}, f32[16,128]{1,0:T(8,128)S(1)}, u32[]{:S(2)}, u32[]{:S(2)}) %collective-permute-start.16) | collective-permute-done | bytes 8224 | tf_op jit(solution)/shard_map/ppermute | solution.py:481
  37.5 2.6 %collective-permute-done.15.refs_4_ = f32[16,128]{1,0:T(8,128)S(1)} collective-permute-done((f32[16,128]{1,0:T(8,128)S(1)}, f32[16,128]{1,0:T(8,128)S(1)}, u32[]{:S(2)}, u32[]{:S(2)}) %collective-permute-start.15) | collective-permute-done | bytes 8224 | tf_op jit(solution)/shard_map/ppermute | solution.py:481
  40.1 0.4 collective-permute-done.14.refs_3_
  40.5 0.7 %shard_map.64 = f32[2,8,128]{2,1,0:T(8,128)} custom-call(f32[24,128]{1,0:T(8,128)S(1)} %shard_map.62.sum_ref.refs_0_, f32[24,128]{1,0:T(8,128)S(1)} %collective-permute-done.13.beside_ref.refs_1_, f32[16,128]{1,0:T(8,128)S(1)} %shard_map.63.refs_2_, f32[16,128]{1,0:T(8,128)S(1)} %collective-permute-done.14.refs_3_, ...), custom_call_target="tpu_custom_call" | custom-call | flops 100000 | bytes 10000 | tf_op jit(solution)/shard_map/pallas_call | solution.py:510
  (4 shorter events, 0.1 us)
Async XLA Ops:
  0.6 11.4 %collective-permute-start.4 = (f32[2,3,2,32,128]{4,3,2,1,0:T(8,128)}, f32[2,3,2,32,128]{4,3,2,1,0:T(8,128)S(1)}, u32[]{:S(2)}, u32[]{:S(2)}) collective-permute-start(f32[2,3,2,32,128]{4,3,2,1,0:T(8,128)} %forces_ref.1), channel_id=1, source_target_pairs={{3,1},{0,2},{5,3},{2,4},{7,5},{4,6},{1,0},{6,7},{11,9},{8,10},{13,... | collective-permute-start | bytes 589832 | tf_op jit(solution)/shard_map/ppermute | solution.py:523
  3.7 8.4 %collective-permute-start.3 = (f32[2,3,2,32,128]{4,3,2,1,0:T(8,128)}, f32[2,3,2,32,128]{4,3,2,1,0:T(8,128)S(1)}, u32[]{:S(2)}, u32[]{:S(2)}) collective-permute-start(f32[2,3,2,32,128]{4,3,2,1,0:T(8,128)} %forces_ref.1), channel_id=1, source_target_pairs={{2,1},{1,2},{4,3},{3,4},{6,5},{5,6},{0,0},{7,7},{10,9},{9,10},{12,... | collective-permute-start | bytes 589832 | tf_op jit(solution)/shard_map/ppermute | solution.py:523
  5.2 5.2 %collective-permute-start.1 = (f32[2,8,128]{2,1,0:T(8,128)}, f32[2,8,128]{2,1,0:T(8,128)S(1)}, u32[]{:S(2)}, u32[]{:S(2)}) collective-permute-start(f32[2,8,128]{2,1,0:T(8,128)} %refs_1_.1), channel_id=1, source_target_pairs={{24,0},{16,8},{8,16},{0,24},{25,1},{17,9},{9,17},{1,25},{26,2},{18... | collective-permute-start | bytes 24584 | tf_op jit(solution)/shard_map/ppermute | solution.py:481
  7.7 3.9 %collective-permute-start = (f32[2,8,128]{2,1,0:T(8,128)}, f32[2,8,128]{2,1,0:T(8,128)S(1)}, u32[]{:S(2)}, u32[]{:S(2)}) collective-permute-start(f32[2,8,128]{2,1,0:T(8,128)} %refs_1_.1), channel_id=1, source_target_pairs={{16,0},{24,8},{0,16},{8,24},{17,1},{25,9},{1,17},{9,25},{18,2},{26... | collective-permute-start | bytes 24584 | tf_op jit(solution)/shard_map/ppermute | solution.py:481
  8.2 3.9 %collective-permute-start.2 = (f32[2,8,128]{2,1,0:T(8,128)}, f32[2,8,128]{2,1,0:T(8,128)S(1)}, u32[]{:S(2)}, u32[]{:S(2)}) collective-permute-start(f32[2,8,128]{2,1,0:T(8,128)} %refs_1_.1), channel_id=1, source_target_pairs={{8,0},{0,8},{24,16},{16,24},{9,1},{1,9},{25,17},{17,25},{10,2},{2,... | collective-permute-start | bytes 24584 | tf_op jit(solution)/shard_map/ppermute | solution.py:481
  8.7 0.9 %copy-start = (f32[2,3,2,32,128]{4,3,2,1,0:T(8,128)S(1)}, f32[2,3,2,32,128]{4,3,2,1,0:T(8,128)}, u32[]{:S(2)}) copy-start(f32[2,3,2,32,128]{4,3,2,1,0:T(8,128)} %forces_ref.1) | copy-start | bytes 589828
  9.7 0.8 %copy-start.1 = (s32[2,32,128]{2,1,0:T(8,128)S(1)}, s32[2,32,128]{2,1,0:T(8,128)}, u32[]{:S(2)}) copy-start(s32[2,32,128]{2,1,0:T(8,128)} %labels_ref.1) | copy-start | bytes 98308
  10.4 1.6 %copy-start.2 = (f32[2,8,128]{2,1,0:T(8,128)S(1)}, f32[2,8,128]{2,1,0:T(8,128)}, u32[]{:S(2)}) copy-start(f32[2,8,128]{2,1,0:T(8,128)} %refs_1_.1) | copy-start | bytes 24580
  12.1 6.9 %copy-start.3 = (s32[8]{0:T(128)S(1)}, s32[8]{0:T(128)}, u32[]{:S(2)}) copy-start(s32[8]{0:T(128)} %refs_0_.1) | copy-start | bytes 100
  12.1 6.8 %collective-permute-start.5 = (f32[16,32,128]{2,1,0:T(8,128)S(1)}, f32[16,32,128]{2,1,0:T(8,128)S(1)}, u32[]{:S(2)}, u32[]{:S(2)}) collective-permute-start(f32[16,32,128]{2,1,0:T(8,128)S(1)} %get-tuple-element.10.refs_1_), channel_id=1, source_target_pairs={{1,0},{0,1},{3,2},{2,3},{5,4},{4,5},{7,6},{6,7},{9,8},{8,9},{11,10... | collective-permute-start | bytes 786440 | tf_op jit(solution)/shard_map/ppermute | solution.py:481
  12.6 6.4 %collective-permute-start.8 = (f32[2,3,2,32,128]{4,3,2,1,0:T(8,128)S(1)}, f32[2,3,2,32,128]{4,3,2,1,0:T(8,128)S(1)}, u32[]{:S(2)}, u32[]{:S(2)}) collective-permute-start(f32[2,3,2,32,128]{4,3,2,1,0:T(8,128)S(1)} %collective-permute-done.3.refs_5_.refs_4_), channel_id=1, source_target_pairs={{1,0},{0,1},{3,2},{2,3},{5,4},{4,5},{7,6},{6,7},{9,8},{8,9},{11,10... | collective-permute-start | bytes 589832 | tf_op jit(solution)/shard_map/ppermute | solution.py:481
  12.7 3.9 %collective-permute-start.9 = (f32[4,32,128]{2,1,0:T(8,128)S(1)}, f32[4,32,128]{2,1,0:T(8,128)S(1)}, u32[]{:S(2)}, u32[]{:S(2)}) collective-permute-start(f32[4,32,128]{2,1,0:T(8,128)S(1)} %get-tuple-element.11), channel_id=1, source_target_pairs={{3,1},{0,2},{5,3},{2,4},{7,5},{4,6},{1,0},{6,7},{11,9},{8,10},{13,... | collective-permute-start | bytes 196616 | tf_op jit(solution)/shard_map/ppermute | solution.py:543
  14.7 4.3 %collective-permute-start.7 = (f32[4,32,128]{2,1,0:T(8,128)S(1)}, f32[4,32,128]{2,1,0:T(8,128)S(1)}, u32[]{:S(2)}, u32[]{:S(2)}) collective-permute-start(f32[4,32,128]{2,1,0:T(8,128)S(1)} %get-tuple-element.11), channel_id=1, source_target_pairs={{2,0},{4,2},{1,3},{6,4},{3,5},{5,7},{0,1},{7,6},{10,8},{12,10},{9,... | collective-permute-start | bytes 196616 | tf_op jit(solution)/shard_map/ppermute | solution.py:541
  14.7 4.3 %collective-permute-start.6 = (f32[4,32,128]{2,1,0:T(8,128)S(1)}, f32[4,32,128]{2,1,0:T(8,128)S(1)}, u32[]{:S(2)}, u32[]{:S(2)}) collective-permute-start(f32[4,32,128]{2,1,0:T(8,128)S(1)} %get-tuple-element.11), channel_id=1, source_target_pairs={{2,1},{1,2},{4,3},{3,4},{6,5},{5,6},{0,0},{7,7},{10,9},{9,10},{12,... | collective-permute-start | bytes 196616 | tf_op jit(solution)/shard_map/ppermute | solution.py:543
  24.7 4.7 %collective-permute-start.10 = (f32[24,128]{1,0:T(8,128)S(1)}, f32[24,128]{1,0:T(8,128)S(1)}, u32[]{:S(2)}, u32[]{:S(2)}) collective-permute-start(f32[24,128]{1,0:T(8,128)S(1)} %get-tuple-element.13), channel_id=1, source_target_pairs={{24,0},{16,8},{8,16},{0,24},{25,1},{17,9},{9,17},{1,25},{26,2},{18... | collective-permute-start | bytes 36872 | tf_op jit(solution)/shard_map/ppermute | solution.py:481
  26.7 3.7 %collective-permute-start.11 = (f32[24,128]{1,0:T(8,128)S(1)}, f32[24,128]{1,0:T(8,128)S(1)}, u32[]{:S(2)}, u32[]{:S(2)}) collective-permute-start(f32[24,128]{1,0:T(8,128)S(1)} %get-tuple-element.14), channel_id=1, source_target_pairs={{16,0},{24,8},{0,16},{8,24},{17,1},{25,9},{1,17},{9,25},{18,2},{26... | collective-permute-start | bytes 36872 | tf_op jit(solution)/shard_map/ppermute | solution.py:481
  27.2 3.7 %collective-permute-start.12 = (f32[24,128]{1,0:T(8,128)S(1)}, f32[24,128]{1,0:T(8,128)S(1)}, u32[]{:S(2)}, u32[]{:S(2)}) collective-permute-start(f32[24,128]{1,0:T(8,128)S(1)} %get-tuple-element.15), channel_id=1, source_target_pairs={{8,0},{0,8},{24,16},{16,24},{9,1},{1,9},{25,17},{17,25},{10,2},{2,... | collective-permute-start | bytes 36872 | tf_op jit(solution)/shard_map/ppermute | solution.py:481
  30.9 1.2 %collective-permute-start.13 = (f32[24,128]{1,0:T(8,128)S(1)}, f32[24,128]{1,0:T(8,128)S(1)}, u32[]{:S(2)}, u32[]{:S(2)}) collective-permute-start(f32[24,128]{1,0:T(8,128)S(1)} %shard_map.62.sum_ref.refs_0_), channel_id=1, source_target_pairs={{1,0},{0,1},{3,2},{2,3},{5,4},{4,5},{7,6},{6,7},{9,8},{8,9},{11,10... | collective-permute-start | bytes 36872 | tf_op jit(solution)/shard_map/ppermute | solution.py:481
  32.1 5.4 %collective-permute-start.16 = (f32[16,128]{1,0:T(8,128)S(1)}, f32[16,128]{1,0:T(8,128)S(1)}, u32[]{:S(2)}, u32[]{:S(2)}) collective-permute-start(f32[16,128]{1,0:T(8,128)S(1)} %shard_map.63.refs_2_), channel_id=1, source_target_pairs={{6,0},{7,1},{4,2},{5,3},{2,4},{3,5},{0,6},{1,7},{14,8},{15,9},{12,... | collective-permute-start | bytes 24584 | tf_op jit(solution)/shard_map/ppermute | solution.py:481
  35.6 4.5 %collective-permute-start.15 = (f32[16,128]{1,0:T(8,128)S(1)}, f32[16,128]{1,0:T(8,128)S(1)}, u32[]{:S(2)}, u32[]{:S(2)}) collective-permute-start(f32[16,128]{1,0:T(8,128)S(1)} %shard_map.63.refs_2_), channel_id=1, source_target_pairs={{4,0},{5,1},{6,2},{7,3},{0,4},{1,5},{2,6},{3,7},{12,8},{13,9},{14,... | collective-permute-start | bytes 24584 | tf_op jit(solution)/shard_map/ppermute | solution.py:481
  36.8 3.7 %collective-permute-start.14 = (f32[16,128]{1,0:T(8,128)S(1)}, f32[16,128]{1,0:T(8,128)S(1)}, u32[]{:S(2)}, u32[]{:S(2)}) collective-permute-start(f32[16,128]{1,0:T(8,128)S(1)} %shard_map.63.refs_2_), channel_id=1, source_target_pairs={{2,0},{3,1},{0,2},{1,3},{6,4},{7,5},{4,6},{5,7},{10,8},{11,9},{8,1... | collective-permute-start | bytes 24584 | tf_op jit(solution)/shard_map/ppermute | solution.py:481

commit v10 on v8

--- a/solution.py
+++ b/solution.py
@@ -259,7 +259,8 @@
                 for node in range(first, end + 1):
                     for comp in range(3):
                         store_modes(node, comp, [step_ref[comp, node, chunk] for chunk in chunks])
-            for chunk in chunks:
+            def column(at, carry, first=first, end=end):
+                chunk = pl.ds(pl.multiple_of(at * 8, 8), 8)
                 low = load_modes(first, chunk)
                 up = None
                 for element in range(first, end):
@@ -270,17 +271,20 @@
                     for comp in range(3):
                         for i, pq in enumerate(PLANE):
                             diff = f[comp][pq + "d"]
-                            at = comp * 4 + i
+                            where = comp * 4 + i
                             if pq == "ss":
                                 ups.append(diff)
                                 if up:
-                                    node_ref[element, at, chunk] = up[at] - diff
+                                    node_ref[element, where, chunk] = up[where] - diff
                             else:
                                 both = f[comp][pq + "s"]
                                 ups.append(both + diff)
                                 if up:
-                                    node_ref[element, at, chunk] = up[at] + (both - diff)
+                                    node_ref[element, where, chunk] = up[where] + (both - diff)
                     low, up = high, ups
+                return carry
+
+            lax.fori_loop(0, len(chunks), column, 0)
             for node in range(first + 1, end):
                 for comp in range(3):
                     g = [[node_ref[node, comp * 4 + i, chunk] for chunk in chunks] for i in range(4)]

time: 41.5 us -> 41.5 us (level)
  no operation moved by 1% of the time
where the time goes in v10:
time: 41.5 us; the launch traced here: 41.2 us
  starting transfers between devices  19.8 us (48%)
  waiting for transfers between devices  12.5 us (30%)
  Pallas kernels  6.53 us (16%)
  local copies, waits for them, and re-layouts  1.69 us (4%)
  between operations  0.7 us (2%)
    ppermute x12, starting transfers between devices, met(): lax.ppermute(block, axis, [(partner(i, step), i) for i in range(count)])  12.5 us
    ppermute x12, waiting for transfers between devices, met(): lax.ppermute(block, axis, [(partner(i, step), i) for i in range(count)])  8.9 us
    pallas_call x6, Pallas kernels, call(): pl.pallas_call(kernel, out_shape=out, in_specs=in_specs or [vmem] * len(a...  6.53 us
    ppermute x2, starting transfers between devices, on_device(): lax.ppermute(forces, 'gz', far_pairs(far, count_gz, True))  4.61 us
    ppermute x2, starting transfers between devices, on_device(): lax.ppermute(design, 'gz', far_pairs(far, count_gz, True))  2.64 us
    ppermute x1, waiting for transfers between devices, on_device(): packs.append(lax.ppermute(design, 'gz', far_pairs(far, count_gz, False)))  2.36 us
    unnamed x8, local copies, waits for them, and re-layouts  1.69 us
    ppermute x2, waiting for transfers between devices, on_device(): lax.ppermute(design, 'gz', far_pairs(far, count_gz, True))  1.24 us
  transfers between devices with their start and end apart: 17, of which 11 were waited for; matrix products, arithmetic and copies ran while one was open for 0% of the time, Pallas kernels for 0%

profile of v10, /device:TPU:0, one launch (start us, length us, event | category | flops | bytes accessed | tf_op | source)
XLA Modules:
  0.0 41.2 jit_solution(1926271185937876828)
XLA Ops:
  0.6 3.0 %collective-permute-start.4 = (f32[2,3,2,32,128]{4,3,2,1,0:T(8,128)}, f32[2,3,2,32,128]{4,3,2,1,0:T(8,128)S(1)}, u32[]{:S(2)}, u32[]{:S(2)}) collective-permute-start(f32[2,3,2,32,128]{4,3,2,1,0:T(8,128)} %forces_ref.1), channel_id=1, source_target_pairs={{3,1},{0,2},{5,3},{2,4},{7,5},{4,6},{1,0},{6,7},{11,9},{8,10},{13,... | collective-permute-start | bytes 589832 | tf_op jit(solution)/shard_map/ppermute | solution.py:508
  3.7 1.6 %collective-permute-start.3 = (f32[2,3,2,32,128]{4,3,2,1,0:T(8,128)}, f32[2,3,2,32,128]{4,3,2,1,0:T(8,128)S(1)}, u32[]{:S(2)}, u32[]{:S(2)}) collective-permute-start(f32[2,3,2,32,128]{4,3,2,1,0:T(8,128)} %forces_ref.1), channel_id=1, source_target_pairs={{2,1},{1,2},{4,3},{3,4},{6,5},{5,6},{0,0},{7,7},{10,9},{9,10},{12,... | collective-permute-start | bytes 589832 | tf_op jit(solution)/shard_map/ppermute | solution.py:508
  5.2 2.4 %collective-permute-start.1 = (f32[2,8,128]{2,1,0:T(8,128)}, f32[2,8,128]{2,1,0:T(8,128)S(1)}, u32[]{:S(2)}, u32[]{:S(2)}) collective-permute-start(f32[2,8,128]{2,1,0:T(8,128)} %refs_1_.1), channel_id=1, source_target_pairs={{24,0},{16,8},{8,16},{0,24},{25,1},{17,9},{9,17},{1,25},{26,2},{18... | collective-permute-start | bytes 24584 | tf_op jit(solution)/shard_map/ppermute | solution.py:466
  7.7 0.5 %collective-permute-start = (f32[2,8,128]{2,1,0:T(8,128)}, f32[2,8,128]{2,1,0:T(8,128)S(1)}, u32[]{:S(2)}, u32[]{:S(2)}) collective-permute-start(f32[2,8,128]{2,1,0:T(8,128)} %refs_1_.1), channel_id=1, source_target_pairs={{16,0},{24,8},{0,16},{8,24},{17,1},{25,9},{1,17},{9,25},{18,2},{26... | collective-permute-start | bytes 24584 | tf_op jit(solution)/shard_map/ppermute | solution.py:466
  8.2 0.5 %collective-permute-start.2 = (f32[2,8,128]{2,1,0:T(8,128)}, f32[2,8,128]{2,1,0:T(8,128)S(1)}, u32[]{:S(2)}, u32[]{:S(2)}) collective-permute-start(f32[2,8,128]{2,1,0:T(8,128)} %refs_1_.1), channel_id=1, source_target_pairs={{8,0},{0,8},{24,16},{16,24},{9,1},{1,9},{25,17},{17,25},{10,2},{2,... | collective-permute-start | bytes 24584 | tf_op jit(solution)/shard_map/ppermute | solution.py:466
  8.7 0.0 copy-start
  8.7 0.9 %copy-done = f32[2,3,2,32,128]{4,3,2,1,0:T(8,128)S(1)} copy-done((f32[2,3,2,32,128]{4,3,2,1,0:T(8,128)S(1)}, f32[2,3,2,32,128]{4,3,2,1,0:T(8,128)}, u32[]{:S(2)}) %copy-start) | copy-done | bytes 196632
  9.7 0.0 copy-start.1
  9.7 0.8 %copy-done.1 = s32[2,32,128]{2,1,0:T(8,128)S(1)} copy-done((s32[2,32,128]{2,1,0:T(8,128)S(1)}, s32[2,32,128]{2,1,0:T(8,128)}, u32[]{:S(2)}) %copy-start.1) | copy-done | bytes 32792
  10.4 0.0 copy-start.2
  10.4 0.0 collective-permute-done.1.refs_3_
  10.5 1.1 %collective-permute-done.refs_2_ = f32[2,8,128]{2,1,0:T(8,128)S(1)} collective-permute-done((f32[2,8,128]{2,1,0:T(8,128)}, f32[2,8,128]{2,1,0:T(8,128)S(1)}, u32[]{:S(2)}, u32[]{:S(2)}) %collective-permute-start) | collective-permute-done | bytes 8224 | tf_op jit(solution)/shard_map/ppermute | solution.py:466
  11.6 0.5 %collective-permute-done.2.refs_4_ = f32[2,8,128]{2,1,0:T(8,128)S(1)} collective-permute-done((f32[2,8,128]{2,1,0:T(8,128)}, f32[2,8,128]{2,1,0:T(8,128)S(1)}, u32[]{:S(2)}, u32[]{:S(2)}) %collective-permute-start.2) | collective-permute-done | bytes 8224 | tf_op jit(solution)/shard_map/ppermute | solution.py:466
  12.1 0.0 collective-permute-done.4.refs_6_.refs_8_
  12.1 0.0 collective-permute-done.3.refs_5_.refs_4_
  12.1 0.0 copy-done.2
  12.1 0.0 copy-start.3
  12.1 0.4 %collective-permute-start.5 = (f32[16,32,128]{2,1,0:T(8,128)S(1)}, f32[16,32,128]{2,1,0:T(8,128)S(1)}, u32[]{:S(2)}, u32[]{:S(2)}) collective-permute-start(f32[16,32,128]{2,1,0:T(8,128)S(1)} %get-tuple-element.10.refs_1_), channel_id=1, source_target_pairs={{1,0},{0,1},{3,2},{2,3},{5,4},{4,5},{7,6},{6,7},{9,8},{8,9},{11,10... | collective-permute-start | bytes 786440 | tf_op jit(solution)/shard_map/ppermute | solution.py:466
  12.6 0.1 collective-permute-start.8
  12.7 2.0 %collective-permute-start.9 = (f32[4,32,128]{2,1,0:T(8,128)S(1)}, f32[4,32,128]{2,1,0:T(8,128)S(1)}, u32[]{:S(2)}, u32[]{:S(2)}) collective-permute-start(f32[4,32,128]{2,1,0:T(8,128)S(1)} %get-tuple-element.11), channel_id=1, source_target_pairs={{3,1},{0,2},{5,3},{2,4},{7,5},{4,6},{1,0},{6,7},{11,9},{8,10},{13,... | collective-permute-start | bytes 196616 | tf_op jit(solution)/shard_map/ppermute | solution.py:528
  14.7 0.0 collective-permute-start.7
  14.7 0.7 %collective-permute-start.6 = (f32[4,32,128]{2,1,0:T(8,128)S(1)}, f32[4,32,128]{2,1,0:T(8,128)S(1)}, u32[]{:S(2)}, u32[]{:S(2)}) collective-permute-start(f32[4,32,128]{2,1,0:T(8,128)S(1)} %get-tuple-element.11), channel_id=1, source_target_pairs={{2,1},{1,2},{4,3},{3,4},{6,5},{5,6},{0,0},{7,7},{10,9},{9,10},{12,... | collective-permute-start | bytes 196616 | tf_op jit(solution)/shard_map/ppermute | solution.py:528
  15.3 1.2 %collective-permute-done.9.refs_7_ = f32[4,32,128]{2,1,0:T(8,128)S(1)} collective-permute-done((f32[4,32,128]{2,1,0:T(8,128)S(1)}, f32[4,32,128]{2,1,0:T(8,128)S(1)}, u32[]{:S(2)}, u32[]{:S(2)}) %collective-permute-start.9) | collective-permute-done | bytes 65568 | tf_op jit(solution)/shard_map/ppermute | solution.py:528
  16.6 2.4 %collective-permute-done.7.refs_5_ = f32[4,32,128]{2,1,0:T(8,128)S(1)} collective-permute-done((f32[4,32,128]{2,1,0:T(8,128)S(1)}, f32[4,32,128]{2,1,0:T(8,128)S(1)}, u32[]{:S(2)}, u32[]{:S(2)}) %collective-permute-start.7) | collective-permute-done | bytes 65568 | tf_op jit(solution)/shard_map/ppermute | solution.py:526
  18.9 0.0 collective-permute-done.6.refs_3_
  18.9 0.0 collective-permute-done.8.refs_6_
  18.9 0.0 collective-permute-done.5.refs_2_
  19.0 0.0 copy-done.3
  19.0 5.7 %shard_map.61 = (f32[2,3,2,32,128]{4,3,2,1,0:T(8,128)}, f32[3,2,8,128]{3,2,1,0:T(8,128)S(1)}, f32[24,128]{1,0:T(8,128)S(1)}, f32[24,128]{1,0:T(8,128)S(1)}, f32[...) custom-call(s32[8]{0:T(128)S(1)} %copy-done.3, f32[16,32,128]{2,1,0:T(8,128)S(1)} %get-tuple-element.10.refs_1_, ...), custom_call_target="tpu_custom_call" | custom-call | flops 60000000 | bytes 6000000 | tf_op jit(solution)/shard_map/pallas_call | solution.py:495
  24.7 1.9 %collective-permute-start.10 = (f32[24,128]{1,0:T(8,128)S(1)}, f32[24,128]{1,0:T(8,128)S(1)}, u32[]{:S(2)}, u32[]{:S(2)}) collective-permute-start(f32[24,128]{1,0:T(8,128)S(1)} %get-tuple-element.13), channel_id=1, source_target_pairs={{24,0},{16,8},{8,16},{0,24},{25,1},{17,9},{9,17},{1,25},{26,2},{18... | collective-permute-start | bytes 36872 | tf_op jit(solution)/shard_map/ppermute | solution.py:466
  26.6 0.5 %collective-permute-start.11 = (f32[24,128]{1,0:T(8,128)S(1)}, f32[24,128]{1,0:T(8,128)S(1)}, u32[]{:S(2)}, u32[]{:S(2)}) collective-permute-start(f32[24,128]{1,0:T(8,128)S(1)} %get-tuple-element.14), channel_id=1, source_target_pairs={{16,0},{24,8},{0,16},{8,24},{17,1},{25,9},{1,17},{9,25},{18,2},{26... | collective-permute-start | bytes 36872 | tf_op jit(solution)/shard_map/ppermute | solution.py:466
  27.2 1.1 %collective-permute-start.12 = (f32[24,128]{1,0:T(8,128)S(1)}, f32[24,128]{1,0:T(8,128)S(1)}, u32[]{:S(2)}, u32[]{:S(2)}) collective-permute-start(f32[24,128]{1,0:T(8,128)S(1)} %get-tuple-element.15), channel_id=1, source_target_pairs={{8,0},{0,8},{24,16},{16,24},{9,1},{1,9},{25,17},{17,25},{10,2},{2,... | collective-permute-start | bytes 36872 | tf_op jit(solution)/shard_map/ppermute | solution.py:466
  28.3 1.1 %collective-permute-done.10.refs_1_ = f32[24,128]{1,0:T(8,128)S(1)} collective-permute-done((f32[24,128]{1,0:T(8,128)S(1)}, f32[24,128]{1,0:T(8,128)S(1)}, u32[]{:S(2)}, u32[]{:S(2)}) %collective-permute-start.10) | collective-permute-done | bytes 12320 | tf_op jit(solution)/shard_map/ppermute | solution.py:466
  29.4 1.0 %collective-permute-done.11.refs_2_ = f32[24,128]{1,0:T(8,128)S(1)} collective-permute-done((f32[24,128]{1,0:T(8,128)S(1)}, f32[24,128]{1,0:T(8,128)S(1)}, u32[]{:S(2)}, u32[]{:S(2)}) %collective-permute-start.11) | collective-permute-done | bytes 12320 | tf_op jit(solution)/shard_map/ppermute | solution.py:466
  30.3 0.5 %collective-permute-done.12.refs_3_ = f32[24,128]{1,0:T(8,128)S(1)} collective-permute-done((f32[24,128]{1,0:T(8,128)S(1)}, f32[24,128]{1,0:T(8,128)S(1)}, u32[]{:S(2)}, u32[]{:S(2)}) %collective-permute-start.12) | collective-permute-done | bytes 12320 | tf_op jit(solution)/shard_map/ppermute | solution.py:466
  30.9 0.1 collective-permute-start.13
  31.0 1.0 %collective-permute-done.13.beside_ref.refs_1_ = f32[24,128]{1,0:T(8,128)S(1)} collective-permute-done((f32[24,128]{1,0:T(8,128)S(1)}, f32[24,128]{1,0:T(8,128)S(1)}, u32[]{:S(2)}, u32[]{:S(2)}) %collective-permute-start.13) | collective-permute-done | bytes 12320 | tf_op jit(solution)/shard_map/ppermute | solution.py:466
  32.0 3.5 %collective-permute-start.16 = (f32[16,128]{1,0:T(8,128)S(1)}, f32[16,128]{1,0:T(8,128)S(1)}, u32[]{:S(2)}, u32[]{:S(2)}) collective-permute-start(f32[16,128]{1,0:T(8,128)S(1)} %shard_map.63.refs_2_), channel_id=1, source_target_pairs={{6,0},{7,1},{4,2},{5,3},{2,4},{3,5},{0,6},{1,7},{14,8},{15,9},{12,... | collective-permute-start | bytes 24584 | tf_op jit(solution)/shard_map/ppermute | solution.py:466
  35.5 1.3 %collective-permute-start.15 = (f32[16,128]{1,0:T(8,128)S(1)}, f32[16,128]{1,0:T(8,128)S(1)}, u32[]{:S(2)}, u32[]{:S(2)}) collective-permute-start(f32[16,128]{1,0:T(8,128)S(1)} %shard_map.63.refs_2_), channel_id=1, source_target_pairs={{4,0},{5,1},{6,2},{7,3},{0,4},{1,5},{2,6},{3,7},{12,8},{13,9},{14,... | collective-permute-start | bytes 24584 | tf_op jit(solution)/shard_map/ppermute | solution.py:466
  36.8 0.0 collective-permute-start.14
  36.8 0.7 %collective-permute-done.16.refs_5_ = f32[16,128]{1,0:T(8,128)S(1)} collective-permute-done((f32[16,128]{1,0:T(8,128)S(1)}, f32[16,128]{1,0:T(8,128)S(1)}, u32[]{:S(2)}, u32[]{:S(2)}) %collective-permute-start.16) | collective-permute-done | bytes 8224 | tf_op jit(solution)/shard_map/ppermute | solution.py:466
  37.5 2.6 %collective-permute-done.15.refs_4_ = f32[16,128]{1,0:T(8,128)S(1)} collective-permute-done((f32[16,128]{1,0:T(8,128)S(1)}, f32[16,128]{1,0:T(8,128)S(1)}, u32[]{:S(2)}, u32[]{:S(2)}) %collective-permute-start.15) | collective-permute-done | bytes 8224 | tf_op jit(solution)/shard_map/ppermute | solution.py:466
  40.1 0.4 collective-permute-done.14.refs_3_
  40.5 0.7 %shard_map.64 = f32[2,8,128]{2,1,0:T(8,128)} custom-call(f32[24,128]{1,0:T(8,128)S(1)} %shard_map.62.sum_ref.refs_0_, f32[24,128]{1,0:T(8,128)S(1)} %collective-permute-done.13.beside_ref.refs_1_, f32[16,128]{1,0:T(8,128)S(1)} %shard_map.63.refs_2_, f32[16,128]{1,0:T(8,128)S(1)} %collective-permute-done.14.refs_3_, ...), custom_call_target="tpu_custom_call" | custom-call | flops 100000 | bytes 10000 | tf_op jit(solution)/shard_map/pallas_call | solution.py:495
  (4 shorter events, 0.1 us)
Async XLA Ops:
  0.6 11.4 %collective-permute-start.4 = (f32[2,3,2,32,128]{4,3,2,1,0:T(8,128)}, f32[2,3,2,32,128]{4,3,2,1,0:T(8,128)S(1)}, u32[]{:S(2)}, u32[]{:S(2)}) collective-permute-start(f32[2,3,2,32,128]{4,3,2,1,0:T(8,128)} %forces_ref.1), channel_id=1, source_target_pairs={{3,1},{0,2},{5,3},{2,4},{7,5},{4,6},{1,0},{6,7},{11,9},{8,10},{13,... | collective-permute-start | bytes 589832 | tf_op jit(solution)/shard_map/ppermute | solution.py:508
  3.7 8.4 %collective-permute-start.3 = (f32[2,3,2,32,128]{4,3,2,1,0:T(8,128)}, f32[2,3,2,32,128]{4,3,2,1,0:T(8,128)S(1)}, u32[]{:S(2)}, u32[]{:S(2)}) collective-permute-start(f32[2,3,2,32,128]{4,3,2,1,0:T(8,128)} %forces_ref.1), channel_id=1, source_target_pairs={{2,1},{1,2},{4,3},{3,4},{6,5},{5,6},{0,0},{7,7},{10,9},{9,10},{12,... | collective-permute-start | bytes 589832 | tf_op jit(solution)/shard_map/ppermute | solution.py:508
  5.2 5.2 %collective-permute-start.1 = (f32[2,8,128]{2,1,0:T(8,128)}, f32[2,8,128]{2,1,0:T(8,128)S(1)}, u32[]{:S(2)}, u32[]{:S(2)}) collective-permute-start(f32[2,8,128]{2,1,0:T(8,128)} %refs_1_.1), channel_id=1, source_target_pairs={{24,0},{16,8},{8,16},{0,24},{25,1},{17,9},{9,17},{1,25},{26,2},{18... | collective-permute-start | bytes 24584 | tf_op jit(solution)/shard_map/ppermute | solution.py:466
  7.7 3.9 %collective-permute-start = (f32[2,8,128]{2,1,0:T(8,128)}, f32[2,8,128]{2,1,0:T(8,128)S(1)}, u32[]{:S(2)}, u32[]{:S(2)}) collective-permute-start(f32[2,8,128]{2,1,0:T(8,128)} %refs_1_.1), channel_id=1, source_target_pairs={{16,0},{24,8},{0,16},{8,24},{17,1},{25,9},{1,17},{9,25},{18,2},{26... | collective-permute-start | bytes 24584 | tf_op jit(solution)/shard_map/ppermute | solution.py:466
  8.2 3.9 %collective-permute-start.2 = (f32[2,8,128]{2,1,0:T(8,128)}, f32[2,8,128]{2,1,0:T(8,128)S(1)}, u32[]{:S(2)}, u32[]{:S(2)}) collective-permute-start(f32[2,8,128]{2,1,0:T(8,128)} %refs_1_.1), channel_id=1, source_target_pairs={{8,0},{0,8},{24,16},{16,24},{9,1},{1,9},{25,17},{17,25},{10,2},{2,... | collective-permute-start | bytes 24584 | tf_op jit(solution)/shard_map/ppermute | solution.py:466
  8.7 0.9 %copy-start = (f32[2,3,2,32,128]{4,3,2,1,0:T(8,128)S(1)}, f32[2,3,2,32,128]{4,3,2,1,0:T(8,128)}, u32[]{:S(2)}) copy-start(f32[2,3,2,32,128]{4,3,2,1,0:T(8,128)} %forces_ref.1) | copy-start | bytes 589828
  9.7 0.8 %copy-start.1 = (s32[2,32,128]{2,1,0:T(8,128)S(1)}, s32[2,32,128]{2,1,0:T(8,128)}, u32[]{:S(2)}) copy-start(s32[2,32,128]{2,1,0:T(8,128)} %labels_ref.1) | copy-start | bytes 98308
  10.4 1.6 %copy-start.2 = (f32[2,8,128]{2,1,0:T(8,128)S(1)}, f32[2,8,128]{2,1,0:T(8,128)}, u32[]{:S(2)}) copy-start(f32[2,8,128]{2,1,0:T(8,128)} %refs_1_.1) | copy-start | bytes 24580
  12.1 6.9 %copy-start.3 = (s32[8]{0:T(128)S(1)}, s32[8]{0:T(128)}, u32[]{:S(2)}) copy-start(s32[8]{0:T(128)} %refs_0_.1) | copy-start | bytes 100
  12.1 6.8 %collective-permute-start.5 = (f32[16,32,128]{2,1,0:T(8,128)S(1)}, f32[16,32,128]{2,1,0:T(8,128)S(1)}, u32[]{:S(2)}, u32[]{:S(2)}) collective-permute-start(f32[16,32,128]{2,1,0:T(8,128)S(1)} %get-tuple-element.10.refs_1_), channel_id=1, source_target_pairs={{1,0},{0,1},{3,2},{2,3},{5,4},{4,5},{7,6},{6,7},{9,8},{8,9},{11,10... | collective-permute-start | bytes 786440 | tf_op jit(solution)/shard_map/ppermute | solution.py:466
  12.6 6.4 %collective-permute-start.8 = (f32[2,3,2,32,128]{4,3,2,1,0:T(8,128)S(1)}, f32[2,3,2,32,128]{4,3,2,1,0:T(8,128)S(1)}, u32[]{:S(2)}, u32[]{:S(2)}) collective-permute-start(f32[2,3,2,32,128]{4,3,2,1,0:T(8,128)S(1)} %collective-permute-done.3.refs_5_.refs_4_), channel_id=1, source_target_pairs={{1,0},{0,1},{3,2},{2,3},{5,4},{4,5},{7,6},{6,7},{9,8},{8,9},{11,10... | collective-permute-start | bytes 589832 | tf_op jit(solution)/shard_map/ppermute | solution.py:466
  12.7 3.9 %collective-permute-start.9 = (f32[4,32,128]{2,1,0:T(8,128)S(1)}, f32[4,32,128]{2,1,0:T(8,128)S(1)}, u32[]{:S(2)}, u32[]{:S(2)}) collective-permute-start(f32[4,32,128]{2,1,0:T(8,128)S(1)} %get-tuple-element.11), channel_id=1, source_target_pairs={{3,1},{0,2},{5,3},{2,4},{7,5},{4,6},{1,0},{6,7},{11,9},{8,10},{13,... | collective-permute-start | bytes 196616 | tf_op jit(solution)/shard_map/ppermute | solution.py:528
  14.7 4.3 %collective-permute-start.7 = (f32[4,32,128]{2,1,0:T(8,128)S(1)}, f32[4,32,128]{2,1,0:T(8,128)S(1)}, u32[]{:S(2)}, u32[]{:S(2)}) collective-permute-start(f32[4,32,128]{2,1,0:T(8,128)S(1)} %get-tuple-element.11), channel_id=1, source_target_pairs={{2,0},{4,2},{1,3},{6,4},{3,5},{5,7},{0,1},{7,6},{10,8},{12,10},{9,... | collective-permute-start | bytes 196616 | tf_op jit(solution)/shard_map/ppermute | solution.py:526
  14.7 4.3 %collective-permute-start.6 = (f32[4,32,128]{2,1,0:T(8,128)S(1)}, f32[4,32,128]{2,1,0:T(8,128)S(1)}, u32[]{:S(2)}, u32[]{:S(2)}) collective-permute-start(f32[4,32,128]{2,1,0:T(8,128)S(1)} %get-tuple-element.11), channel_id=1, source_target_pairs={{2,1},{1,2},{4,3},{3,4},{6,5},{5,6},{0,0},{7,7},{10,9},{9,10},{12,... | collective-permute-start | bytes 196616 | tf_op jit(solution)/shard_map/ppermute | solution.py:528
  24.7 4.7 %collective-permute-start.10 = (f32[24,128]{1,0:T(8,128)S(1)}, f32[24,128]{1,0:T(8,128)S(1)}, u32[]{:S(2)}, u32[]{:S(2)}) collective-permute-start(f32[24,128]{1,0:T(8,128)S(1)} %get-tuple-element.13), channel_id=1, source_target_pairs={{24,0},{16,8},{8,16},{0,24},{25,1},{17,9},{9,17},{1,25},{26,2},{18... | collective-permute-start | bytes 36872 | tf_op jit(solution)/shard_map/ppermute | solution.py:466
  26.6 3.7 %collective-permute-start.11 = (f32[24,128]{1,0:T(8,128)S(1)}, f32[24,128]{1,0:T(8,128)S(1)}, u32[]{:S(2)}, u32[]{:S(2)}) collective-permute-start(f32[24,128]{1,0:T(8,128)S(1)} %get-tuple-element.14), channel_id=1, source_target_pairs={{16,0},{24,8},{0,16},{8,24},{17,1},{25,9},{1,17},{9,25},{18,2},{26... | collective-permute-start | bytes 36872 | tf_op jit(solution)/shard_map/ppermute | solution.py:466
  27.2 3.7 %collective-permute-start.12 = (f32[24,128]{1,0:T(8,128)S(1)}, f32[24,128]{1,0:T(8,128)S(1)}, u32[]{:S(2)}, u32[]{:S(2)}) collective-permute-start(f32[24,128]{1,0:T(8,128)S(1)} %get-tuple-element.15), channel_id=1, source_target_pairs={{8,0},{0,8},{24,16},{16,24},{9,1},{1,9},{25,17},{17,25},{10,2},{2,... | collective-permute-start | bytes 36872 | tf_op jit(solution)/shard_map/ppermute | solution.py:466
  30.9 1.2 %collective-permute-start.13 = (f32[24,128]{1,0:T(8,128)S(1)}, f32[24,128]{1,0:T(8,128)S(1)}, u32[]{:S(2)}, u32[]{:S(2)}) collective-permute-start(f32[24,128]{1,0:T(8,128)S(1)} %shard_map.62.sum_ref.refs_0_), channel_id=1, source_target_pairs={{1,0},{0,1},{3,2},{2,3},{5,4},{4,5},{7,6},{6,7},{9,8},{8,9},{11,10... | collective-permute-start | bytes 36872 | tf_op jit(solution)/shard_map/ppermute | solution.py:466
  32.0 5.4 %collective-permute-start.16 = (f32[16,128]{1,0:T(8,128)S(1)}, f32[16,128]{1,0:T(8,128)S(1)}, u32[]{:S(2)}, u32[]{:S(2)}) collective-permute-start(f32[16,128]{1,0:T(8,128)S(1)} %shard_map.63.refs_2_), channel_id=1, source_target_pairs={{6,0},{7,1},{4,2},{5,3},{2,4},{3,5},{0,6},{1,7},{14,8},{15,9},{12,... | collective-permute-start | bytes 24584 | tf_op jit(solution)/shard_map/ppermute | solution.py:466
  35.5 4.5 %collective-permute-start.15 = (f32[16,128]{1,0:T(8,128)S(1)}, f32[16,128]{1,0:T(8,128)S(1)}, u32[]{:S(2)}, u32[]{:S(2)}) collective-permute-start(f32[16,128]{1,0:T(8,128)S(1)} %shard_map.63.refs_2_), channel_id=1, source_target_pairs={{4,0},{5,1},{6,2},{7,3},{0,4},{1,5},{2,6},{3,7},{12,8},{13,9},{14,... | collective-permute-start | bytes 24584 | tf_op jit(solution)/shard_map/ppermute | solution.py:466
  36.8 3.7 %collective-permute-start.14 = (f32[16,128]{1,0:T(8,128)S(1)}, f32[16,128]{1,0:T(8,128)S(1)}, u32[]{:S(2)}, u32[]{:S(2)}) collective-permute-start(f32[16,128]{1,0:T(8,128)S(1)} %shard_map.63.refs_2_), channel_id=1, source_target_pairs={{2,0},{3,1},{0,2},{1,3},{6,4},{7,5},{4,6},{5,7},{10,8},{11,9},{8,1... | collective-permute-start | bytes 24584 | tf_op jit(solution)/shard_map/ppermute | solution.py:466

commit v11 on v8

--- a/solution.py
+++ b/solution.py
@@ -157,7 +157,7 @@
 
 
 def smooth_kernel(hops, count_gz, *refs):
-    blocks = 4 * hops
+    blocks = 4 * hops - 1
     weights_ref = refs[0]
     pack_refs = refs[1 : 1 + blocks]
     disp_hbm, own_ref = refs[1 + blocks : 3 + blocks]
@@ -185,7 +185,10 @@
             return [force_ref[group, kind, inner, chunk] for chunk in chunks]
 
         at = 4 * abs(hop) - 2
-        across = pick(*pack_refs[at : at + 2])
+        if abs(hop) == hops:
+            across = [pack_refs[at][plane, chunk] for chunk in chunks]
+        else:
+            across = pick(*pack_refs[at : at + 2])
         if abs(hop) == 1:
             beside = [pack_refs[1][plane, chunk] for chunk in chunks]
         else:
@@ -501,7 +504,7 @@
 
     planes = (cases * 3 + 2) * layers
     far_forces = [
-        lax.ppermute(forces, "gz", far_pairs(far, count_gz, True)) for far in range(1, hops + 1)
+        lax.ppermute(forces, "gz", far_pairs(far, count_gz, True)) for far in range(1, hops)
     ]
     pack = call(stage_kernel, shape(planes, rows, columns), (labels, forces), 2 * planes, 1_000_000)
     steps = [0] + list(range(2, count_load)) + [1]
@@ -512,16 +515,20 @@
         (pack, *densities, *far_forces),
         2 * planes + 6 * layers,
         100_000,
-        in_specs=[vmem] * (1 + count_load) + [pl.BlockSpec(memory_space=pl.ANY)] * hops,
+        in_specs=[vmem] * (1 + count_load) + [pl.BlockSpec(memory_space=pl.ANY)] * (hops - 1),
         out_specs=(vmem, vmem),
         input_output_aliases={0: 0},
     )
     packs = [pack, met(pack, "gz", 1)]
-    for far, forces_far in enumerate(far_forces, 1):
+    for far in range(1, hops + 1):
         if far > 1:
             packs.append(lax.ppermute(design, "gz", far_pairs(far, count_gz, False)))
             packs.append(met(far_forces[far - 2], "gz", 1))
-        packs += [lax.ppermute(design, "gz", far_pairs(far, count_gz, True)), forces_far]
+        if far < hops:
+            packs.append(lax.ppermute(design, "gz", far_pairs(far, count_gz, True)))
+            packs.append(far_forces[far - 1])
+        else:
+            packs.append(lax.ppermute(pack, "gz", far_pairs(far, count_gz, True)))
 
     slot_rows = -(-(layers * wide + 1) // 8) * 8
     scratch = [

time: 41.5 us -> 40.9 us (0.986)
  starting transfers between devices: 19.8 us -> 18.2 us
  waiting for transfers between devices: 12.5 us -> 13.5 us
    ppermute x2 -> x1, starting transfers between devices: 4.61 us -> 1.58 us  [on_device(): lax.ppermute(forces, 'gz', far_pairs(far, count_gz, True))]
    ppermute x12, starting transfers between devices: 12.5 us -> 14 us  [met(): lax.ppermute(block, axis, [(partner(i, step), i) for i in range(count)])]
    ppermute x1, waiting for transfers between devices: 2.36 us -> 3.6 us  [on_device(): packs.append(lax.ppermute(design, 'gz', far_pairs(far, count_gz, False)))]
    ppermute x2, waiting for transfers between devices: 1.24 us -> 0.01 us  [the longest x1 0.01 us: on_device(): packs.append(lax.ppermute(design, 'gz', far_pairs(far, count_gz, True)))]
    ppermute x12, waiting for transfers between devices: 8.9 us -> 9.92 us  [met(): lax.ppermute(block, axis, [(partner(i, step), i) for i in range(count)])]
  transfers between devices with their start and end apart: 17 -> 16, of which waited for: 11 -> 9; matrix products, arithmetic and copies ran while one was open for 0% -> 0% of each run, Pallas kernels for 0% -> 0%
where the time goes in v11:
time: 40.9 us; the launch traced here: 40.7 us
  starting transfers between devices  18.2 us (44%)
  waiting for transfers between devices  13.5 us (33%)
  Pallas kernels  6.54 us (16%)
  local copies, waits for them, and re-layouts  1.69 us (4%)
  between operations  0.71 us (2%)
    ppermute x12, starting transfers between devices, met(): lax.ppermute(block, axis, [(partner(i, step), i) for i in range(count)])  14 us
    ppermute x12, waiting for transfers between devices, met(): lax.ppermute(block, axis, [(partner(i, step), i) for i in range(count)])  9.92 us
    pallas_call x6, Pallas kernels, call(): pl.pallas_call(kernel, out_shape=out, in_specs=in_specs or [vmem] * len(a...  6.54 us
    ppermute x1, waiting for transfers between devices, on_device(): packs.append(lax.ppermute(design, 'gz', far_pairs(far, count_gz, False)))  3.6 us
    ppermute x1, starting transfers between devices, on_device(): packs.append(lax.ppermute(pack, 'gz', far_pairs(far, count_gz, True)))  2 us
    unnamed x8, local copies, waits for them, and re-layouts  1.69 us
    ppermute x1, starting transfers between devices, on_device(): lax.ppermute(forces, 'gz', far_pairs(far, count_gz, True))  1.58 us
  transfers between devices with their start and end apart: 16, of which 9 were waited for; matrix products, arithmetic and copies ran while one was open for 0% of the time, Pallas kernels for 0%

profile of v11, /device:TPU:0, one launch (start us, length us, event | category | flops | bytes accessed | tf_op | source)
XLA Modules:
  0.0 40.7 jit_solution(11027988030989631123)
XLA Ops:
  0.6 1.6 %collective-permute-start.3 = (f32[2,3,2,32,128]{4,3,2,1,0:T(8,128)}, f32[2,3,2,32,128]{4,3,2,1,0:T(8,128)S(1)}, u32[]{:S(2)}, u32[]{:S(2)}) collective-permute-start(f32[2,3,2,32,128]{4,3,2,1,0:T(8,128)} %forces_ref.1), channel_id=1, source_target_pairs={{2,1},{1,2},{4,3},{3,4},{6,5},{5,6},{0,0},{7,7},{10,9},{9,10},{12,... | collective-permute-start | bytes 589832 | tf_op jit(solution)/shard_map/ppermute | solution.py:507
  2.2 3.9 %collective-permute-start.1 = (f32[2,8,128]{2,1,0:T(8,128)}, f32[2,8,128]{2,1,0:T(8,128)S(1)}, u32[]{:S(2)}, u32[]{:S(2)}) collective-permute-start(f32[2,8,128]{2,1,0:T(8,128)} %refs_1_.1), channel_id=1, source_target_pairs={{24,0},{16,8},{8,16},{0,24},{25,1},{17,9},{9,17},{1,25},{26,2},{18... | collective-permute-start | bytes 24584 | tf_op jit(solution)/shard_map/ppermute | solution.py:465
  6.1 0.5 %collective-permute-start = (f32[2,8,128]{2,1,0:T(8,128)}, f32[2,8,128]{2,1,0:T(8,128)S(1)}, u32[]{:S(2)}, u32[]{:S(2)}) collective-permute-start(f32[2,8,128]{2,1,0:T(8,128)} %refs_1_.1), channel_id=1, source_target_pairs={{16,0},{24,8},{0,16},{8,24},{17,1},{25,9},{1,17},{9,25},{18,2},{26... | collective-permute-start | bytes 24584 | tf_op jit(solution)/shard_map/ppermute | solution.py:465
  6.6 0.1 collective-permute-start.2
  6.7 0.0 copy-start
  6.7 0.9 %copy-done = f32[2,3,2,32,128]{4,3,2,1,0:T(8,128)S(1)} copy-done((f32[2,3,2,32,128]{4,3,2,1,0:T(8,128)S(1)}, f32[2,3,2,32,128]{4,3,2,1,0:T(8,128)}, u32[]{:S(2)}) %copy-start) | copy-done | bytes 196632
  7.6 0.0 copy-start.1
  7.6 0.8 %copy-done.1 = s32[2,32,128]{2,1,0:T(8,128)S(1)} copy-done((s32[2,32,128]{2,1,0:T(8,128)S(1)}, s32[2,32,128]{2,1,0:T(8,128)}, u32[]{:S(2)}) %copy-start.1) | copy-done | bytes 32792
  8.4 0.0 copy-start.2
  8.4 0.0 collective-permute-done.1.refs_3_
  8.4 1.6 %collective-permute-done.refs_2_ = f32[2,8,128]{2,1,0:T(8,128)S(1)} collective-permute-done((f32[2,8,128]{2,1,0:T(8,128)}, f32[2,8,128]{2,1,0:T(8,128)S(1)}, u32[]{:S(2)}, u32[]{:S(2)}) %collective-permute-start) | collective-permute-done | bytes 8224 | tf_op jit(solution)/shard_map/ppermute | solution.py:465
  10.0 0.5 %collective-permute-done.2.refs_4_ = f32[2,8,128]{2,1,0:T(8,128)S(1)} collective-permute-done((f32[2,8,128]{2,1,0:T(8,128)}, f32[2,8,128]{2,1,0:T(8,128)S(1)}, u32[]{:S(2)}, u32[]{:S(2)}) %collective-permute-start.2) | collective-permute-done | bytes 8224 | tf_op jit(solution)/shard_map/ppermute | solution.py:465
  10.5 0.0 collective-permute-done.3.refs_5_.refs_4_
  10.5 0.0 copy-done.2
  10.5 0.0 copy-start.3
  10.5 2.0 %collective-permute-start.8 = (f32[16,32,128]{2,1,0:T(8,128)S(1)}, f32[16,32,128]{2,1,0:T(8,128)S(1)}, u32[]{:S(2)}, u32[]{:S(2)}) collective-permute-start(f32[16,32,128]{2,1,0:T(8,128)S(1)} %get-tuple-element.10.refs_1_), channel_id=1, source_target_pairs={{3,1},{0,2},{5,3},{2,4},{7,5},{4,6},{1,0},{6,7},{11,9},{8,10},{13,... | collective-permute-start | bytes 786440 | tf_op jit(solution)/shard_map/ppermute | solution.py:531
  12.5 0.0 collective-permute-start.4
  12.5 0.5 %collective-permute-start.7 = (f32[2,3,2,32,128]{4,3,2,1,0:T(8,128)S(1)}, f32[2,3,2,32,128]{4,3,2,1,0:T(8,128)S(1)}, u32[]{:S(2)}, u32[]{:S(2)}) collective-permute-start(f32[2,3,2,32,128]{4,3,2,1,0:T(8,128)S(1)} %collective-permute-done.3.refs_5_.refs_4_), channel_id=1, source_target_pairs={{1,0},{0,1},{3,2},{2,3},{5,4},{4,5},{7,6},{6,7},{9,8},{8,9},{11,10... | collective-permute-start | bytes 589832 | tf_op jit(solution)/shard_map/ppermute | solution.py:465
  13.0 0.0 collective-permute-start.6
  13.0 0.7 %collective-permute-start.5 = (f32[4,32,128]{2,1,0:T(8,128)S(1)}, f32[4,32,128]{2,1,0:T(8,128)S(1)}, u32[]{:S(2)}, u32[]{:S(2)}) collective-permute-start(f32[4,32,128]{2,1,0:T(8,128)S(1)} %get-tuple-element.11), channel_id=1, source_target_pairs={{2,1},{1,2},{4,3},{3,4},{6,5},{5,6},{0,0},{7,7},{10,9},{9,10},{12,... | collective-permute-start | bytes 196616 | tf_op jit(solution)/shard_map/ppermute | solution.py:528
  13.7 3.6 %collective-permute-done.6.refs_5_ = f32[4,32,128]{2,1,0:T(8,128)S(1)} collective-permute-done((f32[4,32,128]{2,1,0:T(8,128)S(1)}, f32[4,32,128]{2,1,0:T(8,128)S(1)}, u32[]{:S(2)}, u32[]{:S(2)}) %collective-permute-start.6) | collective-permute-done | bytes 65568 | tf_op jit(solution)/shard_map/ppermute | solution.py:525
  17.3 0.0 collective-permute-done.5.refs_3_
  17.3 0.0 collective-permute-done.7.refs_6_
  17.3 0.0 collective-permute-done.8.refs_7_
  17.3 0.0 collective-permute-done.4.refs_2_
  17.3 0.0 copy-done.3
  17.3 5.8 %shard_map.61 = (f32[2,3,2,32,128]{4,3,2,1,0:T(8,128)}, f32[3,2,8,128]{3,2,1,0:T(8,128)S(1)}, f32[24,128]{1,0:T(8,128)S(1)}, f32[24,128]{1,0:T(8,128)S(1)}, f32[...) custom-call(s32[8]{0:T(128)S(1)} %copy-done.3, f32[16,32,128]{2,1,0:T(8,128)S(1)} %get-tuple-element.10.refs_1_, ...), custom_call_target="tpu_custom_call" | custom-call | flops 60000000 | bytes 6000000 | tf_op jit(solution)/shard_map/pallas_call | solution.py:494
  23.1 2.1 %collective-permute-start.9 = (f32[24,128]{1,0:T(8,128)S(1)}, f32[24,128]{1,0:T(8,128)S(1)}, u32[]{:S(2)}, u32[]{:S(2)}) collective-permute-start(f32[24,128]{1,0:T(8,128)S(1)} %get-tuple-element.13), channel_id=1, source_target_pairs={{24,0},{16,8},{8,16},{0,24},{25,1},{17,9},{9,17},{1,25},{26,2},{18... | collective-permute-start | bytes 36872 | tf_op jit(solution)/shard_map/ppermute | solution.py:465
  25.2 0.5 %collective-permute-start.10 = (f32[24,128]{1,0:T(8,128)S(1)}, f32[24,128]{1,0:T(8,128)S(1)}, u32[]{:S(2)}, u32[]{:S(2)}) collective-permute-start(f32[24,128]{1,0:T(8,128)S(1)} %get-tuple-element.14), channel_id=1, source_target_pairs={{16,0},{24,8},{0,16},{8,24},{17,1},{25,9},{1,17},{9,25},{18,2},{26... | collective-permute-start | bytes 36872 | tf_op jit(solution)/shard_map/ppermute | solution.py:465
  25.7 0.9 %collective-permute-start.11 = (f32[24,128]{1,0:T(8,128)S(1)}, f32[24,128]{1,0:T(8,128)S(1)}, u32[]{:S(2)}, u32[]{:S(2)}) collective-permute-start(f32[24,128]{1,0:T(8,128)S(1)} %get-tuple-element.15), channel_id=1, source_target_pairs={{8,0},{0,8},{24,16},{16,24},{9,1},{1,9},{25,17},{17,25},{10,2},{2,... | collective-permute-start | bytes 36872 | tf_op jit(solution)/shard_map/ppermute | solution.py:465
  26.6 1.1 %collective-permute-done.9.refs_1_ = f32[24,128]{1,0:T(8,128)S(1)} collective-permute-done((f32[24,128]{1,0:T(8,128)S(1)}, f32[24,128]{1,0:T(8,128)S(1)}, u32[]{:S(2)}, u32[]{:S(2)}) %collective-permute-start.9) | collective-permute-done | bytes 12320 | tf_op jit(solution)/shard_map/ppermute | solution.py:465
  27.8 1.2 %collective-permute-done.10.refs_2_ = f32[24,128]{1,0:T(8,128)S(1)} collective-permute-done((f32[24,128]{1,0:T(8,128)S(1)}, f32[24,128]{1,0:T(8,128)S(1)}, u32[]{:S(2)}, u32[]{:S(2)}) %collective-permute-start.10) | collective-permute-done | bytes 12320 | tf_op jit(solution)/shard_map/ppermute | solution.py:465
  28.9 0.6 %collective-permute-done.11.refs_3_ = f32[24,128]{1,0:T(8,128)S(1)} collective-permute-done((f32[24,128]{1,0:T(8,128)S(1)}, f32[24,128]{1,0:T(8,128)S(1)}, u32[]{:S(2)}, u32[]{:S(2)}) %collective-permute-start.11) | collective-permute-done | bytes 12320 | tf_op jit(solution)/shard_map/ppermute | solution.py:465
  29.6 0.2 collective-permute-start.12
  29.8 1.0 %collective-permute-done.12.beside_ref.refs_1_ = f32[24,128]{1,0:T(8,128)S(1)} collective-permute-done((f32[24,128]{1,0:T(8,128)S(1)}, f32[24,128]{1,0:T(8,128)S(1)}, u32[]{:S(2)}, u32[]{:S(2)}) %collective-permute-start.12) | collective-permute-done | bytes 12320 | tf_op jit(solution)/shard_map/ppermute | solution.py:465
  30.8 4.6 %collective-permute-start.15 = (f32[16,128]{1,0:T(8,128)S(1)}, f32[16,128]{1,0:T(8,128)S(1)}, u32[]{:S(2)}, u32[]{:S(2)}) collective-permute-start(f32[16,128]{1,0:T(8,128)S(1)} %shard_map.63.refs_2_), channel_id=1, source_target_pairs={{6,0},{7,1},{4,2},{5,3},{2,4},{3,5},{0,6},{1,7},{14,8},{15,9},{12,... | collective-permute-start | bytes 24584 | tf_op jit(solution)/shard_map/ppermute | solution.py:465
  35.4 0.0 collective-permute-start.14
  35.4 0.6 %collective-permute-start.13 = (f32[16,128]{1,0:T(8,128)S(1)}, f32[16,128]{1,0:T(8,128)S(1)}, u32[]{:S(2)}, u32[]{:S(2)}) collective-permute-start(f32[16,128]{1,0:T(8,128)S(1)} %shard_map.63.refs_2_), channel_id=1, source_target_pairs={{2,0},{3,1},{0,2},{1,3},{6,4},{7,5},{4,6},{5,7},{10,8},{11,9},{8,1... | collective-permute-start | bytes 24584 | tf_op jit(solution)/shard_map/ppermute | solution.py:465
  36.0 1.0 %collective-permute-done.15.refs_5_ = f32[16,128]{1,0:T(8,128)S(1)} collective-permute-done((f32[16,128]{1,0:T(8,128)S(1)}, f32[16,128]{1,0:T(8,128)S(1)}, u32[]{:S(2)}, u32[]{:S(2)}) %collective-permute-start.15) | collective-permute-done | bytes 8224 | tf_op jit(solution)/shard_map/ppermute | solution.py:465
  37.0 2.9 %collective-permute-done.14.refs_4_ = f32[16,128]{1,0:T(8,128)S(1)} collective-permute-done((f32[16,128]{1,0:T(8,128)S(1)}, f32[16,128]{1,0:T(8,128)S(1)}, u32[]{:S(2)}, u32[]{:S(2)}) %collective-permute-start.14) | collective-permute-done | bytes 8224 | tf_op jit(solution)/shard_map/ppermute | solution.py:465
  39.9 0.0 collective-permute-done.13.refs_3_
  39.9 0.7 %shard_map.64 = f32[2,8,128]{2,1,0:T(8,128)} custom-call(f32[24,128]{1,0:T(8,128)S(1)} %shard_map.62.sum_ref.refs_0_, f32[24,128]{1,0:T(8,128)S(1)} %collective-permute-done.12.beside_ref.refs_1_, f32[16,128]{1,0:T(8,128)S(1)} %shard_map.63.refs_2_, f32[16,128]{1,0:T(8,128)S(1)} %collective-permute-done.13.refs_3_, ...), custom_call_target="tpu_custom_call" | custom-call | flops 100000 | bytes 10000 | tf_op jit(solution)/shard_map/pallas_call | solution.py:494
  (4 shorter events, 0.0 us)
Async XLA Ops:
  0.6 9.9 %collective-permute-start.3 = (f32[2,3,2,32,128]{4,3,2,1,0:T(8,128)}, f32[2,3,2,32,128]{4,3,2,1,0:T(8,128)S(1)}, u32[]{:S(2)}, u32[]{:S(2)}) collective-permute-start(f32[2,3,2,32,128]{4,3,2,1,0:T(8,128)} %forces_ref.1), channel_id=1, source_target_pairs={{2,1},{1,2},{4,3},{3,4},{6,5},{5,6},{0,0},{7,7},{10,9},{9,10},{12,... | collective-permute-start | bytes 589832 | tf_op jit(solution)/shard_map/ppermute | solution.py:507
  2.2 6.2 %collective-permute-start.1 = (f32[2,8,128]{2,1,0:T(8,128)}, f32[2,8,128]{2,1,0:T(8,128)S(1)}, u32[]{:S(2)}, u32[]{:S(2)}) collective-permute-start(f32[2,8,128]{2,1,0:T(8,128)} %refs_1_.1), channel_id=1, source_target_pairs={{24,0},{16,8},{8,16},{0,24},{25,1},{17,9},{9,17},{1,25},{26,2},{18... | collective-permute-start | bytes 24584 | tf_op jit(solution)/shard_map/ppermute | solution.py:465
  6.1 3.9 %collective-permute-start = (f32[2,8,128]{2,1,0:T(8,128)}, f32[2,8,128]{2,1,0:T(8,128)S(1)}, u32[]{:S(2)}, u32[]{:S(2)}) collective-permute-start(f32[2,8,128]{2,1,0:T(8,128)} %refs_1_.1), channel_id=1, source_target_pairs={{16,0},{24,8},{0,16},{8,24},{17,1},{25,9},{1,17},{9,25},{18,2},{26... | collective-permute-start | bytes 24584 | tf_op jit(solution)/shard_map/ppermute | solution.py:465
  6.6 3.9 %collective-permute-start.2 = (f32[2,8,128]{2,1,0:T(8,128)}, f32[2,8,128]{2,1,0:T(8,128)S(1)}, u32[]{:S(2)}, u32[]{:S(2)}) collective-permute-start(f32[2,8,128]{2,1,0:T(8,128)} %refs_1_.1), channel_id=1, source_target_pairs={{8,0},{0,8},{24,16},{16,24},{9,1},{1,9},{25,17},{17,25},{10,2},{2,... | collective-permute-start | bytes 24584 | tf_op jit(solution)/shard_map/ppermute | solution.py:465
  6.7 0.9 %copy-start = (f32[2,3,2,32,128]{4,3,2,1,0:T(8,128)S(1)}, f32[2,3,2,32,128]{4,3,2,1,0:T(8,128)}, u32[]{:S(2)}) copy-start(f32[2,3,2,32,128]{4,3,2,1,0:T(8,128)} %forces_ref.1) | copy-start | bytes 589828
  7.6 0.8 %copy-start.1 = (s32[2,32,128]{2,1,0:T(8,128)S(1)}, s32[2,32,128]{2,1,0:T(8,128)}, u32[]{:S(2)}) copy-start(s32[2,32,128]{2,1,0:T(8,128)} %labels_ref.1) | copy-start | bytes 98308
  8.4 2.1 %copy-start.2 = (f32[2,8,128]{2,1,0:T(8,128)S(1)}, f32[2,8,128]{2,1,0:T(8,128)}, u32[]{:S(2)}) copy-start(f32[2,8,128]{2,1,0:T(8,128)} %refs_1_.1) | copy-start | bytes 24580
  10.5 6.8 %copy-start.3 = (s32[8]{0:T(128)S(1)}, s32[8]{0:T(128)}, u32[]{:S(2)}) copy-start(s32[8]{0:T(128)} %refs_0_.1) | copy-start | bytes 100
  10.5 6.8 %collective-permute-start.8 = (f32[16,32,128]{2,1,0:T(8,128)S(1)}, f32[16,32,128]{2,1,0:T(8,128)S(1)}, u32[]{:S(2)}, u32[]{:S(2)}) collective-permute-start(f32[16,32,128]{2,1,0:T(8,128)S(1)} %get-tuple-element.10.refs_1_), channel_id=1, source_target_pairs={{3,1},{0,2},{5,3},{2,4},{7,5},{4,6},{1,0},{6,7},{11,9},{8,10},{13,... | collective-permute-start | bytes 786440 | tf_op jit(solution)/shard_map/ppermute | solution.py:531
  12.5 4.8 %collective-permute-start.4 = (f32[16,32,128]{2,1,0:T(8,128)S(1)}, f32[16,32,128]{2,1,0:T(8,128)S(1)}, u32[]{:S(2)}, u32[]{:S(2)}) collective-permute-start(f32[16,32,128]{2,1,0:T(8,128)S(1)} %get-tuple-element.10.refs_1_), channel_id=1, source_target_pairs={{1,0},{0,1},{3,2},{2,3},{5,4},{4,5},{7,6},{6,7},{9,8},{8,9},{11,10... | collective-permute-start | bytes 786440 | tf_op jit(solution)/shard_map/ppermute | solution.py:465
  12.5 4.8 %collective-permute-start.7 = (f32[2,3,2,32,128]{4,3,2,1,0:T(8,128)S(1)}, f32[2,3,2,32,128]{4,3,2,1,0:T(8,128)S(1)}, u32[]{:S(2)}, u32[]{:S(2)}) collective-permute-start(f32[2,3,2,32,128]{4,3,2,1,0:T(8,128)S(1)} %collective-permute-done.3.refs_5_.refs_4_), channel_id=1, source_target_pairs={{1,0},{0,1},{3,2},{2,3},{5,4},{4,5},{7,6},{6,7},{9,8},{8,9},{11,10... | collective-permute-start | bytes 589832 | tf_op jit(solution)/shard_map/ppermute | solution.py:465
  13.0 4.3 %collective-permute-start.6 = (f32[4,32,128]{2,1,0:T(8,128)S(1)}, f32[4,32,128]{2,1,0:T(8,128)S(1)}, u32[]{:S(2)}, u32[]{:S(2)}) collective-permute-start(f32[4,32,128]{2,1,0:T(8,128)S(1)} %get-tuple-element.11), channel_id=1, source_target_pairs={{2,0},{4,2},{1,3},{6,4},{3,5},{5,7},{0,1},{7,6},{10,8},{12,10},{9,... | collective-permute-start | bytes 196616 | tf_op jit(solution)/shard_map/ppermute | solution.py:525
  13.0 4.3 %collective-permute-start.5 = (f32[4,32,128]{2,1,0:T(8,128)S(1)}, f32[4,32,128]{2,1,0:T(8,128)S(1)}, u32[]{:S(2)}, u32[]{:S(2)}) collective-permute-start(f32[4,32,128]{2,1,0:T(8,128)S(1)} %get-tuple-element.11), channel_id=1, source_target_pairs={{2,1},{1,2},{4,3},{3,4},{6,5},{5,6},{0,0},{7,7},{10,9},{9,10},{12,... | collective-permute-start | bytes 196616 | tf_op jit(solution)/shard_map/ppermute | solution.py:528
  23.1 4.7 %collective-permute-start.9 = (f32[24,128]{1,0:T(8,128)S(1)}, f32[24,128]{1,0:T(8,128)S(1)}, u32[]{:S(2)}, u32[]{:S(2)}) collective-permute-start(f32[24,128]{1,0:T(8,128)S(1)} %get-tuple-element.13), channel_id=1, source_target_pairs={{24,0},{16,8},{8,16},{0,24},{25,1},{17,9},{9,17},{1,25},{26,2},{18... | collective-permute-start | bytes 36872 | tf_op jit(solution)/shard_map/ppermute | solution.py:465
  25.2 3.7 %collective-permute-start.10 = (f32[24,128]{1,0:T(8,128)S(1)}, f32[24,128]{1,0:T(8,128)S(1)}, u32[]{:S(2)}, u32[]{:S(2)}) collective-permute-start(f32[24,128]{1,0:T(8,128)S(1)} %get-tuple-element.14), channel_id=1, source_target_pairs={{16,0},{24,8},{0,16},{8,24},{17,1},{25,9},{1,17},{9,25},{18,2},{26... | collective-permute-start | bytes 36872 | tf_op jit(solution)/shard_map/ppermute | solution.py:465
  25.7 3.8 %collective-permute-start.11 = (f32[24,128]{1,0:T(8,128)S(1)}, f32[24,128]{1,0:T(8,128)S(1)}, u32[]{:S(2)}, u32[]{:S(2)}) collective-permute-start(f32[24,128]{1,0:T(8,128)S(1)} %get-tuple-element.15), channel_id=1, source_target_pairs={{8,0},{0,8},{24,16},{16,24},{9,1},{1,9},{25,17},{17,25},{10,2},{2,... | collective-permute-start | bytes 36872 | tf_op jit(solution)/shard_map/ppermute | solution.py:465
  29.6 1.2 %collective-permute-start.12 = (f32[24,128]{1,0:T(8,128)S(1)}, f32[24,128]{1,0:T(8,128)S(1)}, u32[]{:S(2)}, u32[]{:S(2)}) collective-permute-start(f32[24,128]{1,0:T(8,128)S(1)} %shard_map.62.sum_ref.refs_0_), channel_id=1, source_target_pairs={{1,0},{0,1},{3,2},{2,3},{5,4},{4,5},{7,6},{6,7},{9,8},{8,9},{11,10... | collective-permute-start | bytes 36872 | tf_op jit(solution)/shard_map/ppermute | solution.py:465
  30.8 6.3 %collective-permute-start.15 = (f32[16,128]{1,0:T(8,128)S(1)}, f32[16,128]{1,0:T(8,128)S(1)}, u32[]{:S(2)}, u32[]{:S(2)}) collective-permute-start(f32[16,128]{1,0:T(8,128)S(1)} %shard_map.63.refs_2_), channel_id=1, source_target_pairs={{6,0},{7,1},{4,2},{5,3},{2,4},{3,5},{0,6},{1,7},{14,8},{15,9},{12,... | collective-permute-start | bytes 24584 | tf_op jit(solution)/shard_map/ppermute | solution.py:465
  35.4 4.5 %collective-permute-start.14 = (f32[16,128]{1,0:T(8,128)S(1)}, f32[16,128]{1,0:T(8,128)S(1)}, u32[]{:S(2)}, u32[]{:S(2)}) collective-permute-start(f32[16,128]{1,0:T(8,128)S(1)} %shard_map.63.refs_2_), channel_id=1, source_target_pairs={{4,0},{5,1},{6,2},{7,3},{0,4},{1,5},{2,6},{3,7},{12,8},{13,9},{14,... | collective-permute-start | bytes 24584 | tf_op jit(solution)/shard_map/ppermute | solution.py:465
  35.4 4.5 %collective-permute-start.13 = (f32[16,128]{1,0:T(8,128)S(1)}, f32[16,128]{1,0:T(8,128)S(1)}, u32[]{:S(2)}, u32[]{:S(2)}) collective-permute-start(f32[16,128]{1,0:T(8,128)S(1)} %shard_map.63.refs_2_), channel_id=1, source_target_pairs={{2,0},{3,1},{0,2},{1,3},{6,4},{7,5},{4,6},{5,7},{10,8},{11,9},{8,1... | collective-permute-start | bytes 24584 | tf_op jit(solution)/shard_map/ppermute | solution.py:465

commit v12 on v11

--- a/solution.py
+++ b/solution.py
@@ -506,16 +506,17 @@
     far_forces = [
         lax.ppermute(forces, "gz", far_pairs(far, count_gz, True)) for far in range(1, hops)
     ]
+    beside_forces = [met(block, "gz", 1) for block in far_forces]
     pack = call(stage_kernel, shape(planes, rows, columns), (labels, forces), 2 * planes, 1_000_000)
     steps = [0] + list(range(2, count_load)) + [1]
     densities = [density] + [met(density, "load", step) for step in steps[1:]]
     pack, design = call(
         functools.partial(design_kernel, cases, steps),
         (shape(planes, rows, columns), shape(2 * layers, rows, columns)),
-        (pack, *densities, *far_forces),
+        (pack, *densities, *far_forces, *beside_forces),
         2 * planes + 6 * layers,
         100_000,
-        in_specs=[vmem] * (1 + count_load) + [pl.BlockSpec(memory_space=pl.ANY)] * (hops - 1),
+        in_specs=[vmem] * (1 + count_load) + [pl.BlockSpec(memory_space=pl.ANY)] * (2 * (hops - 1)),
         out_specs=(vmem, vmem),
         input_output_aliases={0: 0},
     )
@@ -523,7 +524,7 @@
     for far in range(1, hops + 1):
         if far > 1:
             packs.append(lax.ppermute(design, "gz", far_pairs(far, count_gz, False)))
-            packs.append(met(far_forces[far - 2], "gz", 1))
+            packs.append(beside_forces[far - 2])
         if far < hops:
             packs.append(lax.ppermute(design, "gz", far_pairs(far, count_gz, True)))
             packs.append(far_forces[far - 1])

time: 40.9 us -> 45.6 us (1.11)
  starting transfers between devices: 18.2 us -> 24.4 us
  waiting for transfers between devices: 13.5 us -> 12.1 us
    ppermute x12, starting transfers between devices: 14 us -> 19.8 us  [met(): lax.ppermute(block, axis, [(partner(i, step), i) for i in range(count)])]
    ppermute x12, waiting for transfers between devices: 9.92 us -> 8.57 us  [met(): lax.ppermute(block, axis, [(partner(i, step), i) for i in range(count)])]
    ppermute x1, starting transfers between devices: 0.01 us -> 0.51 us  [on_device(): packs.append(lax.ppermute(design, 'gz', far_pairs(far, count_gz, False)))]
    ppermute x1, waiting for transfers between devices: 3.6 us -> 3.1 us  [on_device(): packs.append(lax.ppermute(design, 'gz', far_pairs(far, count_gz, False)))]
  transfers between devices with their start and end apart: 16 -> 16, of which waited for: 9 -> 10; matrix products, arithmetic and copies ran while one was open for 0% -> 0% of each run, Pallas kernels for 0% -> 0%
where the time goes in v12:
time: 45.6 us; the launch traced here: 45.4 us
  starting transfers between devices  24.4 us (54%)
  waiting for transfers between devices  12.1 us (27%)
  Pallas kernels  6.52 us (14%)
  local copies, waits for them, and re-layouts  1.69 us (4%)
  between operations  0.69 us (2%)
    ppermute x12, starting transfers between devices, met(): lax.ppermute(block, axis, [(partner(i, step), i) for i in range(count)])  19.8 us
    ppermute x12, waiting for transfers between devices, met(): lax.ppermute(block, axis, [(partner(i, step), i) for i in range(count)])  8.57 us
    pallas_call x6, Pallas kernels, call(): pl.pallas_call(kernel, out_shape=out, in_specs=in_specs or [vmem] * len(a...  6.52 us
    ppermute x1, waiting for transfers between devices, on_device(): packs.append(lax.ppermute(design, 'gz', far_pairs(far, count_gz, False)))  3.1 us
    ppermute x1, starting transfers between devices, on_device(): packs.append(lax.ppermute(pack, 'gz', far_pairs(far, count_gz, True)))  1.78 us
    unnamed x8, local copies, waits for them, and re-layouts  1.69 us
    ppermute x1, starting transfers between devices, on_device(): lax.ppermute(forces, 'gz', far_pairs(far, count_gz, True))  1.58 us
  transfers between devices with their start and end apart: 16, of which 10 were waited for; matrix products, arithmetic and copies ran while one was open for 0% of the time, Pallas kernels for 0%

profile of v12, /device:TPU:0, one launch (start us, length us, event | category | flops | bytes accessed | tf_op | source)
XLA Modules:
  0.0 45.4 jit_solution(12002541863454731014)
XLA Ops:
  0.6 1.6 %collective-permute-start.3 = (f32[2,3,2,32,128]{4,3,2,1,0:T(8,128)}, f32[2,3,2,32,128]{4,3,2,1,0:T(8,128)S(1)}, u32[]{:S(2)}, u32[]{:S(2)}) collective-permute-start(f32[2,3,2,32,128]{4,3,2,1,0:T(8,128)} %forces_ref.1), channel_id=1, source_target_pairs={{2,1},{1,2},{4,3},{3,4},{6,5},{5,6},{0,0},{7,7},{10,9},{9,10},{12,... | collective-permute-start | bytes 589832 | tf_op jit(solution)/shard_map/ppermute | solution.py:507
  2.2 0.0 collective-permute-done.3.refs_5_.refs_4_
  2.2 7.0 %collective-permute-start.4 = (f32[2,3,2,32,128]{4,3,2,1,0:T(8,128)S(1)}, f32[2,3,2,32,128]{4,3,2,1,0:T(8,128)S(1)}, u32[]{:S(2)}, u32[]{:S(2)}) collective-permute-start(f32[2,3,2,32,128]{4,3,2,1,0:T(8,128)S(1)} %collective-permute-done.3.refs_5_.refs_4_), channel_id=1, source_target_pairs={{1,0},{0,1},{3,2},{2,3},{5,4},{4,5},{7,6},{6,7},{9,8},{8,9},{11,10... | collective-permute-start | bytes 589832 | tf_op jit(solution)/shard_map/ppermute | solution.py:465
  9.2 2.4 %collective-permute-start.1 = (f32[2,8,128]{2,1,0:T(8,128)}, f32[2,8,128]{2,1,0:T(8,128)S(1)}, u32[]{:S(2)}, u32[]{:S(2)}) collective-permute-start(f32[2,8,128]{2,1,0:T(8,128)} %refs_1_.1), channel_id=1, source_target_pairs={{24,0},{16,8},{8,16},{0,24},{25,1},{17,9},{9,17},{1,25},{26,2},{18... | collective-permute-start | bytes 24584 | tf_op jit(solution)/shard_map/ppermute | solution.py:465
  11.7 0.5 %collective-permute-start = (f32[2,8,128]{2,1,0:T(8,128)}, f32[2,8,128]{2,1,0:T(8,128)S(1)}, u32[]{:S(2)}, u32[]{:S(2)}) collective-permute-start(f32[2,8,128]{2,1,0:T(8,128)} %refs_1_.1), channel_id=1, source_target_pairs={{16,0},{24,8},{0,16},{8,24},{17,1},{25,9},{1,17},{9,25},{18,2},{26... | collective-permute-start | bytes 24584 | tf_op jit(solution)/shard_map/ppermute | solution.py:465
  12.2 0.5 %collective-permute-start.2 = (f32[2,8,128]{2,1,0:T(8,128)}, f32[2,8,128]{2,1,0:T(8,128)S(1)}, u32[]{:S(2)}, u32[]{:S(2)}) collective-permute-start(f32[2,8,128]{2,1,0:T(8,128)} %refs_1_.1), channel_id=1, source_target_pairs={{8,0},{0,8},{24,16},{16,24},{9,1},{1,9},{25,17},{17,25},{10,2},{2,... | collective-permute-start | bytes 24584 | tf_op jit(solution)/shard_map/ppermute | solution.py:465
  12.7 0.0 copy-start
  12.7 0.9 %copy-done = f32[2,3,2,32,128]{4,3,2,1,0:T(8,128)S(1)} copy-done((f32[2,3,2,32,128]{4,3,2,1,0:T(8,128)S(1)}, f32[2,3,2,32,128]{4,3,2,1,0:T(8,128)}, u32[]{:S(2)}) %copy-start) | copy-done | bytes 196632
  13.7 0.0 copy-start.1
  13.7 0.8 %copy-done.1 = s32[2,32,128]{2,1,0:T(8,128)S(1)} copy-done((s32[2,32,128]{2,1,0:T(8,128)S(1)}, s32[2,32,128]{2,1,0:T(8,128)}, u32[]{:S(2)}) %copy-start.1) | copy-done | bytes 32792
  14.4 0.0 copy-start.2
  14.4 0.0 collective-permute-done.1.refs_3_
  14.4 1.1 %collective-permute-done.refs_2_ = f32[2,8,128]{2,1,0:T(8,128)S(1)} collective-permute-done((f32[2,8,128]{2,1,0:T(8,128)}, f32[2,8,128]{2,1,0:T(8,128)S(1)}, u32[]{:S(2)}, u32[]{:S(2)}) %collective-permute-start) | collective-permute-done | bytes 8224 | tf_op jit(solution)/shard_map/ppermute | solution.py:465
  15.5 0.5 %collective-permute-done.2.refs_4_ = f32[2,8,128]{2,1,0:T(8,128)S(1)} collective-permute-done((f32[2,8,128]{2,1,0:T(8,128)}, f32[2,8,128]{2,1,0:T(8,128)S(1)}, u32[]{:S(2)}, u32[]{:S(2)}) %collective-permute-start.2) | collective-permute-done | bytes 8224 | tf_op jit(solution)/shard_map/ppermute | solution.py:465
  16.1 0.0 collective-permute-done.4.refs_6_
  16.1 0.0 copy-done.2
  16.1 0.0 copy-start.3
  16.1 1.8 %collective-permute-start.8 = (f32[16,32,128]{2,1,0:T(8,128)S(1)}, f32[16,32,128]{2,1,0:T(8,128)S(1)}, u32[]{:S(2)}, u32[]{:S(2)}) collective-permute-start(f32[16,32,128]{2,1,0:T(8,128)S(1)} %get-tuple-element.10.refs_1_), channel_id=1, source_target_pairs={{3,1},{0,2},{5,3},{2,4},{7,5},{4,6},{1,0},{6,7},{11,9},{8,10},{13,... | collective-permute-start | bytes 786440 | tf_op jit(solution)/shard_map/ppermute | solution.py:532
  17.9 0.0 collective-permute-start.5
  17.9 0.5 %collective-permute-start.7 = (f32[4,32,128]{2,1,0:T(8,128)S(1)}, f32[4,32,128]{2,1,0:T(8,128)S(1)}, u32[]{:S(2)}, u32[]{:S(2)}) collective-permute-start(f32[4,32,128]{2,1,0:T(8,128)S(1)} %get-tuple-element.11), channel_id=1, source_target_pairs={{2,0},{4,2},{1,3},{6,4},{3,5},{5,7},{0,1},{7,6},{10,8},{12,10},{9,... | collective-permute-start | bytes 196616 | tf_op jit(solution)/shard_map/ppermute | solution.py:526
  18.4 0.7 %collective-permute-start.6 = (f32[4,32,128]{2,1,0:T(8,128)S(1)}, f32[4,32,128]{2,1,0:T(8,128)S(1)}, u32[]{:S(2)}, u32[]{:S(2)}) collective-permute-start(f32[4,32,128]{2,1,0:T(8,128)S(1)} %get-tuple-element.11), channel_id=1, source_target_pairs={{2,1},{1,2},{4,3},{3,4},{6,5},{5,6},{0,0},{7,7},{10,9},{9,10},{12,... | collective-permute-start | bytes 196616 | tf_op jit(solution)/shard_map/ppermute | solution.py:529
  19.0 3.1 %collective-permute-done.7.refs_5_ = f32[4,32,128]{2,1,0:T(8,128)S(1)} collective-permute-done((f32[4,32,128]{2,1,0:T(8,128)S(1)}, f32[4,32,128]{2,1,0:T(8,128)S(1)}, u32[]{:S(2)}, u32[]{:S(2)}) %collective-permute-start.7) | collective-permute-done | bytes 65568 | tf_op jit(solution)/shard_map/ppermute | solution.py:526
  22.1 0.0 collective-permute-done.6.refs_3_
  22.1 0.4 collective-permute-done.8.refs_7_
  22.6 0.0 collective-permute-done.5.refs_2_
  22.6 0.0 copy-done.3
  22.6 5.7 %shard_map.61 = (f32[2,3,2,32,128]{4,3,2,1,0:T(8,128)}, f32[3,2,8,128]{3,2,1,0:T(8,128)S(1)}, f32[24,128]{1,0:T(8,128)S(1)}, f32[24,128]{1,0:T(8,128)S(1)}, f32[...) custom-call(s32[8]{0:T(128)S(1)} %copy-done.3, f32[16,32,128]{2,1,0:T(8,128)S(1)} %get-tuple-element.10.refs_1_, ...), custom_call_target="tpu_custom_call" | custom-call | flops 60000000 | bytes 6000000 | tf_op jit(solution)/shard_map/pallas_call | solution.py:494
  28.3 1.6 %collective-permute-start.9 = (f32[24,128]{1,0:T(8,128)S(1)}, f32[24,128]{1,0:T(8,128)S(1)}, u32[]{:S(2)}, u32[]{:S(2)}) collective-permute-start(f32[24,128]{1,0:T(8,128)S(1)} %get-tuple-element.13), channel_id=1, source_target_pairs={{24,0},{16,8},{8,16},{0,24},{25,1},{17,9},{9,17},{1,25},{26,2},{18... | collective-permute-start | bytes 36872 | tf_op jit(solution)/shard_map/ppermute | solution.py:465
  29.9 0.5 %collective-permute-start.10 = (f32[24,128]{1,0:T(8,128)S(1)}, f32[24,128]{1,0:T(8,128)S(1)}, u32[]{:S(2)}, u32[]{:S(2)}) collective-permute-start(f32[24,128]{1,0:T(8,128)S(1)} %get-tuple-element.14), channel_id=1, source_target_pairs={{16,0},{24,8},{0,16},{8,24},{17,1},{25,9},{1,17},{9,25},{18,2},{26... | collective-permute-start | bytes 36872 | tf_op jit(solution)/shard_map/ppermute | solution.py:465
  30.4 1.5 %collective-permute-start.11 = (f32[24,128]{1,0:T(8,128)S(1)}, f32[24,128]{1,0:T(8,128)S(1)}, u32[]{:S(2)}, u32[]{:S(2)}) collective-permute-start(f32[24,128]{1,0:T(8,128)S(1)} %get-tuple-element.15), channel_id=1, source_target_pairs={{8,0},{0,8},{24,16},{16,24},{9,1},{1,9},{25,17},{17,25},{10,2},{2,... | collective-permute-start | bytes 36872 | tf_op jit(solution)/shard_map/ppermute | solution.py:465
  31.9 1.1 %collective-permute-done.9.refs_1_ = f32[24,128]{1,0:T(8,128)S(1)} collective-permute-done((f32[24,128]{1,0:T(8,128)S(1)}, f32[24,128]{1,0:T(8,128)S(1)}, u32[]{:S(2)}, u32[]{:S(2)}) %collective-permute-start.9) | collective-permute-done | bytes 12320 | tf_op jit(solution)/shard_map/ppermute | solution.py:465
  33.0 0.6 %collective-permute-done.10.refs_2_ = f32[24,128]{1,0:T(8,128)S(1)} collective-permute-done((f32[24,128]{1,0:T(8,128)S(1)}, f32[24,128]{1,0:T(8,128)S(1)}, u32[]{:S(2)}, u32[]{:S(2)}) %collective-permute-start.10) | collective-permute-done | bytes 12320 | tf_op jit(solution)/shard_map/ppermute | solution.py:465
  33.6 0.5 %collective-permute-done.11.refs_3_ = f32[24,128]{1,0:T(8,128)S(1)} collective-permute-done((f32[24,128]{1,0:T(8,128)S(1)}, f32[24,128]{1,0:T(8,128)S(1)}, u32[]{:S(2)}, u32[]{:S(2)}) %collective-permute-start.11) | collective-permute-done | bytes 12320 | tf_op jit(solution)/shard_map/ppermute | solution.py:465
  34.1 1.0 %collective-permute-start.12 = (f32[24,128]{1,0:T(8,128)S(1)}, f32[24,128]{1,0:T(8,128)S(1)}, u32[]{:S(2)}, u32[]{:S(2)}) collective-permute-start(f32[24,128]{1,0:T(8,128)S(1)} %shard_map.62.sum_ref.refs_0_), channel_id=1, source_target_pairs={{1,0},{0,1},{3,2},{2,3},{5,4},{4,5},{7,6},{6,7},{9,8},{8,9},{11,10... | collective-permute-start | bytes 36872 | tf_op jit(solution)/shard_map/ppermute | solution.py:465
  35.1 0.8 %collective-permute-done.12.beside_ref.refs_1_ = f32[24,128]{1,0:T(8,128)S(1)} collective-permute-done((f32[24,128]{1,0:T(8,128)S(1)}, f32[24,128]{1,0:T(8,128)S(1)}, u32[]{:S(2)}, u32[]{:S(2)}) %collective-permute-start.12) | collective-permute-done | bytes 12320 | tf_op jit(solution)/shard_map/ppermute | solution.py:465
  35.9 4.2 %collective-permute-start.15 = (f32[16,128]{1,0:T(8,128)S(1)}, f32[16,128]{1,0:T(8,128)S(1)}, u32[]{:S(2)}, u32[]{:S(2)}) collective-permute-start(f32[16,128]{1,0:T(8,128)S(1)} %shard_map.63.refs_2_), channel_id=1, source_target_pairs={{6,0},{7,1},{4,2},{5,3},{2,4},{3,5},{0,6},{1,7},{14,8},{15,9},{12,... | collective-permute-start | bytes 24584 | tf_op jit(solution)/shard_map/ppermute | solution.py:465
  40.1 0.0 collective-permute-start.14
  40.1 0.6 %collective-permute-start.13 = (f32[16,128]{1,0:T(8,128)S(1)}, f32[16,128]{1,0:T(8,128)S(1)}, u32[]{:S(2)}, u32[]{:S(2)}) collective-permute-start(f32[16,128]{1,0:T(8,128)S(1)} %shard_map.63.refs_2_), channel_id=1, source_target_pairs={{2,0},{3,1},{0,2},{1,3},{6,4},{7,5},{4,6},{5,7},{10,8},{11,9},{8,1... | collective-permute-start | bytes 24584 | tf_op jit(solution)/shard_map/ppermute | solution.py:465
  40.7 1.0 %collective-permute-done.15.refs_5_ = f32[16,128]{1,0:T(8,128)S(1)} collective-permute-done((f32[16,128]{1,0:T(8,128)S(1)}, f32[16,128]{1,0:T(8,128)S(1)}, u32[]{:S(2)}, u32[]{:S(2)}) %collective-permute-start.15) | collective-permute-done | bytes 8224 | tf_op jit(solution)/shard_map/ppermute | solution.py:465
  41.7 2.9 %collective-permute-done.14.refs_4_ = f32[16,128]{1,0:T(8,128)S(1)} collective-permute-done((f32[16,128]{1,0:T(8,128)S(1)}, f32[16,128]{1,0:T(8,128)S(1)}, u32[]{:S(2)}, u32[]{:S(2)}) %collective-permute-start.14) | collective-permute-done | bytes 8224 | tf_op jit(solution)/shard_map/ppermute | solution.py:465
  44.6 0.0 collective-permute-done.13.refs_3_
  44.6 0.7 %shard_map.64 = f32[2,8,128]{2,1,0:T(8,128)} custom-call(f32[24,128]{1,0:T(8,128)S(1)} %shard_map.62.sum_ref.refs_0_, f32[24,128]{1,0:T(8,128)S(1)} %collective-permute-done.12.beside_ref.refs_1_, f32[16,128]{1,0:T(8,128)S(1)} %shard_map.63.refs_2_, f32[16,128]{1,0:T(8,128)S(1)} %collective-permute-done.13.refs_3_, ...), custom_call_target="tpu_custom_call" | custom-call | flops 100000 | bytes 10000 | tf_op jit(solution)/shard_map/pallas_call | solution.py:494
  (4 shorter events, 0.0 us)
Async XLA Ops:
  0.6 1.6 %collective-permute-start.3 = (f32[2,3,2,32,128]{4,3,2,1,0:T(8,128)}, f32[2,3,2,32,128]{4,3,2,1,0:T(8,128)S(1)}, u32[]{:S(2)}, u32[]{:S(2)}) collective-permute-start(f32[2,3,2,32,128]{4,3,2,1,0:T(8,128)} %forces_ref.1), channel_id=1, source_target_pairs={{2,1},{1,2},{4,3},{3,4},{6,5},{5,6},{0,0},{7,7},{10,9},{9,10},{12,... | collective-permute-start | bytes 589832 | tf_op jit(solution)/shard_map/ppermute | solution.py:507
  2.2 13.8 %collective-permute-start.4 = (f32[2,3,2,32,128]{4,3,2,1,0:T(8,128)S(1)}, f32[2,3,2,32,128]{4,3,2,1,0:T(8,128)S(1)}, u32[]{:S(2)}, u32[]{:S(2)}) collective-permute-start(f32[2,3,2,32,128]{4,3,2,1,0:T(8,128)S(1)} %collective-permute-done.3.refs_5_.refs_4_), channel_id=1, source_target_pairs={{1,0},{0,1},{3,2},{2,3},{5,4},{4,5},{7,6},{6,7},{9,8},{8,9},{11,10... | collective-permute-start | bytes 589832 | tf_op jit(solution)/shard_map/ppermute | solution.py:465
  9.2 5.2 %collective-permute-start.1 = (f32[2,8,128]{2,1,0:T(8,128)}, f32[2,8,128]{2,1,0:T(8,128)S(1)}, u32[]{:S(2)}, u32[]{:S(2)}) collective-permute-start(f32[2,8,128]{2,1,0:T(8,128)} %refs_1_.1), channel_id=1, source_target_pairs={{24,0},{16,8},{8,16},{0,24},{25,1},{17,9},{9,17},{1,25},{26,2},{18... | collective-permute-start | bytes 24584 | tf_op jit(solution)/shard_map/ppermute | solution.py:465
  11.7 3.9 %collective-permute-start = (f32[2,8,128]{2,1,0:T(8,128)}, f32[2,8,128]{2,1,0:T(8,128)S(1)}, u32[]{:S(2)}, u32[]{:S(2)}) collective-permute-start(f32[2,8,128]{2,1,0:T(8,128)} %refs_1_.1), channel_id=1, source_target_pairs={{16,0},{24,8},{0,16},{8,24},{17,1},{25,9},{1,17},{9,25},{18,2},{26... | collective-permute-start | bytes 24584 | tf_op jit(solution)/shard_map/ppermute | solution.py:465
  12.2 3.9 %collective-permute-start.2 = (f32[2,8,128]{2,1,0:T(8,128)}, f32[2,8,128]{2,1,0:T(8,128)S(1)}, u32[]{:S(2)}, u32[]{:S(2)}) collective-permute-start(f32[2,8,128]{2,1,0:T(8,128)} %refs_1_.1), channel_id=1, source_target_pairs={{8,0},{0,8},{24,16},{16,24},{9,1},{1,9},{25,17},{17,25},{10,2},{2,... | collective-permute-start | bytes 24584 | tf_op jit(solution)/shard_map/ppermute | solution.py:465
  12.7 0.9 %copy-start = (f32[2,3,2,32,128]{4,3,2,1,0:T(8,128)S(1)}, f32[2,3,2,32,128]{4,3,2,1,0:T(8,128)}, u32[]{:S(2)}) copy-start(f32[2,3,2,32,128]{4,3,2,1,0:T(8,128)} %forces_ref.1) | copy-start | bytes 589828
  13.7 0.8 %copy-start.1 = (s32[2,32,128]{2,1,0:T(8,128)S(1)}, s32[2,32,128]{2,1,0:T(8,128)}, u32[]{:S(2)}) copy-start(s32[2,32,128]{2,1,0:T(8,128)} %labels_ref.1) | copy-start | bytes 98308
  14.4 1.6 %copy-start.2 = (f32[2,8,128]{2,1,0:T(8,128)S(1)}, f32[2,8,128]{2,1,0:T(8,128)}, u32[]{:S(2)}) copy-start(f32[2,8,128]{2,1,0:T(8,128)} %refs_1_.1) | copy-start | bytes 24580
  16.1 6.5 %copy-start.3 = (s32[8]{0:T(128)S(1)}, s32[8]{0:T(128)}, u32[]{:S(2)}) copy-start(s32[8]{0:T(128)} %refs_0_.1) | copy-start | bytes 100
  16.1 6.5 %collective-permute-start.8 = (f32[16,32,128]{2,1,0:T(8,128)S(1)}, f32[16,32,128]{2,1,0:T(8,128)S(1)}, u32[]{:S(2)}, u32[]{:S(2)}) collective-permute-start(f32[16,32,128]{2,1,0:T(8,128)S(1)} %get-tuple-element.10.refs_1_), channel_id=1, source_target_pairs={{3,1},{0,2},{5,3},{2,4},{7,5},{4,6},{1,0},{6,7},{11,9},{8,10},{13,... | collective-permute-start | bytes 786440 | tf_op jit(solution)/shard_map/ppermute | solution.py:532
  17.9 4.7 %collective-permute-start.5 = (f32[16,32,128]{2,1,0:T(8,128)S(1)}, f32[16,32,128]{2,1,0:T(8,128)S(1)}, u32[]{:S(2)}, u32[]{:S(2)}) collective-permute-start(f32[16,32,128]{2,1,0:T(8,128)S(1)} %get-tuple-element.10.refs_1_), channel_id=1, source_target_pairs={{1,0},{0,1},{3,2},{2,3},{5,4},{4,5},{7,6},{6,7},{9,8},{8,9},{11,10... | collective-permute-start | bytes 786440 | tf_op jit(solution)/shard_map/ppermute | solution.py:465
  17.9 4.3 %collective-permute-start.7 = (f32[4,32,128]{2,1,0:T(8,128)S(1)}, f32[4,32,128]{2,1,0:T(8,128)S(1)}, u32[]{:S(2)}, u32[]{:S(2)}) collective-permute-start(f32[4,32,128]{2,1,0:T(8,128)S(1)} %get-tuple-element.11), channel_id=1, source_target_pairs={{2,0},{4,2},{1,3},{6,4},{3,5},{5,7},{0,1},{7,6},{10,8},{12,10},{9,... | collective-permute-start | bytes 196616 | tf_op jit(solution)/shard_map/ppermute | solution.py:526
  18.4 3.8 %collective-permute-start.6 = (f32[4,32,128]{2,1,0:T(8,128)S(1)}, f32[4,32,128]{2,1,0:T(8,128)S(1)}, u32[]{:S(2)}, u32[]{:S(2)}) collective-permute-start(f32[4,32,128]{2,1,0:T(8,128)S(1)} %get-tuple-element.11), channel_id=1, source_target_pairs={{2,1},{1,2},{4,3},{3,4},{6,5},{5,6},{0,0},{7,7},{10,9},{9,10},{12,... | collective-permute-start | bytes 196616 | tf_op jit(solution)/shard_map/ppermute | solution.py:529
  28.3 4.7 %collective-permute-start.9 = (f32[24,128]{1,0:T(8,128)S(1)}, f32[24,128]{1,0:T(8,128)S(1)}, u32[]{:S(2)}, u32[]{:S(2)}) collective-permute-start(f32[24,128]{1,0:T(8,128)S(1)} %get-tuple-element.13), channel_id=1, source_target_pairs={{24,0},{16,8},{8,16},{0,24},{25,1},{17,9},{9,17},{1,25},{26,2},{18... | collective-permute-start | bytes 36872 | tf_op jit(solution)/shard_map/ppermute | solution.py:465
  29.9 3.7 %collective-permute-start.10 = (f32[24,128]{1,0:T(8,128)S(1)}, f32[24,128]{1,0:T(8,128)S(1)}, u32[]{:S(2)}, u32[]{:S(2)}) collective-permute-start(f32[24,128]{1,0:T(8,128)S(1)} %get-tuple-element.14), channel_id=1, source_target_pairs={{16,0},{24,8},{0,16},{8,24},{17,1},{25,9},{1,17},{9,25},{18,2},{26... | collective-permute-start | bytes 36872 | tf_op jit(solution)/shard_map/ppermute | solution.py:465
  30.4 3.7 %collective-permute-start.11 = (f32[24,128]{1,0:T(8,128)S(1)}, f32[24,128]{1,0:T(8,128)S(1)}, u32[]{:S(2)}, u32[]{:S(2)}) collective-permute-start(f32[24,128]{1,0:T(8,128)S(1)} %get-tuple-element.15), channel_id=1, source_target_pairs={{8,0},{0,8},{24,16},{16,24},{9,1},{1,9},{25,17},{17,25},{10,2},{2,... | collective-permute-start | bytes 36872 | tf_op jit(solution)/shard_map/ppermute | solution.py:465
  34.1 1.8 %collective-permute-start.12 = (f32[24,128]{1,0:T(8,128)S(1)}, f32[24,128]{1,0:T(8,128)S(1)}, u32[]{:S(2)}, u32[]{:S(2)}) collective-permute-start(f32[24,128]{1,0:T(8,128)S(1)} %shard_map.62.sum_ref.refs_0_), channel_id=1, source_target_pairs={{1,0},{0,1},{3,2},{2,3},{5,4},{4,5},{7,6},{6,7},{9,8},{8,9},{11,10... | collective-permute-start | bytes 36872 | tf_op jit(solution)/shard_map/ppermute | solution.py:465
  35.9 5.8 %collective-permute-start.15 = (f32[16,128]{1,0:T(8,128)S(1)}, f32[16,128]{1,0:T(8,128)S(1)}, u32[]{:S(2)}, u32[]{:S(2)}) collective-permute-start(f32[16,128]{1,0:T(8,128)S(1)} %shard_map.63.refs_2_), channel_id=1, source_target_pairs={{6,0},{7,1},{4,2},{5,3},{2,4},{3,5},{0,6},{1,7},{14,8},{15,9},{12,... | collective-permute-start | bytes 24584 | tf_op jit(solution)/shard_map/ppermute | solution.py:465
  40.1 4.5 %collective-permute-start.14 = (f32[16,128]{1,0:T(8,128)S(1)}, f32[16,128]{1,0:T(8,128)S(1)}, u32[]{:S(2)}, u32[]{:S(2)}) collective-permute-start(f32[16,128]{1,0:T(8,128)S(1)} %shard_map.63.refs_2_), channel_id=1, source_target_pairs={{4,0},{5,1},{6,2},{7,3},{0,4},{1,5},{2,6},{3,7},{12,8},{13,9},{14,... | collective-permute-start | bytes 24584 | tf_op jit(solution)/shard_map/ppermute | solution.py:465
  40.1 4.5 %collective-permute-start.13 = (f32[16,128]{1,0:T(8,128)S(1)}, f32[16,128]{1,0:T(8,128)S(1)}, u32[]{:S(2)}, u32[]{:S(2)}) collective-permute-start(f32[16,128]{1,0:T(8,128)S(1)} %shard_map.63.refs_2_), channel_id=1, source_target_pairs={{2,0},{3,1},{0,2},{1,3},{6,4},{7,5},{4,6},{5,7},{10,8},{11,9},{8,1... | collective-permute-start | bytes 24584 | tf_op jit(solution)/shard_map/ppermute | solution.py:465
